TPU v7x, 32 devices: a whole 2x2x4 slice. The times are simulated.
32 devices in a mesh: groups: 2 (over y), gx: 4 (over x, core), gy: 4 (over z).
Axes of the slice: x: 2, y: 2, z: 4, core: 2. Of those that a mesh axis runs over, the one named last changes fastest.
Arguments:
- fine_features: bfloat16 [8, 4, 32, 4096], P(('groups', 'gx'), 'gy'), parts along dimension 0, may hold values from -6 to 6
- coarse_items: bfloat16 [8, 4, 64, 1024], P(('groups', 'gx'), 'gy'), parts along dimension 0, may hold values from -6 to 6
- conv_weight: bfloat16 [27, 64, 64], replicated, may hold values from -0.15625 to 0.15625
- up_weight: bfloat16 [8, 128, 64], replicated, may hold values from -0.5 to 0.5
- neighbours: int32 [8, 4, 32, 27], P(('groups', 'gx'), 'gy'), parts along dimension 0, may hold values from 0 to 64, as said below
- side_sends: int32 [8, 4, 2, 8], P(('groups', 'gx'), 'gy'), parts along dimension 0, may hold values from 0 to 31
- cross_sends: int32 [8, 4, 2, 8], P(('groups', 'gx'), 'gy'), parts along dimension 0, may hold values from 0 to 47
- parent_slots: int32 [8, 4, 32], P(('groups', 'gx'), 'gy'), parts along dimension 0, may hold values from 0 to 63, as said below
- coarse_sends: int32 [8, 4, 16, 4], P(('groups', 'gx'), 'gy'), parts along dimension 0, may hold values from 0 to 64, as said below
- cotangent: bfloat16 [8, 4, 32, 4096], P(('groups', 'gx'), 'gy'), parts along dimension 0, may hold values from -6 to 6
Outputs:
- conv_out: bfloat16 [8, 4, 32, 4096], P(('groups', 'gx'), 'gy'), parts along dimension 0
- grad_fine: bfloat16 [8, 4, 32, 4096], P(('groups', 'gx'), 'gy'), parts along dimension 0
- grad_coarse: bfloat16 [8, 4, 64, 1024], P(('groups', 'gx'), 'gy'), parts along dimension 0
- grad_conv: float32 [54, 64, 64], P('groups'), parts along dimension 0
- grad_up: float32 [16, 128, 64], P('groups'), parts along dimension 0
There are 2 independent parts, one for each index of `groups`. A program takes and returns all parts, laid end to end along the dimension named above; an argument that names none is the same for every part. Nothing has to cross between parts.
Inputs may be any that keep to these rules, and one draw needn't show every extreme that they name: `neighbours`: entry 13 of brick b's row is b itself; the value 65 - 1 names the zero row (an empty neighbour brick). `parent_slots`: the 32 values of one device are distinct and each names a slot that its owner fills; some pair of devices fills all 4 slots. `coarse_sends`: each owned item is named at most once over all destinations; 64 marks an empty slot.
All inputs are finite; a program needn't handle non-finite values.
Results may differ from a plain program's by a relative error of at most 0.0052.
Values may be sent and summed in bfloat16 or wider, within the bound.
No kernel may reach another device: no remote copies, remote signals or barrier semaphores. Data moves between devices by JAX's collectives and lax.ppermute only.
A program may use at most 192 MiB of HBM per device.

v0:
```python
import functools
import math

import jax
import jax.numpy as jnp
from jax import lax
from jax.experimental import pallas as pl
from jax.experimental.pallas import tpu as pltpu
from jax.sharding import PartitionSpec as P

BF = jnp.bfloat16
F32 = jnp.float32
I32 = jnp.int32

C = 64
RUN = 4 * C
WIDE = RUN + 2 * C


def iota(shape, axis):
    return lax.broadcasted_iota(I32, shape, axis)


def ones_where(mask):
    return jnp.where(mask, 1.0, 0.0).astype(BF)


def dot(a, b):
    return jnp.dot(a, b, preferred_element_type=F32)


def dot_tn(a, b):
    return lax.dot_general(a, b, (((0,), (0,)), ((), ())), preferred_element_type=F32)


def dot_nt(a, b):
    return lax.dot_general(a, b, (((1,), (1,)), ((), ())), preferred_element_type=F32)


def column_of(row):
    size = row.shape[1]
    diagonal = iota((size, size), 0) == iota((size, size), 1)
    spread = jnp.broadcast_to(row.astype(F32), (size, size))
    return jnp.sum(jnp.where(diagonal, spread, 0.0), axis=1, keepdims=True).astype(I32)


def call(body, outs, *args, scratch=(), flops=0):
    moved = sum(a.size * a.dtype.itemsize for a in list(args) + list(outs))
    return pl.pallas_call(
        body,
        out_shape=tuple(outs),
        scratch_shapes=tuple(scratch),
        cost_estimate=pl.CostEstimate(flops=flops, bytes_accessed=moved, transcendentals=0),
        compiler_params=pltpu.CompilerParams(vmem_limit_bytes=28 * 2**20),
    )(*args)


def shape(dims, dtype=BF):
    return jax.ShapeDtypeStruct(dims, dtype)


def send_index(sends, group):
    capacity, devices = sends.shape
    lanes = devices * group
    spread = ones_where(iota((devices, lanes), 1) // group == iota((devices, lanes), 0))
    rows = dot(sends.astype(F32).astype(BF), spread)
    slot = iota((capacity, lanes), 1) % group
    picked = jnp.where(slot // 2 == iota((capacity, lanes), 0), rows, 0.0)
    return jnp.sum(picked, axis=0, keepdims=True).astype(I32)


def items_out_body(sends_ref, items_ref, out_ref):
    capacity, devices = sends_ref.shape
    count, width = items_ref.shape
    half = width // 2
    index = send_index(sends_ref[...], 2 * capacity)
    lanes = index.shape[1]
    odd = iota((count, lanes), 1) % 2
    named = iota((count, lanes), 0) == index
    total = dot_tn(ones_where(named & (odd == 0)), items_ref[:, :half])
    total += dot_tn(ones_where(named & (odd == 1)), items_ref[:, half:])
    out_ref[...] = total.astype(BF)


def merge_body(received_ref, slots_ref, up_ref, fine_ref, sides_ref, merged_ref, parents_ref, a_ref, b_ref):
    bricks = fine_ref.shape[0]
    lanes, half = received_ref.shape
    slot = column_of(slots_ref[...])
    place = iota((bricks, lanes), 1)
    named = place // 2 == slot
    received = received_ref[...]
    parents = jnp.concatenate(
        [dot(ones_where(named & (place % 2 == h)), received) for h in (0, 1)], axis=1
    ).astype(BF)
    coarse = 2 * half // 8
    stacked = jnp.concatenate([parents[:, v * coarse : (v + 1) * coarse] for v in range(8)], axis=0)
    parents_ref[...] = stacked
    lifted = dot_nt(stacked, up_ref[...])
    for v in range(8):
        cx, cy, cz = (v // 4, v // 2 % 2, v % 2)
        for parity in range(4):
            vx, vy = (2 * cx + parity // 2, 2 * cy + parity % 2)
            at = (vx * 4 + vy) * RUN + cz * 2 * C
            add = lifted[v * bricks : (v + 1) * bricks, parity * 2 * C : (parity + 1) * 2 * C]
            merged_ref[:, at : at + 2 * C] = (fine_ref[:, at : at + 2 * C].astype(F32) + add).astype(BF)
    pick_rows(sides_ref[...], merged_ref[...], a_ref, b_ref)


def pick_rows(lists, rows, a_ref, b_ref):
    count = rows.shape[0]
    for which, out_ref in ((0, a_ref), (1, b_ref)):
        face = lists.shape[1]
        chosen = ones_where(iota((count, face), 0) == lists[which : which + 1])
        out_ref[...] = dot_tn(chosen, rows).astype(BF)


def stack_rows(*refs):
    return jnp.concatenate([r[...].astype(F32) for r in refs], axis=0).astype(BF)


def cross_body(merged_ref, low_ref, high_ref, crosses_ref, a_ref, b_ref):
    rows = jnp.concatenate([merged_ref[...], stack_rows(low_ref, high_ref)], axis=0)
    pick_rows(crosses_ref[...], rows, a_ref, b_ref)


def build_bands(weight_ref, band_ref):
    zero = jnp.zeros((C, C), BF)
    blank = jnp.zeros((C, 2 * C), BF)

    def pair(a, b):
        return jnp.concatenate([a, b], axis=1)

    for e in range(9):
        low, mid, high = (weight_ref[3 * e + z] for z in range(3))
        first, second = (pair(mid, low), pair(high, mid))
        left, right = (pair(low, zero), pair(zero, high))
        rows = (
            (first, blank),
            (second, left),
            (right, first),
            (blank, second),
            (blank, right),
            (left, blank),
        )
        for z, halves in enumerate(rows):
            for s in range(2):
                band_ref[e, z * C : (z + 1) * C, s * 2 * C : (s + 1) * 2 * C] = halves[s]


def options(at):
    return [(at + 1, 0)] + ([(5, 1)] if at == 0 else []) + ([(0, -1)] if at == 3 else [])


def offset_of(dx, dy, dz):
    return (dx + 1) * 9 + (dy + 1) * 3 + dz + 1


def stack_runs(ref):
    return jnp.concatenate([ref[:, p * RUN : (p + 1) * RUN] for p in range(16)], axis=0)


def split_two(value):
    head = value.astype(BF)
    return head, (value - head.astype(F32)).astype(BF)


def table_grad_body(cot_ref, weight_ref, near_ref, ext_ref, low_ref, high_ref, band_ref, pad_ref):
    bricks = cot_ref.shape[0]
    face = low_ref.shape[0]
    start = ext_ref.shape[0]
    rows = start + 2 * face
    build_bands(weight_ref, band_ref)
    cot = stack_runs(cot_ref)
    pad_ref[...] = jnp.zeros(pad_ref.shape, F32)
    for e in range(9):
        ex, ey = (e // 3, e % 3)
        part = dot_nt(cot, band_ref[e]).reshape(4, 4, bricks, WIDE)
        pad_ref[ex : ex + 4, ey : ey + 4] += part
    near = [near_ref[o] for o in range(27)]

    def chooser(which):
        index = jnp.concatenate([near[o] for o in which], axis=1)
        return ones_where(iota((rows, index.shape[1]), 0) == index)

    lower_half = iota((rows, 2 * C), 1) < C
    cache = {}
    for x in range(4):
        for y in range(4):
            places = [(X, Y, dx, dy) for X, dx in options(x) for Y, dy in options(y)]
            key = tuple((dx, dy) for _, _, dx, dy in places)
            if key not in cache:
                moved = [d for d in key if d != (0, 0)]
                main = chooser([offset_of(*d, 0) for d in moved] * 2) if moved else None
                up = chooser([offset_of(*d, 1) for d in key] * 2)
                down = chooser([offset_of(*d, -1) for d in key] * 2)
                cache[key] = (main, jnp.concatenate([up, down], axis=0))
            main, ends = cache[key]
            own = pad_ref[x + 1, y + 1, :, :RUN]
            own = jnp.concatenate([own, jnp.zeros((rows - bricks, RUN), F32)], axis=0)
            if main is not None:
                parts = [split_two(pad_ref[X, Y, :, :RUN]) for X, Y, dx, dy in places if (dx, dy) != (0, 0)]
                value = jnp.concatenate([p[0] for p in parts] + [p[1] for p in parts], axis=0)
                own += dot(main, value)
            parts = [split_two(pad_ref[X, Y, :, RUN:]) for X, Y, _, _ in places]
            value = jnp.concatenate([p[0] for p in parts] + [p[1] for p in parts], axis=0)
            halo = dot(ends, value)
            first = own[:, : 2 * C] + jnp.where(lower_half, halo[:rows], 0.0)
            second = own[:, 2 * C :] + jnp.where(lower_half, 0.0, halo[rows:])
            total = jnp.concatenate([first, second], axis=1)
            at = (x * 4 + y) * RUN
            ext_ref[:, at : at + RUN] = total[:start]
            low_ref[:, at : at + RUN] = total[start : start + face].astype(BF)
            high_ref[:, at : at + RUN] = total[start + face :].astype(BF)


def conv_body(
    merged_ref, low_ref, high_ref, below_ref, above_ref, cot_ref, weight_ref, near_ref,
    out_ref, grad_ref, band_ref, pad_ref, table_ref,
):
    bricks = merged_ref.shape[0]
    rows = bricks + 4 * low_ref.shape[0]
    build_bands(weight_ref, band_ref)
    table_ref[:bricks] = merged_ref[...]
    table_ref[bricks:] = stack_rows(low_ref, high_ref, below_ref, above_ref)
    near = jnp.concatenate([near_ref[o] for o in range(27)] + [jnp.zeros((5, bricks), I32)], axis=0)
    near = near.astype(F32).T.astype(I32)

    def one_of(dx, dy, dz):
        o = offset_of(dx, dy, dz)
        return near[:, o : o + 1]

    place = iota((bricks, rows), 1)
    pair_place = iota((bricks, 2 * rows), 1)
    lower_half = iota((rows, 2 * C), 1) < C
    zero = jnp.zeros((rows, 2 * C), BF)
    cache = {}
    for x in range(4):
        for y in range(4):
            places = [(X, Y, dx, dy) for X, dx in options(x) for Y, dy in options(y)]
            for _, _, dx, dy in places:
                if (dx, dy) not in cache:
                    main = ones_where(place == one_of(dx, dy, 0))
                    ends = jnp.where(pair_place < rows, one_of(dx, dy, 1), one_of(dx, dy, -1) + rows)
                    cache[dx, dy] = (main, ones_where(pair_place == ends))
            at = (x * 4 + y) * RUN
            columns = table_ref[:, at : at + RUN]
            first = jnp.where(lower_half, columns[:, : 2 * C], zero)
            second = jnp.where(lower_half, zero, columns[:, 2 * C :])
            ends = jnp.concatenate([cache[dx, dy][1] for _, _, dx, dy in places], axis=0)
            halo = dot(ends, jnp.concatenate([first, second], axis=0)).astype(BF)
            for i, (X, Y, _, _) in enumerate(places):
                pad_ref[X, Y, :, RUN:] = halo[i * bricks : (i + 1) * bricks]
            pad_ref[x + 1, y + 1, :, :RUN] = columns[:bricks]
            moved = [p for p in places if p[2:] != (0, 0)]
            if moved:
                main = jnp.concatenate([cache[dx, dy][0] for _, _, dx, dy in moved], axis=0)
                got = dot(main, columns).astype(BF)
                for i, (X, Y, _, _) in enumerate(moved):
                    pad_ref[X, Y, :, :RUN] = got[i * bricks : (i + 1) * bricks]

    turned = stack_runs(cot_ref).T
    total = None
    lanes_low = iota((C, 2 * C), 1) < C
    sums = []
    for e in range(9):
        ex, ey = (e // 3, e % 3)
        inputs = pad_ref[ex : ex + 4, ey : ey + 4].reshape(16 * bricks, WIDE)
        part = dot(inputs, band_ref[e])
        total = part if total is None else total + part
        wide = dot(turned, inputs)

        def block(z, s):
            return wide[z * C : (z + 1) * C, s * 2 * C : (s + 1) * 2 * C]

        low = jnp.where(lanes_low, block(1, 0) + block(3, 1), block(0, 2) + block(2, 0))
        mid = jnp.where(lanes_low, block(0, 0) + block(2, 1), block(1, 0) + block(3, 1))
        high = jnp.where(lanes_low, block(1, 1) + block(3, 2), block(0, 0) + block(2, 1))
        for value in (low, mid, high):
            sums.append(value + pltpu.roll(value, C, 1))
    sums.append(jnp.zeros((C, 2 * C), F32))
    for p in range(16):
        out_ref[:, p * RUN : (p + 1) * RUN] = total[p * bricks : (p + 1) * bricks].astype(BF)
    for pair in range(7):
        both = [jnp.where(lanes_low, sums[14 * h + 2 * pair], sums[14 * h + 2 * pair + 1]) for h in range(2)]
        grad_ref[:, pair * 2 * C : (pair + 1) * 2 * C] = jnp.concatenate(both, axis=0).astype(BF)


def add_rows(base, lists, first_ref, second_ref):
    count, face = (base.shape[0], lists.shape[1])
    index = jnp.concatenate([lists[0:1], lists[1:2]], axis=1)
    chosen = ones_where(iota((count, 2 * face), 0) == index)
    return base + dot(chosen, stack_rows(first_ref, second_ref))


def side_grad_body(ext_ref, crosses_ref, next_ref, prev_ref, fine_ref, low_ref, high_ref):
    bricks, face = (fine_ref.shape[0], low_ref.shape[0])
    total = add_rows(ext_ref[...], crosses_ref[...], next_ref, prev_ref)
    fine_ref[...] = total[:bricks]
    low_ref[...] = total[bricks : bricks + face].astype(BF)
    high_ref[...] = total[bricks + face :].astype(BF)


def fine_grad_body(
    fine_ref, sides_ref, next_ref, prev_ref, up_ref, parents_ref, slots_ref, grad_ref, replies_ref, devices
):
    bricks = fine_ref.shape[0]
    grad_ref[...] = add_rows(fine_ref[...], sides_ref[...], next_ref, prev_ref).astype(BF)
    stacked = []
    for v in range(8):
        cx, cy, cz = (v // 4, v // 2 % 2, v % 2)
        lanes = []
        for parity in range(4):
            at = ((2 * cx + parity // 2) * 4 + 2 * cy + parity % 2) * RUN + cz * 2 * C
            lanes.append(grad_ref[:, at : at + 2 * C])
        stacked.append(jnp.concatenate(lanes, axis=1))
    stacked = jnp.concatenate(stacked, axis=0)
    items = dot(stacked, up_ref[...]).astype(BF)
    items = jnp.concatenate([items[v * bricks : (v + 1) * bricks] for v in range(8)], axis=1)
    up_sum = dot_tn(stacked, parents_ref[...]).astype(BF)
    coarse = up_sum.shape[1]
    quarter = up_sum.shape[0] // 4
    up_sum = jnp.concatenate([up_sum[q * quarter : (q + 1) * quarter] for q in range(4)], axis=1)
    half = items.shape[1] // 2
    count = replies_ref.shape[0]
    share = quarter // devices
    group = count // devices
    item_rows = group - share
    row = iota((count, bricks), 0)
    inside = row % group
    place = row // group * item_rows + inside
    named = (place // 2 == slots_ref[...]) & (inside < item_rows)
    row = iota((count, quarter), 0)
    inside = row % group
    chosen = (inside >= item_rows) & (row // group * share + inside - item_rows == iota((count, quarter), 1))
    replies = dot(ones_where(named & (place % 2 == 0)), items[:, :half])
    replies += dot(ones_where(named & (place % 2 == 1)), items[:, half:])
    replies += dot(ones_where(chosen), up_sum)
    replies_ref[...] = replies.astype(BF)


def coarse_grad_body(returned_ref, sends_ref, out_ref, share_ref):
    capacity, devices = sends_ref.shape
    count = out_ref.shape[0]
    lanes, half = returned_ref.shape
    group = lanes // devices
    share = share_ref.shape[0]
    item_rows = group - share
    index = send_index(sends_ref[...], group)
    inside = iota((count, lanes), 1) % group
    named = (iota((count, lanes), 0) == index) & (inside < item_rows)
    returned = returned_ref[...]
    for h in range(2):
        chosen = ones_where(named & (inside % 2 == h))
        out_ref[:, h * half : (h + 1) * half] = dot(chosen, returned).astype(BF)
    inside = iota((share, lanes), 1) % group
    share_ref[...] = dot(ones_where(inside - item_rows == iota((share, lanes), 0)), returned).astype(BF)


def share_body(arrived_ref, up_ref, out_ref):
    lanes, width = arrived_ref.shape
    share = up_ref.shape[0]
    chosen = ones_where(iota((share, lanes), 1) % share == iota((share, lanes), 0))
    out_ref[:, :width] = dot(chosen, arrived_ref[...]).astype(BF)
    out_ref[:, width:] = up_ref[...]


def final_body(totals_ref, conv_ref, up_ref, scale):
    width = 14 * C
    for pair in range(7):
        turned = totals_ref[:, pair * 2 * C : (pair + 1) * 2 * C].astype(F32).T * scale
        for h in range(2):
            for s in range(2):
                o = 14 * h + 2 * pair + s
                if o < 27:
                    conv_ref[o] = turned[s * C : (s + 1) * C, h * C : (h + 1) * C]
    quarter = totals_ref.shape[0]
    coarse = up_ref.shape[1]
    for q in range(4):
        up_ref[q * quarter : (q + 1) * quarter] = (
            totals_ref[:, width + q * coarse : width + (q + 1) * coarse].astype(F32) * scale
        )


def passed_along(value, axis, steps):
    count = lax.axis_size(axis)
    initial, last = (max(0, -steps), min(count, count - steps))
    return lax.ppermute(value, axis, [(source, source + steps) for source in range(initial, last)])


def trade_rows(values, devices):
    rows, width = values.shape
    grid_view = values.reshape(devices, rows // devices, width)
    return lax.all_to_all(grid_view, ("gx", "gy"), split_axis=0, concat_axis=0, tiled=True).reshape(rows, width)


def on_device(
    fine_features, coarse_items, conv_weight, up_weight, neighbours,
    side_sends, cross_sends, parent_slots, coarse_sends, cotangent,
):
    fine = fine_features[0, 0]
    items = coarse_items[0, 0]
    cot = cotangent[0, 0]
    bricks, width = fine.shape
    face = side_sends.shape[-1]
    across_x, across_y = (lax.axis_size("gx"), lax.axis_size("gy"))
    devices = across_x * across_y
    capacity = coarse_sends.shape[-1]
    item_count, item_width = items.shape
    coarse = up_weight.shape[1]
    start = bricks + 2 * face
    sends = coarse_sends[0, 0].T
    slots = parent_slots[0]
    sides = side_sends[0, 0]
    crosses = cross_sends[0, 0]
    near = neighbours[0, 0].T.reshape(27, 1, bricks)
    up_turned = up_weight.transpose(0, 2, 1).reshape(8 * C, coarse)
    half = item_width // 2
    share = 2 * C // devices
    band = pltpu.VMEM((9, WIDE, RUN), BF)
    face_rows = shape((face, width))
    conv_flops = 2 * 9 * 16 * bricks * WIDE * RUN

    (outgoing,) = call(items_out_body, [shape((2 * capacity * devices, half))], sends, items)
    received = trade_rows(outgoing, devices)
    ext_grad, low_cross, high_cross = call(
        table_grad_body, [shape((start, width), F32), face_rows, face_rows], cot, conv_weight, near,
        scratch=[band, pltpu.VMEM((6, 6, bricks, WIDE), F32)], flops=2 * conv_flops,
    )
    merged, parents, to_next, to_prev = call(
        merge_body, [shape((bricks, width)), shape((8 * bricks, coarse)), face_rows, face_rows],
        received, slots, up_turned, fine, sides,
    )
    low_side = passed_along(to_next, "gy", 1)
    high_side = passed_along(to_prev, "gy", -1)
    grad_prev = passed_along(high_cross, "gx", 1)
    grad_next = passed_along(low_cross, "gx", -1)
    to_next, to_prev = call(cross_body, [face_rows, face_rows], merged, low_side, high_side, crosses)
    below = passed_along(to_next, "gx", 1)
    above = passed_along(to_prev, "gx", -1)
    fine_part, low_grad, high_grad = call(
        side_grad_body, [shape((bricks, width), F32), face_rows, face_rows], ext_grad, crosses, grad_next, grad_prev
    )
    grad_prev = passed_along(high_grad, "gy", 1)
    grad_next = passed_along(low_grad, "gy", -1)
    grad_fine, replies = call(
        functools.partial(fine_grad_body, devices=devices),
        [shape((bricks, width)), shape((devices * (2 * capacity + share), half))],
        fine_part, sides, grad_next, grad_prev, up_turned, parents, slots,
    )
    returned = trade_rows(replies, devices)
    output, conv_sum = call(
        conv_body, [shape((bricks, width)), shape((2 * C, 14 * C))],
        merged, low_side, high_side, below, above, cot, conv_weight, near,
        scratch=[band, pltpu.VMEM((6, 6, bricks, WIDE), BF), pltpu.VMEM((bricks + 4 * face, width), BF)],
        flops=2 * conv_flops,
    )
    coarse_grad, up_share = call(
        coarse_grad_body, [shape((item_count, item_width)), shape((share, half))], returned, sends
    )
    arrived = trade_rows(conv_sum, devices)
    (own_share,) = call(share_body, [shape((share, 14 * C + half))], arrived, up_share)
    totals = lax.all_gather(own_share, ("gx", "gy"), axis=0, tiled=True)
    scale = 1.0 / math.sqrt(64 * bricks * devices)
    grad_conv, grad_up = call(
        functools.partial(final_body, scale=scale),
        [shape((27, C, C), F32), shape((8 * C, coarse), F32)], totals,
    )
    return (
        output.reshape(1, 1, bricks, width),
        grad_fine.reshape(1, 1, bricks, width),
        coarse_grad.reshape(1, 1, item_count, item_width),
        grad_conv,
        grad_up.reshape(8, C, coarse).transpose(0, 2, 1),
    )


def solution(mesh):
    split = P(("groups", "gx"), "gy", None, None)
    placed = (split, split, P(), P(), split, split, split, P(("groups", "gx"), "gy", None), split, split)
    return jax.shard_map(
        on_device,
        mesh=mesh,
        in_specs=placed,
        out_specs=(split, split, split, P("groups", None, None), P("groups", None, None)),
        check_vma=False,
    )
```

profile of v0, /device:TPU:0, one launch (start us, length us, event | category | flops | bytes accessed | tf_op | source)
XLA Modules:
  0.0 109.6 jit_solution(8424961400798133140)
XLA Ops:
  0.6 0.0 copy-start.3
  0.6 0.7 copy-done.3
  1.3 0.9 copy-done.2
  2.2 1.0 shard_map.137
  3.3 7.5 %all-to-all-start = ((bf16[16,8,512]{2,1,0:T(8,128)(2,1)}), bf16[16,8,512]{2,1,0:T(8,128)(2,1)S(1)}, u32[]{:S(2)}, u32[]{:S(2)}) async-start(bf16[16,8,512]{2,1,0:T(8,128)(2,1)} %bitcast.3), calls=%async_computation | async-start | bytes 262144 | tf_op jit(solution)/shard_map/all_to_all | solution.py:393
  10.8 0.0 copy-done.10
  10.8 0.0 copy-done.7
  10.8 0.0 copy-start.8
  10.8 0.9 copy-done.8
  11.8 1.9 %shard_map.141 = (f32[48,4096]{1,0:T(8,128)S(1)}, bf16[8,4096]{1,0:T(8,128)(2,1)S(1)}, bf16[8,4096]{1,0:T(8,128)(2,1)S(1)}) custom-call(bf16[32,4096]{1,0:T(8,128)(2,1)S(1)} %bitcast.44, bf16[27,64,64]{2,1,0:T(8,128)(2,1)S(1)} %copy-done.7, s32[27,1,32]{2,1,0:T(1,128)S(1)} %reshape.49.near_ref), custom_call_target="tpu_custom_call" | custom-call | flops 1811939328 | bytes 1404288 | tf_op jit(solution)/shard_map/pallas_call | solution.py:49
  13.7 1.3 %collective-permute-start.4 = (bf16[8,4096]{1,0:T(8,128)(2,1)S(1)}, bf16[8,4096]{1,0:T(8,128)(2,1)S(1)}, u32[]{:S(2)}, u32[]{:S(2)}) collective-permute-start(bf16[8,4096]{1,0:T(8,128)(2,1)S(1)} %get-tuple-element.32), channel_id=1, source_target_pairs={{4,0},{8,4},{12,8},{5,1},{9,5},{13,9},{6,2},{10,6},{14,10},{7,3},{... | collective-permute-start | bytes 196616 | tf_op jit(solution)/shard_map/ppermute | solution.py:387
  15.0 3.0 %collective-permute-start.5 = (bf16[8,4096]{1,0:T(8,128)(2,1)S(1)}, bf16[8,4096]{1,0:T(8,128)(2,1)S(1)}, u32[]{:S(2)}, u32[]{:S(2)}) collective-permute-start(bf16[8,4096]{1,0:T(8,128)(2,1)S(1)} %get-tuple-element.33), channel_id=1, source_target_pairs={{0,4},{4,8},{8,12},{1,5},{5,9},{9,13},{2,6},{6,10},{10,14},{3,7},{... | collective-permute-start | bytes 196616 | tf_op jit(solution)/shard_map/ppermute | solution.py:387
  18.0 0.0 collective-permute-done.4.next_ref
  18.0 0.9 collective-permute-done.5.prev_ref
  18.9 0.7 copy-done.5
  19.6 0.3 shard_map.142
  19.9 1.3 %collective-permute-start.6 = (bf16[8,4096]{1,0:T(8,128)(2,1)S(1)}, bf16[8,4096]{1,0:T(8,128)(2,1)S(1)}, u32[]{:S(2)}, u32[]{:S(2)}) collective-permute-start(bf16[8,4096]{1,0:T(8,128)(2,1)S(1)} %get-tuple-element.35), channel_id=1, source_target_pairs={{1,0},{2,1},{3,2},{5,4},{6,5},{7,6},{9,8},{10,9},{11,10},{13,12},{... | collective-permute-start | bytes 196616 | tf_op jit(solution)/shard_map/ppermute | solution.py:387
  21.2 4.5 %collective-permute-start.7 = (bf16[8,4096]{1,0:T(8,128)(2,1)S(1)}, bf16[8,4096]{1,0:T(8,128)(2,1)S(1)}, u32[]{:S(2)}, u32[]{:S(2)}) collective-permute-start(bf16[8,4096]{1,0:T(8,128)(2,1)S(1)} %get-tuple-element.36), channel_id=1, source_target_pairs={{0,1},{1,2},{2,3},{4,5},{5,6},{6,7},{8,9},{9,10},{10,11},{12,13},{... | collective-permute-start | bytes 196616 | tf_op jit(solution)/shard_map/ppermute | solution.py:387
  25.8 0.0 all-to-all-done
  25.8 0.0 copy-start.4
  25.8 0.0 copy-start.6
  25.8 0.0 copy-done
  25.8 0.0 copy-done.1
  25.8 0.6 copy-done.4
  26.5 0.0 copy-done.6
  26.5 0.6 shard_map.138
  27.0 0.0 collective-permute-done.6.next_ref
  27.1 0.6 collective-permute-done.7.prev_ref
  27.6 1.6 %shard_map.143 = (bf16[32,4096]{1,0:T(8,128)(2,1)}, bf16[256,512]{1,0:T(8,128)(2,1)}) custom-call(f32[32,4096]{1,0:T(8,128)S(1)} %get-tuple-element.34.fine_ref, s32[2,8]{1,0:T(2,128)S(1)} %bitcast.39, bf16[8,4096]{1,0:T(8,128)(2,1)S(1)} %collective-permute-done.6.next_ref, bf16[8,4096]{1,0:T(8,128)(2,1)S(1)} %collective-permute-done.7.prev_ref, ...), custom_call_target="tpu_custom_call" | custom-call | bytes 1376448 | tf_op jit(solution)/shard_map/pallas_call | solution.py:49
  29.3 9.5 %all-to-all-start.1 = ((bf16[16,16,512]{2,1,0:T(8,128)(2,1)}), bf16[16,16,512]{2,1,0:T(8,128)(2,1)S(1)}, u32[]{:S(2)}, u32[]{:S(2)}) async-start(bf16[16,16,512]{2,1,0:T(8,128)(2,1)} %bitcast.16), calls=%async_computation.1 | async-start | bytes 524288 | tf_op jit(solution)/shard_map/all_to_all | solution.py:393
  38.8 0.0 copy-start.9
  38.8 4.0 %collective-permute-start = (bf16[8,4096]{1,0:T(8,128)(2,1)S(1)}, bf16[8,4096]{1,0:T(8,128)(2,1)S(1)}, u32[]{:S(2)}, u32[]{:S(2)}) collective-permute-start(bf16[8,4096]{1,0:T(8,128)(2,1)S(1)} %get-tuple-element.26), channel_id=1, source_target_pairs={{0,1},{1,2},{2,3},{4,5},{5,6},{6,7},{8,9},{9,10},{10,11},{12,13},{... | collective-permute-start | bytes 196616 | tf_op jit(solution)/shard_map/ppermute | solution.py:387
  42.8 1.3 %collective-permute-start.1 = (bf16[8,4096]{1,0:T(8,128)(2,1)S(1)}, bf16[8,4096]{1,0:T(8,128)(2,1)S(1)}, u32[]{:S(2)}, u32[]{:S(2)}) collective-permute-start(bf16[8,4096]{1,0:T(8,128)(2,1)S(1)} %get-tuple-element.27), channel_id=1, source_target_pairs={{1,0},{2,1},{3,2},{5,4},{6,5},{7,6},{9,8},{10,9},{11,10},{13,12},{... | collective-permute-start | bytes 196616 | tf_op jit(solution)/shard_map/ppermute | solution.py:387
  44.1 1.3 %collective-permute-done.low_ref = bf16[8,4096]{1,0:T(8,128)(2,1)S(1)} collective-permute-done((bf16[8,4096]{1,0:T(8,128)(2,1)S(1)}, bf16[8,4096]{1,0:T(8,128)(2,1)S(1)}, u32[]{:S(2)}, u32[]{:S(2)}) %collective-permute-start) | collective-permute-done | bytes 65568 | tf_op jit(solution)/shard_map/ppermute | solution.py:387
  45.4 3.7 %collective-permute-done.1.high_ref = bf16[8,4096]{1,0:T(8,128)(2,1)S(1)} collective-permute-done((bf16[8,4096]{1,0:T(8,128)(2,1)S(1)}, bf16[8,4096]{1,0:T(8,128)(2,1)S(1)}, u32[]{:S(2)}, u32[]{:S(2)}) %collective-permute-start.1) | collective-permute-done | bytes 65568 | tf_op jit(solution)/shard_map/ppermute | solution.py:387
  49.1 0.3 shard_map.139
  49.4 1.3 %collective-permute-start.2 = (bf16[8,4096]{1,0:T(8,128)(2,1)S(1)}, bf16[8,4096]{1,0:T(8,128)(2,1)S(1)}, u32[]{:S(2)}, u32[]{:S(2)}) collective-permute-start(bf16[8,4096]{1,0:T(8,128)(2,1)S(1)} %get-tuple-element.28), channel_id=1, source_target_pairs={{0,4},{4,8},{8,12},{1,5},{5,9},{9,13},{2,6},{6,10},{10,14},{3,7},{... | collective-permute-start | bytes 196616 | tf_op jit(solution)/shard_map/ppermute | solution.py:387
  50.7 1.3 %collective-permute-start.3 = (bf16[8,4096]{1,0:T(8,128)(2,1)S(1)}, bf16[8,4096]{1,0:T(8,128)(2,1)S(1)}, u32[]{:S(2)}, u32[]{:S(2)}) collective-permute-start(bf16[8,4096]{1,0:T(8,128)(2,1)S(1)} %get-tuple-element.29), channel_id=1, source_target_pairs={{4,0},{8,4},{12,8},{5,1},{9,5},{13,9},{6,2},{10,6},{14,10},{7,3},{... | collective-permute-start | bytes 196616 | tf_op jit(solution)/shard_map/ppermute | solution.py:387
  52.0 0.0 collective-permute-done.2.below_ref
  52.0 3.5 %collective-permute-done.3.above_ref = bf16[8,4096]{1,0:T(8,128)(2,1)S(1)} collective-permute-done((bf16[8,4096]{1,0:T(8,128)(2,1)S(1)}, bf16[8,4096]{1,0:T(8,128)(2,1)S(1)}, u32[]{:S(2)}, u32[]{:S(2)}) %collective-permute-start.3) | collective-permute-done | bytes 65568 | tf_op jit(solution)/shard_map/ppermute | solution.py:387
  55.5 4.0 %shard_map.140 = (bf16[32,4096]{1,0:T(8,128)(2,1)}, bf16[128,896]{1,0:T(8,128)(2,1)}) custom-call(bf16[32,4096]{1,0:T(8,128)(2,1)S(1)} %get-tuple-element.25.merged_ref, bf16[8,4096]{1,0:T(8,128)(2,1)S(1)} %collective-permute-done.low_ref, bf16[8,4096]{1,0:T(8,128)(2,1)S(1)} %collective-permute-done.1.high_ref, ...), custom_call_target="tpu_custom_call" | custom-call | flops 1811939328 | bytes 1502592 | tf_op jit(solution)/shard_map/pallas_call | solution.py:49
  59.5 0.0 all-to-all-done.1
  59.5 6.1 %all-to-all-start.2 = ((bf16[16,8,896]{2,1,0:T(8,128)(2,1)}), bf16[16,8,896]{2,1,0:T(8,128)(2,1)S(1)}, u32[]{:S(2)}, u32[]{:S(2)}) async-start(bf16[16,8,896]{2,1,0:T(8,128)(2,1)} %bitcast.20), calls=%async_computation.2 | async-start | bytes 458752 | tf_op jit(solution)/shard_map/all_to_all | solution.py:393
  65.6 1.0 shard_map.144
  66.6 8.2 %all-to-all-done.2 = bf16[16,8,896]{2,1,0:T(8,128)(2,1)S(1)} async-done(((bf16[16,8,896]{2,1,0:T(8,128)(2,1)}), bf16[16,8,896]{2,1,0:T(8,128)(2,1)S(1)}, u32[]{:S(2)}, u32[]{:S(2)}) %all-to-all-start.2) | async-done | bytes 229408 | tf_op jit(solution)/shard_map/all_to_all | solution.py:393
  74.8 0.1 shard_map.145
  75.0 33.4 %all_gather.3.totals_ref = bf16[128,1408]{1,0:T(8,128)(2,1)S(1)} all-gather(bf16[8,1408]{1,0:T(8,128)(2,1)S(1)} %shard_map.145), channel_id=1, replica_groups=mesh['groups'=2,'gx'=4,'gy'=4] {'gx','gy'}, dimensions={0}, use_global_device_ids=true | all-gather | bytes 382976 | tf_op jit(solution)/shard_map/all_gather | solution.py:462
  108.4 1.2 %shard_map.146 = (f32[27,64,64]{2,1,0:T(8,128)}, f32[512,128]{1,0:T(8,128)}) custom-call(bf16[128,1408]{1,0:T(8,128)(2,1)S(1)} %all_gather.3.totals_ref), custom_call_target="tpu_custom_call" | custom-call | bytes 1064960 | tf_op jit(solution)/shard_map/pallas_call | solution.py:49
  (9 shorter events, 0.0 us)
Async XLA Ops:
  0.6 0.7 copy-start.3
  1.3 0.9 copy-start.2
  2.2 8.6 %copy-start.7 = (bf16[27,64,64]{2,1,0:T(8,128)(2,1)S(1)}, bf16[27,64,64]{2,1,0:T(8,128)(2,1)}, u32[]{:S(2)}) copy-start(bf16[27,64,64]{2,1,0:T(8,128)(2,1)} %weight_ref.3) | copy-start | bytes 663556
  3.3 7.5 %copy-start.10 = (s32[1,1,32,27]{2,1,3,0:T(1,128)S(1)}, s32[1,1,32,27]{2,1,3,0:T(1,128)}, u32[]{:S(2)}) copy-start(s32[1,1,32,27]{2,1,3,0:T(1,128)} %param.14) | copy-start | bytes 10372
  3.3 22.5 %all-to-all-start = ((bf16[16,8,512]{2,1,0:T(8,128)(2,1)}), bf16[16,8,512]{2,1,0:T(8,128)(2,1)S(1)}, u32[]{:S(2)}, u32[]{:S(2)}) async-start(bf16[16,8,512]{2,1,0:T(8,128)(2,1)} %bitcast.3), calls=%async_computation | async-start | bytes 262144 | tf_op jit(solution)/shard_map/all_to_all | solution.py:393
  10.8 1.0 copy-start.8
  13.7 4.3 %collective-permute-start.4 = (bf16[8,4096]{1,0:T(8,128)(2,1)S(1)}, bf16[8,4096]{1,0:T(8,128)(2,1)S(1)}, u32[]{:S(2)}, u32[]{:S(2)}) collective-permute-start(bf16[8,4096]{1,0:T(8,128)(2,1)S(1)} %get-tuple-element.32), channel_id=1, source_target_pairs={{4,0},{8,4},{12,8},{5,1},{9,5},{13,9},{6,2},{10,6},{14,10},{7,3},{... | collective-permute-start | bytes 196616 | tf_op jit(solution)/shard_map/ppermute | solution.py:387
  15.0 3.9 %collective-permute-start.5 = (bf16[8,4096]{1,0:T(8,128)(2,1)S(1)}, bf16[8,4096]{1,0:T(8,128)(2,1)S(1)}, u32[]{:S(2)}, u32[]{:S(2)}) collective-permute-start(bf16[8,4096]{1,0:T(8,128)(2,1)S(1)} %get-tuple-element.33), channel_id=1, source_target_pairs={{0,4},{4,8},{8,12},{1,5},{5,9},{9,13},{2,6},{6,10},{10,14},{3,7},{... | collective-permute-start | bytes 196616 | tf_op jit(solution)/shard_map/ppermute | solution.py:387
  18.9 0.7 copy-start.5
  19.6 6.2 %copy-start = (bf16[8,128,64]{1,2,0:T(8,128)(2,1)S(1)}, bf16[8,128,64]{1,2,0:T(8,128)(2,1)}, u32[]{:S(2)}) copy-start(bf16[8,128,64]{1,2,0:T(8,128)(2,1)} %param.13) | copy-start | bytes 393220
  19.6 6.2 %copy-start.1 = (bf16[1,1,32,4096]{3,2,1,0:T(8,128)(2,1)S(1)}, bf16[1,1,32,4096]{3,2,1,0:T(8,128)(2,1)}, u32[]{:S(2)}) copy-start(bf16[1,1,32,4096]{3,2,1,0:T(8,128)(2,1)} %param.10) | copy-start | bytes 786436
  19.9 7.1 %collective-permute-start.6 = (bf16[8,4096]{1,0:T(8,128)(2,1)S(1)}, bf16[8,4096]{1,0:T(8,128)(2,1)S(1)}, u32[]{:S(2)}, u32[]{:S(2)}) collective-permute-start(bf16[8,4096]{1,0:T(8,128)(2,1)S(1)} %get-tuple-element.35), channel_id=1, source_target_pairs={{1,0},{2,1},{3,2},{5,4},{6,5},{7,6},{9,8},{10,9},{11,10},{13,12},{... | collective-permute-start | bytes 196616 | tf_op jit(solution)/shard_map/ppermute | solution.py:387
  21.2 6.4 %collective-permute-start.7 = (bf16[8,4096]{1,0:T(8,128)(2,1)S(1)}, bf16[8,4096]{1,0:T(8,128)(2,1)S(1)}, u32[]{:S(2)}, u32[]{:S(2)}) collective-permute-start(bf16[8,4096]{1,0:T(8,128)(2,1)S(1)} %get-tuple-element.36), channel_id=1, source_target_pairs={{0,1},{1,2},{2,3},{4,5},{5,6},{6,7},{8,9},{9,10},{10,11},{12,13},{... | collective-permute-start | bytes 196616 | tf_op jit(solution)/shard_map/ppermute | solution.py:387
  25.8 0.7 copy-start.4
  25.8 0.7 copy-start.6
  29.3 30.2 %all-to-all-start.1 = ((bf16[16,16,512]{2,1,0:T(8,128)(2,1)}), bf16[16,16,512]{2,1,0:T(8,128)(2,1)S(1)}, u32[]{:S(2)}, u32[]{:S(2)}) async-start(bf16[16,16,512]{2,1,0:T(8,128)(2,1)} %bitcast.16), calls=%async_computation.1 | async-start | bytes 524288 | tf_op jit(solution)/shard_map/all_to_all | solution.py:393
  38.8 16.7 %copy-start.9 = (bf16[1,1,32,4096]{3,2,1,0:T(8,128)(2,1)S(1)}, bf16[1,1,32,4096]{3,2,1,0:T(8,128)(2,1)}, u32[]{:S(2)}) copy-start(bf16[1,1,32,4096]{3,2,1,0:T(8,128)(2,1)} %param.19) | copy-start | bytes 786436
  38.8 6.6 %collective-permute-start = (bf16[8,4096]{1,0:T(8,128)(2,1)S(1)}, bf16[8,4096]{1,0:T(8,128)(2,1)S(1)}, u32[]{:S(2)}, u32[]{:S(2)}) collective-permute-start(bf16[8,4096]{1,0:T(8,128)(2,1)S(1)} %get-tuple-element.26), channel_id=1, source_target_pairs={{0,1},{1,2},{2,3},{4,5},{5,6},{6,7},{8,9},{9,10},{10,11},{12,13},{... | collective-permute-start | bytes 196616 | tf_op jit(solution)/shard_map/ppermute | solution.py:387
  42.8 6.3 %collective-permute-start.1 = (bf16[8,4096]{1,0:T(8,128)(2,1)S(1)}, bf16[8,4096]{1,0:T(8,128)(2,1)S(1)}, u32[]{:S(2)}, u32[]{:S(2)}) collective-permute-start(bf16[8,4096]{1,0:T(8,128)(2,1)S(1)} %get-tuple-element.27), channel_id=1, source_target_pairs={{1,0},{2,1},{3,2},{5,4},{6,5},{7,6},{9,8},{10,9},{11,10},{13,12},{... | collective-permute-start | bytes 196616 | tf_op jit(solution)/shard_map/ppermute | solution.py:387
  49.4 2.6 %collective-permute-start.2 = (bf16[8,4096]{1,0:T(8,128)(2,1)S(1)}, bf16[8,4096]{1,0:T(8,128)(2,1)S(1)}, u32[]{:S(2)}, u32[]{:S(2)}) collective-permute-start(bf16[8,4096]{1,0:T(8,128)(2,1)S(1)} %get-tuple-element.28), channel_id=1, source_target_pairs={{0,4},{4,8},{8,12},{1,5},{5,9},{9,13},{2,6},{6,10},{10,14},{3,7},{... | collective-permute-start | bytes 196616 | tf_op jit(solution)/shard_map/ppermute | solution.py:387
  50.7 4.9 %collective-permute-start.3 = (bf16[8,4096]{1,0:T(8,128)(2,1)S(1)}, bf16[8,4096]{1,0:T(8,128)(2,1)S(1)}, u32[]{:S(2)}, u32[]{:S(2)}) collective-permute-start(bf16[8,4096]{1,0:T(8,128)(2,1)S(1)} %get-tuple-element.29), channel_id=1, source_target_pairs={{4,0},{8,4},{12,8},{5,1},{9,5},{13,9},{6,2},{10,6},{14,10},{7,3},{... | collective-permute-start | bytes 196616 | tf_op jit(solution)/shard_map/ppermute | solution.py:387
  59.5 15.3 %all-to-all-start.2 = ((bf16[16,8,896]{2,1,0:T(8,128)(2,1)}), bf16[16,8,896]{2,1,0:T(8,128)(2,1)S(1)}, u32[]{:S(2)}, u32[]{:S(2)}) async-start(bf16[16,8,896]{2,1,0:T(8,128)(2,1)} %bitcast.20), calls=%async_computation.2 | async-start | bytes 458752 | tf_op jit(solution)/shard_map/all_to_all | solution.py:393
where the time goes:
time: 110 us
  starting transfers between devices  41.1 us (37%)
  blocking collectives  33.4 us (30%)
  waiting for transfers between devices  18.3 us (17%)
  Pallas kernels  12.1 us (11%)
  local copies, waits for them, and re-layouts  3.89 us (4%)
    all_gather x1, blocking collectives, on_device(): totals = lax.all_gather(own_share, ('gx', 'gy'), axis=0, tiled=True)  33.4 us
    all_to_all x3, starting transfers between devices, trade_rows(): lax.all_to_all(grid_view, ('gx', 'gy'), split_axis=0, concat_axis=0, tile...  23.1 us
    ppermute x8, starting transfers between devices, passed_along(): lax.ppermute(value, axis, [(source, source + steps) for source in range(i...  18 us
    pallas_call x10, Pallas kernels, call(): pl.pallas_call(body, out_shape=tuple(outs), scratch_shapes=tuple(scratch)...  12.1 us
    ppermute x8, waiting for transfers between devices, passed_along(): lax.ppermute(value, axis, [(source, source + steps) for source in range(i...  10 us
    all_to_all x3, waiting for transfers between devices, trade_rows(): lax.all_to_all(grid_view, ('gx', 'gy'), split_axis=0, concat_axis=0, tile...  8.25 us
    unnamed x23, local copies, waits for them, and re-layouts  3.87 us
  transfers between devices with their start and end apart: 11, of which 6 were waited for; matrix products, arithmetic and copies ran while one was open for 0% of the time, Pallas kernels for 7%

commit v1 on v0

--- a/solution.py
+++ b/solution.py
@@ -59,13 +59,13 @@
     return jax.ShapeDtypeStruct(dims, dtype)
 
 
-def send_index(sends, group):
+def send_index(sends, group, pieces=1, j=0):
     capacity, devices = sends.shape
     lanes = devices * group
     spread = ones_where(iota((devices, lanes), 1) // group == iota((devices, lanes), 0))
     rows = dot(sends.astype(F32).astype(BF), spread)
-    slot = iota((capacity, lanes), 1) % group
-    picked = jnp.where(slot // 2 == iota((capacity, lanes), 0), rows, 0.0)
+    slot = (iota((capacity, lanes), 1) % group * pieces + j) // 2
+    picked = jnp.where(slot == iota((capacity, lanes), 0), rows, 0.0)
     return jnp.sum(picked, axis=0, keepdims=True).astype(I32)
 
 
@@ -215,7 +215,7 @@
 
 def conv_body(
     merged_ref, low_ref, high_ref, below_ref, above_ref, cot_ref, weight_ref, near_ref,
-    out_ref, grad_ref, band_ref, pad_ref, table_ref,
+    out_ref, back_ref, band_ref, pad_ref, table_ref,
 ):
     bricks = merged_ref.shape[0]
     rows = bricks + 4 * low_ref.shape[0]
@@ -282,7 +282,8 @@
         out_ref[:, p * RUN : (p + 1) * RUN] = total[p * bricks : (p + 1) * bricks].astype(BF)
     for pair in range(7):
         both = [jnp.where(lanes_low, sums[14 * h + 2 * pair], sums[14 * h + 2 * pair + 1]) for h in range(2)]
-        grad_ref[:, pair * 2 * C : (pair + 1) * 2 * C] = jnp.concatenate(both, axis=0).astype(BF)
+        at = back_ref.shape[1] - 14 * C + pair * 2 * C
+        back_ref[:, at : at + 2 * C] = jnp.concatenate(both, axis=0).astype(BF)
 
 
 def add_rows(base, lists, first_ref, second_ref):
@@ -300,9 +301,7 @@
     high_ref[...] = total[bricks + face :].astype(BF)
 
 
-def fine_grad_body(
-    fine_ref, sides_ref, next_ref, prev_ref, up_ref, parents_ref, slots_ref, grad_ref, replies_ref, devices
-):
+def fine_grad_body(fine_ref, sides_ref, next_ref, prev_ref, up_ref, parents_ref, slots_ref, grad_ref, back_ref, devices):
     bricks = fine_ref.shape[0]
     grad_ref[...] = add_rows(fine_ref[...], sides_ref[...], next_ref, prev_ref).astype(BF)
     stacked = []
@@ -316,69 +315,76 @@
     stacked = jnp.concatenate(stacked, axis=0)
     items = dot(stacked, up_ref[...]).astype(BF)
     items = jnp.concatenate([items[v * bricks : (v + 1) * bricks] for v in range(8)], axis=1)
+    half = items.shape[1] // 2
+    count = back_ref.shape[0]
     up_sum = dot_tn(stacked, parents_ref[...]).astype(BF)
     coarse = up_sum.shape[1]
-    quarter = up_sum.shape[0] // 4
-    up_sum = jnp.concatenate([up_sum[q * quarter : (q + 1) * quarter] for q in range(4)], axis=1)
-    half = items.shape[1] // 2
-    count = replies_ref.shape[0]
-    share = quarter // devices
-    group = count // devices
-    item_rows = group - share
-    row = iota((count, bricks), 0)
-    inside = row % group
-    place = row // group * item_rows + inside
-    named = (place // 2 == slots_ref[...]) & (inside < item_rows)
-    row = iota((count, quarter), 0)
-    inside = row % group
-    chosen = (inside >= item_rows) & (row // group * share + inside - item_rows == iota((count, quarter), 1))
-    replies = dot(ones_where(named & (place % 2 == 0)), items[:, :half])
-    replies += dot(ones_where(named & (place % 2 == 1)), items[:, half:])
-    replies += dot(ones_where(chosen), up_sum)
-    replies_ref[...] = replies.astype(BF)
-
-
-def coarse_grad_body(returned_ref, sends_ref, out_ref, share_ref):
+    parts = up_sum.shape[0] // count
+    item_lanes = back_ref.shape[1] - 14 * C - parts * coarse
+    for q in range(parts):
+        at = item_lanes + q * coarse
+        back_ref[:, at : at + coarse] = up_sum[q * count : (q + 1) * count]
+    for j in range(item_lanes // half):
+        piece = iota((count, bricks), 0) * (item_lanes // half) + j
+        named = piece // 2 == slots_ref[...]
+        rows = dot(ones_where(named & (piece % 2 == 0)), items[:, :half])
+        rows += dot(ones_where(named & (piece % 2 == 1)), items[:, half:])
+        back_ref[:, j * half : (j + 1) * half] = rows.astype(BF)
+
+
+def last_body(
+    merged_ref, low_ref, high_ref, below_ref, above_ref, cot_ref, weight_ref, near_ref,
+    fine_ref, sides_ref, next_ref, prev_ref, up_ref, parents_ref, slots_ref,
+    out_ref, grad_ref, back_ref, band_ref, pad_ref, table_ref, devices,
+):
+    conv_body(
+        merged_ref, low_ref, high_ref, below_ref, above_ref, cot_ref, weight_ref, near_ref,
+        out_ref, back_ref, band_ref, pad_ref, table_ref,
+    )
+    fine_grad_body(
+        fine_ref, sides_ref, next_ref, prev_ref, up_ref, parents_ref, slots_ref, grad_ref, back_ref, devices
+    )
+
+
+def share_body(back_ref, out_ref, devices):
+    count, width = out_ref.shape
+    share = count // devices
+    same = iota((count, count), 0) % share == iota((count, count), 1) % share
+    out_ref[...] = dot(ones_where(same), back_ref[:, back_ref.shape[1] - width :]).astype(BF)
+
+
+def coarse_grad_body(back_ref, sends_ref, out_ref):
     capacity, devices = sends_ref.shape
-    count = out_ref.shape[0]
-    lanes, half = returned_ref.shape
+    count, item_width = out_ref.shape
+    half = item_width // 2
+    lanes = back_ref.shape[0]
+    pieces = 2 * capacity * devices // lanes
     group = lanes // devices
-    share = share_ref.shape[0]
-    item_rows = group - share
-    index = send_index(sends_ref[...], group)
-    inside = iota((count, lanes), 1) % group
-    named = (iota((count, lanes), 0) == index) & (inside < item_rows)
-    returned = returned_ref[...]
     for h in range(2):
-        chosen = ones_where(named & (inside % 2 == h))
-        out_ref[:, h * half : (h + 1) * half] = dot(chosen, returned).astype(BF)
-    inside = iota((share, lanes), 1) % group
-    share_ref[...] = dot(ones_where(inside - item_rows == iota((share, lanes), 0)), returned).astype(BF)
-
-
-def share_body(arrived_ref, up_ref, out_ref):
-    lanes, width = arrived_ref.shape
-    share = up_ref.shape[0]
-    chosen = ones_where(iota((share, lanes), 1) % share == iota((share, lanes), 0))
-    out_ref[:, :width] = dot(chosen, arrived_ref[...]).astype(BF)
-    out_ref[:, width:] = up_ref[...]
+        total = None
+        for j in range(pieces):
+            index = send_index(sends_ref[...], group, pieces, j)
+            place = iota((count, lanes), 1) % group * pieces + j
+            chosen = (iota((count, lanes), 0) == index) & (place % 2 == h)
+            part = dot(ones_where(chosen), back_ref[:, j * half : (j + 1) * half])
+            total = part if total is None else total + part
+        out_ref[:, h * half : (h + 1) * half] = total.astype(BF)
 
 
 def final_body(totals_ref, conv_ref, up_ref, scale):
-    width = 14 * C
+    count = totals_ref.shape[0]
+    coarse = up_ref.shape[1]
+    parts = up_ref.shape[0] // count
+    for q in range(parts):
+        up_ref[q * count : (q + 1) * count] = totals_ref[:, q * coarse : (q + 1) * coarse].astype(F32) * scale
     for pair in range(7):
-        turned = totals_ref[:, pair * 2 * C : (pair + 1) * 2 * C].astype(F32).T * scale
+        at = parts * coarse + pair * 2 * C
+        turned = totals_ref[:, at : at + 2 * C].astype(F32).T * scale
         for h in range(2):
             for s in range(2):
                 o = 14 * h + 2 * pair + s
                 if o < 27:
                     conv_ref[o] = turned[s * C : (s + 1) * C, h * C : (h + 1) * C]
-    quarter = totals_ref.shape[0]
-    coarse = up_ref.shape[1]
-    for q in range(4):
-        up_ref[q * quarter : (q + 1) * quarter] = (
-            totals_ref[:, width + q * coarse : width + (q + 1) * coarse].astype(F32) * scale
-        )
 
 
 def passed_along(value, axis, steps):
@@ -415,7 +421,9 @@
     near = neighbours[0, 0].T.reshape(27, 1, bricks)
     up_turned = up_weight.transpose(0, 2, 1).reshape(8 * C, coarse)
     half = item_width // 2
-    share = 2 * C // devices
+    count = 2 * C
+    sums_width = 14 * C + 8 * C * coarse // count
+    back_width = capacity * devices * item_width // count + sums_width
     band = pltpu.VMEM((9, WIDE, RUN), BF)
     face_rows = shape((face, width))
     conv_flops = 2 * 9 * 16 * bricks * WIDE * RUN
@@ -442,24 +450,18 @@
     )
     grad_prev = passed_along(high_grad, "gy", 1)
     grad_next = passed_along(low_grad, "gy", -1)
-    grad_fine, replies = call(
-        functools.partial(fine_grad_body, devices=devices),
-        [shape((bricks, width)), shape((devices * (2 * capacity + share), half))],
+    output, grad_fine, back = call(
+        functools.partial(last_body, devices=devices),
+        [shape((bricks, width)), shape((bricks, width)), shape((count, back_width))],
+        merged, low_side, high_side, below, above, cot, conv_weight, near,
         fine_part, sides, grad_next, grad_prev, up_turned, parents, slots,
-    )
-    returned = trade_rows(replies, devices)
-    output, conv_sum = call(
-        conv_body, [shape((bricks, width)), shape((2 * C, 14 * C))],
-        merged, low_side, high_side, below, above, cot, conv_weight, near,
         scratch=[band, pltpu.VMEM((6, 6, bricks, WIDE), BF), pltpu.VMEM((bricks + 4 * face, width), BF)],
         flops=2 * conv_flops,
     )
-    coarse_grad, up_share = call(
-        coarse_grad_body, [shape((item_count, item_width)), shape((share, half))], returned, sends
-    )
-    arrived = trade_rows(conv_sum, devices)
-    (own_share,) = call(share_body, [shape((share, 14 * C + half))], arrived, up_share)
-    totals = lax.all_gather(own_share, ("gx", "gy"), axis=0, tiled=True)
+    back = trade_rows(back, devices)
+    (sums,) = call(functools.partial(share_body, devices=devices), [shape((count, sums_width))], back)
+    totals = trade_rows(sums, devices)
+    (coarse_grad,) = call(coarse_grad_body, [shape((item_count, item_width))], back, sends)
     scale = 1.0 / math.sqrt(64 * bricks * devices)
     grad_conv, grad_up = call(
         functools.partial(final_body, scale=scale),

time: 110 us -> 82.8 us (0.75)
  blocking collectives: 33.4 us -> 21.6 us
  starting transfers between devices: 41.1 us -> 30.8 us
  waiting for transfers between devices: 18.3 us -> 13.5 us
    all_gather x1 -> x0, blocking collectives: 33.4 us -> none  [on_device(): totals = lax.all_gather(own_share, ('gx', 'gy'), axis=0, tiled=True)]
    all_to_all x0 -> x1, blocking collectives: none -> 21.6 us  [trade_rows(): lax.all_to_all(grid_view, ('gx', 'gy'), split_axis=0, concat_axis=0, tile...]
    all_to_all x3 -> x2, starting transfers between devices: 23.1 us -> 11 us  [trade_rows(): lax.all_to_all(grid_view, ('gx', 'gy'), split_axis=0, concat_axis=0, tile...]
    ppermute x8, waiting for transfers between devices: 10 us -> 2.38 us  [passed_along(): lax.ppermute(value, axis, [(source, source + steps) for source in range(i...]
    all_to_all x3 -> x2, waiting for transfers between devices: 8.25 us -> 11.1 us  [trade_rows(): lax.all_to_all(grid_view, ('gx', 'gy'), split_axis=0, concat_axis=0, tile...]
    ppermute x8, starting transfers between devices: 18 us -> 19.7 us  [passed_along(): lax.ppermute(value, axis, [(source, source + steps) for source in range(i...]
    pallas_call x10 -> x9, Pallas kernels: 12.1 us -> 11.6 us  [call(): pl.pallas_call(body, out_shape=tuple(outs), scratch_shapes=tuple(scratch)...]
  transfers between devices with their start and end apart: 11 -> 10, of which waited for: 6 -> 3; matrix products, arithmetic and copies ran while one was open for 0% -> 0% of each run, Pallas kernels for 7% -> 5%
where the time goes in v1:
time: 82.8 us; the launch traced here: 82.2 us
  starting transfers between devices  30.8 us (37%)
  blocking collectives  21.6 us (26%)
  waiting for transfers between devices  13.5 us (16%)
  Pallas kernels  11.6 us (14%)
  local copies, waits for them, and re-layouts  3.91 us (5%)
  between operations  0.86 us (1%)
    all_to_all x1, blocking collectives, trade_rows(): lax.all_to_all(grid_view, ('gx', 'gy'), split_axis=0, concat_axis=0, tile...  21.6 us
    ppermute x8, starting transfers between devices, passed_along(): lax.ppermute(value, axis, [(source, source + steps) for source in range(i...  19.7 us
    pallas_call x9, Pallas kernels, call(): pl.pallas_call(body, out_shape=tuple(outs), scratch_shapes=tuple(scratch)...  11.6 us
    all_to_all x2, waiting for transfers between devices, trade_rows(): lax.all_to_all(grid_view, ('gx', 'gy'), split_axis=0, concat_axis=0, tile...  11.1 us
    all_to_all x2, starting transfers between devices, trade_rows(): lax.all_to_all(grid_view, ('gx', 'gy'), split_axis=0, concat_axis=0, tile...  11 us
    unnamed x23, local copies, waits for them, and re-layouts  3.89 us
    ppermute x8, waiting for transfers between devices, passed_along(): lax.ppermute(value, axis, [(source, source + steps) for source in range(i...  2.38 us
  transfers between devices with their start and end apart: 10, of which 3 were waited for; matrix products, arithmetic and copies ran while one was open for 0% of the time, Pallas kernels for 5%

profile of v1, /device:TPU:0, one launch (start us, length us, event | category | flops | bytes accessed | tf_op | source)
XLA Modules:
  0.0 82.2 jit_solution(3753106017721524777)
XLA Ops:
  0.6 0.0 copy-start.3
  0.6 0.7 copy-done.3
  1.3 0.9 %copy-done.2 = bf16[1,1,64,1024]{3,2,1,0:T(8,128)(2,1)S(1)} copy-done((bf16[1,1,64,1024]{3,2,1,0:T(8,128)(2,1)S(1)}, bf16[1,1,64,1024]{3,2,1,0:T(8,128)(2,1)}, u32[]{:S(2)}) %copy-start.2) | copy-done | bytes 131096
  2.2 0.0 copy-start.7
  2.2 1.0 %shard_map.137 = bf16[128,512]{1,0:T(8,128)(2,1)} custom-call(s32[4,16]{1,0:T(4,128)S(1)} %bitcast.38, bf16[64,1024]{1,0:T(8,128)(2,1)S(1)} %bitcast.37), custom_call_target="tpu_custom_call" | custom-call | bytes 262400 | tf_op jit(solution)/shard_map/pallas_call | solution.py:49
  3.3 0.0 copy-start.10
  3.3 7.5 %all-to-all-start = ((bf16[16,8,512]{2,1,0:T(8,128)(2,1)}), bf16[16,8,512]{2,1,0:T(8,128)(2,1)S(1)}, u32[]{:S(2)}, u32[]{:S(2)}) async-start(bf16[16,8,512]{2,1,0:T(8,128)(2,1)} %bitcast.3), calls=%async_computation | async-start | bytes 262144 | tf_op jit(solution)/shard_map/all_to_all | solution.py:399
  10.8 0.0 copy-done.10
  10.8 0.0 copy-done.7
  10.8 0.0 copy-start.8
  10.8 0.9 %copy-done.8 = bf16[1,1,32,4096]{3,2,1,0:T(8,128)(2,1)S(1)} copy-done((bf16[1,1,32,4096]{3,2,1,0:T(8,128)(2,1)S(1)}, bf16[1,1,32,4096]{3,2,1,0:T(8,128)(2,1)}, u32[]{:S(2)}) %copy-start.8) | copy-done | bytes 262168
  11.8 0.0 copy-start
  11.8 1.9 %shard_map.140 = (f32[48,4096]{1,0:T(8,128)S(1)}, bf16[8,4096]{1,0:T(8,128)(2,1)S(1)}, bf16[8,4096]{1,0:T(8,128)(2,1)S(1)}) custom-call(bf16[32,4096]{1,0:T(8,128)(2,1)S(1)} %bitcast.46, bf16[27,64,64]{2,1,0:T(8,128)(2,1)S(1)} %copy-done.7, s32[27,1,32]{2,1,0:T(1,128)S(1)} %reshape.49.near_ref), custom_call_target="tpu_custom_call" | custom-call | flops 1811939328 | bytes 1404288 | tf_op jit(solution)/shard_map/pallas_call | solution.py:49
  13.7 1.3 %collective-permute-start.4 = (bf16[8,4096]{1,0:T(8,128)(2,1)S(1)}, bf16[8,4096]{1,0:T(8,128)(2,1)S(1)}, u32[]{:S(2)}, u32[]{:S(2)}) collective-permute-start(bf16[8,4096]{1,0:T(8,128)(2,1)S(1)} %get-tuple-element.28), channel_id=1, source_target_pairs={{4,0},{8,4},{12,8},{5,1},{9,5},{13,9},{6,2},{10,6},{14,10},{7,3},{... | collective-permute-start | bytes 196616 | tf_op jit(solution)/shard_map/ppermute | solution.py:393
  15.0 3.0 %collective-permute-start.5 = (bf16[8,4096]{1,0:T(8,128)(2,1)S(1)}, bf16[8,4096]{1,0:T(8,128)(2,1)S(1)}, u32[]{:S(2)}, u32[]{:S(2)}) collective-permute-start(bf16[8,4096]{1,0:T(8,128)(2,1)S(1)} %get-tuple-element.29), channel_id=1, source_target_pairs={{0,4},{4,8},{8,12},{1,5},{5,9},{9,13},{2,6},{6,10},{10,14},{3,7},{... | collective-permute-start | bytes 196616 | tf_op jit(solution)/shard_map/ppermute | solution.py:393
  18.0 0.1 all-to-all-done
  18.1 0.0 copy-done
  18.1 0.0 copy-done.1
  18.1 0.7 copy-done.5
  18.8 0.0 copy-done.6
  18.8 0.6 shard_map.138
  19.4 3.8 %collective-permute-start = (bf16[8,4096]{1,0:T(8,128)(2,1)S(1)}, bf16[8,4096]{1,0:T(8,128)(2,1)S(1)}, u32[]{:S(2)}, u32[]{:S(2)}) collective-permute-start(bf16[8,4096]{1,0:T(8,128)(2,1)S(1)} %get-tuple-element.23), channel_id=1, source_target_pairs={{0,1},{1,2},{2,3},{4,5},{5,6},{6,7},{8,9},{9,10},{10,11},{12,13},{... | collective-permute-start | bytes 196616 | tf_op jit(solution)/shard_map/ppermute | solution.py:393
  23.2 1.3 %collective-permute-start.1 = (bf16[8,4096]{1,0:T(8,128)(2,1)S(1)}, bf16[8,4096]{1,0:T(8,128)(2,1)S(1)}, u32[]{:S(2)}, u32[]{:S(2)}) collective-permute-start(bf16[8,4096]{1,0:T(8,128)(2,1)S(1)} %get-tuple-element.24), channel_id=1, source_target_pairs={{1,0},{2,1},{3,2},{5,4},{6,5},{7,6},{9,8},{10,9},{11,10},{13,12},{... | collective-permute-start | bytes 196616 | tf_op jit(solution)/shard_map/ppermute | solution.py:393
  24.5 0.0 collective-permute-done.4.next_ref
  24.5 0.0 collective-permute-done.5.prev_ref
  24.5 0.0 copy-start.4
  24.5 0.7 copy-done.4
  25.2 0.3 shard_map.141
  25.5 0.0 copy-start.9
  25.5 1.4 %collective-permute-start.6 = (bf16[8,4096]{1,0:T(8,128)(2,1)S(1)}, bf16[8,4096]{1,0:T(8,128)(2,1)S(1)}, u32[]{:S(2)}, u32[]{:S(2)}) collective-permute-start(bf16[8,4096]{1,0:T(8,128)(2,1)S(1)} %get-tuple-element.31), channel_id=1, source_target_pairs={{1,0},{2,1},{3,2},{5,4},{6,5},{7,6},{9,8},{10,9},{11,10},{13,12},{... | collective-permute-start | bytes 196616 | tf_op jit(solution)/shard_map/ppermute | solution.py:393
  26.9 5.2 %collective-permute-start.7 = (bf16[8,4096]{1,0:T(8,128)(2,1)S(1)}, bf16[8,4096]{1,0:T(8,128)(2,1)S(1)}, u32[]{:S(2)}, u32[]{:S(2)}) collective-permute-start(bf16[8,4096]{1,0:T(8,128)(2,1)S(1)} %get-tuple-element.32), channel_id=1, source_target_pairs={{0,1},{1,2},{2,3},{4,5},{5,6},{6,7},{8,9},{9,10},{10,11},{12,13},{... | collective-permute-start | bytes 196616 | tf_op jit(solution)/shard_map/ppermute | solution.py:393
  32.1 0.0 collective-permute-done.low_ref
  32.1 0.0 collective-permute-done.1.high_ref
  32.1 0.3 shard_map.139
  32.4 2.5 %collective-permute-start.2 = (bf16[8,4096]{1,0:T(8,128)(2,1)S(1)}, bf16[8,4096]{1,0:T(8,128)(2,1)S(1)}, u32[]{:S(2)}, u32[]{:S(2)}) collective-permute-start(bf16[8,4096]{1,0:T(8,128)(2,1)S(1)} %get-tuple-element.25), channel_id=1, source_target_pairs={{0,4},{4,8},{8,12},{1,5},{5,9},{9,13},{2,6},{6,10},{10,14},{3,7},{... | collective-permute-start | bytes 196616 | tf_op jit(solution)/shard_map/ppermute | solution.py:393
  34.9 1.3 %collective-permute-start.3 = (bf16[8,4096]{1,0:T(8,128)(2,1)S(1)}, bf16[8,4096]{1,0:T(8,128)(2,1)S(1)}, u32[]{:S(2)}, u32[]{:S(2)}) collective-permute-start(bf16[8,4096]{1,0:T(8,128)(2,1)S(1)} %get-tuple-element.26), channel_id=1, source_target_pairs={{4,0},{8,4},{12,8},{5,1},{9,5},{13,9},{6,2},{10,6},{14,10},{7,3},{... | collective-permute-start | bytes 196616 | tf_op jit(solution)/shard_map/ppermute | solution.py:393
  36.2 0.0 collective-permute-done.6.next_ref
  36.2 0.0 collective-permute-done.7.prev_ref
  36.2 0.0 collective-permute-done.2.below_ref
  36.2 2.4 %collective-permute-done.3.above_ref = bf16[8,4096]{1,0:T(8,128)(2,1)S(1)} collective-permute-done((bf16[8,4096]{1,0:T(8,128)(2,1)S(1)}, bf16[8,4096]{1,0:T(8,128)(2,1)S(1)}, u32[]{:S(2)}, u32[]{:S(2)}) %collective-permute-start.3) | collective-permute-done | bytes 65568 | tf_op jit(solution)/shard_map/ppermute | solution.py:393
  38.6 0.0 copy-done.9
  38.6 4.1 %shard_map.142 = (bf16[32,4096]{1,0:T(8,128)(2,1)}, bf16[32,4096]{1,0:T(8,128)(2,1)}, bf16[128,1920]{1,0:T(8,128)(2,1)S(1)}) custom-call(bf16[32,4096]{1,0:T(8,128)(2,1)S(1)} %get-tuple-element.22.merged_ref, bf16[8,4096]{1,0:T(8,128)(2,1)S(1)} %collective-permute-done.low_ref, bf16[8,4096]{1,0:T(8,128)(2,1)S(1)} %collective-permute-done.1.high_ref, ...), custom_call_target="tpu_custom_call" | custom-call | flops 1811939328 | bytes 2879040 | tf_op jit(solution)/shard_map/pallas_call | solution.py:49
  42.7 21.6 %all_to_all.15 = bf16[16,8,1920]{2,1,0:T(8,128)(2,1)S(1)} all-to-all(bf16[16,8,1920]{2,1,0:T(8,128)(2,1)S(1)} %bitcast.33), channel_id=1, replica_groups=mesh['groups'=2,'gx'=4,'gy'=4] {'gx','gy'}, dimensions={0} | all-to-all | bytes 983040 | tf_op jit(solution)/shard_map/all_to_all | solution.py:399
  64.3 1.0 %shard_map.144 = bf16[128,1408]{1,0:T(8,128)(2,1)} custom-call(bf16[128,1920]{1,0:T(8,128)(2,1)S(1)} %bitcast.29), custom_call_target="tpu_custom_call" | custom-call | bytes 851968 | tf_op jit(solution)/shard_map/pallas_call | solution.py:49
  65.2 3.5 %all-to-all-start.2 = ((bf16[16,8,1408]{2,1,0:T(8,128)(2,1)}), bf16[16,8,1408]{2,1,0:T(8,128)(2,1)S(1)}, u32[]{:S(2)}, u32[]{:S(2)}) async-start(bf16[16,8,1408]{2,1,0:T(8,128)(2,1)} %bitcast.19), calls=%async_computation.2 | async-start | bytes 720896 | tf_op jit(solution)/shard_map/all_to_all | solution.py:399
  68.8 1.1 %shard_map.143 = bf16[64,1024]{1,0:T(8,128)(2,1)} custom-call(bf16[128,1920]{1,0:T(8,128)(2,1)S(1)} %bitcast.30, s32[4,16]{1,0:T(4,128)S(1)} %bitcast.39), custom_call_target="tpu_custom_call" | custom-call | bytes 622848 | tf_op jit(solution)/shard_map/pallas_call | solution.py:49
  69.9 11.0 %all-to-all-done.2 = bf16[16,8,1408]{2,1,0:T(8,128)(2,1)S(1)} async-done(((bf16[16,8,1408]{2,1,0:T(8,128)(2,1)}), bf16[16,8,1408]{2,1,0:T(8,128)(2,1)S(1)}, u32[]{:S(2)}, u32[]{:S(2)}) %all-to-all-start.2) | async-done | bytes 360480 | tf_op jit(solution)/shard_map/all_to_all | solution.py:399
  80.9 1.2 %shard_map.145 = (f32[27,64,64]{2,1,0:T(8,128)}, f32[512,128]{1,0:T(8,128)}) custom-call(bf16[128,1408]{1,0:T(8,128)(2,1)S(1)} %bitcast.31), custom_call_target="tpu_custom_call" | custom-call | bytes 1064960 | tf_op jit(solution)/shard_map/pallas_call | solution.py:49
  (6 shorter events, 0.0 us)
Async XLA Ops:
  0.6 0.7 copy-start.3
  1.3 0.9 %copy-start.2 = (bf16[1,1,64,1024]{3,2,1,0:T(8,128)(2,1)S(1)}, bf16[1,1,64,1024]{3,2,1,0:T(8,128)(2,1)}, u32[]{:S(2)}) copy-start(bf16[1,1,64,1024]{3,2,1,0:T(8,128)(2,1)} %param.11) | copy-start | bytes 393220
  2.2 8.6 %copy-start.7 = (bf16[27,64,64]{2,1,0:T(8,128)(2,1)S(1)}, bf16[27,64,64]{2,1,0:T(8,128)(2,1)}, u32[]{:S(2)}) copy-start(bf16[27,64,64]{2,1,0:T(8,128)(2,1)} %weight_ref.3) | copy-start | bytes 663556
  3.3 7.5 %copy-start.10 = (s32[1,1,32,27]{2,1,3,0:T(1,128)S(1)}, s32[1,1,32,27]{2,1,3,0:T(1,128)}, u32[]{:S(2)}) copy-start(s32[1,1,32,27]{2,1,3,0:T(1,128)} %param.14) | copy-start | bytes 10372
  3.3 14.8 %all-to-all-start = ((bf16[16,8,512]{2,1,0:T(8,128)(2,1)}), bf16[16,8,512]{2,1,0:T(8,128)(2,1)S(1)}, u32[]{:S(2)}, u32[]{:S(2)}) async-start(bf16[16,8,512]{2,1,0:T(8,128)(2,1)} %bitcast.3), calls=%async_computation | async-start | bytes 262144 | tf_op jit(solution)/shard_map/all_to_all | solution.py:399
  10.8 1.0 %copy-start.8 = (bf16[1,1,32,4096]{3,2,1,0:T(8,128)(2,1)S(1)}, bf16[1,1,32,4096]{3,2,1,0:T(8,128)(2,1)}, u32[]{:S(2)}) copy-start(bf16[1,1,32,4096]{3,2,1,0:T(8,128)(2,1)} %param.19) | copy-start | bytes 786436
  11.8 6.4 %copy-start = (bf16[1,1,32,4096]{3,2,1,0:T(8,128)(2,1)S(1)}, bf16[1,1,32,4096]{3,2,1,0:T(8,128)(2,1)}, u32[]{:S(2)}) copy-start(bf16[1,1,32,4096]{3,2,1,0:T(8,128)(2,1)} %param.10) | copy-start | bytes 786436
  11.8 6.4 %copy-start.1 = (bf16[8,128,64]{1,2,0:T(8,128)(2,1)S(1)}, bf16[8,128,64]{1,2,0:T(8,128)(2,1)}, u32[]{:S(2)}) copy-start(bf16[8,128,64]{1,2,0:T(8,128)(2,1)} %param.13) | copy-start | bytes 393220
  13.7 10.8 %collective-permute-start.4 = (bf16[8,4096]{1,0:T(8,128)(2,1)S(1)}, bf16[8,4096]{1,0:T(8,128)(2,1)S(1)}, u32[]{:S(2)}, u32[]{:S(2)}) collective-permute-start(bf16[8,4096]{1,0:T(8,128)(2,1)S(1)} %get-tuple-element.28), channel_id=1, source_target_pairs={{4,0},{8,4},{12,8},{5,1},{9,5},{13,9},{6,2},{10,6},{14,10},{7,3},{... | collective-permute-start | bytes 196616 | tf_op jit(solution)/shard_map/ppermute | solution.py:393
  15.0 9.5 %collective-permute-start.5 = (bf16[8,4096]{1,0:T(8,128)(2,1)S(1)}, bf16[8,4096]{1,0:T(8,128)(2,1)S(1)}, u32[]{:S(2)}, u32[]{:S(2)}) collective-permute-start(bf16[8,4096]{1,0:T(8,128)(2,1)S(1)} %get-tuple-element.29), channel_id=1, source_target_pairs={{0,4},{4,8},{8,12},{1,5},{5,9},{9,13},{2,6},{6,10},{10,14},{3,7},{... | collective-permute-start | bytes 196616 | tf_op jit(solution)/shard_map/ppermute | solution.py:393
  18.1 0.7 copy-start.5
  18.1 0.7 copy-start.6
  19.4 12.7 %collective-permute-start = (bf16[8,4096]{1,0:T(8,128)(2,1)S(1)}, bf16[8,4096]{1,0:T(8,128)(2,1)S(1)}, u32[]{:S(2)}, u32[]{:S(2)}) collective-permute-start(bf16[8,4096]{1,0:T(8,128)(2,1)S(1)} %get-tuple-element.23), channel_id=1, source_target_pairs={{0,1},{1,2},{2,3},{4,5},{5,6},{6,7},{8,9},{9,10},{10,11},{12,13},{... | collective-permute-start | bytes 196616 | tf_op jit(solution)/shard_map/ppermute | solution.py:393
  23.2 9.0 %collective-permute-start.1 = (bf16[8,4096]{1,0:T(8,128)(2,1)S(1)}, bf16[8,4096]{1,0:T(8,128)(2,1)S(1)}, u32[]{:S(2)}, u32[]{:S(2)}) collective-permute-start(bf16[8,4096]{1,0:T(8,128)(2,1)S(1)} %get-tuple-element.24), channel_id=1, source_target_pairs={{1,0},{2,1},{3,2},{5,4},{6,5},{7,6},{9,8},{10,9},{11,10},{13,12},{... | collective-permute-start | bytes 196616 | tf_op jit(solution)/shard_map/ppermute | solution.py:393
  24.5 0.7 copy-start.4
  25.5 13.1 %copy-start.9 = (bf16[1,1,32,4096]{3,2,1,0:T(8,128)(2,1)S(1)}, bf16[1,1,32,4096]{3,2,1,0:T(8,128)(2,1)}, u32[]{:S(2)}) copy-start(bf16[1,1,32,4096]{3,2,1,0:T(8,128)(2,1)} %param.19) | copy-start | bytes 786436
  25.5 10.7 %collective-permute-start.6 = (bf16[8,4096]{1,0:T(8,128)(2,1)S(1)}, bf16[8,4096]{1,0:T(8,128)(2,1)S(1)}, u32[]{:S(2)}, u32[]{:S(2)}) collective-permute-start(bf16[8,4096]{1,0:T(8,128)(2,1)S(1)} %get-tuple-element.31), channel_id=1, source_target_pairs={{1,0},{2,1},{3,2},{5,4},{6,5},{7,6},{9,8},{10,9},{11,10},{13,12},{... | collective-permute-start | bytes 196616 | tf_op jit(solution)/shard_map/ppermute | solution.py:393
  26.9 9.3 %collective-permute-start.7 = (bf16[8,4096]{1,0:T(8,128)(2,1)S(1)}, bf16[8,4096]{1,0:T(8,128)(2,1)S(1)}, u32[]{:S(2)}, u32[]{:S(2)}) collective-permute-start(bf16[8,4096]{1,0:T(8,128)(2,1)S(1)} %get-tuple-element.32), channel_id=1, source_target_pairs={{0,1},{1,2},{2,3},{4,5},{5,6},{6,7},{8,9},{9,10},{10,11},{12,13},{... | collective-permute-start | bytes 196616 | tf_op jit(solution)/shard_map/ppermute | solution.py:393
  32.4 3.8 %collective-permute-start.2 = (bf16[8,4096]{1,0:T(8,128)(2,1)S(1)}, bf16[8,4096]{1,0:T(8,128)(2,1)S(1)}, u32[]{:S(2)}, u32[]{:S(2)}) collective-permute-start(bf16[8,4096]{1,0:T(8,128)(2,1)S(1)} %get-tuple-element.25), channel_id=1, source_target_pairs={{0,4},{4,8},{8,12},{1,5},{5,9},{9,13},{2,6},{6,10},{10,14},{3,7},{... | collective-permute-start | bytes 196616 | tf_op jit(solution)/shard_map/ppermute | solution.py:393
  34.9 3.7 %collective-permute-start.3 = (bf16[8,4096]{1,0:T(8,128)(2,1)S(1)}, bf16[8,4096]{1,0:T(8,128)(2,1)S(1)}, u32[]{:S(2)}, u32[]{:S(2)}) collective-permute-start(bf16[8,4096]{1,0:T(8,128)(2,1)S(1)} %get-tuple-element.26), channel_id=1, source_target_pairs={{4,0},{8,4},{12,8},{5,1},{9,5},{13,9},{6,2},{10,6},{14,10},{7,3},{... | collective-permute-start | bytes 196616 | tf_op jit(solution)/shard_map/ppermute | solution.py:393
  65.2 15.7 %all-to-all-start.2 = ((bf16[16,8,1408]{2,1,0:T(8,128)(2,1)}), bf16[16,8,1408]{2,1,0:T(8,128)(2,1)S(1)}, u32[]{:S(2)}, u32[]{:S(2)}) async-start(bf16[16,8,1408]{2,1,0:T(8,128)(2,1)} %bitcast.19), calls=%async_computation.2 | async-start | bytes 720896 | tf_op jit(solution)/shard_map/all_to_all | solution.py:399

commit v2 on v1

--- a/solution.py
+++ b/solution.py
@@ -44,11 +44,12 @@
     return jnp.sum(jnp.where(diagonal, spread, 0.0), axis=1, keepdims=True).astype(I32)
 
 
-def call(body, outs, *args, scratch=(), flops=0):
+def call(body, outs, *args, scratch=(), flops=0, in_hbm=False):
     moved = sum(a.size * a.dtype.itemsize for a in list(args) + list(outs))
     return pl.pallas_call(
         body,
         out_shape=tuple(outs),
+        in_specs=[pl.BlockSpec(memory_space=pl.ANY) if in_hbm else pl.BlockSpec() for _ in args],
         scratch_shapes=tuple(scratch),
         cost_estimate=pl.CostEstimate(flops=flops, bytes_accessed=moved, transcendentals=0),
         compiler_params=pltpu.CompilerParams(vmem_limit_bytes=28 * 2**20),
@@ -69,7 +70,7 @@
     return jnp.sum(picked, axis=0, keepdims=True).astype(I32)
 
 
-def items_out_body(sends_ref, items_ref, out_ref):
+def items_out(sends_ref, items_ref, out_ref):
     capacity, devices = sends_ref.shape
     count, width = items_ref.shape
     half = width // 2
@@ -82,10 +83,10 @@
     out_ref[...] = total.astype(BF)
 
 
-def merge_body(received_ref, slots_ref, up_ref, fine_ref, sides_ref, merged_ref, parents_ref, a_ref, b_ref):
+def merge(received_ref, slots, up_ref, fine_ref, merged_ref, parents_ref):
     bricks = fine_ref.shape[0]
     lanes, half = received_ref.shape
-    slot = column_of(slots_ref[...])
+    slot = column_of(slots)
     place = iota((bricks, lanes), 1)
     named = place // 2 == slot
     received = received_ref[...]
@@ -103,24 +104,36 @@
             at = (vx * 4 + vy) * RUN + cz * 2 * C
             add = lifted[v * bricks : (v + 1) * bricks, parity * 2 * C : (parity + 1) * 2 * C]
             merged_ref[:, at : at + 2 * C] = (fine_ref[:, at : at + 2 * C].astype(F32) + add).astype(BF)
-    pick_rows(sides_ref[...], merged_ref[...], a_ref, b_ref)
-
-
-def pick_rows(lists, rows, a_ref, b_ref):
-    count = rows.shape[0]
-    for which, out_ref in ((0, a_ref), (1, b_ref)):
-        face = lists.shape[1]
-        chosen = ones_where(iota((count, face), 0) == lists[which : which + 1])
-        out_ref[...] = dot_tn(chosen, rows).astype(BF)
-
-
-def stack_rows(*refs):
-    return jnp.concatenate([r[...].astype(F32) for r in refs], axis=0).astype(BF)
-
-
-def cross_body(merged_ref, low_ref, high_ref, crosses_ref, a_ref, b_ref):
-    rows = jnp.concatenate([merged_ref[...], stack_rows(low_ref, high_ref)], axis=0)
-    pick_rows(crosses_ref[...], rows, a_ref, b_ref)
+
+
+def pick_rows(lists, rows):
+    place = iota((rows.shape[0], lists.shape[1]), 0)
+    return [dot_tn(ones_where(place == lists[w : w + 1]), rows) for w in (0, 1)]
+
+
+def stack_rows(*parts):
+    return jnp.concatenate([p.astype(F32) for p in parts], axis=0).astype(BF)
+
+
+def sides_of(lists_ref, face):
+    return lists_ref[0:2, :face]
+
+
+def crosses_of(lists_ref, face):
+    return lists_ref[2:4, :face]
+
+
+def slots_of(lists_ref, bricks):
+    return lists_ref[4:5, :bricks]
+
+
+def cross_body(merged_ref, low_ref, high_ref, lists_ref, a_ref, b_ref):
+    face = a_ref.shape[0]
+    sides = stack_rows(low_ref[...].astype(F32)[:face], high_ref[...].astype(F32)[:face])
+    rows = jnp.concatenate([merged_ref[...], sides], axis=0)
+    first, second = pick_rows(crosses_of(lists_ref, face), rows)
+    a_ref[...] = first.astype(BF)
+    b_ref[...] = second.astype(BF)
 
 
 def build_bands(weight_ref, band_ref):
@@ -164,7 +177,7 @@
     return head, (value - head.astype(F32)).astype(BF)
 
 
-def table_grad_body(cot_ref, weight_ref, near_ref, ext_ref, low_ref, high_ref, band_ref, pad_ref):
+def table_grad(cot_ref, weight_ref, near_ref, ext_ref, low_ref, high_ref, band_ref, pad_ref):
     bricks = cot_ref.shape[0]
     face = low_ref.shape[0]
     start = ext_ref.shape[0]
@@ -213,15 +226,41 @@
             high_ref[:, at : at + RUN] = total[start + face :].astype(BF)
 
 
+def first_body(
+    sends_hbm, items_hbm, weight_hbm, cot_hbm, near_hbm, sides_hbm, crosses_hbm, slots_hbm,
+    out_ref, ext_ref, low_ref, high_ref, lists_ref,
+    sends_ref, items_ref, weight_ref, cot_ref, near_ref, sides_ref, crosses_ref, slots_ref, band_ref, pad_ref, arrived,
+):
+    sources = (sends_hbm, items_hbm, weight_hbm, cot_hbm, near_hbm, sides_hbm, crosses_hbm, slots_hbm)
+    places = (sends_ref, items_ref, weight_ref, cot_ref, near_ref, sides_ref, crosses_ref, slots_ref)
+    copies = [pltpu.make_async_copy(s, p, arrived.at[i]) for i, (s, p) in enumerate(zip(sources, places))]
+    for copy in copies:
+        copy.start()
+    copies[0].wait()
+    copies[1].wait()
+    items_out(sends_ref, items_ref, out_ref)
+    for copy in copies[2:]:
+        copy.wait()
+    face, bricks = (sides_ref.shape[1], slots_ref.shape[1])
+    lists_ref[...] = jnp.zeros(lists_ref.shape, I32)
+    lists_ref[0:2, :face] = sides_ref[...]
+    lists_ref[2:4, :face] = crosses_ref[...]
+    lists_ref[4:5, :bricks] = slots_ref[...]
+    table_grad(cot_ref, weight_ref, near_ref, ext_ref, low_ref, high_ref, band_ref, pad_ref)
+
+
 def conv_body(
     merged_ref, low_ref, high_ref, below_ref, above_ref, cot_ref, weight_ref, near_ref,
     out_ref, back_ref, band_ref, pad_ref, table_ref,
 ):
     bricks = merged_ref.shape[0]
-    rows = bricks + 4 * low_ref.shape[0]
+    face = below_ref.shape[0]
+    rows = bricks + 4 * face
     build_bands(weight_ref, band_ref)
     table_ref[:bricks] = merged_ref[...]
-    table_ref[bricks:] = stack_rows(low_ref, high_ref, below_ref, above_ref)
+    table_ref[bricks:] = stack_rows(
+        low_ref[...].astype(F32)[:face], high_ref[...].astype(F32)[:face], below_ref[...], above_ref[...]
+    )
     near = jnp.concatenate([near_ref[o] for o in range(27)] + [jnp.zeros((5, bricks), I32)], axis=0)
     near = near.astype(F32).T.astype(I32)
 
@@ -282,28 +321,36 @@
         out_ref[:, p * RUN : (p + 1) * RUN] = total[p * bricks : (p + 1) * bricks].astype(BF)
     for pair in range(7):
         both = [jnp.where(lanes_low, sums[14 * h + 2 * pair], sums[14 * h + 2 * pair + 1]) for h in range(2)]
-        at = back_ref.shape[1] - 14 * C + pair * 2 * C
+        at = pair * 2 * C
         back_ref[:, at : at + 2 * C] = jnp.concatenate(both, axis=0).astype(BF)
 
 
-def add_rows(base, lists, first_ref, second_ref):
+def add_rows(base, lists, first, second):
     count, face = (base.shape[0], lists.shape[1])
     index = jnp.concatenate([lists[0:1], lists[1:2]], axis=1)
     chosen = ones_where(iota((count, 2 * face), 0) == index)
-    return base + dot(chosen, stack_rows(first_ref, second_ref))
-
-
-def side_grad_body(ext_ref, crosses_ref, next_ref, prev_ref, fine_ref, low_ref, high_ref):
-    bricks, face = (fine_ref.shape[0], low_ref.shape[0])
-    total = add_rows(ext_ref[...], crosses_ref[...], next_ref, prev_ref)
-    fine_ref[...] = total[:bricks]
-    low_ref[...] = total[bricks : bricks + face].astype(BF)
-    high_ref[...] = total[bricks + face :].astype(BF)
-
-
-def fine_grad_body(fine_ref, sides_ref, next_ref, prev_ref, up_ref, parents_ref, slots_ref, grad_ref, back_ref, devices):
-    bricks = fine_ref.shape[0]
-    grad_ref[...] = add_rows(fine_ref[...], sides_ref[...], next_ref, prev_ref).astype(BF)
+    return base + dot(chosen, stack_rows(first, second))
+
+
+def merge_body(
+    received_ref, up_ref, fine_ref, lists_ref, ext_ref, next_ref, prev_ref,
+    merged_ref, parents_ref, part_ref, a_ref, b_ref,
+):
+    bricks, face = (fine_ref.shape[0], next_ref.shape[0])
+    total = add_rows(ext_ref[...], crosses_of(lists_ref, face), next_ref[...], prev_ref[...])
+    part_ref[...] = total[:bricks]
+    merge(received_ref, slots_of(lists_ref, bricks), up_ref, fine_ref, merged_ref, parents_ref)
+    first, second = pick_rows(sides_of(lists_ref, face), merged_ref[...])
+    a_ref[...] = stack_rows(first, total[bricks + face :])
+    b_ref[...] = stack_rows(second, total[bricks : bricks + face])
+
+
+def fine_grad_body(part_ref, lists_ref, next_ref, prev_ref, up_ref, parents_ref, grad_ref, back_ref):
+    bricks = part_ref.shape[0]
+    face = next_ref.shape[0] // 2
+    grad_ref[...] = add_rows(
+        part_ref[...], sides_of(lists_ref, face), next_ref[...].astype(F32)[face:], prev_ref[...].astype(F32)[face:]
+    ).astype(BF)
     stacked = []
     for v in range(8):
         cx, cy, cz = (v // 4, v // 2 % 2, v % 2)
@@ -320,37 +367,27 @@
     up_sum = dot_tn(stacked, parents_ref[...]).astype(BF)
     coarse = up_sum.shape[1]
     parts = up_sum.shape[0] // count
-    item_lanes = back_ref.shape[1] - 14 * C - parts * coarse
+    item_lanes = back_ref.shape[1] - parts * coarse
     for q in range(parts):
         at = item_lanes + q * coarse
         back_ref[:, at : at + coarse] = up_sum[q * count : (q + 1) * count]
+    slots = slots_of(lists_ref, bricks)
     for j in range(item_lanes // half):
         piece = iota((count, bricks), 0) * (item_lanes // half) + j
-        named = piece // 2 == slots_ref[...]
+        named = piece // 2 == slots
         rows = dot(ones_where(named & (piece % 2 == 0)), items[:, :half])
         rows += dot(ones_where(named & (piece % 2 == 1)), items[:, half:])
         back_ref[:, j * half : (j + 1) * half] = rows.astype(BF)
 
 
-def last_body(
-    merged_ref, low_ref, high_ref, below_ref, above_ref, cot_ref, weight_ref, near_ref,
-    fine_ref, sides_ref, next_ref, prev_ref, up_ref, parents_ref, slots_ref,
-    out_ref, grad_ref, back_ref, band_ref, pad_ref, table_ref, devices,
-):
-    conv_body(
-        merged_ref, low_ref, high_ref, below_ref, above_ref, cot_ref, weight_ref, near_ref,
-        out_ref, back_ref, band_ref, pad_ref, table_ref,
-    )
-    fine_grad_body(
-        fine_ref, sides_ref, next_ref, prev_ref, up_ref, parents_ref, slots_ref, grad_ref, back_ref, devices
-    )
-
-
-def share_body(back_ref, out_ref, devices):
+def share_body(back_ref, conv_ref, out_ref, devices):
     count, width = out_ref.shape
+    conv_width = conv_ref.shape[1]
+    up_width = width - conv_width
     share = count // devices
-    same = iota((count, count), 0) % share == iota((count, count), 1) % share
-    out_ref[...] = dot(ones_where(same), back_ref[:, back_ref.shape[1] - width :]).astype(BF)
+    same = ones_where(iota((count, count), 0) % share == iota((count, count), 1) % share)
+    out_ref[:, :up_width] = dot(same, back_ref[:, back_ref.shape[1] - up_width :]).astype(BF)
+    out_ref[:, up_width:] = dot(same, conv_ref[...]).astype(BF)
 
 
 def coarse_grad_body(back_ref, sends_ref, out_ref):
@@ -414,52 +451,59 @@
     item_count, item_width = items.shape
     coarse = up_weight.shape[1]
     start = bricks + 2 * face
-    sends = coarse_sends[0, 0].T
+    sends = coarse_sends.transpose(0, 1, 3, 2)[0, 0]
     slots = parent_slots[0]
     sides = side_sends[0, 0]
     crosses = cross_sends[0, 0]
-    near = neighbours[0, 0].T.reshape(27, 1, bricks)
+    near = neighbours.transpose(0, 3, 1, 2)[0]
     up_turned = up_weight.transpose(0, 2, 1).reshape(8 * C, coarse)
     half = item_width // 2
     count = 2 * C
-    sums_width = 14 * C + 8 * C * coarse // count
-    back_width = capacity * devices * item_width // count + sums_width
+    up_width = 8 * C * coarse // count
+    back_width = capacity * devices * item_width // count + up_width
     band = pltpu.VMEM((9, WIDE, RUN), BF)
     face_rows = shape((face, width))
+    two_faces = shape((2 * face, width))
     conv_flops = 2 * 9 * 16 * bricks * WIDE * RUN
 
-    (outgoing,) = call(items_out_body, [shape((2 * capacity * devices, half))], sends, items)
+    loaded = (sends, items, conv_weight, cot, near, sides, crosses, slots)
+    outgoing, ext_grad, low_cross, high_cross, lists = call(
+        first_body,
+        [shape((2 * capacity * devices, half)), shape((start, width), F32), face_rows, face_rows, shape((8, 128), I32)],
+        *loaded,
+        scratch=[pltpu.VMEM(a.shape, a.dtype) for a in loaded]
+        + [band, pltpu.VMEM((6, 6, bricks, WIDE), F32), pltpu.SemaphoreType.DMA((len(loaded),))],
+        flops=2 * conv_flops,
+        in_hbm=True,
+    )
     received = trade_rows(outgoing, devices)
-    ext_grad, low_cross, high_cross = call(
-        table_grad_body, [shape((start, width), F32), face_rows, face_rows], cot, conv_weight, near,
-        scratch=[band, pltpu.VMEM((6, 6, bricks, WIDE), F32)], flops=2 * conv_flops,
-    )
-    merged, parents, to_next, to_prev = call(
-        merge_body, [shape((bricks, width)), shape((8 * bricks, coarse)), face_rows, face_rows],
-        received, slots, up_turned, fine, sides,
+    grad_prev = passed_along(high_cross, "gx", 1)
+    grad_next = passed_along(low_cross, "gx", -1)
+    merged, parents, fine_part, to_next, to_prev = call(
+        merge_body,
+        [shape((bricks, width)), shape((8 * bricks, coarse)), shape((bricks, width), F32), two_faces, two_faces],
+        received, up_turned, fine, lists, ext_grad, grad_next, grad_prev,
     )
     low_side = passed_along(to_next, "gy", 1)
     high_side = passed_along(to_prev, "gy", -1)
-    grad_prev = passed_along(high_cross, "gx", 1)
-    grad_next = passed_along(low_cross, "gx", -1)
-    to_next, to_prev = call(cross_body, [face_rows, face_rows], merged, low_side, high_side, crosses)
+    to_next, to_prev = call(cross_body, [face_rows, face_rows], merged, low_side, high_side, lists)
     below = passed_along(to_next, "gx", 1)
     above = passed_along(to_prev, "gx", -1)
-    fine_part, low_grad, high_grad = call(
-        side_grad_body, [shape((bricks, width), F32), face_rows, face_rows], ext_grad, crosses, grad_next, grad_prev
-    )
-    grad_prev = passed_along(high_grad, "gy", 1)
-    grad_next = passed_along(low_grad, "gy", -1)
-    output, grad_fine, back = call(
-        functools.partial(last_body, devices=devices),
-        [shape((bricks, width)), shape((bricks, width)), shape((count, back_width))],
+    grad_fine, back = call(
+        fine_grad_body, [shape((bricks, width)), shape((count, back_width))],
+        fine_part, lists, high_side, low_side, up_turned, parents,
+    )
+    back = trade_rows(back, devices)
+    output, conv_sum = call(
+        conv_body, [shape((bricks, width)), shape((count, 14 * C))],
         merged, low_side, high_side, below, above, cot, conv_weight, near,
-        fine_part, sides, grad_next, grad_prev, up_turned, parents, slots,
         scratch=[band, pltpu.VMEM((6, 6, bricks, WIDE), BF), pltpu.VMEM((bricks + 4 * face, width), BF)],
         flops=2 * conv_flops,
     )
-    back = trade_rows(back, devices)
-    (sums,) = call(functools.partial(share_body, devices=devices), [shape((count, sums_width))], back)
+    conv_sum = trade_rows(conv_sum, devices)
+    (sums,) = call(
+        functools.partial(share_body, devices=devices), [shape((count, up_width + 14 * C))], back, conv_sum
+    )
     totals = trade_rows(sums, devices)
     (coarse_grad,) = call(coarse_grad_body, [shape((item_count, item_width))], back, sends)
     scale = 1.0 / math.sqrt(64 * bricks * devices)

time: 82.8 us -> 86.3 us (1.042)
  waiting for transfers between devices: 13.5 us -> 23.7 us
  blocking collectives: 21.6 us -> 16.2 us
  starting transfers between devices: 30.8 us -> 28.2 us
    ppermute x8 -> x6, waiting for transfers between devices: 2.38 us -> 10.5 us  [passed_along(): lax.ppermute(value, axis, [(source, source + steps) for source in range(i...]
    ppermute x8 -> x6, starting transfers between devices: 19.7 us -> 11.8 us  [passed_along(): lax.ppermute(value, axis, [(source, source + steps) for source in range(i...]
    all_to_all x1, blocking collectives: 21.6 us -> 16.2 us  [trade_rows(): lax.all_to_all(grid_view, ('gx', 'gy'), split_axis=0, concat_axis=0, tile...]
    all_to_all x2 -> x3, starting transfers between devices: 11 us -> 16.4 us  [trade_rows(): lax.all_to_all(grid_view, ('gx', 'gy'), split_axis=0, concat_axis=0, tile...]
    all_to_all x2 -> x3, waiting for transfers between devices: 11.1 us -> 13.2 us  [trade_rows(): lax.all_to_all(grid_view, ('gx', 'gy'), split_axis=0, concat_axis=0, tile...]
    pallas_call x9 -> x8, Pallas kernels: 11.6 us -> 12.4 us  [call(): pl.pallas_call(body, out_shape=tuple(outs), in_specs=[pl.BlockSpec(memory...]
    unnamed x23 -> x26, local copies, waits for them, and re-layouts: 3.89 us -> 4.28 us
  transfers between devices with their start and end apart: 10 -> 9, of which waited for: 3 -> 6; matrix products, arithmetic and copies ran while one was open for 0% -> 0% of each run, Pallas kernels for 5% -> 6%
where the time goes in v2:
time: 86.3 us; the launch traced here: 85.6 us
  starting transfers between devices  28.2 us (33%)
  waiting for transfers between devices  23.7 us (27%)
  blocking collectives  16.2 us (19%)
  Pallas kernels  12.4 us (14%)
  local copies, waits for them, and re-layouts  4.28 us (5%)
    all_to_all x3, starting transfers between devices, trade_rows(): lax.all_to_all(grid_view, ('gx', 'gy'), split_axis=0, concat_axis=0, tile...  16.4 us
    all_to_all x1, blocking collectives, trade_rows(): lax.all_to_all(grid_view, ('gx', 'gy'), split_axis=0, concat_axis=0, tile...  16.2 us
    all_to_all x3, waiting for transfers between devices, trade_rows(): lax.all_to_all(grid_view, ('gx', 'gy'), split_axis=0, concat_axis=0, tile...  13.2 us
    pallas_call x8, Pallas kernels, call(): pl.pallas_call(body, out_shape=tuple(outs), in_specs=[pl.BlockSpec(memory...  12.4 us
    ppermute x6, starting transfers between devices, passed_along(): lax.ppermute(value, axis, [(source, source + steps) for source in range(i...  11.8 us
    ppermute x6, waiting for transfers between devices, passed_along(): lax.ppermute(value, axis, [(source, source + steps) for source in range(i...  10.5 us
    unnamed x26, local copies, waits for them, and re-layouts  4.28 us
  transfers between devices with their start and end apart: 9, of which 6 were waited for; matrix products, arithmetic and copies ran while one was open for 0% of the time, Pallas kernels for 6%

profile of v2, /device:TPU:0, one launch (start us, length us, event | category | flops | bytes accessed | tf_op | source)
XLA Modules:
  0.0 85.6 jit_solution(11556712639297904288)
XLA Ops:
  0.6 0.0 copy-start.11
  0.6 0.0 copy-start.2
  0.7 0.0 copy-start.10
  0.7 0.0 copy-start.12
  0.7 0.6 copy-done.11
  1.3 0.0 copy-done.2
  1.3 0.0 copy-done.10
  1.3 0.0 copy-done.12
  1.3 0.0 copy-start.3
  1.3 1.0 %copy-done.3 = bf16[27,64,64]{2,1,0:T(8,128)(2,1)S(1)} copy-done((bf16[27,64,64]{2,1,0:T(8,128)(2,1)S(1)}, bf16[27,64,64]{2,1,0:T(8,128)(2,1)}, u32[]{:S(2)}) %copy-start.3) | copy-done | bytes 221208
  2.4 0.9 %copy-done.5 = bf16[1,1,32,4096]{3,2,1,0:T(8,128)(2,1)S(1)} copy-done((bf16[1,1,32,4096]{3,2,1,0:T(8,128)(2,1)S(1)}, bf16[1,1,32,4096]{3,2,1,0:T(8,128)(2,1)}, u32[]{:S(2)}) %copy-start.5) | copy-done | bytes 262168
  3.3 0.9 %copy-done.7 = bf16[1,1,64,1024]{3,2,1,0:T(8,128)(2,1)S(1)} copy-done((bf16[1,1,64,1024]{3,2,1,0:T(8,128)(2,1)S(1)}, bf16[1,1,64,1024]{3,2,1,0:T(8,128)(2,1)}, u32[]{:S(2)}) %copy-start.7) | copy-done | bytes 131096
  4.2 0.7 copy-done.8
  4.9 2.8 %shard_map.137 = (bf16[128,512]{1,0:T(8,128)(2,1)}, f32[48,4096]{1,0:T(8,128)S(1)}, bf16[8,4096]{1,0:T(8,128)(2,1)S(1)}, bf16[8,4096]{1,0:T(8,128)(2,1)S(1)}, s32[8,128]{1,0:T(8,128)S(1)}) custom-call(s32[4,16]{1,0:T(4,128)S(1)} %bitcast.38, bf16[64,1024]{1,0:T(8,128)(2,1)S(1)} %bitcast.42, bf16[27,64,64]{2,1,0:T(8,128)(2,1)S(1)} %copy-done.3, ...), custom_call_target="tpu_custom_call" | custom-call | flops 1811939328 | bytes 1671040 | tf_op jit(solution)/shard_map/pallas_call | solution.py:49
  7.8 0.0 copy-start
  7.8 7.5 %all-to-all-start = ((bf16[16,8,512]{2,1,0:T(8,128)(2,1)}), bf16[16,8,512]{2,1,0:T(8,128)(2,1)S(1)}, u32[]{:S(2)}, u32[]{:S(2)}) async-start(bf16[16,8,512]{2,1,0:T(8,128)(2,1)} %bitcast.9), calls=%async_computation | async-start | bytes 262144 | tf_op jit(solution)/shard_map/all_to_all | solution.py:436
  15.3 1.3 %collective-permute-start = (bf16[8,4096]{1,0:T(8,128)(2,1)S(1)}, bf16[8,4096]{1,0:T(8,128)(2,1)S(1)}, u32[]{:S(2)}, u32[]{:S(2)}) collective-permute-start(bf16[8,4096]{1,0:T(8,128)(2,1)S(1)} %get-tuple-element.26), channel_id=1, source_target_pairs={{4,0},{8,4},{12,8},{5,1},{9,5},{13,9},{6,2},{10,6},{14,10},{7,3},{... | collective-permute-start | bytes 196616 | tf_op jit(solution)/shard_map/ppermute | solution.py:430
  16.6 3.0 %collective-permute-start.1 = (bf16[8,4096]{1,0:T(8,128)(2,1)S(1)}, bf16[8,4096]{1,0:T(8,128)(2,1)S(1)}, u32[]{:S(2)}, u32[]{:S(2)}) collective-permute-start(bf16[8,4096]{1,0:T(8,128)(2,1)S(1)} %get-tuple-element.27), channel_id=1, source_target_pairs={{0,4},{4,8},{8,12},{1,5},{5,9},{9,13},{2,6},{6,10},{10,14},{3,7},{... | collective-permute-start | bytes 196616 | tf_op jit(solution)/shard_map/ppermute | solution.py:430
  19.6 0.0 collective-permute-done.next_ref
  19.6 0.9 %collective-permute-done.1.prev_ref = bf16[8,4096]{1,0:T(8,128)(2,1)S(1)} collective-permute-done((bf16[8,4096]{1,0:T(8,128)(2,1)S(1)}, bf16[8,4096]{1,0:T(8,128)(2,1)S(1)}, u32[]{:S(2)}, u32[]{:S(2)}) %collective-permute-start.1) | collective-permute-done | bytes 65568 | tf_op jit(solution)/shard_map/ppermute | solution.py:430
  20.5 2.1 %all-to-all-done = bf16[16,8,512]{2,1,0:T(8,128)(2,1)S(1)} async-done(((bf16[16,8,512]{2,1,0:T(8,128)(2,1)}), bf16[16,8,512]{2,1,0:T(8,128)(2,1)S(1)}, u32[]{:S(2)}, u32[]{:S(2)}) %all-to-all-start) | async-done | bytes 131104 | tf_op jit(solution)/shard_map/all_to_all | solution.py:436
  22.6 0.0 copy-done.1
  22.6 0.0 copy-done
  22.6 0.7 shard_map.138
  23.3 2.6 %collective-permute-start.2 = (bf16[16,4096]{1,0:T(8,128)(2,1)S(1)}, bf16[16,4096]{1,0:T(8,128)(2,1)S(1)}, u32[]{:S(2)}, u32[]{:S(2)}) collective-permute-start(bf16[16,4096]{1,0:T(8,128)(2,1)S(1)} %get-tuple-element.29), channel_id=1, source_target_pairs={{0,1},{1,2},{2,3},{4,5},{5,6},{6,7},{8,9},{9,10},{10,11},{12,13},{... | collective-permute-start | bytes 393224 | tf_op jit(solution)/shard_map/ppermute | solution.py:430
  25.9 1.3 %collective-permute-start.3 = (bf16[16,4096]{1,0:T(8,128)(2,1)S(1)}, bf16[16,4096]{1,0:T(8,128)(2,1)S(1)}, u32[]{:S(2)}, u32[]{:S(2)}) collective-permute-start(bf16[16,4096]{1,0:T(8,128)(2,1)S(1)} %get-tuple-element.30), channel_id=1, source_target_pairs={{1,0},{2,1},{3,2},{5,4},{6,5},{7,6},{9,8},{10,9},{11,10},{13,12},{... | collective-permute-start | bytes 393224 | tf_op jit(solution)/shard_map/ppermute | solution.py:430
  27.2 2.6 %collective-permute-done.2.low_ref.prev_ref = bf16[16,4096]{1,0:T(8,128)(2,1)S(1)} collective-permute-done((bf16[16,4096]{1,0:T(8,128)(2,1)S(1)}, bf16[16,4096]{1,0:T(8,128)(2,1)S(1)}, u32[]{:S(2)}, u32[]{:S(2)}) %collective-permute-start.2) | collective-permute-done | bytes 131104 | tf_op jit(solution)/shard_map/ppermute | solution.py:430
  29.8 4.1 %collective-permute-done.3.high_ref.next_ref = bf16[16,4096]{1,0:T(8,128)(2,1)S(1)} collective-permute-done((bf16[16,4096]{1,0:T(8,128)(2,1)S(1)}, bf16[16,4096]{1,0:T(8,128)(2,1)S(1)}, u32[]{:S(2)}, u32[]{:S(2)}) %collective-permute-start.3) | collective-permute-done | bytes 131104 | tf_op jit(solution)/shard_map/ppermute | solution.py:430
  33.9 1.4 %shard_map.141 = (bf16[32,4096]{1,0:T(8,128)(2,1)}, bf16[128,1024]{1,0:T(8,128)(2,1)}) custom-call(f32[32,4096]{1,0:T(8,128)S(1)} %get-tuple-element.34.part_ref, s32[8,128]{1,0:T(8,128)S(1)} %get-tuple-element.24.lists_ref, bf16[16,4096]{1,0:T(8,128)(2,1)S(1)} %collective-permute-done.3.high_ref.next_ref, ...), custom_call_target="tpu_custom_call" | custom-call | bytes 1511424 | tf_op jit(solution)/shard_map/pallas_call | solution.py:49
  35.3 5.4 %all-to-all-start.1 = ((bf16[16,8,1024]{2,1,0:T(8,128)(2,1)}), bf16[16,8,1024]{2,1,0:T(8,128)(2,1)S(1)}, u32[]{:S(2)}, u32[]{:S(2)}) async-start(bf16[16,8,1024]{2,1,0:T(8,128)(2,1)} %bitcast.17), calls=%async_computation.1 | async-start | bytes 524288 | tf_op jit(solution)/shard_map/all_to_all | solution.py:436
  40.7 0.0 copy-start.6
  40.7 0.0 copy-start.9
  40.7 0.3 shard_map.139
  41.0 2.3 %collective-permute-start.4 = (bf16[8,4096]{1,0:T(8,128)(2,1)S(1)}, bf16[8,4096]{1,0:T(8,128)(2,1)S(1)}, u32[]{:S(2)}, u32[]{:S(2)}) collective-permute-start(bf16[8,4096]{1,0:T(8,128)(2,1)S(1)} %get-tuple-element.31), channel_id=1, source_target_pairs={{0,4},{4,8},{8,12},{1,5},{5,9},{9,13},{2,6},{6,10},{10,14},{3,7},{... | collective-permute-start | bytes 196616 | tf_op jit(solution)/shard_map/ppermute | solution.py:430
  43.3 1.3 %collective-permute-start.5 = (bf16[8,4096]{1,0:T(8,128)(2,1)S(1)}, bf16[8,4096]{1,0:T(8,128)(2,1)S(1)}, u32[]{:S(2)}, u32[]{:S(2)}) collective-permute-start(bf16[8,4096]{1,0:T(8,128)(2,1)S(1)} %get-tuple-element.32), channel_id=1, source_target_pairs={{4,0},{8,4},{12,8},{5,1},{9,5},{13,9},{6,2},{10,6},{14,10},{7,3},{... | collective-permute-start | bytes 196616 | tf_op jit(solution)/shard_map/ppermute | solution.py:430
  44.6 0.0 collective-permute-done.4.below_ref
  44.6 3.0 %collective-permute-done.5.above_ref = bf16[8,4096]{1,0:T(8,128)(2,1)S(1)} collective-permute-done((bf16[8,4096]{1,0:T(8,128)(2,1)S(1)}, bf16[8,4096]{1,0:T(8,128)(2,1)S(1)}, u32[]{:S(2)}, u32[]{:S(2)}) %collective-permute-start.5) | collective-permute-done | bytes 65568 | tf_op jit(solution)/shard_map/ppermute | solution.py:430
  47.6 0.0 copy-done.4
  47.6 0.0 copy-done.6
  47.6 0.0 copy-done.9
  47.6 3.9 %shard_map.140 = (bf16[32,4096]{1,0:T(8,128)(2,1)}, bf16[128,896]{1,0:T(8,128)(2,1)S(1)}) custom-call(bf16[32,4096]{1,0:T(8,128)(2,1)S(1)} %get-tuple-element.28.merged_ref, bf16[16,4096]{1,0:T(8,128)(2,1)S(1)} %collective-permute-done.2.low_ref.prev_ref, bf16[16,4096]{1,0:T(8,128)(2,1)S(1)} %collective-permute-done.3.high_ref.next_ref, ...), custom_call_target="tpu_custom_call" | custom-call | flops 1811939328 | bytes 1633664 | tf_op jit(solution)/shard_map/pallas_call | solution.py:49
  51.5 0.0 all-to-all-done.1
  51.5 16.2 %all_to_all.20 = bf16[16,8,896]{2,1,0:T(8,128)(2,1)S(1)} all-to-all(bf16[16,8,896]{2,1,0:T(8,128)(2,1)S(1)} %bitcast.37), channel_id=1, replica_groups=mesh['groups'=2,'gx'=4,'gy'=4] {'gx','gy'}, dimensions={0} | all-to-all | bytes 458752 | tf_op jit(solution)/shard_map/all_to_all | solution.py:436
  67.7 1.0 %shard_map.143 = bf16[128,1408]{1,0:T(8,128)(2,1)} custom-call(bf16[128,1024]{1,0:T(8,128)(2,1)S(1)} %bitcast.29, bf16[128,896]{1,0:T(8,128)(2,1)S(1)} %bitcast.32), custom_call_target="tpu_custom_call" | custom-call | bytes 851968 | tf_op jit(solution)/shard_map/pallas_call | solution.py:49
  68.7 3.5 %all-to-all-start.3 = ((bf16[16,8,1408]{2,1,0:T(8,128)(2,1)}), bf16[16,8,1408]{2,1,0:T(8,128)(2,1)S(1)}, u32[]{:S(2)}, u32[]{:S(2)}) async-start(bf16[16,8,1408]{2,1,0:T(8,128)(2,1)} %bitcast.23), calls=%async_computation.3 | async-start | bytes 720896 | tf_op jit(solution)/shard_map/all_to_all | solution.py:436
  72.2 1.1 %shard_map.142 = bf16[64,1024]{1,0:T(8,128)(2,1)} custom-call(bf16[128,1024]{1,0:T(8,128)(2,1)S(1)} %bitcast.30, s32[4,16]{1,0:T(4,128)S(1)} %bitcast.39), custom_call_target="tpu_custom_call" | custom-call | bytes 393472 | tf_op jit(solution)/shard_map/pallas_call | solution.py:49
  73.3 11.0 %all-to-all-done.3 = bf16[16,8,1408]{2,1,0:T(8,128)(2,1)S(1)} async-done(((bf16[16,8,1408]{2,1,0:T(8,128)(2,1)}), bf16[16,8,1408]{2,1,0:T(8,128)(2,1)S(1)}, u32[]{:S(2)}, u32[]{:S(2)}) %all-to-all-start.3) | async-done | bytes 360480 | tf_op jit(solution)/shard_map/all_to_all | solution.py:436
  84.4 1.2 %shard_map.144 = (f32[27,64,64]{2,1,0:T(8,128)}, f32[512,128]{1,0:T(8,128)}) custom-call(bf16[128,1408]{1,0:T(8,128)(2,1)S(1)} %bitcast.31), custom_call_target="tpu_custom_call" | custom-call | bytes 1064960 | tf_op jit(solution)/shard_map/pallas_call | solution.py:49
  (5 shorter events, 0.0 us)
Async XLA Ops:
  0.6 0.7 copy-start.11
  0.6 0.7 copy-start.2
  0.7 0.7 copy-start.10
  0.7 0.7 copy-start.12
  1.3 1.0 %copy-start.3 = (bf16[27,64,64]{2,1,0:T(8,128)(2,1)S(1)}, bf16[27,64,64]{2,1,0:T(8,128)(2,1)}, u32[]{:S(2)}) copy-start(bf16[27,64,64]{2,1,0:T(8,128)(2,1)} %weight_ref.1) | copy-start | bytes 663556
  2.4 0.9 %copy-start.5 = (bf16[1,1,32,4096]{3,2,1,0:T(8,128)(2,1)S(1)}, bf16[1,1,32,4096]{3,2,1,0:T(8,128)(2,1)}, u32[]{:S(2)}) copy-start(bf16[1,1,32,4096]{3,2,1,0:T(8,128)(2,1)} %param.19) | copy-start | bytes 786436
  3.3 0.9 %copy-start.7 = (bf16[1,1,64,1024]{3,2,1,0:T(8,128)(2,1)S(1)}, bf16[1,1,64,1024]{3,2,1,0:T(8,128)(2,1)}, u32[]{:S(2)}) copy-start(bf16[1,1,64,1024]{3,2,1,0:T(8,128)(2,1)} %param.11) | copy-start | bytes 393220
  4.2 0.7 copy-start.8
  4.9 17.7 %copy-start.1 = (bf16[1,1,32,4096]{3,2,1,0:T(8,128)(2,1)S(1)}, bf16[1,1,32,4096]{3,2,1,0:T(8,128)(2,1)}, u32[]{:S(2)}) copy-start(bf16[1,1,32,4096]{3,2,1,0:T(8,128)(2,1)} %param.10) | copy-start | bytes 786436
  7.8 14.9 %copy-start = (bf16[8,128,64]{1,2,0:T(8,128)(2,1)S(1)}, bf16[8,128,64]{1,2,0:T(8,128)(2,1)}, u32[]{:S(2)}) copy-start(bf16[8,128,64]{1,2,0:T(8,128)(2,1)} %param.13) | copy-start | bytes 393220
  7.8 14.8 %all-to-all-start = ((bf16[16,8,512]{2,1,0:T(8,128)(2,1)}), bf16[16,8,512]{2,1,0:T(8,128)(2,1)S(1)}, u32[]{:S(2)}, u32[]{:S(2)}) async-start(bf16[16,8,512]{2,1,0:T(8,128)(2,1)} %bitcast.9), calls=%async_computation | async-start | bytes 262144 | tf_op jit(solution)/shard_map/all_to_all | solution.py:436
  15.3 4.3 %collective-permute-start = (bf16[8,4096]{1,0:T(8,128)(2,1)S(1)}, bf16[8,4096]{1,0:T(8,128)(2,1)S(1)}, u32[]{:S(2)}, u32[]{:S(2)}) collective-permute-start(bf16[8,4096]{1,0:T(8,128)(2,1)S(1)} %get-tuple-element.26), channel_id=1, source_target_pairs={{4,0},{8,4},{12,8},{5,1},{9,5},{13,9},{6,2},{10,6},{14,10},{7,3},{... | collective-permute-start | bytes 196616 | tf_op jit(solution)/shard_map/ppermute | solution.py:430
  16.6 3.9 %collective-permute-start.1 = (bf16[8,4096]{1,0:T(8,128)(2,1)S(1)}, bf16[8,4096]{1,0:T(8,128)(2,1)S(1)}, u32[]{:S(2)}, u32[]{:S(2)}) collective-permute-start(bf16[8,4096]{1,0:T(8,128)(2,1)S(1)} %get-tuple-element.27), channel_id=1, source_target_pairs={{0,4},{4,8},{8,12},{1,5},{5,9},{9,13},{2,6},{6,10},{10,14},{3,7},{... | collective-permute-start | bytes 196616 | tf_op jit(solution)/shard_map/ppermute | solution.py:430
  23.3 6.4 %collective-permute-start.2 = (bf16[16,4096]{1,0:T(8,128)(2,1)S(1)}, bf16[16,4096]{1,0:T(8,128)(2,1)S(1)}, u32[]{:S(2)}, u32[]{:S(2)}) collective-permute-start(bf16[16,4096]{1,0:T(8,128)(2,1)S(1)} %get-tuple-element.29), channel_id=1, source_target_pairs={{0,1},{1,2},{2,3},{4,5},{5,6},{6,7},{8,9},{9,10},{10,11},{12,13},{... | collective-permute-start | bytes 393224 | tf_op jit(solution)/shard_map/ppermute | solution.py:430
  25.9 8.0 %collective-permute-start.3 = (bf16[16,4096]{1,0:T(8,128)(2,1)S(1)}, bf16[16,4096]{1,0:T(8,128)(2,1)S(1)}, u32[]{:S(2)}, u32[]{:S(2)}) collective-permute-start(bf16[16,4096]{1,0:T(8,128)(2,1)S(1)} %get-tuple-element.30), channel_id=1, source_target_pairs={{1,0},{2,1},{3,2},{5,4},{6,5},{7,6},{9,8},{10,9},{11,10},{13,12},{... | collective-permute-start | bytes 393224 | tf_op jit(solution)/shard_map/ppermute | solution.py:430
  35.3 12.3 %copy-start.4 = (bf16[27,64,64]{2,1,0:T(8,128)(2,1)S(1)}, bf16[27,64,64]{2,1,0:T(8,128)(2,1)}, u32[]{:S(2)}) copy-start(bf16[27,64,64]{2,1,0:T(8,128)(2,1)} %weight_ref.1) | copy-start | bytes 663556
  35.3 16.2 %all-to-all-start.1 = ((bf16[16,8,1024]{2,1,0:T(8,128)(2,1)}), bf16[16,8,1024]{2,1,0:T(8,128)(2,1)S(1)}, u32[]{:S(2)}, u32[]{:S(2)}) async-start(bf16[16,8,1024]{2,1,0:T(8,128)(2,1)} %bitcast.17), calls=%async_computation.1 | async-start | bytes 524288 | tf_op jit(solution)/shard_map/all_to_all | solution.py:436
  40.7 6.9 %copy-start.6 = (bf16[1,1,32,4096]{3,2,1,0:T(8,128)(2,1)S(1)}, bf16[1,1,32,4096]{3,2,1,0:T(8,128)(2,1)}, u32[]{:S(2)}) copy-start(bf16[1,1,32,4096]{3,2,1,0:T(8,128)(2,1)} %param.19) | copy-start | bytes 786436
  40.7 6.9 %copy-start.9 = (s32[1,1,32,27]{2,1,3,0:T(1,128)S(1)}, s32[1,1,32,27]{2,1,3,0:T(1,128)}, u32[]{:S(2)}) copy-start(s32[1,1,32,27]{2,1,3,0:T(1,128)} %param.14) | copy-start | bytes 10372
  41.0 3.6 %collective-permute-start.4 = (bf16[8,4096]{1,0:T(8,128)(2,1)S(1)}, bf16[8,4096]{1,0:T(8,128)(2,1)S(1)}, u32[]{:S(2)}, u32[]{:S(2)}) collective-permute-start(bf16[8,4096]{1,0:T(8,128)(2,1)S(1)} %get-tuple-element.31), channel_id=1, source_target_pairs={{0,4},{4,8},{8,12},{1,5},{5,9},{9,13},{2,6},{6,10},{10,14},{3,7},{... | collective-permute-start | bytes 196616 | tf_op jit(solution)/shard_map/ppermute | solution.py:430
  43.3 4.3 %collective-permute-start.5 = (bf16[8,4096]{1,0:T(8,128)(2,1)S(1)}, bf16[8,4096]{1,0:T(8,128)(2,1)S(1)}, u32[]{:S(2)}, u32[]{:S(2)}) collective-permute-start(bf16[8,4096]{1,0:T(8,128)(2,1)S(1)} %get-tuple-element.32), channel_id=1, source_target_pairs={{4,0},{8,4},{12,8},{5,1},{9,5},{13,9},{6,2},{10,6},{14,10},{7,3},{... | collective-permute-start | bytes 196616 | tf_op jit(solution)/shard_map/ppermute | solution.py:430
  68.7 15.7 %all-to-all-start.3 = ((bf16[16,8,1408]{2,1,0:T(8,128)(2,1)}), bf16[16,8,1408]{2,1,0:T(8,128)(2,1)S(1)}, u32[]{:S(2)}, u32[]{:S(2)}) async-start(bf16[16,8,1408]{2,1,0:T(8,128)(2,1)} %bitcast.23), calls=%async_computation.3 | async-start | bytes 720896 | tf_op jit(solution)/shard_map/all_to_all | solution.py:436

commit v3 on v2

--- a/solution.py
+++ b/solution.py
@@ -49,7 +49,7 @@
     return pl.pallas_call(
         body,
         out_shape=tuple(outs),
-        in_specs=[pl.BlockSpec(memory_space=pl.ANY) if in_hbm else pl.BlockSpec() for _ in args],
+        in_specs=[pl.BlockSpec(memory_space=pltpu.HBM) if in_hbm else pl.BlockSpec() for _ in args],
         scratch_shapes=tuple(scratch),
         cost_estimate=pl.CostEstimate(flops=flops, bytes_accessed=moved, transcendentals=0),
         compiler_params=pltpu.CompilerParams(vmem_limit_bytes=28 * 2**20),
@@ -127,7 +127,8 @@
     return lists_ref[4:5, :bricks]
 
 
-def cross_body(merged_ref, low_ref, high_ref, lists_ref, a_ref, b_ref):
+def cross_body(merged_ref, low_ref, high_ref, lists_ref, a_ref, b_ref, again_ref):
+    again_ref[...] = lists_ref[...]
     face = a_ref.shape[0]
     sides = stack_rows(low_ref[...].astype(F32)[:face], high_ref[...].astype(F32)[:face])
     rows = jnp.concatenate([merged_ref[...], sides], axis=0)
@@ -177,7 +178,7 @@
     return head, (value - head.astype(F32)).astype(BF)
 
 
-def table_grad(cot_ref, weight_ref, near_ref, ext_ref, low_ref, high_ref, band_ref, pad_ref):
+def table_grad_body(cot_ref, weight_ref, near_ref, ext_ref, low_ref, high_ref, band_ref, pad_ref):
     bricks = cot_ref.shape[0]
     face = low_ref.shape[0]
     start = ext_ref.shape[0]
@@ -227,12 +228,14 @@
 
 
 def first_body(
-    sends_hbm, items_hbm, weight_hbm, cot_hbm, near_hbm, sides_hbm, crosses_hbm, slots_hbm,
-    out_ref, ext_ref, low_ref, high_ref, lists_ref,
-    sends_ref, items_ref, weight_ref, cot_ref, near_ref, sides_ref, crosses_ref, slots_ref, band_ref, pad_ref, arrived,
+    sends_hbm, items_hbm, sides_hbm, crosses_hbm, slots_hbm, weight_hbm, cot_hbm, near_hbm, fine_hbm, up_hbm,
+    out_ref, lists_ref, weight_ref, cot_ref, near_ref, fine_ref, up_ref,
+    sends_ref, items_ref, sides_ref, crosses_ref, slots_ref, arrived,
 ):
-    sources = (sends_hbm, items_hbm, weight_hbm, cot_hbm, near_hbm, sides_hbm, crosses_hbm, slots_hbm)
-    places = (sends_ref, items_ref, weight_ref, cot_ref, near_ref, sides_ref, crosses_ref, slots_ref)
+    sources = (
+        sends_hbm, items_hbm, sides_hbm, crosses_hbm, slots_hbm, weight_hbm, cot_hbm, near_hbm, fine_hbm, up_hbm,
+    )
+    places = (sends_ref, items_ref, sides_ref, crosses_ref, slots_ref, weight_ref, cot_ref, near_ref, fine_ref, up_ref)
     copies = [pltpu.make_async_copy(s, p, arrived.at[i]) for i, (s, p) in enumerate(zip(sources, places))]
     for copy in copies:
         copy.start()
@@ -246,21 +249,19 @@
     lists_ref[0:2, :face] = sides_ref[...]
     lists_ref[2:4, :face] = crosses_ref[...]
     lists_ref[4:5, :bricks] = slots_ref[...]
-    table_grad(cot_ref, weight_ref, near_ref, ext_ref, low_ref, high_ref, band_ref, pad_ref)
-
-
-def conv_body(
-    merged_ref, low_ref, high_ref, below_ref, above_ref, cot_ref, weight_ref, near_ref,
-    out_ref, back_ref, band_ref, pad_ref, table_ref,
+
+
+def weight_grad_body(
+    merged_ref, low_ref, high_ref, below_ref, above_ref, turned_ref, near_ref, part_ref, back_ref, pad_ref, table_ref
 ):
     bricks = merged_ref.shape[0]
     face = below_ref.shape[0]
     rows = bricks + 4 * face
-    build_bands(weight_ref, band_ref)
     table_ref[:bricks] = merged_ref[...]
     table_ref[bricks:] = stack_rows(
         low_ref[...].astype(F32)[:face], high_ref[...].astype(F32)[:face], below_ref[...], above_ref[...]
     )
+    back_ref[:, : part_ref.shape[1]] = part_ref[...]
     near = jnp.concatenate([near_ref[o] for o in range(27)] + [jnp.zeros((5, bricks), I32)], axis=0)
     near = near.astype(F32).T.astype(I32)
 
@@ -297,16 +298,11 @@
                 for i, (X, Y, _, _) in enumerate(moved):
                     pad_ref[X, Y, :, :RUN] = got[i * bricks : (i + 1) * bricks]
 
-    turned = stack_runs(cot_ref).T
-    total = None
+    turned = turned_ref[...]
     lanes_low = iota((C, 2 * C), 1) < C
     sums = []
     for e in range(9):
-        ex, ey = (e // 3, e % 3)
-        inputs = pad_ref[ex : ex + 4, ey : ey + 4].reshape(16 * bricks, WIDE)
-        part = dot(inputs, band_ref[e])
-        total = part if total is None else total + part
-        wide = dot(turned, inputs)
+        wide = dot(turned, inputs_at(pad_ref, e))
 
         def block(z, s):
             return wide[z * C : (z + 1) * C, s * 2 * C : (s + 1) * 2 * C]
@@ -317,12 +313,26 @@
         for value in (low, mid, high):
             sums.append(value + pltpu.roll(value, C, 1))
     sums.append(jnp.zeros((C, 2 * C), F32))
+    for pair in range(7):
+        both = [jnp.where(lanes_low, sums[14 * h + 2 * pair], sums[14 * h + 2 * pair + 1]) for h in range(2)]
+        at = part_ref.shape[1] + pair * 2 * C
+        back_ref[:, at : at + 2 * C] = jnp.concatenate(both, axis=0).astype(BF)
+
+
+def inputs_at(pad_ref, e):
+    bricks = pad_ref.shape[2]
+    ex, ey = (e // 3, e % 3)
+    return pad_ref[ex : ex + 4, ey : ey + 4].reshape(16 * bricks, WIDE)
+
+
+def conv_body(pad_ref, band_ref, out_ref):
+    bricks = pad_ref.shape[2]
+    total = None
+    for e in range(9):
+        part = dot(inputs_at(pad_ref, e), band_ref[e])
+        total = part if total is None else total + part
     for p in range(16):
         out_ref[:, p * RUN : (p + 1) * RUN] = total[p * bricks : (p + 1) * bricks].astype(BF)
-    for pair in range(7):
-        both = [jnp.where(lanes_low, sums[14 * h + 2 * pair], sums[14 * h + 2 * pair + 1]) for h in range(2)]
-        at = pair * 2 * C
-        back_ref[:, at : at + 2 * C] = jnp.concatenate(both, axis=0).astype(BF)
 
 
 def add_rows(base, lists, first, second):
@@ -345,7 +355,10 @@
     b_ref[...] = stack_rows(second, total[bricks : bricks + face])
 
 
-def fine_grad_body(part_ref, lists_ref, next_ref, prev_ref, up_ref, parents_ref, grad_ref, back_ref):
+def fine_grad_body(
+    part_ref, lists_ref, next_ref, prev_ref, up_ref, parents_ref, cot_ref, grad_ref, back_ref, turned_ref
+):
+    turned_ref[...] = stack_runs(cot_ref).T
     bricks = part_ref.shape[0]
     face = next_ref.shape[0] // 2
     grad_ref[...] = add_rows(
@@ -380,14 +393,11 @@
         back_ref[:, j * half : (j + 1) * half] = rows.astype(BF)
 
 
-def share_body(back_ref, conv_ref, out_ref, devices):
+def share_body(back_ref, out_ref, devices):
     count, width = out_ref.shape
-    conv_width = conv_ref.shape[1]
-    up_width = width - conv_width
     share = count // devices
     same = ones_where(iota((count, count), 0) % share == iota((count, count), 1) % share)
-    out_ref[:, :up_width] = dot(same, back_ref[:, back_ref.shape[1] - up_width :]).astype(BF)
-    out_ref[:, up_width:] = dot(same, conv_ref[...]).astype(BF)
+    out_ref[...] = dot(same, back_ref[:, back_ref.shape[1] - width :]).astype(BF)
 
 
 def coarse_grad_body(back_ref, sends_ref, out_ref):
@@ -461,22 +471,26 @@
     count = 2 * C
     up_width = 8 * C * coarse // count
     back_width = capacity * devices * item_width // count + up_width
-    band = pltpu.VMEM((9, WIDE, RUN), BF)
     face_rows = shape((face, width))
     two_faces = shape((2 * face, width))
     conv_flops = 2 * 9 * 16 * bricks * WIDE * RUN
 
-    loaded = (sends, items, conv_weight, cot, near, sides, crosses, slots)
-    outgoing, ext_grad, low_cross, high_cross, lists = call(
+    listed = (sends, items, sides, crosses, slots)
+    kept = (conv_weight, cot, near, fine, up_turned)
+    outgoing, lists, weight, cot, near, fine, up_turned = call(
         first_body,
-        [shape((2 * capacity * devices, half)), shape((start, width), F32), face_rows, face_rows, shape((8, 128), I32)],
-        *loaded,
-        scratch=[pltpu.VMEM(a.shape, a.dtype) for a in loaded]
-        + [band, pltpu.VMEM((6, 6, bricks, WIDE), F32), pltpu.SemaphoreType.DMA((len(loaded),))],
-        flops=2 * conv_flops,
+        [shape((2 * capacity * devices, half)), shape((8, 128), I32)] + [shape(a.shape, a.dtype) for a in kept],
+        *listed, *kept,
+        scratch=[pltpu.VMEM(a.shape, a.dtype) for a in listed]
+        + [pltpu.SemaphoreType.DMA((len(listed) + len(kept),))],
         in_hbm=True,
     )
     received = trade_rows(outgoing, devices)
+    ext_grad, low_cross, high_cross, band = call(
+        table_grad_body,
+        [shape((start, width), F32), face_rows, face_rows, shape((9, WIDE, RUN))],
+        cot, weight, near, scratch=[pltpu.VMEM((6, 6, bricks, WIDE), F32)], flops=2 * conv_flops,
+    )
     grad_prev = passed_along(high_cross, "gx", 1)
     grad_next = passed_along(low_cross, "gx", -1)
     merged, parents, fine_part, to_next, to_prev = call(
@@ -486,23 +500,25 @@
     )
     low_side = passed_along(to_next, "gy", 1)
     high_side = passed_along(to_prev, "gy", -1)
-    to_next, to_prev = call(cross_body, [face_rows, face_rows], merged, low_side, high_side, lists)
+    to_next, to_prev, lists = call(
+        cross_body, [face_rows, face_rows, shape((8, 128), I32)], merged, low_side, high_side, lists
+    )
     below = passed_along(to_next, "gx", 1)
     above = passed_along(to_prev, "gx", -1)
-    grad_fine, back = call(
-        fine_grad_body, [shape((bricks, width)), shape((count, back_width))],
-        fine_part, lists, high_side, low_side, up_turned, parents,
+    grad_fine, part, turned = call(
+        fine_grad_body,
+        [shape((bricks, width)), shape((count, back_width)), shape((RUN, 16 * bricks))],
+        fine_part, lists, high_side, low_side, up_turned, parents, cot,
+    )
+    back, pad = call(
+        weight_grad_body, [shape((count, back_width + 14 * C)), shape((6, 6, bricks, WIDE))],
+        merged, low_side, high_side, below, above, turned, near, part,
+        scratch=[pltpu.VMEM((bricks + 4 * face, width), BF)], flops=conv_flops,
     )
     back = trade_rows(back, devices)
-    output, conv_sum = call(
-        conv_body, [shape((bricks, width)), shape((count, 14 * C))],
-        merged, low_side, high_side, below, above, cot, conv_weight, near,
-        scratch=[band, pltpu.VMEM((6, 6, bricks, WIDE), BF), pltpu.VMEM((bricks + 4 * face, width), BF)],
-        flops=2 * conv_flops,
-    )
-    conv_sum = trade_rows(conv_sum, devices)
+    (output,) = call(conv_body, [shape((bricks, width))], pad, band, flops=conv_flops)
     (sums,) = call(
-        functools.partial(share_body, devices=devices), [shape((count, up_width + 14 * C))], back, conv_sum
+        functools.partial(share_body, devices=devices), [shape((count, up_width + 14 * C))], back
     )
     totals = trade_rows(sums, devices)
     (coarse_grad,) = call(coarse_grad_body, [shape((item_count, item_width))], back, sends)

time: 86.3 us -> 88.7 us (1.028)
  local copies, waits for them, and re-layouts: 4.28 us -> 9.36 us
  blocking collectives: 16.2 us -> 21.2 us
  waiting for transfers between devices: 23.7 us -> 19.3 us
  starting transfers between devices: 28.2 us -> 23.9 us
  Pallas kernels: 12.4 us -> 13.4 us
    all_to_all x3 -> x2, starting transfers between devices: 16.4 us -> 10.9 us  [trade_rows(): lax.all_to_all(grid_view, ('gx', 'gy'), split_axis=0, concat_axis=0, tile...]
    unnamed x26, local copies, waits for them, and re-layouts: 4.28 us -> 9.36 us
    all_to_all x1, blocking collectives: 16.2 us -> 21.2 us  [trade_rows(): lax.all_to_all(grid_view, ('gx', 'gy'), split_axis=0, concat_axis=0, tile...]
    all_to_all x3 -> x2, waiting for transfers between devices: 13.2 us -> 8.95 us  [trade_rows(): lax.all_to_all(grid_view, ('gx', 'gy'), split_axis=0, concat_axis=0, tile...]
    ppermute x6, starting transfers between devices: 11.8 us -> 13 us  [passed_along(): lax.ppermute(value, axis, [(source, source + steps) for source in range(i...]
    pallas_call x8 -> x10, Pallas kernels: 12.4 us -> 13.4 us  [call(): pl.pallas_call(body, out_shape=tuple(outs), in_specs=[pl.BlockSpec(memory...]
  transfers between devices with their start and end apart: 9 -> 8, of which waited for: 6 -> 5; matrix products, arithmetic and copies ran while one was open for 0% -> 0% of each run, Pallas kernels for 6% -> 7%
where the time goes in v3:
time: 88.7 us; the launch traced here: 87.9 us
  starting transfers between devices  23.9 us (27%)
  blocking collectives  21.2 us (24%)
  waiting for transfers between devices  19.3 us (22%)
  Pallas kernels  13.4 us (15%)
  local copies, waits for them, and re-layouts  9.36 us (11%)
    all_to_all x1, blocking collectives, trade_rows(): lax.all_to_all(grid_view, ('gx', 'gy'), split_axis=0, concat_axis=0, tile...  21.2 us
    pallas_call x10, Pallas kernels, call(): pl.pallas_call(body, out_shape=tuple(outs), in_specs=[pl.BlockSpec(memory...  13.4 us
    ppermute x6, starting transfers between devices, passed_along(): lax.ppermute(value, axis, [(source, source + steps) for source in range(i...  13 us
    all_to_all x2, starting transfers between devices, trade_rows(): lax.all_to_all(grid_view, ('gx', 'gy'), split_axis=0, concat_axis=0, tile...  10.9 us
    ppermute x6, waiting for transfers between devices, passed_along(): lax.ppermute(value, axis, [(source, source + steps) for source in range(i...  10.4 us
    unnamed x26, local copies, waits for them, and re-layouts  9.36 us
    all_to_all x2, waiting for transfers between devices, trade_rows(): lax.all_to_all(grid_view, ('gx', 'gy'), split_axis=0, concat_axis=0, tile...  8.95 us
  transfers between devices with their start and end apart: 8, of which 5 were waited for; matrix products, arithmetic and copies ran while one was open for 0% of the time, Pallas kernels for 7%

profile of v3, /device:TPU:0, one launch (start us, length us, event | category | flops | bytes accessed | tf_op | source)
XLA Modules:
  0.0 87.9 jit_solution(1796000923163507603)
XLA Ops:
  0.6 0.0 copy-start
  0.6 1.0 %copy-done = bf16[27,64,64]{2,1,0:T(8,128)(2,1)S(1)} copy-done((bf16[27,64,64]{2,1,0:T(8,128)(2,1)S(1)}, bf16[27,64,64]{2,1,0:T(8,128)(2,1)}, u32[]{:S(2)}) %copy-start) | copy-done | bytes 221208
  1.6 0.0 copy-start.1
  1.7 0.9 %copy-done.1 = bf16[1,1,32,4096]{3,2,1,0:T(8,128)(2,1)S(1)} copy-done((bf16[1,1,32,4096]{3,2,1,0:T(8,128)(2,1)S(1)}, bf16[1,1,32,4096]{3,2,1,0:T(8,128)(2,1)}, u32[]{:S(2)}) %copy-start.1) | copy-done | bytes 262168
  2.6 0.0 copy-start.2
  2.6 0.9 %copy-done.2 = bf16[1,1,32,4096]{3,2,1,0:T(8,128)(2,1)S(1)} copy-done((bf16[1,1,32,4096]{3,2,1,0:T(8,128)(2,1)S(1)}, bf16[1,1,32,4096]{3,2,1,0:T(8,128)(2,1)}, u32[]{:S(2)}) %copy-start.2) | copy-done | bytes 262168
  3.5 0.0 copy-start.3
  3.6 0.9 %copy-done.3 = bf16[1,1,64,1024]{3,2,1,0:T(8,128)(2,1)S(1)} copy-done((bf16[1,1,64,1024]{3,2,1,0:T(8,128)(2,1)S(1)}, bf16[1,1,64,1024]{3,2,1,0:T(8,128)(2,1)}, u32[]{:S(2)}) %copy-start.3) | copy-done | bytes 131096
  4.5 0.9 %copy-done.4 = bf16[8,128,64]{1,2,0:T(8,128)(2,1)S(1)} copy-done((bf16[8,128,64]{1,2,0:T(8,128)(2,1)S(1)}, bf16[8,128,64]{1,2,0:T(8,128)(2,1)}, u32[]{:S(2)}) %copy-start.4) | copy-done | bytes 131096
  5.4 0.0 copy-start.5
  5.4 0.7 copy-done.5
  6.1 0.7 copy-done.6
  6.8 0.7 copy-done.8
  7.4 0.7 copy-done.9
  8.1 0.7 copy-done.10
  8.8 1.8 %shard_map.137 = (bf16[128,512]{1,0:T(8,128)(2,1)}, s32[8,128]{1,0:T(8,128)S(1)}, bf16[27,64,64]{2,1,0:T(8,128)(2,1)S(1)}, bf16[32,4096]{1,0:T(8,128)(2,1)S(1)},...) custom-call(s32[4,16]{1,0:T(4,128)S(1)} %bitcast.37, ...), custom_call_target="tpu_custom_call" | custom-call | bytes 2026752 | tf_op jit(solution)/shard_map/pallas_call | solution.py:49
  10.5 7.4 %all-to-all-start = ((bf16[16,8,512]{2,1,0:T(8,128)(2,1)}), bf16[16,8,512]{2,1,0:T(8,128)(2,1)S(1)}, u32[]{:S(2)}, u32[]{:S(2)}) async-start(bf16[16,8,512]{2,1,0:T(8,128)(2,1)} %bitcast.12), calls=%async_computation | async-start | bytes 262144 | tf_op jit(solution)/shard_map/all_to_all | solution.py:446
  17.9 1.9 %shard_map.138 = (f32[48,4096]{1,0:T(8,128)S(1)}, bf16[8,4096]{1,0:T(8,128)(2,1)S(1)}, bf16[8,4096]{1,0:T(8,128)(2,1)S(1)}, bf16[9,384,256]{2,1,0:T(8,128)(2,1)S(1)}) custom-call(bf16[32,4096]{1,0:T(8,128)(2,1)S(1)} %get-tuple-element.35.cot_ref, bf16[27,64,64]{2,1,0:T(8,128)(2,1)S(1)} %get-tuple-element.36.weight_ref, ...), custom_call_target="tpu_custom_call" | custom-call | flops 1811939328 | bytes 3173760 | tf_op jit(solution)/shard_map/pallas_call | solution.py:49
  19.8 0.0 copy-start.11
  19.8 1.2 %copy-done.11 = bf16[9,384,256]{2,1,0:T(8,128)(2,1)} copy-done((bf16[9,384,256]{2,1,0:T(8,128)(2,1)}, bf16[9,384,256]{2,1,0:T(8,128)(2,1)S(1)}, u32[]{:S(2)}) %copy-start.11) | copy-done | bytes 1769496
  21.1 1.3 %collective-permute-start = (bf16[8,4096]{1,0:T(8,128)(2,1)S(1)}, bf16[8,4096]{1,0:T(8,128)(2,1)S(1)}, u32[]{:S(2)}, u32[]{:S(2)}) collective-permute-start(bf16[8,4096]{1,0:T(8,128)(2,1)S(1)} %get-tuple-element.39), channel_id=1, source_target_pairs={{4,0},{8,4},{12,8},{5,1},{9,5},{13,9},{6,2},{10,6},{14,10},{7,3},{... | collective-permute-start | bytes 196616 | tf_op jit(solution)/shard_map/ppermute | solution.py:440
  22.4 3.0 %collective-permute-start.1 = (bf16[8,4096]{1,0:T(8,128)(2,1)S(1)}, bf16[8,4096]{1,0:T(8,128)(2,1)S(1)}, u32[]{:S(2)}, u32[]{:S(2)}) collective-permute-start(bf16[8,4096]{1,0:T(8,128)(2,1)S(1)} %get-tuple-element.40), channel_id=1, source_target_pairs={{0,4},{4,8},{8,12},{1,5},{5,9},{9,13},{2,6},{6,10},{10,14},{3,7},{... | collective-permute-start | bytes 196616 | tf_op jit(solution)/shard_map/ppermute | solution.py:440
  25.4 0.0 collective-permute-done.next_ref
  25.4 0.9 collective-permute-done.1.prev_ref
  26.3 0.0 all-to-all-done
  26.3 0.7 shard_map.139
  27.0 3.8 %collective-permute-start.2 = (bf16[16,4096]{1,0:T(8,128)(2,1)S(1)}, bf16[16,4096]{1,0:T(8,128)(2,1)S(1)}, u32[]{:S(2)}, u32[]{:S(2)}) collective-permute-start(bf16[16,4096]{1,0:T(8,128)(2,1)S(1)} %get-tuple-element.42), channel_id=1, source_target_pairs={{0,1},{1,2},{2,3},{4,5},{5,6},{6,7},{8,9},{9,10},{10,11},{12,13},{... | collective-permute-start | bytes 393224 | tf_op jit(solution)/shard_map/ppermute | solution.py:440
  30.8 1.3 %collective-permute-start.3 = (bf16[16,4096]{1,0:T(8,128)(2,1)S(1)}, bf16[16,4096]{1,0:T(8,128)(2,1)S(1)}, u32[]{:S(2)}, u32[]{:S(2)}) collective-permute-start(bf16[16,4096]{1,0:T(8,128)(2,1)S(1)} %get-tuple-element.43), channel_id=1, source_target_pairs={{1,0},{2,1},{3,2},{5,4},{6,5},{7,6},{9,8},{10,9},{11,10},{13,12},{... | collective-permute-start | bytes 393224 | tf_op jit(solution)/shard_map/ppermute | solution.py:440
  32.1 1.7 %collective-permute-done.2.low_ref.prev_ref = bf16[16,4096]{1,0:T(8,128)(2,1)S(1)} collective-permute-done((bf16[16,4096]{1,0:T(8,128)(2,1)S(1)}, bf16[16,4096]{1,0:T(8,128)(2,1)S(1)}, u32[]{:S(2)}, u32[]{:S(2)}) %collective-permute-start.2) | collective-permute-done | bytes 131104 | tf_op jit(solution)/shard_map/ppermute | solution.py:440
  33.9 4.7 %collective-permute-done.3.high_ref.next_ref = bf16[16,4096]{1,0:T(8,128)(2,1)S(1)} collective-permute-done((bf16[16,4096]{1,0:T(8,128)(2,1)S(1)}, bf16[16,4096]{1,0:T(8,128)(2,1)S(1)}, u32[]{:S(2)}, u32[]{:S(2)}) %collective-permute-start.3) | collective-permute-done | bytes 131104 | tf_op jit(solution)/shard_map/ppermute | solution.py:440
  38.6 0.3 shard_map.140
  38.9 2.3 %collective-permute-start.4 = (bf16[8,4096]{1,0:T(8,128)(2,1)S(1)}, bf16[8,4096]{1,0:T(8,128)(2,1)S(1)}, u32[]{:S(2)}, u32[]{:S(2)}) collective-permute-start(bf16[8,4096]{1,0:T(8,128)(2,1)S(1)} %get-tuple-element.44), channel_id=1, source_target_pairs={{0,4},{4,8},{8,12},{1,5},{5,9},{9,13},{2,6},{6,10},{10,14},{3,7},{... | collective-permute-start | bytes 196616 | tf_op jit(solution)/shard_map/ppermute | solution.py:440
  41.1 1.3 %collective-permute-start.5 = (bf16[8,4096]{1,0:T(8,128)(2,1)S(1)}, bf16[8,4096]{1,0:T(8,128)(2,1)S(1)}, u32[]{:S(2)}, u32[]{:S(2)}) collective-permute-start(bf16[8,4096]{1,0:T(8,128)(2,1)S(1)} %get-tuple-element.45), channel_id=1, source_target_pairs={{4,0},{8,4},{12,8},{5,1},{9,5},{13,9},{6,2},{10,6},{14,10},{7,3},{... | collective-permute-start | bytes 196616 | tf_op jit(solution)/shard_map/ppermute | solution.py:440
  42.4 1.2 %shard_map.141 = (bf16[32,4096]{1,0:T(8,128)(2,1)}, bf16[128,1024]{1,0:T(8,128)(2,1)S(1)}, bf16[256,512]{1,0:T(8,128)(2,1)S(1)}) custom-call(f32[32,4096]{1,0:T(8,128)S(1)} %get-tuple-element.46.part_ref, s32[8,128]{1,0:T(8,128)S(1)} %get-tuple-element.47.lists_ref, bf16[16,4096]{1,0:T(8,128)(2,1)S(1)} %collective-permute-done.3.high_ref.next_ref, ...), custom_call_target="tpu_custom_call" | custom-call | bytes 2035712 | tf_op jit(solution)/shard_map/pallas_call | solution.py:49
  43.7 0.0 collective-permute-done.4.below_ref
  43.7 3.1 %collective-permute-done.5.above_ref = bf16[8,4096]{1,0:T(8,128)(2,1)S(1)} collective-permute-done((bf16[8,4096]{1,0:T(8,128)(2,1)S(1)}, bf16[8,4096]{1,0:T(8,128)(2,1)S(1)}, u32[]{:S(2)}, u32[]{:S(2)}) %collective-permute-start.5) | collective-permute-done | bytes 65568 | tf_op jit(solution)/shard_map/ppermute | solution.py:440
  46.7 2.1 %shard_map.142 = (bf16[128,1920]{1,0:T(8,128)(2,1)S(1)}, bf16[6,6,32,384]{3,2,1,0:T(8,128)(2,1)S(1)}) custom-call(bf16[32,4096]{1,0:T(8,128)(2,1)S(1)} %get-tuple-element.41.merged_ref, bf16[16,4096]{1,0:T(8,128)(2,1)S(1)} %collective-permute-done.2.low_ref.prev_ref, bf16[16,4096]{1,0:T(8,128)(2,1)S(1)} %collective-permute-done.3.high_ref.next_ref, ...), custom_call_target="tpu_custom_call" | custom-call | flops 905969664 | bytes 2559360 | tf_op jit(solution)/shard_map/pallas_call | solution.py:49
  48.8 0.0 copy-start.12
  48.8 21.2 %all_to_all.15 = bf16[16,8,1920]{2,1,0:T(8,128)(2,1)S(1)} all-to-all(bf16[16,8,1920]{2,1,0:T(8,128)(2,1)S(1)} %bitcast.31), channel_id=1, replica_groups=mesh['groups'=2,'gx'=4,'gy'=4] {'gx','gy'}, dimensions={0} | all-to-all | bytes 983040 | tf_op jit(solution)/shard_map/all_to_all | solution.py:446
  70.0 1.0 %shard_map.145 = bf16[128,1408]{1,0:T(8,128)(2,1)} custom-call(bf16[128,1920]{1,0:T(8,128)(2,1)S(1)} %bitcast.27), custom_call_target="tpu_custom_call" | custom-call | bytes 851968 | tf_op jit(solution)/shard_map/pallas_call | solution.py:49
  71.0 3.5 %all-to-all-start.2 = ((bf16[16,8,1408]{2,1,0:T(8,128)(2,1)}), bf16[16,8,1408]{2,1,0:T(8,128)(2,1)S(1)}, u32[]{:S(2)}, u32[]{:S(2)}) async-start(bf16[16,8,1408]{2,1,0:T(8,128)(2,1)} %bitcast.20), calls=%async_computation.2 | async-start | bytes 720896 | tf_op jit(solution)/shard_map/all_to_all | solution.py:446
  74.6 0.0 copy-start.7
  74.6 0.0 copy-done.12
  74.6 2.1 %shard_map.143 = bf16[32,4096]{1,0:T(8,128)(2,1)} custom-call(bf16[6,6,32,384]{3,2,1,0:T(8,128)(2,1)S(1)} %get-tuple-element.51.pad_ref, bf16[9,384,256]{2,1,0:T(8,128)(2,1)S(1)} %copy-done.12), custom_call_target="tpu_custom_call" | custom-call | flops 905969664 | bytes 2916352 | tf_op jit(solution)/shard_map/pallas_call | solution.py:49
  76.7 0.0 copy-done.7
  76.7 1.1 %shard_map.144 = bf16[64,1024]{1,0:T(8,128)(2,1)} custom-call(bf16[128,1920]{1,0:T(8,128)(2,1)S(1)} %bitcast.28, s32[4,16]{1,0:T(4,128)S(1)} %bitcast.38), custom_call_target="tpu_custom_call" | custom-call | bytes 622848 | tf_op jit(solution)/shard_map/pallas_call | solution.py:49
  77.7 8.9 %all-to-all-done.2 = bf16[16,8,1408]{2,1,0:T(8,128)(2,1)S(1)} async-done(((bf16[16,8,1408]{2,1,0:T(8,128)(2,1)}), bf16[16,8,1408]{2,1,0:T(8,128)(2,1)S(1)}, u32[]{:S(2)}, u32[]{:S(2)}) %all-to-all-start.2) | async-done | bytes 360480 | tf_op jit(solution)/shard_map/all_to_all | solution.py:446
  86.7 1.2 %shard_map.146 = (f32[27,64,64]{2,1,0:T(8,128)}, f32[512,128]{1,0:T(8,128)}) custom-call(bf16[128,1408]{1,0:T(8,128)(2,1)S(1)} %bitcast.29), custom_call_target="tpu_custom_call" | custom-call | bytes 1064960 | tf_op jit(solution)/shard_map/pallas_call | solution.py:49
  (5 shorter events, 0.0 us)
Async XLA Ops:
  0.6 1.0 %copy-start = (bf16[27,64,64]{2,1,0:T(8,128)(2,1)S(1)}, bf16[27,64,64]{2,1,0:T(8,128)(2,1)}, u32[]{:S(2)}) copy-start(bf16[27,64,64]{2,1,0:T(8,128)(2,1)} %weight_hbm.1) | copy-start | bytes 663556
  1.6 0.9 %copy-start.1 = (bf16[1,1,32,4096]{3,2,1,0:T(8,128)(2,1)S(1)}, bf16[1,1,32,4096]{3,2,1,0:T(8,128)(2,1)}, u32[]{:S(2)}) copy-start(bf16[1,1,32,4096]{3,2,1,0:T(8,128)(2,1)} %param.19) | copy-start | bytes 786436
  2.6 0.9 %copy-start.2 = (bf16[1,1,32,4096]{3,2,1,0:T(8,128)(2,1)S(1)}, bf16[1,1,32,4096]{3,2,1,0:T(8,128)(2,1)}, u32[]{:S(2)}) copy-start(bf16[1,1,32,4096]{3,2,1,0:T(8,128)(2,1)} %param.10) | copy-start | bytes 786436
  3.5 0.9 %copy-start.3 = (bf16[1,1,64,1024]{3,2,1,0:T(8,128)(2,1)S(1)}, bf16[1,1,64,1024]{3,2,1,0:T(8,128)(2,1)}, u32[]{:S(2)}) copy-start(bf16[1,1,64,1024]{3,2,1,0:T(8,128)(2,1)} %param.11) | copy-start | bytes 393220
  4.5 0.9 %copy-start.4 = (bf16[8,128,64]{1,2,0:T(8,128)(2,1)S(1)}, bf16[8,128,64]{1,2,0:T(8,128)(2,1)}, u32[]{:S(2)}) copy-start(bf16[8,128,64]{1,2,0:T(8,128)(2,1)} %param.13) | copy-start | bytes 393220
  5.4 0.7 copy-start.5
  6.1 0.7 copy-start.6
  6.8 0.7 copy-start.8
  7.4 0.7 copy-start.9
  8.1 0.7 copy-start.10
  10.5 15.8 %all-to-all-start = ((bf16[16,8,512]{2,1,0:T(8,128)(2,1)}), bf16[16,8,512]{2,1,0:T(8,128)(2,1)S(1)}, u32[]{:S(2)}, u32[]{:S(2)}) async-start(bf16[16,8,512]{2,1,0:T(8,128)(2,1)} %bitcast.12), calls=%async_computation | async-start | bytes 262144 | tf_op jit(solution)/shard_map/all_to_all | solution.py:446
  19.8 1.2 %copy-start.11 = (bf16[9,384,256]{2,1,0:T(8,128)(2,1)}, bf16[9,384,256]{2,1,0:T(8,128)(2,1)S(1)}, u32[]{:S(2)}) copy-start(bf16[9,384,256]{2,1,0:T(8,128)(2,1)S(1)} %get-tuple-element.52.band_ref) | copy-start | bytes 5308420
  21.1 4.3 %collective-permute-start = (bf16[8,4096]{1,0:T(8,128)(2,1)S(1)}, bf16[8,4096]{1,0:T(8,128)(2,1)S(1)}, u32[]{:S(2)}, u32[]{:S(2)}) collective-permute-start(bf16[8,4096]{1,0:T(8,128)(2,1)S(1)} %get-tuple-element.39), channel_id=1, source_target_pairs={{4,0},{8,4},{12,8},{5,1},{9,5},{13,9},{6,2},{10,6},{14,10},{7,3},{... | collective-permute-start | bytes 196616 | tf_op jit(solution)/shard_map/ppermute | solution.py:440
  22.4 3.9 %collective-permute-start.1 = (bf16[8,4096]{1,0:T(8,128)(2,1)S(1)}, bf16[8,4096]{1,0:T(8,128)(2,1)S(1)}, u32[]{:S(2)}, u32[]{:S(2)}) collective-permute-start(bf16[8,4096]{1,0:T(8,128)(2,1)S(1)} %get-tuple-element.40), channel_id=1, source_target_pairs={{0,4},{4,8},{8,12},{1,5},{5,9},{9,13},{2,6},{6,10},{10,14},{3,7},{... | collective-permute-start | bytes 196616 | tf_op jit(solution)/shard_map/ppermute | solution.py:440
  27.0 6.9 %collective-permute-start.2 = (bf16[16,4096]{1,0:T(8,128)(2,1)S(1)}, bf16[16,4096]{1,0:T(8,128)(2,1)S(1)}, u32[]{:S(2)}, u32[]{:S(2)}) collective-permute-start(bf16[16,4096]{1,0:T(8,128)(2,1)S(1)} %get-tuple-element.42), channel_id=1, source_target_pairs={{0,1},{1,2},{2,3},{4,5},{5,6},{6,7},{8,9},{9,10},{10,11},{12,13},{... | collective-permute-start | bytes 393224 | tf_op jit(solution)/shard_map/ppermute | solution.py:440
  30.8 7.8 %collective-permute-start.3 = (bf16[16,4096]{1,0:T(8,128)(2,1)S(1)}, bf16[16,4096]{1,0:T(8,128)(2,1)S(1)}, u32[]{:S(2)}, u32[]{:S(2)}) collective-permute-start(bf16[16,4096]{1,0:T(8,128)(2,1)S(1)} %get-tuple-element.43), channel_id=1, source_target_pairs={{1,0},{2,1},{3,2},{5,4},{6,5},{7,6},{9,8},{10,9},{11,10},{13,12},{... | collective-permute-start | bytes 393224 | tf_op jit(solution)/shard_map/ppermute | solution.py:440
  38.9 4.8 %collective-permute-start.4 = (bf16[8,4096]{1,0:T(8,128)(2,1)S(1)}, bf16[8,4096]{1,0:T(8,128)(2,1)S(1)}, u32[]{:S(2)}, u32[]{:S(2)}) collective-permute-start(bf16[8,4096]{1,0:T(8,128)(2,1)S(1)} %get-tuple-element.44), channel_id=1, source_target_pairs={{0,4},{4,8},{8,12},{1,5},{5,9},{9,13},{2,6},{6,10},{10,14},{3,7},{... | collective-permute-start | bytes 196616 | tf_op jit(solution)/shard_map/ppermute | solution.py:440
  41.1 5.6 %collective-permute-start.5 = (bf16[8,4096]{1,0:T(8,128)(2,1)S(1)}, bf16[8,4096]{1,0:T(8,128)(2,1)S(1)}, u32[]{:S(2)}, u32[]{:S(2)}) collective-permute-start(bf16[8,4096]{1,0:T(8,128)(2,1)S(1)} %get-tuple-element.45), channel_id=1, source_target_pairs={{4,0},{8,4},{12,8},{5,1},{9,5},{13,9},{6,2},{10,6},{14,10},{7,3},{... | collective-permute-start | bytes 196616 | tf_op jit(solution)/shard_map/ppermute | solution.py:440
  48.8 25.8 %copy-start.12 = (bf16[9,384,256]{2,1,0:T(8,128)(2,1)S(1)}, bf16[9,384,256]{2,1,0:T(8,128)(2,1)}, u32[]{:S(2)}) copy-start(bf16[9,384,256]{2,1,0:T(8,128)(2,1)} %copy-done.11) | copy-start | bytes 5308420
  71.0 15.7 %all-to-all-start.2 = ((bf16[16,8,1408]{2,1,0:T(8,128)(2,1)}), bf16[16,8,1408]{2,1,0:T(8,128)(2,1)S(1)}, u32[]{:S(2)}, u32[]{:S(2)}) async-start(bf16[16,8,1408]{2,1,0:T(8,128)(2,1)} %bitcast.20), calls=%async_computation.2 | async-start | bytes 720896 | tf_op jit(solution)/shard_map/all_to_all | solution.py:446
  74.6 2.1 %copy-start.7 = (s32[1,1,16,4]{2,3,1,0:T(4,128)S(1)}, s32[1,1,16,4]{2,3,1,0:T(4,128)}, u32[]{:S(2)}) copy-start(s32[1,1,16,4]{2,3,1,0:T(4,128)} %param.18) | copy-start | bytes 772

commit v4 on v3

--- a/solution.py
+++ b/solution.py
@@ -52,7 +52,7 @@
         in_specs=[pl.BlockSpec(memory_space=pltpu.HBM) if in_hbm else pl.BlockSpec() for _ in args],
         scratch_shapes=tuple(scratch),
         cost_estimate=pl.CostEstimate(flops=flops, bytes_accessed=moved, transcendentals=0),
-        compiler_params=pltpu.CompilerParams(vmem_limit_bytes=28 * 2**20),
+        compiler_params=pltpu.CompilerParams(vmem_limit_bytes=None if in_hbm else 28 * 2**20),
     )(*args)
 
 
@@ -104,6 +104,7 @@
             at = (vx * 4 + vy) * RUN + cz * 2 * C
             add = lifted[v * bricks : (v + 1) * bricks, parity * 2 * C : (parity + 1) * 2 * C]
             merged_ref[:, at : at + 2 * C] = (fine_ref[:, at : at + 2 * C].astype(F32) + add).astype(BF)
+    return parents
 
 
 def pick_rows(lists, rows):
@@ -127,14 +128,12 @@
     return lists_ref[4:5, :bricks]
 
 
-def cross_body(merged_ref, low_ref, high_ref, lists_ref, a_ref, b_ref, again_ref):
-    again_ref[...] = lists_ref[...]
-    face = a_ref.shape[0]
-    sides = stack_rows(low_ref[...].astype(F32)[:face], high_ref[...].astype(F32)[:face])
-    rows = jnp.concatenate([merged_ref[...], sides], axis=0)
+def cross_body(merged_ref, low_ref, high_ref, lists_ref, low_grad_ref, high_grad_ref, a_ref, b_ref):
+    face, width = low_grad_ref.shape
+    rows = jnp.concatenate([merged_ref[...], stack_rows(low_ref[:, :width], high_ref[:, :width])], axis=0)
     first, second = pick_rows(crosses_of(lists_ref, face), rows)
-    a_ref[...] = first.astype(BF)
-    b_ref[...] = second.astype(BF)
+    a_ref[...] = stack_rows(first, high_grad_ref[...])
+    b_ref[...] = stack_rows(second, low_grad_ref[...])
 
 
 def build_bands(weight_ref, band_ref):
@@ -169,6 +168,22 @@
     return (dx + 1) * 9 + (dy + 1) * 3 + dz + 1
 
 
+def stack_lanes(value, lanes):
+    return jnp.concatenate([value[:, p * lanes : (p + 1) * lanes] for p in range(value.shape[1] // lanes)], axis=0)
+
+
+def stack_parities(value):
+    stacked = []
+    for v in range(8):
+        cx, cy, cz = (v // 4, v // 2 % 2, v % 2)
+        lanes = []
+        for parity in range(4):
+            at = ((2 * cx + parity // 2) * 4 + 2 * cy + parity % 2) * RUN + cz * 2 * C
+            lanes.append(value[:, at : at + 2 * C])
+        stacked.append(jnp.concatenate(lanes, axis=1))
+    return jnp.concatenate(stacked, axis=0)
+
+
 def stack_runs(ref):
     return jnp.concatenate([ref[:, p * RUN : (p + 1) * RUN] for p in range(16)], axis=0)
 
@@ -178,13 +193,17 @@
     return head, (value - head.astype(F32)).astype(BF)
 
 
-def table_grad_body(cot_ref, weight_ref, near_ref, ext_ref, low_ref, high_ref, band_ref, pad_ref):
+def table_grad_body(
+    cot_ref, weight_ref, near_ref, lists_ref, ext_ref, low_ref, high_ref, turned_ref, again_ref, band_ref, pad_ref
+):
+    again_ref[...] = lists_ref[...]
     bricks = cot_ref.shape[0]
     face = low_ref.shape[0]
     start = ext_ref.shape[0]
     rows = start + 2 * face
     build_bands(weight_ref, band_ref)
     cot = stack_runs(cot_ref)
+    turned_ref[...] = cot.T
     pad_ref[...] = jnp.zeros(pad_ref.shape, F32)
     for e in range(9):
         ex, ey = (e // 3, e % 3)
@@ -228,40 +247,47 @@
 
 
 def first_body(
-    sends_hbm, items_hbm, sides_hbm, crosses_hbm, slots_hbm, weight_hbm, cot_hbm, near_hbm, fine_hbm, up_hbm,
-    out_ref, lists_ref, weight_ref, cot_ref, near_ref, fine_ref, up_ref,
+    sends_hbm, items_hbm, sides_hbm, crosses_hbm, slots_hbm, out_ref, lists_ref,
     sends_ref, items_ref, sides_ref, crosses_ref, slots_ref, arrived,
 ):
-    sources = (
-        sends_hbm, items_hbm, sides_hbm, crosses_hbm, slots_hbm, weight_hbm, cot_hbm, near_hbm, fine_hbm, up_hbm,
-    )
-    places = (sends_ref, items_ref, sides_ref, crosses_ref, slots_ref, weight_ref, cot_ref, near_ref, fine_ref, up_ref)
+    sources = (sends_hbm, items_hbm, sides_hbm, crosses_hbm, slots_hbm)
+    places = (sends_ref, items_ref, sides_ref, crosses_ref, slots_ref)
     copies = [pltpu.make_async_copy(s, p, arrived.at[i]) for i, (s, p) in enumerate(zip(sources, places))]
     for copy in copies:
         copy.start()
-    copies[0].wait()
-    copies[1].wait()
-    items_out(sends_ref, items_ref, out_ref)
-    for copy in copies[2:]:
+    for copy in copies:
         copy.wait()
     face, bricks = (sides_ref.shape[1], slots_ref.shape[1])
     lists_ref[...] = jnp.zeros(lists_ref.shape, I32)
     lists_ref[0:2, :face] = sides_ref[...]
     lists_ref[2:4, :face] = crosses_ref[...]
     lists_ref[4:5, :bricks] = slots_ref[...]
+    items_out(sends_ref, items_ref, out_ref)
 
 
 def weight_grad_body(
-    merged_ref, low_ref, high_ref, below_ref, above_ref, turned_ref, near_ref, part_ref, back_ref, pad_ref, table_ref
+    merged_ref, low_ref, high_ref, below_ref, above_ref, turned_ref, near_ref, lists_ref, ext_ref, parents_ref,
+    sums_ref, pad_ref, part_ref, to_next_ref, to_prev_ref, table_ref,
 ):
-    bricks = merged_ref.shape[0]
-    face = below_ref.shape[0]
+    bricks, width = merged_ref.shape
+    face = low_ref.shape[0]
     rows = bricks + 4 * face
+    below = below_ref[...].astype(F32)
+    above = above_ref[...].astype(F32)
     table_ref[:bricks] = merged_ref[...]
-    table_ref[bricks:] = stack_rows(
-        low_ref[...].astype(F32)[:face], high_ref[...].astype(F32)[:face], below_ref[...], above_ref[...]
-    )
-    back_ref[:, : part_ref.shape[1]] = part_ref[...]
+    table_ref[bricks:] = stack_rows(low_ref[:, :width], high_ref[:, :width], below[:face], above[:face])
+    total = add_rows(ext_ref[...], crosses_of(lists_ref, face), above[face:], below[face:])
+    part_ref[...] = total[:bricks]
+    to_prev_ref[...] = total[bricks : bricks + face].astype(BF)
+    to_next_ref[...] = total[bricks + face :].astype(BF)
+    side_parents = stack_lanes(stack_rows(low_ref[:, width:], high_ref[:, width:]), parents_ref.shape[1])
+    grads = [stack_parities(total[:bricks].astype(BF)), stack_parities(total[bricks:].astype(BF))]
+    up_sum = dot_tn(jnp.concatenate(grads, axis=0), jnp.concatenate([parents_ref[...], side_parents], axis=0))
+    coarse = up_sum.shape[1]
+    count = sums_ref.shape[0]
+    parts = up_sum.shape[0] // count
+    for q in range(parts):
+        sums_ref[:, q * coarse : (q + 1) * coarse] = up_sum[q * count : (q + 1) * count].astype(BF)
     near = jnp.concatenate([near_ref[o] for o in range(27)] + [jnp.zeros((5, bricks), I32)], axis=0)
     near = near.astype(F32).T.astype(I32)
 
@@ -315,8 +341,8 @@
     sums.append(jnp.zeros((C, 2 * C), F32))
     for pair in range(7):
         both = [jnp.where(lanes_low, sums[14 * h + 2 * pair], sums[14 * h + 2 * pair + 1]) for h in range(2)]
-        at = part_ref.shape[1] + pair * 2 * C
-        back_ref[:, at : at + 2 * C] = jnp.concatenate(both, axis=0).astype(BF)
+        at = parts * coarse + pair * 2 * C
+        sums_ref[:, at : at + 2 * C] = jnp.concatenate(both, axis=0).astype(BF)
 
 
 def inputs_at(pad_ref, e):
@@ -325,8 +351,9 @@
     return pad_ref[ex : ex + 4, ey : ey + 4].reshape(16 * bricks, WIDE)
 
 
-def conv_body(pad_ref, band_ref, out_ref):
+def conv_body(pad_ref, weight_ref, out_ref, band_ref):
     bricks = pad_ref.shape[2]
+    build_bands(weight_ref, band_ref)
     total = None
     for e in range(9):
         part = dot(inputs_at(pad_ref, e), band_ref[e])
@@ -342,65 +369,43 @@
     return base + dot(chosen, stack_rows(first, second))
 
 
-def merge_body(
-    received_ref, up_ref, fine_ref, lists_ref, ext_ref, next_ref, prev_ref,
-    merged_ref, parents_ref, part_ref, a_ref, b_ref,
-):
-    bricks, face = (fine_ref.shape[0], next_ref.shape[0])
-    total = add_rows(ext_ref[...], crosses_of(lists_ref, face), next_ref[...], prev_ref[...])
-    part_ref[...] = total[:bricks]
-    merge(received_ref, slots_of(lists_ref, bricks), up_ref, fine_ref, merged_ref, parents_ref)
-    first, second = pick_rows(sides_of(lists_ref, face), merged_ref[...])
-    a_ref[...] = stack_rows(first, total[bricks + face :])
-    b_ref[...] = stack_rows(second, total[bricks : bricks + face])
-
-
-def fine_grad_body(
-    part_ref, lists_ref, next_ref, prev_ref, up_ref, parents_ref, cot_ref, grad_ref, back_ref, turned_ref
-):
-    turned_ref[...] = stack_runs(cot_ref).T
+def merge_body(received_ref, up_ref, fine_ref, lists_ref, merged_ref, parents_ref, a_ref, b_ref):
+    bricks, width = fine_ref.shape
+    face = a_ref.shape[0]
+    parents = merge(received_ref, slots_of(lists_ref, bricks), up_ref, fine_ref, merged_ref, parents_ref)
+    lists = sides_of(lists_ref, face)
+    for out_ref, rows, owners in zip((a_ref, b_ref), pick_rows(lists, merged_ref[...]), pick_rows(lists, parents)):
+        out_ref[:, :width] = rows.astype(BF)
+        out_ref[:, width:] = owners.astype(BF)
+
+
+def fine_grad_body(part_ref, lists_ref, next_ref, prev_ref, up_ref, grad_ref, replies_ref):
     bricks = part_ref.shape[0]
-    face = next_ref.shape[0] // 2
-    grad_ref[...] = add_rows(
-        part_ref[...], sides_of(lists_ref, face), next_ref[...].astype(F32)[face:], prev_ref[...].astype(F32)[face:]
-    ).astype(BF)
-    stacked = []
-    for v in range(8):
-        cx, cy, cz = (v // 4, v // 2 % 2, v % 2)
-        lanes = []
-        for parity in range(4):
-            at = ((2 * cx + parity // 2) * 4 + 2 * cy + parity % 2) * RUN + cz * 2 * C
-            lanes.append(grad_ref[:, at : at + 2 * C])
-        stacked.append(jnp.concatenate(lanes, axis=1))
-    stacked = jnp.concatenate(stacked, axis=0)
-    items = dot(stacked, up_ref[...]).astype(BF)
+    face = next_ref.shape[0]
+    total = add_rows(part_ref[...], sides_of(lists_ref, face), next_ref[...], prev_ref[...])
+    grad_ref[...] = total.astype(BF)
+    items = dot(stack_parities(grad_ref[...]), up_ref[...]).astype(BF)
     items = jnp.concatenate([items[v * bricks : (v + 1) * bricks] for v in range(8)], axis=1)
     half = items.shape[1] // 2
-    count = back_ref.shape[0]
-    up_sum = dot_tn(stacked, parents_ref[...]).astype(BF)
-    coarse = up_sum.shape[1]
-    parts = up_sum.shape[0] // count
-    item_lanes = back_ref.shape[1] - parts * coarse
-    for q in range(parts):
-        at = item_lanes + q * coarse
-        back_ref[:, at : at + coarse] = up_sum[q * count : (q + 1) * count]
+    count, item_lanes = replies_ref.shape
     slots = slots_of(lists_ref, bricks)
     for j in range(item_lanes // half):
         piece = iota((count, bricks), 0) * (item_lanes // half) + j
         named = piece // 2 == slots
         rows = dot(ones_where(named & (piece % 2 == 0)), items[:, :half])
         rows += dot(ones_where(named & (piece % 2 == 1)), items[:, half:])
-        back_ref[:, j * half : (j + 1) * half] = rows.astype(BF)
-
-
-def share_body(back_ref, out_ref, devices):
-    count, width = out_ref.shape
+        replies_ref[:, j * half : (j + 1) * half] = rows.astype(BF)
+
+
+def share_body(sums_ref, replies_ref, out_ref, devices):
+    count, item_lanes = replies_ref.shape
     share = count // devices
-    same = ones_where(iota((count, count), 0) % share == iota((count, count), 1) % share)
-    out_ref[...] = dot(same, back_ref[:, back_ref.shape[1] - width :]).astype(BF)
-
-
-def coarse_grad_body(back_ref, sends_ref, out_ref):
+    same = iota((count, count), 0) % share == iota((count, count), 1) % share
+    out_ref[:, :item_lanes] = replies_ref[...]
+    out_ref[:, item_lanes:] = dot(ones_where(same), sums_ref[...]).astype(BF)
+
+
+def coarse_grad(back_ref, sends_ref, out_ref):
     capacity, devices = sends_ref.shape
     count, item_width = out_ref.shape
     half = item_width // 2
@@ -418,15 +423,18 @@
         out_ref[:, h * half : (h + 1) * half] = total.astype(BF)
 
 
-def final_body(totals_ref, conv_ref, up_ref, scale):
-    count = totals_ref.shape[0]
+def last_body(back_ref, sends_ref, conv_ref, up_ref, out_ref, scale):
+    coarse_grad(back_ref, sends_ref, out_ref)
+    count, width = back_ref.shape
     coarse = up_ref.shape[1]
     parts = up_ref.shape[0] // count
+    at = width - 14 * C - parts * coarse
     for q in range(parts):
-        up_ref[q * count : (q + 1) * count] = totals_ref[:, q * coarse : (q + 1) * coarse].astype(F32) * scale
+        up_ref[q * count : (q + 1) * count] = back_ref[:, at : at + coarse].astype(F32) * scale
+        at += coarse
     for pair in range(7):
-        at = parts * coarse + pair * 2 * C
-        turned = totals_ref[:, at : at + 2 * C].astype(F32).T * scale
+        turned = back_ref[:, at : at + 2 * C].astype(F32).T * scale
+        at += 2 * C
         for h in range(2):
             for s in range(2):
                 o = 14 * h + 2 * pair + s
@@ -469,63 +477,61 @@
     up_turned = up_weight.transpose(0, 2, 1).reshape(8 * C, coarse)
     half = item_width // 2
     count = 2 * C
-    up_width = 8 * C * coarse // count
-    back_width = capacity * devices * item_width // count + up_width
+    item_lanes = capacity * devices * item_width // count
+    sums_width = 8 * C * coarse // count + 14 * C
+    rows = shape((bricks, width))
     face_rows = shape((face, width))
+    faces_and_parents = shape((face, width + item_width))
     two_faces = shape((2 * face, width))
+    lists_shape = shape((8, 128), I32)
+    band = pltpu.VMEM((9, WIDE, RUN), BF)
     conv_flops = 2 * 9 * 16 * bricks * WIDE * RUN
 
     listed = (sends, items, sides, crosses, slots)
-    kept = (conv_weight, cot, near, fine, up_turned)
-    outgoing, lists, weight, cot, near, fine, up_turned = call(
-        first_body,
-        [shape((2 * capacity * devices, half)), shape((8, 128), I32)] + [shape(a.shape, a.dtype) for a in kept],
-        *listed, *kept,
-        scratch=[pltpu.VMEM(a.shape, a.dtype) for a in listed]
-        + [pltpu.SemaphoreType.DMA((len(listed) + len(kept),))],
+    outgoing, lists = call(
+        first_body, [shape((2 * capacity * devices, half)), lists_shape], *listed,
+        scratch=[pltpu.VMEM(a.shape, a.dtype) for a in listed] + [pltpu.SemaphoreType.DMA((len(listed),))],
         in_hbm=True,
     )
     received = trade_rows(outgoing, devices)
-    ext_grad, low_cross, high_cross, band = call(
+    ext_grad, low_cross, high_cross, turned, lists = call(
         table_grad_body,
-        [shape((start, width), F32), face_rows, face_rows, shape((9, WIDE, RUN))],
-        cot, weight, near, scratch=[pltpu.VMEM((6, 6, bricks, WIDE), F32)], flops=2 * conv_flops,
-    )
-    grad_prev = passed_along(high_cross, "gx", 1)
-    grad_next = passed_along(low_cross, "gx", -1)
-    merged, parents, fine_part, to_next, to_prev = call(
-        merge_body,
-        [shape((bricks, width)), shape((8 * bricks, coarse)), shape((bricks, width), F32), two_faces, two_faces],
-        received, up_turned, fine, lists, ext_grad, grad_next, grad_prev,
+        [shape((start, width), F32), face_rows, face_rows, shape((RUN, 16 * bricks)), lists_shape],
+        cot, conv_weight, near, lists,
+        scratch=[band, pltpu.VMEM((6, 6, bricks, WIDE), F32)], flops=2 * conv_flops,
+    )
+    merged, parents, to_next, to_prev = call(
+        merge_body, [rows, shape((8 * bricks, coarse)), faces_and_parents, faces_and_parents],
+        received, up_turned, fine, lists,
     )
     low_side = passed_along(to_next, "gy", 1)
     high_side = passed_along(to_prev, "gy", -1)
-    to_next, to_prev, lists = call(
-        cross_body, [face_rows, face_rows, shape((8, 128), I32)], merged, low_side, high_side, lists
+    to_next, to_prev = call(
+        cross_body, [two_faces, two_faces], merged, low_side, high_side, lists, low_cross, high_cross
     )
     below = passed_along(to_next, "gx", 1)
     above = passed_along(to_prev, "gx", -1)
-    grad_fine, part, turned = call(
-        fine_grad_body,
-        [shape((bricks, width)), shape((count, back_width)), shape((RUN, 16 * bricks))],
-        fine_part, lists, high_side, low_side, up_turned, parents, cot,
-    )
-    back, pad = call(
-        weight_grad_body, [shape((count, back_width + 14 * C)), shape((6, 6, bricks, WIDE))],
-        merged, low_side, high_side, below, above, turned, near, part,
+    sums, pad, fine_part, to_next, to_prev = call(
+        weight_grad_body,
+        [shape((count, sums_width)), shape((6, 6, bricks, WIDE)), shape((bricks, width), F32), face_rows, face_rows],
+        merged, low_side, high_side, below, above, turned, near, lists, ext_grad, parents,
         scratch=[pltpu.VMEM((bricks + 4 * face, width), BF)], flops=conv_flops,
     )
+    sums = trade_rows(sums, devices)
+    grad_prev = passed_along(to_next, "gy", 1)
+    grad_next = passed_along(to_prev, "gy", -1)
+    grad_fine, replies = call(
+        fine_grad_body, [rows, shape((count, item_lanes))], fine_part, lists, grad_next, grad_prev, up_turned
+    )
+    (output,) = call(conv_body, [rows], pad, conv_weight, scratch=[band], flops=conv_flops)
+    (back,) = call(
+        functools.partial(share_body, devices=devices), [shape((count, item_lanes + sums_width))], sums, replies
+    )
     back = trade_rows(back, devices)
-    (output,) = call(conv_body, [shape((bricks, width))], pad, band, flops=conv_flops)
-    (sums,) = call(
-        functools.partial(share_body, devices=devices), [shape((count, up_width + 14 * C))], back
-    )
-    totals = trade_rows(sums, devices)
-    (coarse_grad,) = call(coarse_grad_body, [shape((item_count, item_width))], back, sends)
     scale = 1.0 / math.sqrt(64 * bricks * devices)
-    grad_conv, grad_up = call(
-        functools.partial(final_body, scale=scale),
-        [shape((27, C, C), F32), shape((8 * C, coarse), F32)], totals,
+    grad_conv, grad_up, coarse_grad = call(
+        functools.partial(last_body, scale=scale),
+        [shape((27, C, C), F32), shape((8 * C, coarse), F32), shape((item_count, item_width))], back, sends,
     )
     return (
         output.reshape(1, 1, bricks, width),

time: 88.7 us -> 77.2 us (0.87)
  blocking collectives: 21.2 us -> 0 us
  waiting for transfers between devices: 19.3 us -> 29.5 us
  local copies, waits for them, and re-layouts: 9.36 us -> 1.7 us
  starting transfers between devices: 23.9 us -> 31 us
    all_to_all x1 -> x0, blocking collectives: 21.2 us -> none  [trade_rows(): lax.all_to_all(grid_view, ('gx', 'gy'), split_axis=0, concat_axis=0, tile...]
    all_to_all x2 -> x3, waiting for transfers between devices: 8.95 us -> 18 us  [trade_rows(): lax.all_to_all(grid_view, ('gx', 'gy'), split_axis=0, concat_axis=0, tile...]
    all_to_all x2 -> x3, starting transfers between devices: 10.9 us -> 18.7 us  [trade_rows(): lax.all_to_all(grid_view, ('gx', 'gy'), split_axis=0, concat_axis=0, tile...]
    unnamed x26 -> x16, local copies, waits for them, and re-layouts: 9.36 us -> 1.7 us
    ppermute x6, waiting for transfers between devices: 10.4 us -> 11.5 us  [passed_along(): lax.ppermute(value, axis, [(source, source + steps) for source in range(i...]
    pallas_call x10 -> x9, Pallas kernels: 13.4 us -> 13.5 us  [call(): pl.pallas_call(body, out_shape=tuple(outs), in_specs=[pl.BlockSpec(memory...]
  transfers between devices with their start and end apart: 8 -> 9, of which waited for: 5 -> 7; matrix products, arithmetic and copies ran while one was open for 0% -> 0% of each run, Pallas kernels for 7% -> 7%
where the time goes in v4:
time: 77.2 us; the launch traced here: 76.5 us
  starting transfers between devices  31 us (40%)
  waiting for transfers between devices  29.5 us (38%)
  Pallas kernels  13.5 us (17%)
  local copies, waits for them, and re-layouts  1.7 us (2%)
  between operations  0.81 us (1%)
    all_to_all x3, starting transfers between devices, trade_rows(): lax.all_to_all(grid_view, ('gx', 'gy'), split_axis=0, concat_axis=0, tile...  18.7 us
    all_to_all x3, waiting for transfers between devices, trade_rows(): lax.all_to_all(grid_view, ('gx', 'gy'), split_axis=0, concat_axis=0, tile...  18 us
    pallas_call x9, Pallas kernels, call(): pl.pallas_call(body, out_shape=tuple(outs), in_specs=[pl.BlockSpec(memory...  13.5 us
    ppermute x6, starting transfers between devices, passed_along(): lax.ppermute(value, axis, [(source, source + steps) for source in range(i...  12.3 us
    ppermute x6, waiting for transfers between devices, passed_along(): lax.ppermute(value, axis, [(source, source + steps) for source in range(i...  11.5 us
    unnamed x16, local copies, waits for them, and re-layouts  1.7 us
  transfers between devices with their start and end apart: 9, of which 7 were waited for; matrix products, arithmetic and copies ran while one was open for 0% of the time, Pallas kernels for 7%

profile of v4, /device:TPU:0, one launch (start us, length us, event | category | flops | bytes accessed | tf_op | source)
XLA Modules:
  0.0 76.5 jit_solution(768662856228225013)
XLA Ops:
  0.6 0.0 copy-start.5
  0.6 2.0 %shard_map.137 = (bf16[128,512]{1,0:T(8,128)(2,1)}, s32[8,128]{1,0:T(8,128)}) custom-call(s32[4,16]{1,0:T(4,128)} %bitcast.33, bf16[64,1024]{1,0:T(8,128)(2,1)} %bitcast.38, s32[2,8]{1,0:T(2,128)} %bitcast.40, s32[2,8]{1,0:T(2,128)} %bitcast.41, s32[1,32]{1,0:T(1,128)} %bitcast.42), custom_call_target="tpu_custom_call" | custom-call | bytes 266752 | tf_op jit(solution)/shard_map/pallas_call | solution.py:49
  2.7 0.0 copy-start.6
  2.7 7.4 %all-to-all-start = ((bf16[16,8,512]{2,1,0:T(8,128)(2,1)}), bf16[16,8,512]{2,1,0:T(8,128)(2,1)S(1)}, u32[]{:S(2)}, u32[]{:S(2)}) async-start(bf16[16,8,512]{2,1,0:T(8,128)(2,1)} %bitcast.39), calls=%async_computation | async-start | bytes 262144 | tf_op jit(solution)/shard_map/all_to_all | solution.py:454
  10.1 0.0 copy-start.7
  10.1 0.0 copy-done.5
  10.1 0.0 copy-done.6
  10.1 0.7 copy-done.7
  10.8 0.0 copy-start.3
  10.8 1.0 %copy-done.3 = bf16[27,64,64]{2,1,0:T(8,128)(2,1)S(1)} copy-done((bf16[27,64,64]{2,1,0:T(8,128)(2,1)S(1)}, bf16[27,64,64]{2,1,0:T(8,128)(2,1)}, u32[]{:S(2)}) %copy-start.3) | copy-done | bytes 221208
  11.8 0.0 copy-start
  11.8 0.0 copy-start.1
  11.8 1.9 %shard_map.138 = (f32[48,4096]{1,0:T(8,128)S(1)}, bf16[8,4096]{1,0:T(8,128)(2,1)S(1)}, bf16[8,4096]{1,0:T(8,128)(2,1)S(1)}, bf16[256,512]{1,0:T(8,128)(2,1)S(1)}, s32[8,128]{1,0:T(8,128)S(1)}) custom-call(bf16[32,4096]{1,0:T(8,128)(2,1)S(1)} %bitcast.35, bf16[27,64,64]{2,1,0:T(8,128)(2,1)S(1)} %copy-done.3, s32[27,1,32]{2,1,0:T(1,128)S(1)} %bitcast.36, ...), custom_call_target="tpu_custom_call" | custom-call | flops 1811939328 | bytes 1674624 | tf_op jit(solution)/shard_map/pallas_call | solution.py:49
  13.7 3.7 %all-to-all-done = bf16[16,8,512]{2,1,0:T(8,128)(2,1)S(1)} async-done(((bf16[16,8,512]{2,1,0:T(8,128)(2,1)}), bf16[16,8,512]{2,1,0:T(8,128)(2,1)S(1)}, u32[]{:S(2)}, u32[]{:S(2)}) %all-to-all-start) | async-done | bytes 131104 | tf_op jit(solution)/shard_map/all_to_all | solution.py:454
  17.4 0.0 copy-done
  17.4 0.0 copy-done.1
  17.5 0.6 shard_map.139
  18.1 2.6 %collective-permute-start = (bf16[8,5120]{1,0:T(8,128)(2,1)S(1)}, bf16[8,5120]{1,0:T(8,128)(2,1)S(1)}, u32[]{:S(2)}, u32[]{:S(2)}) collective-permute-start(bf16[8,5120]{1,0:T(8,128)(2,1)S(1)} %get-tuple-element.32), channel_id=1, source_target_pairs={{0,1},{1,2},{2,3},{4,5},{5,6},{6,7},{8,9},{9,10},{10,11},{12,13},{... | collective-permute-start | bytes 245768 | tf_op jit(solution)/shard_map/ppermute | solution.py:448
  20.7 1.3 %collective-permute-start.1 = (bf16[8,5120]{1,0:T(8,128)(2,1)S(1)}, bf16[8,5120]{1,0:T(8,128)(2,1)S(1)}, u32[]{:S(2)}, u32[]{:S(2)}) collective-permute-start(bf16[8,5120]{1,0:T(8,128)(2,1)S(1)} %get-tuple-element.33), channel_id=1, source_target_pairs={{1,0},{2,1},{3,2},{5,4},{6,5},{7,6},{9,8},{10,9},{11,10},{13,12},{... | collective-permute-start | bytes 245768 | tf_op jit(solution)/shard_map/ppermute | solution.py:448
  22.0 0.7 collective-permute-done.low_ref
  22.7 4.3 %collective-permute-done.1.high_ref = bf16[8,5120]{1,0:T(8,128)(2,1)S(1)} collective-permute-done((bf16[8,5120]{1,0:T(8,128)(2,1)S(1)}, bf16[8,5120]{1,0:T(8,128)(2,1)S(1)}, u32[]{:S(2)}, u32[]{:S(2)}) %collective-permute-start.1) | collective-permute-done | bytes 81952 | tf_op jit(solution)/shard_map/ppermute | solution.py:448
  27.0 0.3 shard_map.140
  27.3 1.3 %collective-permute-start.2 = (bf16[16,4096]{1,0:T(8,128)(2,1)S(1)}, bf16[16,4096]{1,0:T(8,128)(2,1)S(1)}, u32[]{:S(2)}, u32[]{:S(2)}) collective-permute-start(bf16[16,4096]{1,0:T(8,128)(2,1)S(1)} %get-tuple-element.36), channel_id=1, source_target_pairs={{0,4},{4,8},{8,12},{1,5},{5,9},{9,13},{2,6},{6,10},{10,14},{3,7},{... | collective-permute-start | bytes 393224 | tf_op jit(solution)/shard_map/ppermute | solution.py:448
  28.6 1.3 %collective-permute-start.3 = (bf16[16,4096]{1,0:T(8,128)(2,1)S(1)}, bf16[16,4096]{1,0:T(8,128)(2,1)S(1)}, u32[]{:S(2)}, u32[]{:S(2)}) collective-permute-start(bf16[16,4096]{1,0:T(8,128)(2,1)S(1)} %get-tuple-element.37), channel_id=1, source_target_pairs={{4,0},{8,4},{12,8},{5,1},{9,5},{13,9},{6,2},{10,6},{14,10},{7,3},{... | collective-permute-start | bytes 393224 | tf_op jit(solution)/shard_map/ppermute | solution.py:448
  29.9 0.0 collective-permute-done.2.below_ref
  29.9 2.7 %collective-permute-done.3.above_ref = bf16[16,4096]{1,0:T(8,128)(2,1)S(1)} collective-permute-done((bf16[16,4096]{1,0:T(8,128)(2,1)S(1)}, bf16[16,4096]{1,0:T(8,128)(2,1)S(1)}, u32[]{:S(2)}, u32[]{:S(2)}) %collective-permute-start.3) | collective-permute-done | bytes 131104 | tf_op jit(solution)/shard_map/ppermute | solution.py:448
  32.6 3.0 %shard_map.141 = (bf16[128,1408]{1,0:T(8,128)(2,1)}, bf16[6,6,32,384]{3,2,1,0:T(8,128)(2,1)S(1)}, f32[32,4096]{1,0:T(8,128)S(1)}, bf16[8,4096]{1,0:T(8,128)(2,1)S(1)}, bf16[8,4096]{1,0:T(8,128)(2,1)S(1)}) custom-call(bf16[32,4096]{1,0:T(8,128)(2,1)S(1)} %get-tuple-element.31.merged_ref, bf16[8,5120]{1,0:T(8,128)(2,1)S(1)} %collective-permute-done.low_ref, ...), custom_call_target="tpu_custom_call" | custom-call | flops 905969664 | bytes 3710336 | tf_op jit(solution)/shard_map/pallas_call | solution.py:49
  35.6 6.3 %all-to-all-start.1 = ((bf16[16,8,1408]{2,1,0:T(8,128)(2,1)}), bf16[16,8,1408]{2,1,0:T(8,128)(2,1)S(1)}, u32[]{:S(2)}, u32[]{:S(2)}) async-start(bf16[16,8,1408]{2,1,0:T(8,128)(2,1)} %bitcast.17), calls=%async_computation.1 | async-start | bytes 720896 | tf_op jit(solution)/shard_map/all_to_all | solution.py:454
  41.9 1.3 %collective-permute-start.4 = (bf16[8,4096]{1,0:T(8,128)(2,1)S(1)}, bf16[8,4096]{1,0:T(8,128)(2,1)S(1)}, u32[]{:S(2)}, u32[]{:S(2)}) collective-permute-start(bf16[8,4096]{1,0:T(8,128)(2,1)S(1)} %get-tuple-element.43), channel_id=1, source_target_pairs={{1,0},{2,1},{3,2},{5,4},{6,5},{7,6},{9,8},{10,9},{11,10},{13,12},{... | collective-permute-start | bytes 196616 | tf_op jit(solution)/shard_map/ppermute | solution.py:448
  43.2 4.5 %collective-permute-start.5 = (bf16[8,4096]{1,0:T(8,128)(2,1)S(1)}, bf16[8,4096]{1,0:T(8,128)(2,1)S(1)}, u32[]{:S(2)}, u32[]{:S(2)}) collective-permute-start(bf16[8,4096]{1,0:T(8,128)(2,1)S(1)} %get-tuple-element.44), channel_id=1, source_target_pairs={{0,1},{1,2},{2,3},{4,5},{5,6},{6,7},{8,9},{9,10},{10,11},{12,13},{... | collective-permute-start | bytes 196616 | tf_op jit(solution)/shard_map/ppermute | solution.py:448
  47.8 3.7 %collective-permute-done.4.next_ref = bf16[8,4096]{1,0:T(8,128)(2,1)S(1)} collective-permute-done((bf16[8,4096]{1,0:T(8,128)(2,1)S(1)}, bf16[8,4096]{1,0:T(8,128)(2,1)S(1)}, u32[]{:S(2)}, u32[]{:S(2)}) %collective-permute-start.4) | collective-permute-done | bytes 65568 | tf_op jit(solution)/shard_map/ppermute | solution.py:448
  51.5 0.0 collective-permute-done.5.prev_ref
  51.5 1.0 %shard_map.143 = (bf16[32,4096]{1,0:T(8,128)(2,1)}, bf16[128,512]{1,0:T(8,128)(2,1)S(1)}) custom-call(f32[32,4096]{1,0:T(8,128)S(1)} %get-tuple-element.42.part_ref, s32[8,128]{1,0:T(8,128)S(1)} %get-tuple-element.30.lists_ref, bf16[8,4096]{1,0:T(8,128)(2,1)S(1)} %collective-permute-done.4.next_ref, bf16[8,4096]{1,0:T(8,128)(2,1)S(1)} %collective-permute-done.5.prev_ref, ...), custom_call_target="tpu_custom_call" | custom-call | bytes 1183744 | tf_op jit(solution)/shard_map/pallas_call | solution.py:49
  52.5 1.5 %all-to-all-done.1 = bf16[16,8,1408]{2,1,0:T(8,128)(2,1)S(1)} async-done(((bf16[16,8,1408]{2,1,0:T(8,128)(2,1)}), bf16[16,8,1408]{2,1,0:T(8,128)(2,1)S(1)}, u32[]{:S(2)}, u32[]{:S(2)}) %all-to-all-start.1) | async-done | bytes 360480 | tf_op jit(solution)/shard_map/all_to_all | solution.py:454
  54.1 1.0 %shard_map.144 = bf16[128,1920]{1,0:T(8,128)(2,1)} custom-call(bf16[128,1408]{1,0:T(8,128)(2,1)S(1)} %bitcast.28, bf16[128,512]{1,0:T(8,128)(2,1)S(1)} %get-tuple-element.47.replies_ref), custom_call_target="tpu_custom_call" | custom-call | bytes 983040 | tf_op jit(solution)/shard_map/pallas_call | solution.py:49
  55.1 0.0 copy-start.4
  55.1 5.0 %all-to-all-start.2 = ((bf16[16,8,1920]{2,1,0:T(8,128)(2,1)}), bf16[16,8,1920]{2,1,0:T(8,128)(2,1)S(1)}, u32[]{:S(2)}, u32[]{:S(2)}) async-start(bf16[16,8,1920]{2,1,0:T(8,128)(2,1)} %bitcast.19), calls=%async_computation.2 | async-start | bytes 983040 | tf_op jit(solution)/shard_map/all_to_all | solution.py:454
  60.2 0.0 copy-done.4
  60.2 0.0 copy-start.2
  60.2 2.2 %shard_map.142 = bf16[32,4096]{1,0:T(8,128)(2,1)} custom-call(bf16[6,6,32,384]{3,2,1,0:T(8,128)(2,1)S(1)} %get-tuple-element.41.pad_ref, bf16[27,64,64]{2,1,0:T(8,128)(2,1)S(1)} %copy-done.4), custom_call_target="tpu_custom_call" | custom-call | flops 905969664 | bytes 1368064 | tf_op jit(solution)/shard_map/pallas_call | solution.py:49
  62.4 12.7 %all-to-all-done.2 = bf16[16,8,1920]{2,1,0:T(8,128)(2,1)S(1)} async-done(((bf16[16,8,1920]{2,1,0:T(8,128)(2,1)}), bf16[16,8,1920]{2,1,0:T(8,128)(2,1)S(1)}, u32[]{:S(2)}, u32[]{:S(2)}) %all-to-all-start.2) | async-done | bytes 491552 | tf_op jit(solution)/shard_map/all_to_all | solution.py:454
  75.1 0.0 copy-done.2
  75.1 1.4 %shard_map.145 = (f32[27,64,64]{2,1,0:T(8,128)}, f32[512,128]{1,0:T(8,128)}, bf16[64,1024]{1,0:T(8,128)(2,1)}) custom-call(bf16[128,1920]{1,0:T(8,128)(2,1)S(1)} %bitcast.27, s32[4,16]{1,0:T(4,128)S(1)} %bitcast.34), custom_call_target="tpu_custom_call" | custom-call | bytes 1327360 | tf_op jit(solution)/shard_map/pallas_call | solution.py:49
Async XLA Ops:
  0.6 9.5 %copy-start.5 = (bf16[1,1,32,4096]{3,2,1,0:T(8,128)(2,1)S(1)}, bf16[1,1,32,4096]{3,2,1,0:T(8,128)(2,1)}, u32[]{:S(2)}) copy-start(bf16[1,1,32,4096]{3,2,1,0:T(8,128)(2,1)} %param.19) | copy-start | bytes 786436
  2.7 7.4 %copy-start.6 = (s32[1,1,32,27]{2,1,3,0:T(1,128)S(1)}, s32[1,1,32,27]{2,1,3,0:T(1,128)}, u32[]{:S(2)}) copy-start(s32[1,1,32,27]{2,1,3,0:T(1,128)} %param.14) | copy-start | bytes 10372
  2.7 14.7 %all-to-all-start = ((bf16[16,8,512]{2,1,0:T(8,128)(2,1)}), bf16[16,8,512]{2,1,0:T(8,128)(2,1)S(1)}, u32[]{:S(2)}, u32[]{:S(2)}) async-start(bf16[16,8,512]{2,1,0:T(8,128)(2,1)} %bitcast.39), calls=%async_computation | async-start | bytes 262144 | tf_op jit(solution)/shard_map/all_to_all | solution.py:454
  10.1 0.7 copy-start.7
  10.8 1.0 %copy-start.3 = (bf16[27,64,64]{2,1,0:T(8,128)(2,1)S(1)}, bf16[27,64,64]{2,1,0:T(8,128)(2,1)}, u32[]{:S(2)}) copy-start(bf16[27,64,64]{2,1,0:T(8,128)(2,1)} %weight_ref.3) | copy-start | bytes 663556
  11.8 5.7 %copy-start = (bf16[8,128,64]{1,2,0:T(8,128)(2,1)S(1)}, bf16[8,128,64]{1,2,0:T(8,128)(2,1)}, u32[]{:S(2)}) copy-start(bf16[8,128,64]{1,2,0:T(8,128)(2,1)} %param.13) | copy-start | bytes 393220
  11.8 5.7 %copy-start.1 = (bf16[1,1,32,4096]{3,2,1,0:T(8,128)(2,1)S(1)}, bf16[1,1,32,4096]{3,2,1,0:T(8,128)(2,1)}, u32[]{:S(2)}) copy-start(bf16[1,1,32,4096]{3,2,1,0:T(8,128)(2,1)} %param.10) | copy-start | bytes 786436
  18.1 4.6 %collective-permute-start = (bf16[8,5120]{1,0:T(8,128)(2,1)S(1)}, bf16[8,5120]{1,0:T(8,128)(2,1)S(1)}, u32[]{:S(2)}, u32[]{:S(2)}) collective-permute-start(bf16[8,5120]{1,0:T(8,128)(2,1)S(1)} %get-tuple-element.32), channel_id=1, source_target_pairs={{0,1},{1,2},{2,3},{4,5},{5,6},{6,7},{8,9},{9,10},{10,11},{12,13},{... | collective-permute-start | bytes 245768 | tf_op jit(solution)/shard_map/ppermute | solution.py:448
  20.7 6.3 %collective-permute-start.1 = (bf16[8,5120]{1,0:T(8,128)(2,1)S(1)}, bf16[8,5120]{1,0:T(8,128)(2,1)S(1)}, u32[]{:S(2)}, u32[]{:S(2)}) collective-permute-start(bf16[8,5120]{1,0:T(8,128)(2,1)S(1)} %get-tuple-element.33), channel_id=1, source_target_pairs={{1,0},{2,1},{3,2},{5,4},{6,5},{7,6},{9,8},{10,9},{11,10},{13,12},{... | collective-permute-start | bytes 245768 | tf_op jit(solution)/shard_map/ppermute | solution.py:448
  27.3 2.6 %collective-permute-start.2 = (bf16[16,4096]{1,0:T(8,128)(2,1)S(1)}, bf16[16,4096]{1,0:T(8,128)(2,1)S(1)}, u32[]{:S(2)}, u32[]{:S(2)}) collective-permute-start(bf16[16,4096]{1,0:T(8,128)(2,1)S(1)} %get-tuple-element.36), channel_id=1, source_target_pairs={{0,4},{4,8},{8,12},{1,5},{5,9},{9,13},{2,6},{6,10},{10,14},{3,7},{... | collective-permute-start | bytes 393224 | tf_op jit(solution)/shard_map/ppermute | solution.py:448
  28.6 4.0 %collective-permute-start.3 = (bf16[16,4096]{1,0:T(8,128)(2,1)S(1)}, bf16[16,4096]{1,0:T(8,128)(2,1)S(1)}, u32[]{:S(2)}, u32[]{:S(2)}) collective-permute-start(bf16[16,4096]{1,0:T(8,128)(2,1)S(1)} %get-tuple-element.37), channel_id=1, source_target_pairs={{4,0},{8,4},{12,8},{5,1},{9,5},{13,9},{6,2},{10,6},{14,10},{7,3},{... | collective-permute-start | bytes 393224 | tf_op jit(solution)/shard_map/ppermute | solution.py:448
  35.6 18.5 %all-to-all-start.1 = ((bf16[16,8,1408]{2,1,0:T(8,128)(2,1)}), bf16[16,8,1408]{2,1,0:T(8,128)(2,1)S(1)}, u32[]{:S(2)}, u32[]{:S(2)}) async-start(bf16[16,8,1408]{2,1,0:T(8,128)(2,1)} %bitcast.17), calls=%async_computation.1 | async-start | bytes 720896 | tf_op jit(solution)/shard_map/all_to_all | solution.py:454
  41.9 9.6 %collective-permute-start.4 = (bf16[8,4096]{1,0:T(8,128)(2,1)S(1)}, bf16[8,4096]{1,0:T(8,128)(2,1)S(1)}, u32[]{:S(2)}, u32[]{:S(2)}) collective-permute-start(bf16[8,4096]{1,0:T(8,128)(2,1)S(1)} %get-tuple-element.43), channel_id=1, source_target_pairs={{1,0},{2,1},{3,2},{5,4},{6,5},{7,6},{9,8},{10,9},{11,10},{13,12},{... | collective-permute-start | bytes 196616 | tf_op jit(solution)/shard_map/ppermute | solution.py:448
  43.2 8.3 %collective-permute-start.5 = (bf16[8,4096]{1,0:T(8,128)(2,1)S(1)}, bf16[8,4096]{1,0:T(8,128)(2,1)S(1)}, u32[]{:S(2)}, u32[]{:S(2)}) collective-permute-start(bf16[8,4096]{1,0:T(8,128)(2,1)S(1)} %get-tuple-element.44), channel_id=1, source_target_pairs={{0,1},{1,2},{2,3},{4,5},{5,6},{6,7},{8,9},{9,10},{10,11},{12,13},{... | collective-permute-start | bytes 196616 | tf_op jit(solution)/shard_map/ppermute | solution.py:448
  55.1 5.1 %copy-start.4 = (bf16[27,64,64]{2,1,0:T(8,128)(2,1)S(1)}, bf16[27,64,64]{2,1,0:T(8,128)(2,1)}, u32[]{:S(2)}) copy-start(bf16[27,64,64]{2,1,0:T(8,128)(2,1)} %weight_ref.3) | copy-start | bytes 663556
  55.1 20.0 %all-to-all-start.2 = ((bf16[16,8,1920]{2,1,0:T(8,128)(2,1)}), bf16[16,8,1920]{2,1,0:T(8,128)(2,1)S(1)}, u32[]{:S(2)}, u32[]{:S(2)}) async-start(bf16[16,8,1920]{2,1,0:T(8,128)(2,1)} %bitcast.19), calls=%async_computation.2 | async-start | bytes 983040 | tf_op jit(solution)/shard_map/all_to_all | solution.py:454
  60.2 15.0 %copy-start.2 = (s32[1,1,16,4]{2,3,1,0:T(4,128)S(1)}, s32[1,1,16,4]{2,3,1,0:T(4,128)}, u32[]{:S(2)}) copy-start(s32[1,1,16,4]{2,3,1,0:T(4,128)} %param.18) | copy-start | bytes 772

commit v5 on v4

--- a/solution.py
+++ b/solution.py
@@ -74,13 +74,15 @@
     capacity, devices = sends_ref.shape
     count, width = items_ref.shape
     half = width // 2
-    index = send_index(sends_ref[...], 2 * capacity)
-    lanes = index.shape[1]
-    odd = iota((count, lanes), 1) % 2
-    named = iota((count, lanes), 0) == index
-    total = dot_tn(ones_where(named & (odd == 0)), items_ref[:, :half])
-    total += dot_tn(ones_where(named & (odd == 1)), items_ref[:, half:])
-    out_ref[...] = total.astype(BF)
+    group = 2 * capacity
+    lanes = devices * group
+    spread = ones_where(iota((lanes, devices), 0) // group == iota((lanes, devices), 1))
+    slot = iota((lanes, capacity), 0) % group // 2
+    values = dot_nt(spread, sends_ref[...].astype(F32).astype(BF))
+    item = jnp.sum(jnp.where(slot == iota((lanes, capacity), 1), values, 0.0), axis=1, keepdims=True).astype(I32)
+    place = jnp.where(item < count, item + iota((lanes, 1), 0) % 2 * count, -1)
+    chosen = ones_where(iota((lanes, 2 * count), 1) == place)
+    out_ref[...] = dot(chosen, jnp.concatenate([items_ref[:, :half], items_ref[:, half:]], axis=0)).astype(BF)
 
 
 def merge(received_ref, slots, up_ref, fine_ref, merged_ref, parents_ref):
@@ -108,8 +110,19 @@
 
 
 def pick_rows(lists, rows):
-    place = iota((rows.shape[0], lists.shape[1]), 0)
-    return [dot_tn(ones_where(place == lists[w : w + 1]), rows) for w in (0, 1)]
+    return [dot_tn(ones_where(iota((rows.shape[0], one.shape[1]), 0) == one), rows) for one in lists]
+
+
+GX, GY = (0, 1)
+
+
+def by_pair(lists_ref, axis, of_next, of_prev):
+    odd = jnp.broadcast_to(lists_ref[5:6, axis : axis + 1], of_next.shape) == 1
+    return jnp.where(odd, of_prev, of_next), jnp.where(odd, of_next, of_prev)
+
+
+def from_pairs(lists_ref, axis, even_ref, odd_ref):
+    return by_pair(lists_ref, axis, even_ref[...].astype(F32), odd_ref[...].astype(F32))
 
 
 def stack_rows(*parts):
@@ -128,12 +141,15 @@
     return lists_ref[4:5, :bricks]
 
 
-def cross_body(merged_ref, low_ref, high_ref, lists_ref, low_grad_ref, high_grad_ref, a_ref, b_ref):
+def cross_body(merged_ref, even_ref, odd_ref, lists_ref, low_grad_ref, high_grad_ref, a_ref, b_ref):
     face, width = low_grad_ref.shape
-    rows = jnp.concatenate([merged_ref[...], stack_rows(low_ref[:, :width], high_ref[:, :width])], axis=0)
-    first, second = pick_rows(crosses_of(lists_ref, face), rows)
-    a_ref[...] = stack_rows(first, high_grad_ref[...])
-    b_ref[...] = stack_rows(second, low_grad_ref[...])
+    high, low = from_pairs(lists_ref, GY, even_ref, odd_ref)
+    rows = jnp.concatenate([merged_ref[...], stack_rows(low[:, :width], high[:, :width])], axis=0)
+    lists = crosses_of(lists_ref, face)
+    picked = pick_rows(by_pair(lists_ref, GX, lists[0:1], lists[1:2]), rows)
+    grads = from_pairs(lists_ref, GX, high_grad_ref, low_grad_ref)
+    a_ref[...] = stack_rows(picked[0], grads[0])
+    b_ref[...] = stack_rows(picked[1], grads[1])
 
 
 def build_bands(weight_ref, band_ref):
@@ -194,9 +210,11 @@
 
 
 def table_grad_body(
-    cot_ref, weight_ref, near_ref, lists_ref, ext_ref, low_ref, high_ref, turned_ref, again_ref, band_ref, pad_ref
+    cot_ref, weight_ref, near_ref, lists_ref, parity_ref,
+    ext_ref, low_ref, high_ref, turned_ref, mains_ref, ends_ref, again_ref, band_ref, pad_ref,
 ):
     again_ref[...] = lists_ref[...]
+    again_ref[5:6] = parity_ref[...]
     bricks = cot_ref.shape[0]
     face = low_ref.shape[0]
     start = ext_ref.shape[0]
@@ -244,6 +262,19 @@
             ext_ref[:, at : at + RUN] = total[:start]
             low_ref[:, at : at + RUN] = total[start : start + face].astype(BF)
             high_ref[:, at : at + RUN] = total[start + face :].astype(BF)
+    make_choosers(near_ref, rows, mains_ref, ends_ref)
+
+
+def make_choosers(near_ref, rows, mains_ref, ends_ref):
+    bricks = mains_ref.shape[1]
+    near = jnp.concatenate([near_ref[o] for o in range(27)] + [jnp.zeros((5, bricks), I32)], axis=0)
+    near = near.astype(F32).T.astype(I32)
+    place = iota((bricks, rows), 1)
+    pair_place = iota((bricks, 2 * rows), 1)
+    for d in range(9):
+        down, straight, up = (near[:, 3 * d + z : 3 * d + z + 1] for z in range(3))
+        mains_ref[d] = ones_where(place == straight)
+        ends_ref[d] = ones_where(pair_place == jnp.where(pair_place < rows, up, down + rows))
 
 
 def first_body(
@@ -266,21 +297,22 @@
 
 
 def weight_grad_body(
-    merged_ref, low_ref, high_ref, below_ref, above_ref, turned_ref, near_ref, lists_ref, ext_ref, parents_ref,
-    sums_ref, pad_ref, part_ref, to_next_ref, to_prev_ref, table_ref,
+    merged_ref, even_side_ref, odd_side_ref, even_cross_ref, odd_cross_ref, turned_ref, mains_ref, ends_ref, lists_ref,
+    ext_ref, parents_ref, sums_ref, pad_ref, part_ref, to_even_ref, to_odd_ref, table_ref,
 ):
     bricks, width = merged_ref.shape
-    face = low_ref.shape[0]
+    face = even_side_ref.shape[0]
     rows = bricks + 4 * face
-    below = below_ref[...].astype(F32)
-    above = above_ref[...].astype(F32)
+    high, low = from_pairs(lists_ref, GY, even_side_ref, odd_side_ref)
+    above, below = from_pairs(lists_ref, GX, even_cross_ref, odd_cross_ref)
     table_ref[:bricks] = merged_ref[...]
-    table_ref[bricks:] = stack_rows(low_ref[:, :width], high_ref[:, :width], below[:face], above[:face])
+    table_ref[bricks:] = stack_rows(low[:, :width], high[:, :width], below[:face], above[:face])
     total = add_rows(ext_ref[...], crosses_of(lists_ref, face), above[face:], below[face:])
     part_ref[...] = total[:bricks]
-    to_prev_ref[...] = total[bricks : bricks + face].astype(BF)
-    to_next_ref[...] = total[bricks + face :].astype(BF)
-    side_parents = stack_lanes(stack_rows(low_ref[:, width:], high_ref[:, width:]), parents_ref.shape[1])
+    to_even, to_odd = by_pair(lists_ref, GY, total[bricks + face :], total[bricks : bricks + face])
+    to_even_ref[...] = to_even.astype(BF)
+    to_odd_ref[...] = to_odd.astype(BF)
+    side_parents = stack_lanes(stack_rows(low[:, width:], high[:, width:]), parents_ref.shape[1])
     grads = [stack_parities(total[:bricks].astype(BF)), stack_parities(total[bricks:].astype(BF))]
     up_sum = dot_tn(jnp.concatenate(grads, axis=0), jnp.concatenate([parents_ref[...], side_parents], axis=0))
     coarse = up_sum.shape[1]
@@ -288,38 +320,23 @@
     parts = up_sum.shape[0] // count
     for q in range(parts):
         sums_ref[:, q * coarse : (q + 1) * coarse] = up_sum[q * count : (q + 1) * count].astype(BF)
-    near = jnp.concatenate([near_ref[o] for o in range(27)] + [jnp.zeros((5, bricks), I32)], axis=0)
-    near = near.astype(F32).T.astype(I32)
-
-    def one_of(dx, dy, dz):
-        o = offset_of(dx, dy, dz)
-        return near[:, o : o + 1]
-
-    place = iota((bricks, rows), 1)
-    pair_place = iota((bricks, 2 * rows), 1)
     lower_half = iota((rows, 2 * C), 1) < C
     zero = jnp.zeros((rows, 2 * C), BF)
-    cache = {}
     for x in range(4):
         for y in range(4):
             places = [(X, Y, dx, dy) for X, dx in options(x) for Y, dy in options(y)]
-            for _, _, dx, dy in places:
-                if (dx, dy) not in cache:
-                    main = ones_where(place == one_of(dx, dy, 0))
-                    ends = jnp.where(pair_place < rows, one_of(dx, dy, 1), one_of(dx, dy, -1) + rows)
-                    cache[dx, dy] = (main, ones_where(pair_place == ends))
             at = (x * 4 + y) * RUN
             columns = table_ref[:, at : at + RUN]
             first = jnp.where(lower_half, columns[:, : 2 * C], zero)
             second = jnp.where(lower_half, zero, columns[:, 2 * C :])
-            ends = jnp.concatenate([cache[dx, dy][1] for _, _, dx, dy in places], axis=0)
+            ends = jnp.concatenate([ends_ref[3 * dx + dy + 4] for _, _, dx, dy in places], axis=0)
             halo = dot(ends, jnp.concatenate([first, second], axis=0)).astype(BF)
             for i, (X, Y, _, _) in enumerate(places):
                 pad_ref[X, Y, :, RUN:] = halo[i * bricks : (i + 1) * bricks]
             pad_ref[x + 1, y + 1, :, :RUN] = columns[:bricks]
             moved = [p for p in places if p[2:] != (0, 0)]
             if moved:
-                main = jnp.concatenate([cache[dx, dy][0] for _, _, dx, dy in moved], axis=0)
+                main = jnp.concatenate([mains_ref[3 * dx + dy + 4] for _, _, dx, dy in moved], axis=0)
                 got = dot(main, columns).astype(BF)
                 for i, (X, Y, _, _) in enumerate(moved):
                     pad_ref[X, Y, :, :RUN] = got[i * bricks : (i + 1) * bricks]
@@ -374,15 +391,17 @@
     face = a_ref.shape[0]
     parents = merge(received_ref, slots_of(lists_ref, bricks), up_ref, fine_ref, merged_ref, parents_ref)
     lists = sides_of(lists_ref, face)
+    lists = by_pair(lists_ref, GY, lists[0:1], lists[1:2])
     for out_ref, rows, owners in zip((a_ref, b_ref), pick_rows(lists, merged_ref[...]), pick_rows(lists, parents)):
         out_ref[:, :width] = rows.astype(BF)
         out_ref[:, width:] = owners.astype(BF)
 
 
-def fine_grad_body(part_ref, lists_ref, next_ref, prev_ref, up_ref, grad_ref, replies_ref):
+def fine_grad_body(part_ref, lists_ref, even_ref, odd_ref, up_ref, grad_ref, replies_ref):
     bricks = part_ref.shape[0]
-    face = next_ref.shape[0]
-    total = add_rows(part_ref[...], sides_of(lists_ref, face), next_ref[...], prev_ref[...])
+    face = even_ref.shape[0]
+    from_next, from_prev = from_pairs(lists_ref, GY, even_ref, odd_ref)
+    total = add_rows(part_ref[...], sides_of(lists_ref, face), from_next, from_prev)
     grad_ref[...] = total.astype(BF)
     items = dot(stack_parities(grad_ref[...]), up_ref[...]).astype(BF)
     items = jnp.concatenate([items[v * bricks : (v + 1) * bricks] for v in range(8)], axis=1)
@@ -397,15 +416,15 @@
         replies_ref[:, j * half : (j + 1) * half] = rows.astype(BF)
 
 
-def share_body(sums_ref, replies_ref, out_ref, devices):
-    count, item_lanes = replies_ref.shape
+def share_body(sums_ref, lists_ref, out_ref, again_ref, devices):
+    again_ref[...] = lists_ref[...]
+    count = sums_ref.shape[0]
     share = count // devices
     same = iota((count, count), 0) % share == iota((count, count), 1) % share
-    out_ref[:, :item_lanes] = replies_ref[...]
-    out_ref[:, item_lanes:] = dot(ones_where(same), sums_ref[...]).astype(BF)
-
-
-def coarse_grad(back_ref, sends_ref, out_ref):
+    out_ref[...] = dot(ones_where(same), sums_ref[...]).astype(BF)
+
+
+def coarse_grad_body(back_ref, sends_ref, out_ref):
     capacity, devices = sends_ref.shape
     count, item_width = out_ref.shape
     half = item_width // 2
@@ -423,12 +442,11 @@
         out_ref[:, h * half : (h + 1) * half] = total.astype(BF)
 
 
-def last_body(back_ref, sends_ref, conv_ref, up_ref, out_ref, scale):
-    coarse_grad(back_ref, sends_ref, out_ref)
-    count, width = back_ref.shape
+def last_body(back_ref, conv_ref, up_ref, scale):
+    count = back_ref.shape[0]
     coarse = up_ref.shape[1]
     parts = up_ref.shape[0] // count
-    at = width - 14 * C - parts * coarse
+    at = 0
     for q in range(parts):
         up_ref[q * count : (q + 1) * count] = back_ref[:, at : at + coarse].astype(F32) * scale
         at += coarse
@@ -442,10 +460,15 @@
                     conv_ref[o] = turned[s * C : (s + 1) * C, h * C : (h + 1) * C]
 
 
-def passed_along(value, axis, steps):
+def swap_pairs(to_even, to_odd, axis):
     count = lax.axis_size(axis)
-    initial, last = (max(0, -steps), min(count, count - steps))
-    return lax.ppermute(value, axis, [(source, source + steps) for source in range(initial, last)])
+
+    def swap(value, first):
+        lower = range(first, count - 1, 2)
+        return lax.ppermute(value, axis, [(i, i + 1) for i in lower] + [(i + 1, i) for i in lower])
+
+    from_odd = swap(to_odd, 1)
+    return swap(to_even, 0), from_odd
 
 
 def trade_rows(values, devices):
@@ -494,45 +517,47 @@
         in_hbm=True,
     )
     received = trade_rows(outgoing, devices)
-    ext_grad, low_cross, high_cross, turned, lists = call(
+    lane = jnp.arange(128, dtype=I32)[None]
+    parity = jnp.where(lane == GX, lax.axis_index("gx") % 2, lax.axis_index("gy") % 2).astype(I32)
+    table_rows = start + 2 * face
+    ext_grad, low_cross, high_cross, turned, mains, ends, lists = call(
         table_grad_body,
-        [shape((start, width), F32), face_rows, face_rows, shape((RUN, 16 * bricks)), lists_shape],
-        cot, conv_weight, near, lists,
+        [
+            shape((start, width), F32), face_rows, face_rows, shape((RUN, 16 * bricks)),
+            shape((9, bricks, table_rows)), shape((9, bricks, 2 * table_rows)), lists_shape,
+        ],
+        cot, conv_weight, near, lists, parity,
         scratch=[band, pltpu.VMEM((6, 6, bricks, WIDE), F32)], flops=2 * conv_flops,
     )
-    merged, parents, to_next, to_prev = call(
+    merged, parents, to_even, to_odd = call(
         merge_body, [rows, shape((8 * bricks, coarse)), faces_and_parents, faces_and_parents],
         received, up_turned, fine, lists,
     )
-    low_side = passed_along(to_next, "gy", 1)
-    high_side = passed_along(to_prev, "gy", -1)
-    to_next, to_prev = call(
-        cross_body, [two_faces, two_faces], merged, low_side, high_side, lists, low_cross, high_cross
-    )
-    below = passed_along(to_next, "gx", 1)
-    above = passed_along(to_prev, "gx", -1)
-    sums, pad, fine_part, to_next, to_prev = call(
+    sides = swap_pairs(to_even, to_odd, "gy")
+    to_even, to_odd = call(cross_body, [two_faces, two_faces], merged, *sides, lists, low_cross, high_cross)
+    crosses = swap_pairs(to_even, to_odd, "gx")
+    sums, pad, fine_part, to_even, to_odd = call(
         weight_grad_body,
         [shape((count, sums_width)), shape((6, 6, bricks, WIDE)), shape((bricks, width), F32), face_rows, face_rows],
-        merged, low_side, high_side, below, above, turned, near, lists, ext_grad, parents,
-        scratch=[pltpu.VMEM((bricks + 4 * face, width), BF)], flops=conv_flops,
+        merged, *sides, *crosses, turned, mains, ends, lists, ext_grad, parents,
+        scratch=[pltpu.VMEM((table_rows, width), BF)], flops=conv_flops,
     )
     sums = trade_rows(sums, devices)
-    grad_prev = passed_along(to_next, "gy", 1)
-    grad_next = passed_along(to_prev, "gy", -1)
+    side_grads = swap_pairs(to_even, to_odd, "gy")
+    sums, lists = call(
+        functools.partial(share_body, devices=devices), [shape((count, sums_width)), lists_shape], sums, lists
+    )
+    sums = trade_rows(sums, devices)
     grad_fine, replies = call(
-        fine_grad_body, [rows, shape((count, item_lanes))], fine_part, lists, grad_next, grad_prev, up_turned
-    )
+        fine_grad_body, [rows, shape((count, item_lanes))], fine_part, lists, *side_grads, up_turned
+    )
+    replies = trade_rows(replies, devices)
     (output,) = call(conv_body, [rows], pad, conv_weight, scratch=[band], flops=conv_flops)
-    (back,) = call(
-        functools.partial(share_body, devices=devices), [shape((count, item_lanes + sums_width))], sums, replies
-    )
-    back = trade_rows(back, devices)
     scale = 1.0 / math.sqrt(64 * bricks * devices)
-    grad_conv, grad_up, coarse_grad = call(
-        functools.partial(last_body, scale=scale),
-        [shape((27, C, C), F32), shape((8 * C, coarse), F32), shape((item_count, item_width))], back, sends,
-    )
+    grad_conv, grad_up = call(
+        functools.partial(last_body, scale=scale), [shape((27, C, C), F32), shape((8 * C, coarse), F32)], sums
+    )
+    (coarse_grad,) = call(coarse_grad_body, [shape((item_count, item_width))], replies, sends)
     return (
         output.reshape(1, 1, bricks, width),
         grad_fine.reshape(1, 1, bricks, width),

time: 77.2 us -> 80.4 us (1.041)
  blocking collectives: 0 us -> 10.6 us
  starting transfers between devices: 31 us -> 26.2 us
  waiting for transfers between devices: 29.5 us -> 25.9 us
  Pallas kernels: 13.5 us -> 14.7 us
    all_to_all x0 -> x1, blocking collectives: none -> 10.6 us  [trade_rows(): lax.all_to_all(grid_view, ('gx', 'gy'), split_axis=0, concat_axis=0, tile...]
    ppermute x6, waiting for transfers between devices: 11.5 us -> 3.8 us  [swap(): lax.ppermute(value, axis, [(i, i + 1) for i in lower] + [(i + 1, i) for i...]
    ppermute x6, starting transfers between devices: 12.3 us -> 4.71 us  [swap(): lax.ppermute(value, axis, [(i, i + 1) for i in lower] + [(i + 1, i) for i...]
    all_to_all x3, waiting for transfers between devices: 18 us -> 22.1 us  [trade_rows(): lax.all_to_all(grid_view, ('gx', 'gy'), split_axis=0, concat_axis=0, tile...]
    all_to_all x3, starting transfers between devices: 18.7 us -> 21.5 us  [trade_rows(): lax.all_to_all(grid_view, ('gx', 'gy'), split_axis=0, concat_axis=0, tile...]
    pallas_call x9 -> x10, Pallas kernels: 13.5 us -> 14.7 us  [call(): pl.pallas_call(body, out_shape=tuple(outs), in_specs=[pl.BlockSpec(memory...]
    unnamed x16 -> x18, local copies, waits for them, and re-layouts: 1.7 us -> 1.65 us
  transfers between devices with their start and end apart: 9 -> 9, of which waited for: 7 -> 5; matrix products, arithmetic and copies ran while one was open for 0% -> 0% of each run, Pallas kernels for 7% -> 8%
where the time goes in v5:
time: 80.4 us; the launch traced here: 79.8 us
  starting transfers between devices  26.2 us (33%)
  waiting for transfers between devices  25.9 us (32%)
  Pallas kernels  14.7 us (18%)
  blocking collectives  10.6 us (13%)
  local copies, waits for them, and re-layouts  1.65 us (2%)
  between operations  0.81 us (1%)
    all_to_all x3, waiting for transfers between devices, trade_rows(): lax.all_to_all(grid_view, ('gx', 'gy'), split_axis=0, concat_axis=0, tile...  22.1 us
    all_to_all x3, starting transfers between devices, trade_rows(): lax.all_to_all(grid_view, ('gx', 'gy'), split_axis=0, concat_axis=0, tile...  21.5 us
    pallas_call x10, Pallas kernels, call(): pl.pallas_call(body, out_shape=tuple(outs), in_specs=[pl.BlockSpec(memory...  14.7 us
    all_to_all x1, blocking collectives, trade_rows(): lax.all_to_all(grid_view, ('gx', 'gy'), split_axis=0, concat_axis=0, tile...  10.6 us
    ppermute x6, starting transfers between devices, swap(): lax.ppermute(value, axis, [(i, i + 1) for i in lower] + [(i + 1, i) for i...  4.71 us
    ppermute x6, waiting for transfers between devices, swap(): lax.ppermute(value, axis, [(i, i + 1) for i in lower] + [(i + 1, i) for i...  3.8 us
    unnamed x18, local copies, waits for them, and re-layouts  1.65 us
  transfers between devices with their start and end apart: 9, of which 5 were waited for; matrix products, arithmetic and copies ran while one was open for 0% of the time, Pallas kernels for 8%

profile of v5, /device:TPU:0, one launch (start us, length us, event | category | flops | bytes accessed | tf_op | source)
XLA Modules:
  0.0 79.8 jit_solution(11784086987638141412)
XLA Ops:
  0.6 0.0 copy-start.3
  0.6 2.0 %shard_map.137 = (bf16[128,512]{1,0:T(8,128)(2,1)}, s32[8,128]{1,0:T(8,128)}) custom-call(s32[4,16]{1,0:T(4,128)} %bitcast.37, bf16[64,1024]{1,0:T(8,128)(2,1)} %bitcast.41, s32[2,8]{1,0:T(2,128)} %bitcast.44, s32[2,8]{1,0:T(2,128)} %bitcast.45, s32[1,32]{1,0:T(1,128)} %bitcast.46), custom_call_target="tpu_custom_call" | custom-call | bytes 266752 | tf_op jit(solution)/shard_map/pallas_call | solution.py:49
  2.7 7.4 %all-to-all-start = ((bf16[16,8,512]{2,1,0:T(8,128)(2,1)}), bf16[16,8,512]{2,1,0:T(8,128)(2,1)S(1)}, u32[]{:S(2)}, u32[]{:S(2)}) async-start(bf16[16,8,512]{2,1,0:T(8,128)(2,1)} %bitcast.42), calls=%async_computation | async-start | bytes 262144 | tf_op jit(solution)/shard_map/all_to_all | solution.py:477
  10.1 0.0 copy-start.5
  10.1 0.0 copy-start.6
  10.1 0.0 copy-done.3
  10.1 0.7 copy-done.5
  10.8 0.0 copy-done.6
  10.8 0.0 copy-start.4
  10.8 0.9 %copy-done.4 = bf16[1,1,32,4096]{3,2,1,0:T(8,128)(2,1)S(1)} copy-done((bf16[1,1,32,4096]{3,2,1,0:T(8,128)(2,1)S(1)}, bf16[1,1,32,4096]{3,2,1,0:T(8,128)(2,1)}, u32[]{:S(2)}) %copy-start.4) | copy-done | bytes 262168
  11.7 0.0 copy-start
  11.7 0.0 copy-start.1
  11.7 1.9 %shard_map.138 = (f32[48,4096]{1,0:T(8,128)S(1)}, bf16[8,4096]{1,0:T(8,128)(2,1)S(1)}, bf16[8,4096]{1,0:T(8,128)(2,1)S(1)}, bf16[256,512]{1,0:T(8,128)(2,1)S(1)}...) custom-call(bf16[32,4096]{1,0:T(8,128)(2,1)S(1)} %bitcast.39, ...), custom_call_target="tpu_custom_call" | custom-call | flops 1811939328 | bytes 1785728 | tf_op jit(solution)/shard_map/pallas_call | solution.py:49
  13.7 0.0 copy-start.7
  13.7 3.7 %all-to-all-done = bf16[16,8,512]{2,1,0:T(8,128)(2,1)S(1)} async-done(((bf16[16,8,512]{2,1,0:T(8,128)(2,1)}), bf16[16,8,512]{2,1,0:T(8,128)(2,1)S(1)}, u32[]{:S(2)}, u32[]{:S(2)}) %all-to-all-start) | async-done | bytes 131104 | tf_op jit(solution)/shard_map/all_to_all | solution.py:477
  17.4 0.0 copy-done
  17.4 0.0 copy-done.1
  17.4 0.6 shard_map.139
  18.0 0.0 copy-done.7
  18.1 0.7 collective-permute-start
  18.8 0.7 collective-permute-start.1
  19.4 3.1 %collective-permute-done.even_ref.even_side_ref = bf16[8,5120]{1,0:T(8,128)(2,1)S(1)} collective-permute-done((bf16[8,5120]{1,0:T(8,128)(2,1)S(1)}, bf16[8,5120]{1,0:T(8,128)(2,1)S(1)}, u32[]{:S(2)}, u32[]{:S(2)}) %collective-permute-start) | collective-permute-done | bytes 81952 | tf_op jit(solution)/shard_map/ppermute | solution.py:468
  22.6 0.0 collective-permute-done.1.odd_ref.odd_side_ref
  22.6 0.0 copy-start.8
  22.6 0.4 shard_map.140
  22.9 0.1 collective-permute-start.2
  23.0 0.7 collective-permute-start.3
  23.7 0.7 collective-permute-done.2.even_cross_ref
  24.4 0.0 collective-permute-done.3.odd_cross_ref
  24.4 0.0 copy-done.8
  24.4 3.1 %shard_map.141 = (bf16[128,1408]{1,0:T(8,128)(2,1)}, bf16[6,6,32,384]{3,2,1,0:T(8,128)(2,1)S(1)}, f32[32,4096]{1,0:T(8,128)S(1)}, bf16[8,4096]{1,0:T(8,128)(2,1)S(1)}, bf16[8,4096]{1,0:T(8,128)(2,1)S(1)}) custom-call(bf16[32,4096]{1,0:T(8,128)(2,1)S(1)} %get-tuple-element.34.merged_ref, bf16[8,5120]{1,0:T(8,128)(2,1)S(1)} %collective-permute-done.even_ref.even_side_ref, ...), custom_call_target="tpu_custom_call" | custom-call | flops 905969664 | bytes 3817472 | tf_op jit(solution)/shard_map/pallas_call | solution.py:49
  27.5 10.6 %all-to-all-start.1 = ((bf16[16,8,1408]{2,1,0:T(8,128)(2,1)}), bf16[16,8,1408]{2,1,0:T(8,128)(2,1)S(1)}, u32[]{:S(2)}, u32[]{:S(2)}) async-start(bf16[16,8,1408]{2,1,0:T(8,128)(2,1)} %bitcast.15), calls=%async_computation.1 | async-start | bytes 720896 | tf_op jit(solution)/shard_map/all_to_all | solution.py:477
  38.1 1.9 %collective-permute-start.4 = (bf16[8,4096]{1,0:T(8,128)(2,1)S(1)}, bf16[8,4096]{1,0:T(8,128)(2,1)S(1)}, u32[]{:S(2)}, u32[]{:S(2)}) collective-permute-start(bf16[8,4096]{1,0:T(8,128)(2,1)S(1)} %get-tuple-element.50), channel_id=1, source_target_pairs={{0,1},{2,3},{1,0},{3,2},{4,5},{6,7},{5,4},{7,6},{8,9},{10,11},{9,8... | collective-permute-start | bytes 196616 | tf_op jit(solution)/shard_map/ppermute | solution.py:468
  40.0 0.7 collective-permute-start.5
  40.7 9.6 %all-to-all-done.1 = bf16[16,8,1408]{2,1,0:T(8,128)(2,1)S(1)} async-done(((bf16[16,8,1408]{2,1,0:T(8,128)(2,1)}), bf16[16,8,1408]{2,1,0:T(8,128)(2,1)S(1)}, u32[]{:S(2)}, u32[]{:S(2)}) %all-to-all-start.1) | async-done | bytes 360480 | tf_op jit(solution)/shard_map/all_to_all | solution.py:477
  50.3 1.0 %shard_map.143 = (bf16[128,1408]{1,0:T(8,128)(2,1)}, s32[8,128]{1,0:T(8,128)S(1)}) custom-call(bf16[128,1408]{1,0:T(8,128)(2,1)S(1)} %bitcast.29, s32[8,128]{1,0:T(8,128)S(1)} %get-tuple-element.33.lists_ref), custom_call_target="tpu_custom_call" | custom-call | bytes 729088 | tf_op jit(solution)/shard_map/pallas_call | solution.py:49
  51.2 0.0 collective-permute-done.4.even_ref
  51.3 0.0 collective-permute-done.5.odd_ref
  51.3 1.1 %shard_map.144 = (bf16[32,4096]{1,0:T(8,128)(2,1)}, bf16[128,512]{1,0:T(8,128)(2,1)S(1)}) custom-call(f32[32,4096]{1,0:T(8,128)S(1)} %get-tuple-element.47.part_ref, s32[8,128]{1,0:T(8,128)S(1)} %get-tuple-element.49.lists_ref, bf16[8,4096]{1,0:T(8,128)(2,1)S(1)} %collective-permute-done.4.even_ref, bf16[8,4096]{1,0:T(8,128)(2,1)S(1)} %collective-permute-done.5.odd_ref, ...), custom_call_target="tpu_custom_call" | custom-call | bytes 1183744 | tf_op jit(solution)/shard_map/pallas_call | solution.py:49
  52.4 10.6 %all_to_all.20 = bf16[16,8,512]{2,1,0:T(8,128)(2,1)S(1)} all-to-all(bf16[16,8,512]{2,1,0:T(8,128)(2,1)S(1)} %bitcast.36), channel_id=1, replica_groups=mesh['groups'=2,'gx'=4,'gy'=4] {'gx','gy'}, dimensions={0} | all-to-all | bytes 262144 | tf_op jit(solution)/shard_map/all_to_all | solution.py:477
  62.9 3.5 %all-to-all-start.3 = ((bf16[16,8,1408]{2,1,0:T(8,128)(2,1)}), bf16[16,8,1408]{2,1,0:T(8,128)(2,1)S(1)}, u32[]{:S(2)}, u32[]{:S(2)}) async-start(bf16[16,8,1408]{2,1,0:T(8,128)(2,1)} %bitcast.23), calls=%async_computation.3 | async-start | bytes 720896 | tf_op jit(solution)/shard_map/all_to_all | solution.py:477
  66.5 0.0 copy-start.2
  66.5 2.2 %shard_map.142 = bf16[32,4096]{1,0:T(8,128)(2,1)} custom-call(bf16[6,6,32,384]{3,2,1,0:T(8,128)(2,1)S(1)} %get-tuple-element.46.pad_ref, bf16[27,64,64]{2,1,0:T(8,128)(2,1)S(1)} %copy-done.3), custom_call_target="tpu_custom_call" | custom-call | flops 905969664 | bytes 1368064 | tf_op jit(solution)/shard_map/pallas_call | solution.py:49
  68.7 0.0 copy-done.2
  68.7 1.1 %shard_map.145 = bf16[64,1024]{1,0:T(8,128)(2,1)} custom-call(bf16[128,512]{1,0:T(8,128)(2,1)S(1)} %bitcast.31, s32[4,16]{1,0:T(4,128)S(1)} %bitcast.38), custom_call_target="tpu_custom_call" | custom-call | bytes 262400 | tf_op jit(solution)/shard_map/pallas_call | solution.py:49
  69.8 8.8 %all-to-all-done.3 = bf16[16,8,1408]{2,1,0:T(8,128)(2,1)S(1)} async-done(((bf16[16,8,1408]{2,1,0:T(8,128)(2,1)}), bf16[16,8,1408]{2,1,0:T(8,128)(2,1)S(1)}, u32[]{:S(2)}, u32[]{:S(2)}) %all-to-all-start.3) | async-done | bytes 360480 | tf_op jit(solution)/shard_map/all_to_all | solution.py:477
  78.6 1.2 %shard_map.146 = (f32[27,64,64]{2,1,0:T(8,128)}, f32[512,128]{1,0:T(8,128)}) custom-call(bf16[128,1408]{1,0:T(8,128)(2,1)S(1)} %bitcast.30), custom_call_target="tpu_custom_call" | custom-call | bytes 1064960 | tf_op jit(solution)/shard_map/pallas_call | solution.py:49
  (1 shorter events, 0.0 us)
Async XLA Ops:
  0.6 9.5 %copy-start.3 = (bf16[27,64,64]{2,1,0:T(8,128)(2,1)S(1)}, bf16[27,64,64]{2,1,0:T(8,128)(2,1)}, u32[]{:S(2)}) copy-start(bf16[27,64,64]{2,1,0:T(8,128)(2,1)} %weight_ref.3) | copy-start | bytes 663556
  2.7 14.7 %all-to-all-start = ((bf16[16,8,512]{2,1,0:T(8,128)(2,1)}), bf16[16,8,512]{2,1,0:T(8,128)(2,1)S(1)}, u32[]{:S(2)}, u32[]{:S(2)}) async-start(bf16[16,8,512]{2,1,0:T(8,128)(2,1)} %bitcast.42), calls=%async_computation | async-start | bytes 262144 | tf_op jit(solution)/shard_map/all_to_all | solution.py:477
  10.1 0.7 copy-start.5
  10.1 0.7 copy-start.6
  10.8 1.0 %copy-start.4 = (bf16[1,1,32,4096]{3,2,1,0:T(8,128)(2,1)S(1)}, bf16[1,1,32,4096]{3,2,1,0:T(8,128)(2,1)}, u32[]{:S(2)}) copy-start(bf16[1,1,32,4096]{3,2,1,0:T(8,128)(2,1)} %param.19) | copy-start | bytes 786436
  11.7 5.7 %copy-start = (bf16[8,128,64]{1,2,0:T(8,128)(2,1)S(1)}, bf16[8,128,64]{1,2,0:T(8,128)(2,1)}, u32[]{:S(2)}) copy-start(bf16[8,128,64]{1,2,0:T(8,128)(2,1)} %param.13) | copy-start | bytes 393220
  11.7 5.7 %copy-start.1 = (bf16[1,1,32,4096]{3,2,1,0:T(8,128)(2,1)S(1)}, bf16[1,1,32,4096]{3,2,1,0:T(8,128)(2,1)}, u32[]{:S(2)}) copy-start(bf16[1,1,32,4096]{3,2,1,0:T(8,128)(2,1)} %param.10) | copy-start | bytes 786436
  13.7 4.3 %copy-start.7 = (bf16[256,512]{1,0:T(8,128)(2,1)}, bf16[256,512]{1,0:T(8,128)(2,1)S(1)}, u32[]{:S(2)}) copy-start(bf16[256,512]{1,0:T(8,128)(2,1)S(1)} %get-tuple-element.41.turned_ref) | copy-start | bytes 786436
  18.1 4.5 %collective-permute-start = (bf16[8,5120]{1,0:T(8,128)(2,1)S(1)}, bf16[8,5120]{1,0:T(8,128)(2,1)S(1)}, u32[]{:S(2)}, u32[]{:S(2)}) collective-permute-start(bf16[8,5120]{1,0:T(8,128)(2,1)S(1)} %get-tuple-element.35), channel_id=1, source_target_pairs={{0,1},{2,3},{1,0},{3,2},{4,5},{6,7},{5,4},{7,6},{8,9},{10,11},{9,8... | collective-permute-start | bytes 245768 | tf_op jit(solution)/shard_map/ppermute | solution.py:468
  18.8 3.8 %collective-permute-start.1 = (bf16[8,5120]{1,0:T(8,128)(2,1)S(1)}, bf16[8,5120]{1,0:T(8,128)(2,1)S(1)}, u32[]{:S(2)}, u32[]{:S(2)}) collective-permute-start(bf16[8,5120]{1,0:T(8,128)(2,1)S(1)} %get-tuple-element.36), channel_id=1, source_target_pairs={{1,2},{2,1},{5,6},{6,5},{9,10},{10,9},{13,14},{14,13},{17,18},{18,... | collective-permute-start | bytes 245768 | tf_op jit(solution)/shard_map/ppermute | solution.py:468
  22.6 1.8 %copy-start.8 = (bf16[256,512]{1,0:T(8,128)(2,1)S(1)}, bf16[256,512]{1,0:T(8,128)(2,1)}, u32[]{:S(2)}) copy-start(bf16[256,512]{1,0:T(8,128)(2,1)} %copy-done.7) | copy-start | bytes 786436
  22.9 1.4 %collective-permute-start.2 = (bf16[16,4096]{1,0:T(8,128)(2,1)S(1)}, bf16[16,4096]{1,0:T(8,128)(2,1)S(1)}, u32[]{:S(2)}, u32[]{:S(2)}) collective-permute-start(bf16[16,4096]{1,0:T(8,128)(2,1)S(1)} %get-tuple-element.39), channel_id=1, source_target_pairs={{0,4},{8,12},{4,0},{12,8},{1,5},{9,13},{5,1},{13,9},{2,6},{10,14},... | collective-permute-start | bytes 393224 | tf_op jit(solution)/shard_map/ppermute | solution.py:468
  23.0 1.3 %collective-permute-start.3 = (bf16[16,4096]{1,0:T(8,128)(2,1)S(1)}, bf16[16,4096]{1,0:T(8,128)(2,1)S(1)}, u32[]{:S(2)}, u32[]{:S(2)}) collective-permute-start(bf16[16,4096]{1,0:T(8,128)(2,1)S(1)} %get-tuple-element.40), channel_id=1, source_target_pairs={{4,8},{8,4},{5,9},{9,5},{6,10},{10,6},{7,11},{11,7},{20,24},{24,20... | collective-permute-start | bytes 393224 | tf_op jit(solution)/shard_map/ppermute | solution.py:468
  27.5 22.8 %all-to-all-start.1 = ((bf16[16,8,1408]{2,1,0:T(8,128)(2,1)}), bf16[16,8,1408]{2,1,0:T(8,128)(2,1)S(1)}, u32[]{:S(2)}, u32[]{:S(2)}) async-start(bf16[16,8,1408]{2,1,0:T(8,128)(2,1)} %bitcast.15), calls=%async_computation.1 | async-start | bytes 720896 | tf_op jit(solution)/shard_map/all_to_all | solution.py:477
  38.1 13.2 %collective-permute-start.4 = (bf16[8,4096]{1,0:T(8,128)(2,1)S(1)}, bf16[8,4096]{1,0:T(8,128)(2,1)S(1)}, u32[]{:S(2)}, u32[]{:S(2)}) collective-permute-start(bf16[8,4096]{1,0:T(8,128)(2,1)S(1)} %get-tuple-element.50), channel_id=1, source_target_pairs={{0,1},{2,3},{1,0},{3,2},{4,5},{6,7},{5,4},{7,6},{8,9},{10,11},{9,8... | collective-permute-start | bytes 196616 | tf_op jit(solution)/shard_map/ppermute | solution.py:468
  40.0 11.2 %collective-permute-start.5 = (bf16[8,4096]{1,0:T(8,128)(2,1)S(1)}, bf16[8,4096]{1,0:T(8,128)(2,1)S(1)}, u32[]{:S(2)}, u32[]{:S(2)}) collective-permute-start(bf16[8,4096]{1,0:T(8,128)(2,1)S(1)} %get-tuple-element.51), channel_id=1, source_target_pairs={{1,2},{2,1},{5,6},{6,5},{9,10},{10,9},{13,14},{14,13},{17,18},{18,... | collective-permute-start | bytes 196616 | tf_op jit(solution)/shard_map/ppermute | solution.py:468
  62.9 15.7 %all-to-all-start.3 = ((bf16[16,8,1408]{2,1,0:T(8,128)(2,1)}), bf16[16,8,1408]{2,1,0:T(8,128)(2,1)S(1)}, u32[]{:S(2)}, u32[]{:S(2)}) async-start(bf16[16,8,1408]{2,1,0:T(8,128)(2,1)} %bitcast.23), calls=%async_computation.3 | async-start | bytes 720896 | tf_op jit(solution)/shard_map/all_to_all | solution.py:477
  66.5 2.2 %copy-start.2 = (s32[1,1,16,4]{2,3,1,0:T(4,128)S(1)}, s32[1,1,16,4]{2,3,1,0:T(4,128)}, u32[]{:S(2)}) copy-start(s32[1,1,16,4]{2,3,1,0:T(4,128)} %param.18) | copy-start | bytes 772

commit v6 on v5

--- a/solution.py
+++ b/solution.py
@@ -416,15 +416,15 @@
         replies_ref[:, j * half : (j + 1) * half] = rows.astype(BF)
 
 
-def share_body(sums_ref, lists_ref, out_ref, again_ref, devices):
-    again_ref[...] = lists_ref[...]
-    count = sums_ref.shape[0]
+def share_body(sums_ref, replies_ref, out_ref, devices):
+    count, item_lanes = replies_ref.shape
     share = count // devices
     same = iota((count, count), 0) % share == iota((count, count), 1) % share
-    out_ref[...] = dot(ones_where(same), sums_ref[...]).astype(BF)
-
-
-def coarse_grad_body(back_ref, sends_ref, out_ref):
+    out_ref[:, :item_lanes] = replies_ref[...]
+    out_ref[:, item_lanes:] = dot(ones_where(same), sums_ref[...]).astype(BF)
+
+
+def coarse_grad(back_ref, sends_ref, out_ref):
     capacity, devices = sends_ref.shape
     count, item_width = out_ref.shape
     half = item_width // 2
@@ -442,11 +442,12 @@
         out_ref[:, h * half : (h + 1) * half] = total.astype(BF)
 
 
-def last_body(back_ref, conv_ref, up_ref, scale):
-    count = back_ref.shape[0]
+def last_body(back_ref, sends_ref, conv_ref, up_ref, out_ref, scale):
+    coarse_grad(back_ref, sends_ref, out_ref)
+    count, width = back_ref.shape
     coarse = up_ref.shape[1]
     parts = up_ref.shape[0] // count
-    at = 0
+    at = width - 14 * C - parts * coarse
     for q in range(parts):
         up_ref[q * count : (q + 1) * count] = back_ref[:, at : at + coarse].astype(F32) * scale
         at += coarse
@@ -544,20 +545,19 @@
     )
     sums = trade_rows(sums, devices)
     side_grads = swap_pairs(to_even, to_odd, "gy")
-    sums, lists = call(
-        functools.partial(share_body, devices=devices), [shape((count, sums_width)), lists_shape], sums, lists
-    )
-    sums = trade_rows(sums, devices)
     grad_fine, replies = call(
         fine_grad_body, [rows, shape((count, item_lanes))], fine_part, lists, *side_grads, up_turned
     )
-    replies = trade_rows(replies, devices)
     (output,) = call(conv_body, [rows], pad, conv_weight, scratch=[band], flops=conv_flops)
+    (back,) = call(
+        functools.partial(share_body, devices=devices), [shape((count, item_lanes + sums_width))], sums, replies
+    )
+    back = trade_rows(back, devices)
     scale = 1.0 / math.sqrt(64 * bricks * devices)
-    grad_conv, grad_up = call(
-        functools.partial(last_body, scale=scale), [shape((27, C, C), F32), shape((8 * C, coarse), F32)], sums
-    )
-    (coarse_grad,) = call(coarse_grad_body, [shape((item_count, item_width))], replies, sends)
+    grad_conv, grad_up, coarse_grad = call(
+        functools.partial(last_body, scale=scale),
+        [shape((27, C, C), F32), shape((8 * C, coarse), F32), shape((item_count, item_width))], back, sends,
+    )
     return (
         output.reshape(1, 1, bricks, width),
         grad_fine.reshape(1, 1, bricks, width),

time: 80.4 us -> 73.2 us (0.910)
  blocking collectives: 10.6 us -> 0 us
  waiting for transfers between devices: 25.9 us -> 28.8 us
  starting transfers between devices: 26.2 us -> 27.7 us
  Pallas kernels: 14.7 us -> 13.7 us
    all_to_all x1 -> x0, blocking collectives: 10.6 us -> none  [trade_rows(): lax.all_to_all(grid_view, ('gx', 'gy'), split_axis=0, concat_axis=0, tile...]
    ppermute x6, waiting for transfers between devices: 3.8 us -> 10.8 us  [swap(): lax.ppermute(value, axis, [(i, i + 1) for i in lower] + [(i + 1, i) for i...]
    all_to_all x3, waiting for transfers between devices: 22.1 us -> 17.9 us  [trade_rows(): lax.all_to_all(grid_view, ('gx', 'gy'), split_axis=0, concat_axis=0, tile...]
    all_to_all x3, starting transfers between devices: 21.5 us -> 23 us  [trade_rows(): lax.all_to_all(grid_view, ('gx', 'gy'), split_axis=0, concat_axis=0, tile...]
    pallas_call x10 -> x9, Pallas kernels: 14.7 us -> 13.7 us  [call(): pl.pallas_call(body, out_shape=tuple(outs), in_specs=[pl.BlockSpec(memory...]
  transfers between devices with their start and end apart: 9 -> 9, of which waited for: 5 -> 6; matrix products, arithmetic and copies ran while one was open for 0% -> 0% of each run, Pallas kernels for 8% -> 7%
where the time goes in v6:
time: 73.2 us; the launch traced here: 72.6 us
  waiting for transfers between devices  28.8 us (39%)
  starting transfers between devices  27.7 us (38%)
  Pallas kernels  13.7 us (19%)
  local copies, waits for them, and re-layouts  1.65 us (2%)
  between operations  0.81 us (1%)
    all_to_all x3, starting transfers between devices, trade_rows(): lax.all_to_all(grid_view, ('gx', 'gy'), split_axis=0, concat_axis=0, tile...  23 us
    all_to_all x3, waiting for transfers between devices, trade_rows(): lax.all_to_all(grid_view, ('gx', 'gy'), split_axis=0, concat_axis=0, tile...  17.9 us
    pallas_call x9, Pallas kernels, call(): pl.pallas_call(body, out_shape=tuple(outs), in_specs=[pl.BlockSpec(memory...  13.7 us
    ppermute x6, waiting for transfers between devices, swap(): lax.ppermute(value, axis, [(i, i + 1) for i in lower] + [(i + 1, i) for i...  10.8 us
    ppermute x6, starting transfers between devices, swap(): lax.ppermute(value, axis, [(i, i + 1) for i in lower] + [(i + 1, i) for i...  4.71 us
    unnamed x18, local copies, waits for them, and re-layouts  1.65 us
  transfers between devices with their start and end apart: 9, of which 6 were waited for; matrix products, arithmetic and copies ran while one was open for 0% of the time, Pallas kernels for 7%

profile of v6, /device:TPU:0, one launch (start us, length us, event | category | flops | bytes accessed | tf_op | source)
XLA Modules:
  0.0 72.6 jit_solution(5677090725500513795)
XLA Ops:
  0.6 0.0 copy-start.3
  0.6 2.0 %shard_map.137 = (bf16[128,512]{1,0:T(8,128)(2,1)}, s32[8,128]{1,0:T(8,128)}) custom-call(s32[4,16]{1,0:T(4,128)} %bitcast.33, bf16[64,1024]{1,0:T(8,128)(2,1)} %bitcast.37, s32[2,8]{1,0:T(2,128)} %bitcast.39, s32[2,8]{1,0:T(2,128)} %bitcast.40, s32[1,32]{1,0:T(1,128)} %bitcast.41), custom_call_target="tpu_custom_call" | custom-call | bytes 266752 | tf_op jit(solution)/shard_map/pallas_call | solution.py:49
  2.7 7.4 %all-to-all-start = ((bf16[16,8,512]{2,1,0:T(8,128)(2,1)}), bf16[16,8,512]{2,1,0:T(8,128)(2,1)S(1)}, u32[]{:S(2)}, u32[]{:S(2)}) async-start(bf16[16,8,512]{2,1,0:T(8,128)(2,1)} %bitcast.38), calls=%async_computation | async-start | bytes 262144 | tf_op jit(solution)/shard_map/all_to_all | solution.py:478
  10.1 0.0 copy-start.5
  10.1 0.0 copy-start.6
  10.1 0.0 copy-done.3
  10.1 0.7 copy-done.5
  10.8 0.0 copy-done.6
  10.8 0.0 copy-start.4
  10.8 0.9 %copy-done.4 = bf16[1,1,32,4096]{3,2,1,0:T(8,128)(2,1)S(1)} copy-done((bf16[1,1,32,4096]{3,2,1,0:T(8,128)(2,1)S(1)}, bf16[1,1,32,4096]{3,2,1,0:T(8,128)(2,1)}, u32[]{:S(2)}) %copy-start.4) | copy-done | bytes 262168
  11.7 0.0 copy-start
  11.7 0.0 copy-start.1
  11.7 1.9 %shard_map.138 = (f32[48,4096]{1,0:T(8,128)S(1)}, bf16[8,4096]{1,0:T(8,128)(2,1)S(1)}, bf16[8,4096]{1,0:T(8,128)(2,1)S(1)}, bf16[256,512]{1,0:T(8,128)(2,1)S(1)}...) custom-call(bf16[32,4096]{1,0:T(8,128)(2,1)S(1)} %bitcast.35, ...), custom_call_target="tpu_custom_call" | custom-call | flops 1811939328 | bytes 1785728 | tf_op jit(solution)/shard_map/pallas_call | solution.py:49
  13.7 0.0 copy-start.7
  13.7 3.7 %all-to-all-done = bf16[16,8,512]{2,1,0:T(8,128)(2,1)S(1)} async-done(((bf16[16,8,512]{2,1,0:T(8,128)(2,1)}), bf16[16,8,512]{2,1,0:T(8,128)(2,1)S(1)}, u32[]{:S(2)}, u32[]{:S(2)}) %all-to-all-start) | async-done | bytes 131104 | tf_op jit(solution)/shard_map/all_to_all | solution.py:478
  17.4 0.0 copy-done
  17.4 0.0 copy-done.1
  17.4 0.6 shard_map.139
  18.0 0.0 copy-done.7
  18.1 0.7 %collective-permute-start = (bf16[8,5120]{1,0:T(8,128)(2,1)S(1)}, bf16[8,5120]{1,0:T(8,128)(2,1)S(1)}, u32[]{:S(2)}, u32[]{:S(2)}) collective-permute-start(bf16[8,5120]{1,0:T(8,128)(2,1)S(1)} %get-tuple-element.34), channel_id=1, source_target_pairs={{0,1},{2,3},{1,0},{3,2},{4,5},{6,7},{5,4},{7,6},{8,9},{10,11},{9,8... | collective-permute-start | bytes 245768 | tf_op jit(solution)/shard_map/ppermute | solution.py:469
  18.8 0.7 collective-permute-start.1
  19.4 3.1 %collective-permute-done.even_ref.even_side_ref = bf16[8,5120]{1,0:T(8,128)(2,1)S(1)} collective-permute-done((bf16[8,5120]{1,0:T(8,128)(2,1)S(1)}, bf16[8,5120]{1,0:T(8,128)(2,1)S(1)}, u32[]{:S(2)}, u32[]{:S(2)}) %collective-permute-start) | collective-permute-done | bytes 81952 | tf_op jit(solution)/shard_map/ppermute | solution.py:469
  22.6 0.0 collective-permute-done.1.odd_ref.odd_side_ref
  22.6 0.0 copy-start.8
  22.6 0.4 shard_map.140
  22.9 0.1 collective-permute-start.2
  23.0 0.7 collective-permute-start.3
  23.7 0.7 collective-permute-done.2.even_cross_ref
  24.4 0.0 collective-permute-done.3.odd_cross_ref
  24.4 0.0 copy-done.8
  24.4 3.1 %shard_map.141 = (bf16[128,1408]{1,0:T(8,128)(2,1)}, bf16[6,6,32,384]{3,2,1,0:T(8,128)(2,1)S(1)}, f32[32,4096]{1,0:T(8,128)S(1)}, bf16[8,4096]{1,0:T(8,128)(2,1)S(1)}, bf16[8,4096]{1,0:T(8,128)(2,1)S(1)}) custom-call(bf16[32,4096]{1,0:T(8,128)(2,1)S(1)} %get-tuple-element.33.merged_ref, bf16[8,5120]{1,0:T(8,128)(2,1)S(1)} %collective-permute-done.even_ref.even_side_ref, ...), custom_call_target="tpu_custom_call" | custom-call | flops 905969664 | bytes 3817472 | tf_op jit(solution)/shard_map/pallas_call | solution.py:49
  27.5 10.6 %all-to-all-start.1 = ((bf16[16,8,1408]{2,1,0:T(8,128)(2,1)}), bf16[16,8,1408]{2,1,0:T(8,128)(2,1)S(1)}, u32[]{:S(2)}, u32[]{:S(2)}) async-start(bf16[16,8,1408]{2,1,0:T(8,128)(2,1)} %bitcast.17), calls=%async_computation.1 | async-start | bytes 720896 | tf_op jit(solution)/shard_map/all_to_all | solution.py:478
  38.1 1.9 %collective-permute-start.4 = (bf16[8,4096]{1,0:T(8,128)(2,1)S(1)}, bf16[8,4096]{1,0:T(8,128)(2,1)S(1)}, u32[]{:S(2)}, u32[]{:S(2)}) collective-permute-start(bf16[8,4096]{1,0:T(8,128)(2,1)S(1)} %get-tuple-element.47), channel_id=1, source_target_pairs={{0,1},{2,3},{1,0},{3,2},{4,5},{6,7},{5,4},{7,6},{8,9},{10,11},{9,8... | collective-permute-start | bytes 196616 | tf_op jit(solution)/shard_map/ppermute | solution.py:469
  40.0 0.7 collective-permute-start.5
  40.7 7.0 %collective-permute-done.4.even_ref = bf16[8,4096]{1,0:T(8,128)(2,1)S(1)} collective-permute-done((bf16[8,4096]{1,0:T(8,128)(2,1)S(1)}, bf16[8,4096]{1,0:T(8,128)(2,1)S(1)}, u32[]{:S(2)}, u32[]{:S(2)}) %collective-permute-start.4) | collective-permute-done | bytes 65568 | tf_op jit(solution)/shard_map/ppermute | solution.py:469
  47.7 0.0 collective-permute-done.5.odd_ref
  47.7 1.1 %shard_map.143 = (bf16[32,4096]{1,0:T(8,128)(2,1)}, bf16[128,512]{1,0:T(8,128)(2,1)S(1)}) custom-call(f32[32,4096]{1,0:T(8,128)S(1)} %get-tuple-element.46.part_ref, s32[8,128]{1,0:T(8,128)S(1)} %get-tuple-element.32.lists_ref, bf16[8,4096]{1,0:T(8,128)(2,1)S(1)} %collective-permute-done.4.even_ref, bf16[8,4096]{1,0:T(8,128)(2,1)S(1)} %collective-permute-done.5.odd_ref, ...), custom_call_target="tpu_custom_call" | custom-call | bytes 1183744 | tf_op jit(solution)/shard_map/pallas_call | solution.py:49
  48.8 1.5 %all-to-all-done.1 = bf16[16,8,1408]{2,1,0:T(8,128)(2,1)S(1)} async-done(((bf16[16,8,1408]{2,1,0:T(8,128)(2,1)}), bf16[16,8,1408]{2,1,0:T(8,128)(2,1)S(1)}, u32[]{:S(2)}, u32[]{:S(2)}) %all-to-all-start.1) | async-done | bytes 360480 | tf_op jit(solution)/shard_map/all_to_all | solution.py:478
  50.3 1.0 %shard_map.144 = bf16[128,1920]{1,0:T(8,128)(2,1)} custom-call(bf16[128,1408]{1,0:T(8,128)(2,1)S(1)} %bitcast.28, bf16[128,512]{1,0:T(8,128)(2,1)S(1)} %get-tuple-element.51.replies_ref), custom_call_target="tpu_custom_call" | custom-call | bytes 983040 | tf_op jit(solution)/shard_map/pallas_call | solution.py:49
  51.3 5.0 %all-to-all-start.2 = ((bf16[16,8,1920]{2,1,0:T(8,128)(2,1)}), bf16[16,8,1920]{2,1,0:T(8,128)(2,1)S(1)}, u32[]{:S(2)}, u32[]{:S(2)}) async-start(bf16[16,8,1920]{2,1,0:T(8,128)(2,1)} %bitcast.19), calls=%async_computation.2 | async-start | bytes 983040 | tf_op jit(solution)/shard_map/all_to_all | solution.py:478
  56.3 0.0 copy-start.2
  56.3 2.2 %shard_map.142 = bf16[32,4096]{1,0:T(8,128)(2,1)} custom-call(bf16[6,6,32,384]{3,2,1,0:T(8,128)(2,1)S(1)} %get-tuple-element.45.pad_ref, bf16[27,64,64]{2,1,0:T(8,128)(2,1)S(1)} %copy-done.3), custom_call_target="tpu_custom_call" | custom-call | flops 905969664 | bytes 1368064 | tf_op jit(solution)/shard_map/pallas_call | solution.py:49
  58.5 12.8 %all-to-all-done.2 = bf16[16,8,1920]{2,1,0:T(8,128)(2,1)S(1)} async-done(((bf16[16,8,1920]{2,1,0:T(8,128)(2,1)}), bf16[16,8,1920]{2,1,0:T(8,128)(2,1)S(1)}, u32[]{:S(2)}, u32[]{:S(2)}) %all-to-all-start.2) | async-done | bytes 491552 | tf_op jit(solution)/shard_map/all_to_all | solution.py:478
  71.3 0.0 copy-done.2
  71.3 1.4 %shard_map.145 = (f32[27,64,64]{2,1,0:T(8,128)}, f32[512,128]{1,0:T(8,128)}, bf16[64,1024]{1,0:T(8,128)(2,1)}) custom-call(bf16[128,1920]{1,0:T(8,128)(2,1)S(1)} %bitcast.27, s32[4,16]{1,0:T(4,128)S(1)} %bitcast.34), custom_call_target="tpu_custom_call" | custom-call | bytes 1327360 | tf_op jit(solution)/shard_map/pallas_call | solution.py:49
  (1 shorter events, 0.0 us)
Async XLA Ops:
  0.6 9.5 %copy-start.3 = (bf16[27,64,64]{2,1,0:T(8,128)(2,1)S(1)}, bf16[27,64,64]{2,1,0:T(8,128)(2,1)}, u32[]{:S(2)}) copy-start(bf16[27,64,64]{2,1,0:T(8,128)(2,1)} %weight_ref.3) | copy-start | bytes 663556
  2.7 14.7 %all-to-all-start = ((bf16[16,8,512]{2,1,0:T(8,128)(2,1)}), bf16[16,8,512]{2,1,0:T(8,128)(2,1)S(1)}, u32[]{:S(2)}, u32[]{:S(2)}) async-start(bf16[16,8,512]{2,1,0:T(8,128)(2,1)} %bitcast.38), calls=%async_computation | async-start | bytes 262144 | tf_op jit(solution)/shard_map/all_to_all | solution.py:478
  10.1 0.7 copy-start.5
  10.1 0.7 copy-start.6
  10.8 1.0 %copy-start.4 = (bf16[1,1,32,4096]{3,2,1,0:T(8,128)(2,1)S(1)}, bf16[1,1,32,4096]{3,2,1,0:T(8,128)(2,1)}, u32[]{:S(2)}) copy-start(bf16[1,1,32,4096]{3,2,1,0:T(8,128)(2,1)} %param.19) | copy-start | bytes 786436
  11.7 5.7 %copy-start = (bf16[8,128,64]{1,2,0:T(8,128)(2,1)S(1)}, bf16[8,128,64]{1,2,0:T(8,128)(2,1)}, u32[]{:S(2)}) copy-start(bf16[8,128,64]{1,2,0:T(8,128)(2,1)} %param.13) | copy-start | bytes 393220
  11.7 5.7 %copy-start.1 = (bf16[1,1,32,4096]{3,2,1,0:T(8,128)(2,1)S(1)}, bf16[1,1,32,4096]{3,2,1,0:T(8,128)(2,1)}, u32[]{:S(2)}) copy-start(bf16[1,1,32,4096]{3,2,1,0:T(8,128)(2,1)} %param.10) | copy-start | bytes 786436
  13.7 4.3 %copy-start.7 = (bf16[256,512]{1,0:T(8,128)(2,1)}, bf16[256,512]{1,0:T(8,128)(2,1)S(1)}, u32[]{:S(2)}) copy-start(bf16[256,512]{1,0:T(8,128)(2,1)S(1)} %get-tuple-element.40.turned_ref) | copy-start | bytes 786436
  18.1 4.5 %collective-permute-start = (bf16[8,5120]{1,0:T(8,128)(2,1)S(1)}, bf16[8,5120]{1,0:T(8,128)(2,1)S(1)}, u32[]{:S(2)}, u32[]{:S(2)}) collective-permute-start(bf16[8,5120]{1,0:T(8,128)(2,1)S(1)} %get-tuple-element.34), channel_id=1, source_target_pairs={{0,1},{2,3},{1,0},{3,2},{4,5},{6,7},{5,4},{7,6},{8,9},{10,11},{9,8... | collective-permute-start | bytes 245768 | tf_op jit(solution)/shard_map/ppermute | solution.py:469
  18.8 3.8 %collective-permute-start.1 = (bf16[8,5120]{1,0:T(8,128)(2,1)S(1)}, bf16[8,5120]{1,0:T(8,128)(2,1)S(1)}, u32[]{:S(2)}, u32[]{:S(2)}) collective-permute-start(bf16[8,5120]{1,0:T(8,128)(2,1)S(1)} %get-tuple-element.35), channel_id=1, source_target_pairs={{1,2},{2,1},{5,6},{6,5},{9,10},{10,9},{13,14},{14,13},{17,18},{18,... | collective-permute-start | bytes 245768 | tf_op jit(solution)/shard_map/ppermute | solution.py:469
  22.6 1.8 %copy-start.8 = (bf16[256,512]{1,0:T(8,128)(2,1)S(1)}, bf16[256,512]{1,0:T(8,128)(2,1)}, u32[]{:S(2)}) copy-start(bf16[256,512]{1,0:T(8,128)(2,1)} %copy-done.7) | copy-start | bytes 786436
  22.9 1.4 %collective-permute-start.2 = (bf16[16,4096]{1,0:T(8,128)(2,1)S(1)}, bf16[16,4096]{1,0:T(8,128)(2,1)S(1)}, u32[]{:S(2)}, u32[]{:S(2)}) collective-permute-start(bf16[16,4096]{1,0:T(8,128)(2,1)S(1)} %get-tuple-element.38), channel_id=1, source_target_pairs={{0,4},{8,12},{4,0},{12,8},{1,5},{9,13},{5,1},{13,9},{2,6},{10,14},... | collective-permute-start | bytes 393224 | tf_op jit(solution)/shard_map/ppermute | solution.py:469
  23.0 1.3 %collective-permute-start.3 = (bf16[16,4096]{1,0:T(8,128)(2,1)S(1)}, bf16[16,4096]{1,0:T(8,128)(2,1)S(1)}, u32[]{:S(2)}, u32[]{:S(2)}) collective-permute-start(bf16[16,4096]{1,0:T(8,128)(2,1)S(1)} %get-tuple-element.39), channel_id=1, source_target_pairs={{4,8},{8,4},{5,9},{9,5},{6,10},{10,6},{7,11},{11,7},{20,24},{24,20... | collective-permute-start | bytes 393224 | tf_op jit(solution)/shard_map/ppermute | solution.py:469
  27.5 22.8 %all-to-all-start.1 = ((bf16[16,8,1408]{2,1,0:T(8,128)(2,1)}), bf16[16,8,1408]{2,1,0:T(8,128)(2,1)S(1)}, u32[]{:S(2)}, u32[]{:S(2)}) async-start(bf16[16,8,1408]{2,1,0:T(8,128)(2,1)} %bitcast.17), calls=%async_computation.1 | async-start | bytes 720896 | tf_op jit(solution)/shard_map/all_to_all | solution.py:478
  38.1 9.6 %collective-permute-start.4 = (bf16[8,4096]{1,0:T(8,128)(2,1)S(1)}, bf16[8,4096]{1,0:T(8,128)(2,1)S(1)}, u32[]{:S(2)}, u32[]{:S(2)}) collective-permute-start(bf16[8,4096]{1,0:T(8,128)(2,1)S(1)} %get-tuple-element.47), channel_id=1, source_target_pairs={{0,1},{2,3},{1,0},{3,2},{4,5},{6,7},{5,4},{7,6},{8,9},{10,11},{9,8... | collective-permute-start | bytes 196616 | tf_op jit(solution)/shard_map/ppermute | solution.py:469
  40.0 7.7 %collective-permute-start.5 = (bf16[8,4096]{1,0:T(8,128)(2,1)S(1)}, bf16[8,4096]{1,0:T(8,128)(2,1)S(1)}, u32[]{:S(2)}, u32[]{:S(2)}) collective-permute-start(bf16[8,4096]{1,0:T(8,128)(2,1)S(1)} %get-tuple-element.48), channel_id=1, source_target_pairs={{1,2},{2,1},{5,6},{6,5},{9,10},{10,9},{13,14},{14,13},{17,18},{18,... | collective-permute-start | bytes 196616 | tf_op jit(solution)/shard_map/ppermute | solution.py:469
  51.3 20.0 %all-to-all-start.2 = ((bf16[16,8,1920]{2,1,0:T(8,128)(2,1)}), bf16[16,8,1920]{2,1,0:T(8,128)(2,1)S(1)}, u32[]{:S(2)}, u32[]{:S(2)}) async-start(bf16[16,8,1920]{2,1,0:T(8,128)(2,1)} %bitcast.19), calls=%async_computation.2 | async-start | bytes 983040 | tf_op jit(solution)/shard_map/all_to_all | solution.py:478
  56.3 15.0 %copy-start.2 = (s32[1,1,16,4]{2,3,1,0:T(4,128)S(1)}, s32[1,1,16,4]{2,3,1,0:T(4,128)}, u32[]{:S(2)}) copy-start(s32[1,1,16,4]{2,3,1,0:T(4,128)} %param.18) | copy-start | bytes 772

commit v7 on v6

--- a/solution.py
+++ b/solution.py
@@ -141,15 +141,14 @@
     return lists_ref[4:5, :bricks]
 
 
-def cross_body(merged_ref, even_ref, odd_ref, lists_ref, low_grad_ref, high_grad_ref, a_ref, b_ref):
-    face, width = low_grad_ref.shape
+def cross_body(merged_ref, even_ref, odd_ref, lists_ref, a_ref, b_ref):
+    face, width = a_ref.shape
     high, low = from_pairs(lists_ref, GY, even_ref, odd_ref)
     rows = jnp.concatenate([merged_ref[...], stack_rows(low[:, :width], high[:, :width])], axis=0)
     lists = crosses_of(lists_ref, face)
     picked = pick_rows(by_pair(lists_ref, GX, lists[0:1], lists[1:2]), rows)
-    grads = from_pairs(lists_ref, GX, high_grad_ref, low_grad_ref)
-    a_ref[...] = stack_rows(picked[0], grads[0])
-    b_ref[...] = stack_rows(picked[1], grads[1])
+    a_ref[...] = picked[0].astype(BF)
+    b_ref[...] = picked[1].astype(BF)
 
 
 def build_bands(weight_ref, band_ref):
@@ -211,12 +210,12 @@
 
 def table_grad_body(
     cot_ref, weight_ref, near_ref, lists_ref, parity_ref,
-    ext_ref, low_ref, high_ref, turned_ref, mains_ref, ends_ref, again_ref, band_ref, pad_ref,
+    ext_ref, even_ref, odd_ref, turned_ref, mains_ref, ends_ref, again_ref, band_ref, pad_ref,
 ):
     again_ref[...] = lists_ref[...]
     again_ref[5:6] = parity_ref[...]
     bricks = cot_ref.shape[0]
-    face = low_ref.shape[0]
+    face = even_ref.shape[0]
     start = ext_ref.shape[0]
     rows = start + 2 * face
     build_bands(weight_ref, band_ref)
@@ -260,8 +259,9 @@
             total = jnp.concatenate([first, second], axis=1)
             at = (x * 4 + y) * RUN
             ext_ref[:, at : at + RUN] = total[:start]
-            low_ref[:, at : at + RUN] = total[start : start + face].astype(BF)
-            high_ref[:, at : at + RUN] = total[start + face :].astype(BF)
+            even, odd = by_pair(again_ref, GX, total[start + face :], total[start : start + face])
+            even_ref[:, at : at + RUN] = even.astype(BF)
+            odd_ref[:, at : at + RUN] = odd.astype(BF)
     make_choosers(near_ref, rows, mains_ref, ends_ref)
 
 
@@ -297,8 +297,8 @@
 
 
 def weight_grad_body(
-    merged_ref, even_side_ref, odd_side_ref, even_cross_ref, odd_cross_ref, turned_ref, mains_ref, ends_ref, lists_ref,
-    ext_ref, parents_ref, sums_ref, pad_ref, part_ref, to_even_ref, to_odd_ref, table_ref,
+    merged_ref, even_side_ref, odd_side_ref, even_cross_ref, odd_cross_ref, even_grad_ref, odd_grad_ref,
+    turned_ref, mains_ref, ends_ref, lists_ref, ext_ref, parents_ref, sums_ref, pad_ref, part_ref, to_even_ref, to_odd_ref, table_ref,
 ):
     bricks, width = merged_ref.shape
     face = even_side_ref.shape[0]
@@ -306,8 +306,9 @@
     high, low = from_pairs(lists_ref, GY, even_side_ref, odd_side_ref)
     above, below = from_pairs(lists_ref, GX, even_cross_ref, odd_cross_ref)
     table_ref[:bricks] = merged_ref[...]
-    table_ref[bricks:] = stack_rows(low[:, :width], high[:, :width], below[:face], above[:face])
-    total = add_rows(ext_ref[...], crosses_of(lists_ref, face), above[face:], below[face:])
+    table_ref[bricks:] = stack_rows(low[:, :width], high[:, :width], below, above)
+    from_next, from_prev = from_pairs(lists_ref, GX, even_grad_ref, odd_grad_ref)
+    total = add_rows(ext_ref[...], crosses_of(lists_ref, face), from_next, from_prev)
     part_ref[...] = total[:bricks]
     to_even, to_odd = by_pair(lists_ref, GY, total[bricks + face :], total[bricks : bricks + face])
     to_even_ref[...] = to_even.astype(BF)
@@ -506,7 +507,6 @@
     rows = shape((bricks, width))
     face_rows = shape((face, width))
     faces_and_parents = shape((face, width + item_width))
-    two_faces = shape((2 * face, width))
     lists_shape = shape((8, 128), I32)
     band = pltpu.VMEM((9, WIDE, RUN), BF)
     conv_flops = 2 * 9 * 16 * bricks * WIDE * RUN
@@ -521,7 +521,7 @@
     lane = jnp.arange(128, dtype=I32)[None]
     parity = jnp.where(lane == GX, lax.axis_index("gx") % 2, lax.axis_index("gy") % 2).astype(I32)
     table_rows = start + 2 * face
-    ext_grad, low_cross, high_cross, turned, mains, ends, lists = call(
+    ext_grad, to_even, to_odd, turned, mains, ends, lists = call(
         table_grad_body,
         [
             shape((start, width), F32), face_rows, face_rows, shape((RUN, 16 * bricks)),
@@ -530,17 +530,18 @@
         cot, conv_weight, near, lists, parity,
         scratch=[band, pltpu.VMEM((6, 6, bricks, WIDE), F32)], flops=2 * conv_flops,
     )
+    cross_grads = swap_pairs(to_even, to_odd, "gx")
     merged, parents, to_even, to_odd = call(
         merge_body, [rows, shape((8 * bricks, coarse)), faces_and_parents, faces_and_parents],
         received, up_turned, fine, lists,
     )
     sides = swap_pairs(to_even, to_odd, "gy")
-    to_even, to_odd = call(cross_body, [two_faces, two_faces], merged, *sides, lists, low_cross, high_cross)
+    to_even, to_odd = call(cross_body, [face_rows, face_rows], merged, *sides, lists)
     crosses = swap_pairs(to_even, to_odd, "gx")
     sums, pad, fine_part, to_even, to_odd = call(
         weight_grad_body,
         [shape((count, sums_width)), shape((6, 6, bricks, WIDE)), shape((bricks, width), F32), face_rows, face_rows],
-        merged, *sides, *crosses, turned, mains, ends, lists, ext_grad, parents,
+        merged, *sides, *crosses, *cross_grads, turned, mains, ends, lists, ext_grad, parents,
         scratch=[pltpu.VMEM((table_rows, width), BF)], flops=conv_flops,
     )
     sums = trade_rows(sums, devices)

time: 73.2 us -> 72.7 us (level)
  waiting for transfers between devices: 28.8 us -> 27.2 us
    ppermute x6 -> x8, waiting for transfers between devices: 10.8 us -> 9.96 us  [swap(): lax.ppermute(value, axis, [(i, i + 1) for i in lower] + [(i + 1, i) for i...]
    ppermute x6 -> x8, starting transfers between devices: 4.71 us -> 5.44 us  [swap(): lax.ppermute(value, axis, [(i, i + 1) for i in lower] + [(i + 1, i) for i...]
    unnamed x18 -> x22, local copies, waits for them, and re-layouts: 1.65 us -> 2.27 us
  transfers between devices with their start and end apart: 9 -> 11, of which waited for: 6 -> 6; matrix products, arithmetic and copies ran while one was open for 0% -> 0% of each run, Pallas kernels for 7% -> 8%
where the time goes in v7:
time: 72.7 us; the launch traced here: 72.1 us
  starting transfers between devices  28 us (39%)
  waiting for transfers between devices  27.2 us (37%)
  Pallas kernels  13.8 us (19%)
  local copies, waits for them, and re-layouts  2.27 us (3%)
  between operations  0.85 us (1%)
    all_to_all x3, starting transfers between devices, trade_rows(): lax.all_to_all(grid_view, ('gx', 'gy'), split_axis=0, concat_axis=0, tile...  22.6 us
    all_to_all x3, waiting for transfers between devices, trade_rows(): lax.all_to_all(grid_view, ('gx', 'gy'), split_axis=0, concat_axis=0, tile...  17.3 us
    pallas_call x9, Pallas kernels, call(): pl.pallas_call(body, out_shape=tuple(outs), in_specs=[pl.BlockSpec(memory...  13.8 us
    ppermute x8, waiting for transfers between devices, swap(): lax.ppermute(value, axis, [(i, i + 1) for i in lower] + [(i + 1, i) for i...  9.96 us
    ppermute x8, starting transfers between devices, swap(): lax.ppermute(value, axis, [(i, i + 1) for i in lower] + [(i + 1, i) for i...  5.44 us
    unnamed x22, local copies, waits for them, and re-layouts  2.27 us
  transfers between devices with their start and end apart: 11, of which 6 were waited for; matrix products, arithmetic and copies ran while one was open for 0% of the time, Pallas kernels for 8%

profile of v7, /device:TPU:0, one launch (start us, length us, event | category | flops | bytes accessed | tf_op | source)
XLA Modules:
  0.0 72.1 jit_solution(13737135698076058207)
XLA Ops:
  0.6 0.0 copy-start.3
  0.6 2.0 %shard_map.137 = (bf16[128,512]{1,0:T(8,128)(2,1)}, s32[8,128]{1,0:T(8,128)}) custom-call(s32[4,16]{1,0:T(4,128)} %bitcast.33, bf16[64,1024]{1,0:T(8,128)(2,1)} %bitcast.37, s32[2,8]{1,0:T(2,128)} %bitcast.39, s32[2,8]{1,0:T(2,128)} %bitcast.40, s32[1,32]{1,0:T(1,128)} %bitcast.41), custom_call_target="tpu_custom_call" | custom-call | bytes 266752 | tf_op jit(solution)/shard_map/pallas_call | solution.py:49
  2.7 7.4 %all-to-all-start = ((bf16[16,8,512]{2,1,0:T(8,128)(2,1)}), bf16[16,8,512]{2,1,0:T(8,128)(2,1)S(1)}, u32[]{:S(2)}, u32[]{:S(2)}) async-start(bf16[16,8,512]{2,1,0:T(8,128)(2,1)} %bitcast.38), calls=%async_computation | async-start | bytes 262144 | tf_op jit(solution)/shard_map/all_to_all | solution.py:479
  10.1 0.0 copy-start.5
  10.1 0.0 copy-start.6
  10.1 0.0 copy-done.3
  10.1 0.7 copy-done.5
  10.8 0.0 copy-done.6
  10.8 0.0 copy-start.4
  10.8 0.9 %copy-done.4 = bf16[1,1,32,4096]{3,2,1,0:T(8,128)(2,1)S(1)} copy-done((bf16[1,1,32,4096]{3,2,1,0:T(8,128)(2,1)S(1)}, bf16[1,1,32,4096]{3,2,1,0:T(8,128)(2,1)}, u32[]{:S(2)}) %copy-start.4) | copy-done | bytes 262168
  11.7 2.0 %shard_map.138 = (f32[48,4096]{1,0:T(8,128)S(1)}, bf16[8,4096]{1,0:T(8,128)(2,1)S(1)}, bf16[8,4096]{1,0:T(8,128)(2,1)S(1)}, bf16[256,512]{1,0:T(8,128)(2,1)S(1)}...) custom-call(bf16[32,4096]{1,0:T(8,128)(2,1)S(1)} %bitcast.35, ...), custom_call_target="tpu_custom_call" | custom-call | flops 1811939328 | bytes 1785728 | tf_op jit(solution)/shard_map/pallas_call | solution.py:49
  13.7 0.0 copy-start.9
  13.7 0.6 copy-done.9
  14.4 3.1 %all-to-all-done = bf16[16,8,512]{2,1,0:T(8,128)(2,1)S(1)} async-done(((bf16[16,8,512]{2,1,0:T(8,128)(2,1)}), bf16[16,8,512]{2,1,0:T(8,128)(2,1)S(1)}, u32[]{:S(2)}, u32[]{:S(2)}) %all-to-all-start) | async-done | bytes 131104 | tf_op jit(solution)/shard_map/all_to_all | solution.py:479
  17.4 0.0 copy-done
  17.4 0.0 copy-done.1
  17.4 0.6 shard_map.139
  18.0 0.0 copy-done.7
  18.1 0.7 %collective-permute-start = (bf16[8,5120]{1,0:T(8,128)(2,1)S(1)}, bf16[8,5120]{1,0:T(8,128)(2,1)S(1)}, u32[]{:S(2)}, u32[]{:S(2)}) collective-permute-start(bf16[8,5120]{1,0:T(8,128)(2,1)S(1)} %get-tuple-element.34), channel_id=1, source_target_pairs={{0,1},{2,3},{1,0},{3,2},{4,5},{6,7},{5,4},{7,6},{8,9},{10,11},{9,8... | collective-permute-start | bytes 245768 | tf_op jit(solution)/shard_map/ppermute | solution.py:470
  18.8 0.7 collective-permute-start.1
  19.4 0.1 collective-permute-start.4
  19.5 0.7 collective-permute-start.5
  20.2 2.4 %collective-permute-done.even_ref.even_side_ref = bf16[8,5120]{1,0:T(8,128)(2,1)S(1)} collective-permute-done((bf16[8,5120]{1,0:T(8,128)(2,1)S(1)}, bf16[8,5120]{1,0:T(8,128)(2,1)S(1)}, u32[]{:S(2)}, u32[]{:S(2)}) %collective-permute-start) | collective-permute-done | bytes 81952 | tf_op jit(solution)/shard_map/ppermute | solution.py:470
  22.6 0.0 collective-permute-done.1.odd_ref.odd_side_ref
  22.6 0.3 shard_map.140
  22.9 0.1 collective-permute-start.2
  23.0 0.7 collective-permute-start.3
  23.7 0.0 collective-permute-done.4.even_grad_ref
  23.7 0.0 collective-permute-done.5.odd_grad_ref
  23.7 0.5 collective-permute-done.2.even_cross_ref
  24.3 0.0 collective-permute-done.3.odd_cross_ref
  24.3 0.0 copy-done.8
  24.3 0.0 copy-done.10
  24.3 3.1 %shard_map.141 = (bf16[128,1408]{1,0:T(8,128)(2,1)}, bf16[6,6,32,384]{3,2,1,0:T(8,128)(2,1)S(1)}, f32[32,4096]{1,0:T(8,128)S(1)}, bf16[8,4096]{1,0:T(8,128)(2,1)S(1)}, bf16[8,4096]{1,0:T(8,128)(2,1)S(1)}) custom-call(bf16[32,4096]{1,0:T(8,128)(2,1)S(1)} %get-tuple-element.33.merged_ref, bf16[8,5120]{1,0:T(8,128)(2,1)S(1)} %collective-permute-done.even_ref.even_side_ref, ...), custom_call_target="tpu_custom_call" | custom-call | flops 905969664 | bytes 3817472 | tf_op jit(solution)/shard_map/pallas_call | solution.py:49
  27.3 10.2 %all-to-all-start.1 = ((bf16[16,8,1408]{2,1,0:T(8,128)(2,1)}), bf16[16,8,1408]{2,1,0:T(8,128)(2,1)S(1)}, u32[]{:S(2)}, u32[]{:S(2)}) async-start(bf16[16,8,1408]{2,1,0:T(8,128)(2,1)} %bitcast.17), calls=%async_computation.1 | async-start | bytes 720896 | tf_op jit(solution)/shard_map/all_to_all | solution.py:479
  37.6 1.9 %collective-permute-start.6 = (bf16[8,4096]{1,0:T(8,128)(2,1)S(1)}, bf16[8,4096]{1,0:T(8,128)(2,1)S(1)}, u32[]{:S(2)}, u32[]{:S(2)}) collective-permute-start(bf16[8,4096]{1,0:T(8,128)(2,1)S(1)} %get-tuple-element.47), channel_id=1, source_target_pairs={{0,1},{2,3},{1,0},{3,2},{4,5},{6,7},{5,4},{7,6},{8,9},{10,11},{9,8... | collective-permute-start | bytes 196616 | tf_op jit(solution)/shard_map/ppermute | solution.py:470
  39.5 0.7 collective-permute-start.7
  40.2 7.0 %collective-permute-done.6.even_ref = bf16[8,4096]{1,0:T(8,128)(2,1)S(1)} collective-permute-done((bf16[8,4096]{1,0:T(8,128)(2,1)S(1)}, bf16[8,4096]{1,0:T(8,128)(2,1)S(1)}, u32[]{:S(2)}, u32[]{:S(2)}) %collective-permute-start.6) | collective-permute-done | bytes 65568 | tf_op jit(solution)/shard_map/ppermute | solution.py:470
  47.2 0.0 collective-permute-done.7.odd_ref
  47.2 1.1 %shard_map.143 = (bf16[32,4096]{1,0:T(8,128)(2,1)}, bf16[128,512]{1,0:T(8,128)(2,1)S(1)}) custom-call(f32[32,4096]{1,0:T(8,128)S(1)} %get-tuple-element.46.part_ref, s32[8,128]{1,0:T(8,128)S(1)} %get-tuple-element.32.lists_ref, bf16[8,4096]{1,0:T(8,128)(2,1)S(1)} %collective-permute-done.6.even_ref, bf16[8,4096]{1,0:T(8,128)(2,1)S(1)} %collective-permute-done.7.odd_ref, ...), custom_call_target="tpu_custom_call" | custom-call | bytes 1183744 | tf_op jit(solution)/shard_map/pallas_call | solution.py:49
  48.3 1.5 %all-to-all-done.1 = bf16[16,8,1408]{2,1,0:T(8,128)(2,1)S(1)} async-done(((bf16[16,8,1408]{2,1,0:T(8,128)(2,1)}), bf16[16,8,1408]{2,1,0:T(8,128)(2,1)S(1)}, u32[]{:S(2)}, u32[]{:S(2)}) %all-to-all-start.1) | async-done | bytes 360480 | tf_op jit(solution)/shard_map/all_to_all | solution.py:479
  49.8 1.0 %shard_map.144 = bf16[128,1920]{1,0:T(8,128)(2,1)} custom-call(bf16[128,1408]{1,0:T(8,128)(2,1)S(1)} %bitcast.28, bf16[128,512]{1,0:T(8,128)(2,1)S(1)} %get-tuple-element.51.replies_ref), custom_call_target="tpu_custom_call" | custom-call | bytes 983040 | tf_op jit(solution)/shard_map/pallas_call | solution.py:49
  50.8 5.0 %all-to-all-start.2 = ((bf16[16,8,1920]{2,1,0:T(8,128)(2,1)}), bf16[16,8,1920]{2,1,0:T(8,128)(2,1)S(1)}, u32[]{:S(2)}, u32[]{:S(2)}) async-start(bf16[16,8,1920]{2,1,0:T(8,128)(2,1)} %bitcast.19), calls=%async_computation.2 | async-start | bytes 983040 | tf_op jit(solution)/shard_map/all_to_all | solution.py:479
  55.8 0.0 copy-start.2
  55.8 2.2 %shard_map.142 = bf16[32,4096]{1,0:T(8,128)(2,1)} custom-call(bf16[6,6,32,384]{3,2,1,0:T(8,128)(2,1)S(1)} %get-tuple-element.45.pad_ref, bf16[27,64,64]{2,1,0:T(8,128)(2,1)S(1)} %copy-done.3), custom_call_target="tpu_custom_call" | custom-call | flops 905969664 | bytes 1368064 | tf_op jit(solution)/shard_map/pallas_call | solution.py:49
  58.0 12.8 %all-to-all-done.2 = bf16[16,8,1920]{2,1,0:T(8,128)(2,1)S(1)} async-done(((bf16[16,8,1920]{2,1,0:T(8,128)(2,1)}), bf16[16,8,1920]{2,1,0:T(8,128)(2,1)S(1)}, u32[]{:S(2)}, u32[]{:S(2)}) %all-to-all-start.2) | async-done | bytes 491552 | tf_op jit(solution)/shard_map/all_to_all | solution.py:479
  70.8 0.0 copy-done.2
  70.8 1.4 %shard_map.145 = (f32[27,64,64]{2,1,0:T(8,128)}, f32[512,128]{1,0:T(8,128)}, bf16[64,1024]{1,0:T(8,128)(2,1)}) custom-call(bf16[128,1920]{1,0:T(8,128)(2,1)S(1)} %bitcast.27, s32[4,16]{1,0:T(4,128)S(1)} %bitcast.34), custom_call_target="tpu_custom_call" | custom-call | bytes 1327360 | tf_op jit(solution)/shard_map/pallas_call | solution.py:49
  (6 shorter events, 0.0 us)
Async XLA Ops:
  0.6 9.5 %copy-start.3 = (bf16[27,64,64]{2,1,0:T(8,128)(2,1)S(1)}, bf16[27,64,64]{2,1,0:T(8,128)(2,1)}, u32[]{:S(2)}) copy-start(bf16[27,64,64]{2,1,0:T(8,128)(2,1)} %weight_ref.3) | copy-start | bytes 663556
  2.7 14.7 %all-to-all-start = ((bf16[16,8,512]{2,1,0:T(8,128)(2,1)}), bf16[16,8,512]{2,1,0:T(8,128)(2,1)S(1)}, u32[]{:S(2)}, u32[]{:S(2)}) async-start(bf16[16,8,512]{2,1,0:T(8,128)(2,1)} %bitcast.38), calls=%async_computation | async-start | bytes 262144 | tf_op jit(solution)/shard_map/all_to_all | solution.py:479
  10.1 0.7 copy-start.5
  10.1 0.7 copy-start.6
  10.8 1.0 %copy-start.4 = (bf16[1,1,32,4096]{3,2,1,0:T(8,128)(2,1)S(1)}, bf16[1,1,32,4096]{3,2,1,0:T(8,128)(2,1)}, u32[]{:S(2)}) copy-start(bf16[1,1,32,4096]{3,2,1,0:T(8,128)(2,1)} %param.19) | copy-start | bytes 786436
  11.7 5.7 %copy-start = (bf16[8,128,64]{1,2,0:T(8,128)(2,1)S(1)}, bf16[8,128,64]{1,2,0:T(8,128)(2,1)}, u32[]{:S(2)}) copy-start(bf16[8,128,64]{1,2,0:T(8,128)(2,1)} %param.13) | copy-start | bytes 393220
  11.7 5.7 %copy-start.1 = (bf16[1,1,32,4096]{3,2,1,0:T(8,128)(2,1)S(1)}, bf16[1,1,32,4096]{3,2,1,0:T(8,128)(2,1)}, u32[]{:S(2)}) copy-start(bf16[1,1,32,4096]{3,2,1,0:T(8,128)(2,1)} %param.10) | copy-start | bytes 786436
  13.7 0.6 copy-start.9
  14.4 3.7 %copy-start.7 = (bf16[9,32,64]{2,1,0:T(8,128)(2,1)}, bf16[9,32,64]{2,1,0:T(8,128)(2,1)S(1)}, u32[]{:S(2)}) copy-start(bf16[9,32,64]{2,1,0:T(8,128)(2,1)S(1)} %get-tuple-element.41.mains_ref) | copy-start | bytes 110596
  18.1 4.5 %collective-permute-start = (bf16[8,5120]{1,0:T(8,128)(2,1)S(1)}, bf16[8,5120]{1,0:T(8,128)(2,1)S(1)}, u32[]{:S(2)}, u32[]{:S(2)}) collective-permute-start(bf16[8,5120]{1,0:T(8,128)(2,1)S(1)} %get-tuple-element.34), channel_id=1, source_target_pairs={{0,1},{2,3},{1,0},{3,2},{4,5},{6,7},{5,4},{7,6},{8,9},{10,11},{9,8... | collective-permute-start | bytes 245768 | tf_op jit(solution)/shard_map/ppermute | solution.py:470
  18.8 3.8 %collective-permute-start.1 = (bf16[8,5120]{1,0:T(8,128)(2,1)S(1)}, bf16[8,5120]{1,0:T(8,128)(2,1)S(1)}, u32[]{:S(2)}, u32[]{:S(2)}) collective-permute-start(bf16[8,5120]{1,0:T(8,128)(2,1)S(1)} %get-tuple-element.35), channel_id=1, source_target_pairs={{1,2},{2,1},{5,6},{6,5},{9,10},{10,9},{13,14},{14,13},{17,18},{18,... | collective-permute-start | bytes 245768 | tf_op jit(solution)/shard_map/ppermute | solution.py:470
  19.4 4.3 %collective-permute-start.4 = (bf16[8,4096]{1,0:T(8,128)(2,1)S(1)}, bf16[8,4096]{1,0:T(8,128)(2,1)S(1)}, u32[]{:S(2)}, u32[]{:S(2)}) collective-permute-start(bf16[8,4096]{1,0:T(8,128)(2,1)S(1)} %get-tuple-element.38), channel_id=1, source_target_pairs={{0,4},{8,12},{4,0},{12,8},{1,5},{9,13},{5,1},{13,9},{2,6},{10,14},... | collective-permute-start | bytes 196616 | tf_op jit(solution)/shard_map/ppermute | solution.py:470
  19.5 4.2 %collective-permute-start.5 = (bf16[8,4096]{1,0:T(8,128)(2,1)S(1)}, bf16[8,4096]{1,0:T(8,128)(2,1)S(1)}, u32[]{:S(2)}, u32[]{:S(2)}) collective-permute-start(bf16[8,4096]{1,0:T(8,128)(2,1)S(1)} %get-tuple-element.39), channel_id=1, source_target_pairs={{4,8},{8,4},{5,9},{9,5},{6,10},{10,6},{7,11},{11,7},{20,24},{24,20... | collective-permute-start | bytes 196616 | tf_op jit(solution)/shard_map/ppermute | solution.py:470
  22.6 1.7 %copy-start.8 = (bf16[9,32,64]{2,1,0:T(8,128)(2,1)S(1)}, bf16[9,32,64]{2,1,0:T(8,128)(2,1)}, u32[]{:S(2)}) copy-start(bf16[9,32,64]{2,1,0:T(8,128)(2,1)} %copy-done.7) | copy-start | bytes 110596
  22.6 1.7 %copy-start.10 = (bf16[9,32,128]{2,1,0:T(8,128)(2,1)S(1)}, bf16[9,32,128]{2,1,0:T(8,128)(2,1)}, u32[]{:S(2)}) copy-start(bf16[9,32,128]{2,1,0:T(8,128)(2,1)} %copy-done.9) | copy-start | bytes 221188
  22.9 1.3 %collective-permute-start.2 = (bf16[8,4096]{1,0:T(8,128)(2,1)S(1)}, bf16[8,4096]{1,0:T(8,128)(2,1)S(1)}, u32[]{:S(2)}, u32[]{:S(2)}) collective-permute-start(bf16[8,4096]{1,0:T(8,128)(2,1)S(1)} %get-tuple-element.36), channel_id=1, source_target_pairs={{0,4},{8,12},{4,0},{12,8},{1,5},{9,13},{5,1},{13,9},{2,6},{10,14},... | collective-permute-start | bytes 196616 | tf_op jit(solution)/shard_map/ppermute | solution.py:470
  23.0 1.2 %collective-permute-start.3 = (bf16[8,4096]{1,0:T(8,128)(2,1)S(1)}, bf16[8,4096]{1,0:T(8,128)(2,1)S(1)}, u32[]{:S(2)}, u32[]{:S(2)}) collective-permute-start(bf16[8,4096]{1,0:T(8,128)(2,1)S(1)} %get-tuple-element.37), channel_id=1, source_target_pairs={{4,8},{8,4},{5,9},{9,5},{6,10},{10,6},{7,11},{11,7},{20,24},{24,20... | collective-permute-start | bytes 196616 | tf_op jit(solution)/shard_map/ppermute | solution.py:470
  27.3 22.4 %all-to-all-start.1 = ((bf16[16,8,1408]{2,1,0:T(8,128)(2,1)}), bf16[16,8,1408]{2,1,0:T(8,128)(2,1)S(1)}, u32[]{:S(2)}, u32[]{:S(2)}) async-start(bf16[16,8,1408]{2,1,0:T(8,128)(2,1)} %bitcast.17), calls=%async_computation.1 | async-start | bytes 720896 | tf_op jit(solution)/shard_map/all_to_all | solution.py:479
  37.6 9.6 %collective-permute-start.6 = (bf16[8,4096]{1,0:T(8,128)(2,1)S(1)}, bf16[8,4096]{1,0:T(8,128)(2,1)S(1)}, u32[]{:S(2)}, u32[]{:S(2)}) collective-permute-start(bf16[8,4096]{1,0:T(8,128)(2,1)S(1)} %get-tuple-element.47), channel_id=1, source_target_pairs={{0,1},{2,3},{1,0},{3,2},{4,5},{6,7},{5,4},{7,6},{8,9},{10,11},{9,8... | collective-permute-start | bytes 196616 | tf_op jit(solution)/shard_map/ppermute | solution.py:470
  39.5 7.7 %collective-permute-start.7 = (bf16[8,4096]{1,0:T(8,128)(2,1)S(1)}, bf16[8,4096]{1,0:T(8,128)(2,1)S(1)}, u32[]{:S(2)}, u32[]{:S(2)}) collective-permute-start(bf16[8,4096]{1,0:T(8,128)(2,1)S(1)} %get-tuple-element.48), channel_id=1, source_target_pairs={{1,2},{2,1},{5,6},{6,5},{9,10},{10,9},{13,14},{14,13},{17,18},{18,... | collective-permute-start | bytes 196616 | tf_op jit(solution)/shard_map/ppermute | solution.py:470
  50.8 20.0 %all-to-all-start.2 = ((bf16[16,8,1920]{2,1,0:T(8,128)(2,1)}), bf16[16,8,1920]{2,1,0:T(8,128)(2,1)S(1)}, u32[]{:S(2)}, u32[]{:S(2)}) async-start(bf16[16,8,1920]{2,1,0:T(8,128)(2,1)} %bitcast.19), calls=%async_computation.2 | async-start | bytes 983040 | tf_op jit(solution)/shard_map/all_to_all | solution.py:479
  55.8 15.0 %copy-start.2 = (s32[1,1,16,4]{2,3,1,0:T(4,128)S(1)}, s32[1,1,16,4]{2,3,1,0:T(4,128)}, u32[]{:S(2)}) copy-start(s32[1,1,16,4]{2,3,1,0:T(4,128)} %param.18) | copy-start | bytes 772

commit v8 on v7

--- a/solution.py
+++ b/solution.py
@@ -6,6 +6,7 @@
 from jax import lax
 from jax.experimental import pallas as pl
 from jax.experimental.pallas import tpu as pltpu
+from jax.sharding import Mesh
 from jax.sharding import PartitionSpec as P
 
 BF = jnp.bfloat16
@@ -58,16 +59,6 @@
 
 def shape(dims, dtype=BF):
     return jax.ShapeDtypeStruct(dims, dtype)
-
-
-def send_index(sends, group, pieces=1, j=0):
-    capacity, devices = sends.shape
-    lanes = devices * group
-    spread = ones_where(iota((devices, lanes), 1) // group == iota((devices, lanes), 0))
-    rows = dot(sends.astype(F32).astype(BF), spread)
-    slot = (iota((capacity, lanes), 1) % group * pieces + j) // 2
-    picked = jnp.where(slot == iota((capacity, lanes), 0), rows, 0.0)
-    return jnp.sum(picked, axis=0, keepdims=True).astype(I32)
 
 
 def items_out(sends_ref, items_ref, out_ref):
@@ -114,6 +105,7 @@
 
 
 GX, GY = (0, 1)
+GX_AXES = ("x", "core")
 
 
 def by_pair(lists_ref, axis, of_next, of_prev):
@@ -298,7 +290,8 @@
 
 def weight_grad_body(
     merged_ref, even_side_ref, odd_side_ref, even_cross_ref, odd_cross_ref, even_grad_ref, odd_grad_ref,
-    turned_ref, mains_ref, ends_ref, lists_ref, ext_ref, parents_ref, sums_ref, pad_ref, part_ref, to_even_ref, to_odd_ref, table_ref,
+    turned_ref, mains_ref, ends_ref, lists_ref, ext_ref, parents_ref,
+    kept_ref, given_ref, pad_ref, part_ref, to_even_ref, to_odd_ref, table_ref, sums_ref,
 ):
     bricks, width = merged_ref.shape
     face = even_side_ref.shape[0]
@@ -320,7 +313,7 @@
     count = sums_ref.shape[0]
     parts = up_sum.shape[0] // count
     for q in range(parts):
-        sums_ref[:, q * coarse : (q + 1) * coarse] = up_sum[q * count : (q + 1) * count].astype(BF)
+        sums_ref[:, q * coarse : (q + 1) * coarse] = up_sum[q * count : (q + 1) * count]
     lower_half = iota((rows, 2 * C), 1) < C
     zero = jnp.zeros((rows, 2 * C), BF)
     for x in range(4):
@@ -360,7 +353,14 @@
     for pair in range(7):
         both = [jnp.where(lanes_low, sums[14 * h + 2 * pair], sums[14 * h + 2 * pair + 1]) for h in range(2)]
         at = parts * coarse + pair * 2 * C
-        sums_ref[:, at : at + 2 * C] = jnp.concatenate(both, axis=0).astype(BF)
+        sums_ref[:, at : at + 2 * C] = jnp.concatenate(both, axis=0)
+    kept, given = by_pair(lists_ref, GX, sums_ref[: count // 2], sums_ref[count // 2 :])
+    kept_ref[...] = kept
+    given_ref[...] = given.astype(BF)
+
+
+def pair_sum_body(kept_ref, given_ref, out_ref):
+    out_ref[...] = (kept_ref[...] + given_ref[...].astype(F32)).astype(BF)
 
 
 def inputs_at(pad_ref, e):
@@ -398,7 +398,7 @@
         out_ref[:, width:] = owners.astype(BF)
 
 
-def fine_grad_body(part_ref, lists_ref, even_ref, odd_ref, up_ref, grad_ref, replies_ref):
+def fine_grad_body(part_ref, lists_ref, even_ref, odd_ref, up_ref, grad_ref, replies_ref, across):
     bricks = part_ref.shape[0]
     face = even_ref.shape[0]
     from_next, from_prev = from_pairs(lists_ref, GY, even_ref, odd_ref)
@@ -407,53 +407,83 @@
     items = dot(stack_parities(grad_ref[...]), up_ref[...]).astype(BF)
     items = jnp.concatenate([items[v * bricks : (v + 1) * bricks] for v in range(8)], axis=1)
     half = items.shape[1] // 2
+    count, both_lanes = replies_ref.shape
+    pieces = both_lanes // 2 // half
+    capacity, group = chip_slots(count, pieces, across)
+    slots = slots_of(lists_ref, bricks)
+    row = iota((count, bricks), 0)
+    for other in range(2):
+        owner = device_of(row // group, lists_ref, other, across)
+        for j in range(pieces):
+            piece = row % group * pieces + j
+            named = owner * capacity + piece // 2 == slots
+            rows = dot(ones_where(named & (piece % 2 == 0)), items[:, :half])
+            rows += dot(ones_where(named & (piece % 2 == 1)), items[:, half:])
+            at = (other * pieces + j) * half
+            replies_ref[:, at : at + half] = rows.astype(BF)
+
+
+def chip_slots(count, pieces, across):
+    group = count // (across[0] * across[1] // 2)
+    return group * pieces // 2, group
+
+
+def device_of(chip, lists_ref, other, across):
+    core = jnp.broadcast_to(lists_ref[5:6, GX : GX + 1], chip.shape)
+    core = 1 - core if other else core
+    return (chip // across[1] * 2 + core) * across[1] + chip % across[1]
+
+
+def share_body(sums_ref, replies_ref, out_ref, across):
     count, item_lanes = replies_ref.shape
-    slots = slots_of(lists_ref, bricks)
-    for j in range(item_lanes // half):
-        piece = iota((count, bricks), 0) * (item_lanes // half) + j
-        named = piece // 2 == slots
-        rows = dot(ones_where(named & (piece % 2 == 0)), items[:, :half])
-        rows += dot(ones_where(named & (piece % 2 == 1)), items[:, half:])
-        replies_ref[:, j * half : (j + 1) * half] = rows.astype(BF)
-
-
-def share_body(sums_ref, replies_ref, out_ref, devices):
-    count, item_lanes = replies_ref.shape
-    share = count // devices
+    share = count // (across[0] * across[1] // 2)
     same = iota((count, count), 0) % share == iota((count, count), 1) % share
     out_ref[:, :item_lanes] = replies_ref[...]
     out_ref[:, item_lanes:] = dot(ones_where(same), sums_ref[...]).astype(BF)
 
 
-def coarse_grad(back_ref, sends_ref, out_ref):
+def coarse_grad(arrivals, sends_ref, lists_ref, out_ref, across):
     capacity, devices = sends_ref.shape
     count, item_width = out_ref.shape
     half = item_width // 2
-    lanes = back_ref.shape[0]
-    pieces = 2 * capacity * devices // lanes
-    group = lanes // devices
+    lanes = arrivals[0].shape[0]
+    pieces = arrivals[0].shape[1] // half
+    _, group = chip_slots(lanes, pieces, across)
+    sends = sends_ref[...].astype(F32).astype(BF)
+    lane = iota((1, lanes), 1)
+    totals = [None, None]
+    for other in range(2):
+        source = device_of(lane // group, lists_ref, other, across)
+        rows = dot(sends, ones_where(source == iota((devices, lanes), 0)))
+        for j in range(pieces):
+            piece = lane % group * pieces + j
+            picked = jnp.where(piece // 2 == iota((capacity, lanes), 0), rows, 0.0)
+            index = jnp.sum(picked, axis=0, keepdims=True).astype(I32)
+            named = iota((count, lanes), 0) == index
+            for h in range(2):
+                part = dot(ones_where(named & (piece % 2 == h)), arrivals[other][:, j * half : (j + 1) * half])
+                totals[h] = part if totals[h] is None else totals[h] + part
     for h in range(2):
-        total = None
-        for j in range(pieces):
-            index = send_index(sends_ref[...], group, pieces, j)
-            place = iota((count, lanes), 1) % group * pieces + j
-            chosen = (iota((count, lanes), 0) == index) & (place % 2 == h)
-            part = dot(ones_where(chosen), back_ref[:, j * half : (j + 1) * half])
-            total = part if total is None else total + part
-        out_ref[:, h * half : (h + 1) * half] = total.astype(BF)
-
-
-def last_body(back_ref, sends_ref, conv_ref, up_ref, out_ref, scale):
-    coarse_grad(back_ref, sends_ref, out_ref)
-    count, width = back_ref.shape
+        out_ref[:, h * half : (h + 1) * half] = totals[h].astype(BF)
+
+
+def last_body(back_ref, given_ref, sends_ref, lists_ref, conv_ref, up_ref, out_ref, item_lanes, across, scale):
+    half_count = back_ref.shape[0]
+    items = (back_ref[:, :item_lanes], given_ref[:, item_lanes : 2 * item_lanes])
+    coarse_grad(items, sends_ref, lists_ref, out_ref, across)
     coarse = up_ref.shape[1]
+    count = 2 * half_count
     parts = up_ref.shape[0] // count
-    at = width - 14 * C - parts * coarse
+    own = back_ref[:, 2 * item_lanes :].astype(F32) * scale
+    others = given_ref[:, 2 * item_lanes :].astype(F32) * scale
+    first, second = by_pair(lists_ref, GX, own, others)
+    at = 0
     for q in range(parts):
-        up_ref[q * count : (q + 1) * count] = back_ref[:, at : at + coarse].astype(F32) * scale
+        up_ref[q * count : q * count + half_count] = first[:, at : at + coarse]
+        up_ref[q * count + half_count : (q + 1) * count] = second[:, at : at + coarse]
         at += coarse
     for pair in range(7):
-        turned = back_ref[:, at : at + 2 * C].astype(F32).T * scale
+        turned = jnp.concatenate([first[:, at : at + 2 * C], second[:, at : at + 2 * C]], axis=0).T
         at += 2 * C
         for h in range(2):
             for s in range(2):
@@ -462,21 +492,21 @@
                     conv_ref[o] = turned[s * C : (s + 1) * C, h * C : (h + 1) * C]
 
 
+def swap(value, axis, first):
+    count = lax.axis_size(axis)
+    lower = range(first, count - 1, 2)
+    return lax.ppermute(value, axis, [(i, i + 1) for i in lower] + [(i + 1, i) for i in lower])
+
+
 def swap_pairs(to_even, to_odd, axis):
-    count = lax.axis_size(axis)
-
-    def swap(value, first):
-        lower = range(first, count - 1, 2)
-        return lax.ppermute(value, axis, [(i, i + 1) for i in lower] + [(i + 1, i) for i in lower])
-
-    from_odd = swap(to_odd, 1)
-    return swap(to_even, 0), from_odd
-
-
-def trade_rows(values, devices):
+    return swap(to_even, axis, 0), swap(to_odd, axis, 1)
+
+
+def trade_rows(values, axes):
     rows, width = values.shape
+    devices = math.prod(lax.axis_size(axis) for axis in axes)
     grid_view = values.reshape(devices, rows // devices, width)
-    return lax.all_to_all(grid_view, ("gx", "gy"), split_axis=0, concat_axis=0, tiled=True).reshape(rows, width)
+    return lax.all_to_all(grid_view, axes, split_axis=0, concat_axis=0, tiled=True).reshape(rows, width)
 
 
 def on_device(
@@ -488,8 +518,8 @@
     cot = cotangent[0, 0]
     bricks, width = fine.shape
     face = side_sends.shape[-1]
-    across_x, across_y = (lax.axis_size("gx"), lax.axis_size("gy"))
-    devices = across_x * across_y
+    across = (lax.axis_size(GX_AXES), lax.axis_size("gy"))
+    devices = across[0] * across[1]
     capacity = coarse_sends.shape[-1]
     item_count, item_width = items.shape
     coarse = up_weight.shape[1]
@@ -502,7 +532,7 @@
     up_turned = up_weight.transpose(0, 2, 1).reshape(8 * C, coarse)
     half = item_width // 2
     count = 2 * C
-    item_lanes = capacity * devices * item_width // count
+    item_lanes = capacity * devices // 2 * item_width // (count // 2)
     sums_width = 8 * C * coarse // count + 14 * C
     rows = shape((bricks, width))
     face_rows = shape((face, width))
@@ -517,9 +547,9 @@
         scratch=[pltpu.VMEM(a.shape, a.dtype) for a in listed] + [pltpu.SemaphoreType.DMA((len(listed),))],
         in_hbm=True,
     )
-    received = trade_rows(outgoing, devices)
+    received = trade_rows(outgoing, ("x", "core", "gy"))
     lane = jnp.arange(128, dtype=I32)[None]
-    parity = jnp.where(lane == GX, lax.axis_index("gx") % 2, lax.axis_index("gy") % 2).astype(I32)
+    parity = jnp.where(lane == GX, lax.axis_index("core"), lax.axis_index("gy") % 2).astype(I32)
     table_rows = start + 2 * face
     ext_grad, to_even, to_odd, turned, mains, ends, lists = call(
         table_grad_body,
@@ -530,34 +560,43 @@
         cot, conv_weight, near, lists, parity,
         scratch=[band, pltpu.VMEM((6, 6, bricks, WIDE), F32)], flops=2 * conv_flops,
     )
-    cross_grads = swap_pairs(to_even, to_odd, "gx")
+    cross_grads = swap_pairs(to_even, to_odd, GX_AXES)
     merged, parents, to_even, to_odd = call(
         merge_body, [rows, shape((8 * bricks, coarse)), faces_and_parents, faces_and_parents],
         received, up_turned, fine, lists,
     )
     sides = swap_pairs(to_even, to_odd, "gy")
     to_even, to_odd = call(cross_body, [face_rows, face_rows], merged, *sides, lists)
-    crosses = swap_pairs(to_even, to_odd, "gx")
-    sums, pad, fine_part, to_even, to_odd = call(
+    crosses = swap_pairs(to_even, to_odd, GX_AXES)
+    half_sums = (count // 2, sums_width)
+    kept, given, pad, fine_part, to_even, to_odd = call(
         weight_grad_body,
-        [shape((count, sums_width)), shape((6, 6, bricks, WIDE)), shape((bricks, width), F32), face_rows, face_rows],
+        [
+            shape(half_sums, F32), shape(half_sums), shape((6, 6, bricks, WIDE)), shape((bricks, width), F32),
+            face_rows, face_rows,
+        ],
         merged, *sides, *crosses, *cross_grads, turned, mains, ends, lists, ext_grad, parents,
-        scratch=[pltpu.VMEM((table_rows, width), BF)], flops=conv_flops,
-    )
-    sums = trade_rows(sums, devices)
+        scratch=[pltpu.VMEM((table_rows, width), BF), pltpu.VMEM((count, sums_width), F32)], flops=conv_flops,
+    )
+    given = swap(given, "core", 0)
+    (sums,) = call(pair_sum_body, [shape(half_sums)], kept, given)
+    sums = trade_rows(sums, ("x", "gy"))
     side_grads = swap_pairs(to_even, to_odd, "gy")
     grad_fine, replies = call(
-        fine_grad_body, [rows, shape((count, item_lanes))], fine_part, lists, *side_grads, up_turned
+        functools.partial(fine_grad_body, across=across), [rows, shape((count // 2, 2 * item_lanes))],
+        fine_part, lists, *side_grads, up_turned,
     )
     (output,) = call(conv_body, [rows], pad, conv_weight, scratch=[band], flops=conv_flops)
     (back,) = call(
-        functools.partial(share_body, devices=devices), [shape((count, item_lanes + sums_width))], sums, replies
-    )
-    back = trade_rows(back, devices)
+        functools.partial(share_body, across=across), [shape((count // 2, 2 * item_lanes + sums_width))], sums, replies
+    )
+    back = trade_rows(back, ("x", "gy"))
+    given = swap(back, "core", 0)
     scale = 1.0 / math.sqrt(64 * bricks * devices)
     grad_conv, grad_up, coarse_grad = call(
-        functools.partial(last_body, scale=scale),
-        [shape((27, C, C), F32), shape((8 * C, coarse), F32), shape((item_count, item_width))], back, sends,
+        functools.partial(last_body, item_lanes=item_lanes, across=across, scale=scale),
+        [shape((27, C, C), F32), shape((8 * C, coarse), F32), shape((item_count, item_width))],
+        back, given, sends, lists,
     )
     return (
         output.reshape(1, 1, bricks, width),
@@ -569,11 +608,14 @@
 
 
 def solution(mesh):
-    split = P(("groups", "gx"), "gy", None, None)
-    placed = (split, split, P(), P(), split, split, split, P(("groups", "gx"), "gy", None), split, split)
+    groups, across_x, across_y = mesh.devices.shape
+    split_mesh = Mesh(mesh.devices.reshape(groups, across_x // 2, 2, across_y), ("groups", "x", "core", "gy"))
+    rows = ("groups", "x", "core")
+    split = P(rows, "gy", None, None)
+    placed = (split, split, P(), P(), split, split, split, P(rows, "gy", None), split, split)
     return jax.shard_map(
         on_device,
-        mesh=mesh,
+        mesh=split_mesh,
         in_specs=placed,
         out_specs=(split, split, split, P("groups", None, None), P("groups", None, None)),
         check_vma=False,

time: 72.7 us -> 66.4 us (0.913)
  waiting for transfers between devices: 27.2 us -> 12.2 us
  blocking collectives: 0 us -> 14.1 us
  starting transfers between devices: 28 us -> 23.4 us
  Pallas kernels: 13.8 us -> 12.9 us
    all_to_all x0 -> x1, blocking collectives: none -> 14.1 us  [trade_rows(): lax.all_to_all(grid_view, axes, split_axis=0, concat_axis=0, tiled=True)]
    all_to_all x3 -> x2, waiting for transfers between devices: 17.3 us -> 4.19 us  [trade_rows(): lax.all_to_all(grid_view, axes, split_axis=0, concat_axis=0, tiled=True)]
    all_to_all x3 -> x2, starting transfers between devices: 22.6 us -> 13 us  [trade_rows(): lax.all_to_all(grid_view, axes, split_axis=0, concat_axis=0, tiled=True)]
    ppermute x8 -> x10, starting transfers between devices: 5.44 us -> 10.4 us  [swap(): lax.ppermute(value, axis, [(i, i + 1) for i in lower] + [(i + 1, i) for i...]
    ppermute x8 -> x10, waiting for transfers between devices: 9.96 us -> 8.03 us  [swap(): lax.ppermute(value, axis, [(i, i + 1) for i in lower] + [(i + 1, i) for i...]
    pallas_call x9 -> x10, Pallas kernels: 13.8 us -> 12.9 us  [call(): pl.pallas_call(body, out_shape=tuple(outs), in_specs=[pl.BlockSpec(memory...]
    unnamed x22 -> x14, local copies, waits for them, and re-layouts: 2.27 us -> 2.33 us
  transfers between devices with their start and end apart: 11 -> 12, of which waited for: 6 -> 6; matrix products, arithmetic and copies ran while one was open for 0% -> 0% of each run, Pallas kernels for 8% -> 9%
where the time goes in v8:
time: 66.4 us; the launch traced here: 65.8 us
  starting transfers between devices  23.4 us (35%)
  blocking collectives  14.1 us (21%)
  Pallas kernels  12.9 us (19%)
  waiting for transfers between devices  12.2 us (18%)
  local copies, waits for them, and re-layouts  2.33 us (4%)
  between operations  0.8 us (1%)
    all_to_all x1, blocking collectives, trade_rows(): lax.all_to_all(grid_view, axes, split_axis=0, concat_axis=0, tiled=True)  14.1 us
    all_to_all x2, starting transfers between devices, trade_rows(): lax.all_to_all(grid_view, axes, split_axis=0, concat_axis=0, tiled=True)  13 us
    pallas_call x10, Pallas kernels, call(): pl.pallas_call(body, out_shape=tuple(outs), in_specs=[pl.BlockSpec(memory...  12.9 us
    ppermute x10, starting transfers between devices, swap(): lax.ppermute(value, axis, [(i, i + 1) for i in lower] + [(i + 1, i) for i...  10.4 us
    ppermute x10, waiting for transfers between devices, swap(): lax.ppermute(value, axis, [(i, i + 1) for i in lower] + [(i + 1, i) for i...  8.03 us
    all_to_all x2, waiting for transfers between devices, trade_rows(): lax.all_to_all(grid_view, axes, split_axis=0, concat_axis=0, tiled=True)  4.19 us
    unnamed x14, local copies, waits for them, and re-layouts  2.33 us
  transfers between devices with their start and end apart: 12, of which 6 were waited for; matrix products, arithmetic and copies ran while one was open for 0% of the time, Pallas kernels for 9%

profile of v8, /device:TPU:0, one launch (start us, length us, event | category | flops | bytes accessed | tf_op | source)
XLA Modules:
  0.0 65.8 jit_solution(705791484581281016)
XLA Ops:
  0.6 0.0 copy-start.3
  0.6 2.0 %shard_map.137 = (bf16[128,512]{1,0:T(8,128)(2,1)}, s32[8,128]{1,0:T(8,128)}) custom-call(s32[4,16]{1,0:T(4,128)} %bitcast.35, bf16[64,1024]{1,0:T(8,128)(2,1)} %bitcast.39, s32[2,8]{1,0:T(2,128)} %bitcast.41, s32[2,8]{1,0:T(2,128)} %bitcast.42, s32[1,32]{1,0:T(1,128)} %bitcast.43), custom_call_target="tpu_custom_call" | custom-call | bytes 266752 | tf_op jit(solution)/shard_map/pallas_call | solution.py:50
  2.7 7.4 %all-to-all-start = ((bf16[16,8,512]{2,1,0:T(8,128)(2,1)}), bf16[16,8,512]{2,1,0:T(8,128)(2,1)S(1)}, u32[]{:S(2)}, u32[]{:S(2)}) async-start(bf16[16,8,512]{2,1,0:T(8,128)(2,1)} %bitcast.40), calls=%async_computation | async-start | bytes 262144 | tf_op jit(solution)/shard_map/all_to_all | solution.py:509
  10.1 0.0 copy-start.6
  10.1 0.0 copy-done.3
  10.1 0.7 copy-done.6
  10.8 0.0 copy-start.4
  10.8 0.9 %copy-done.4 = bf16[1,1,32,4096]{3,2,1,0:T(8,128)(2,1)S(1)} copy-done((bf16[1,1,32,4096]{3,2,1,0:T(8,128)(2,1)S(1)}, bf16[1,1,32,4096]{3,2,1,0:T(8,128)(2,1)}, u32[]{:S(2)}) %copy-start.4) | copy-done | bytes 262168
  11.7 0.0 copy-start.5
  11.7 0.7 %copy-done.5 = s32[1,1,32,27]{2,1,3,0:T(1,128)S(1)} copy-done((s32[1,1,32,27]{2,1,3,0:T(1,128)S(1)}, s32[1,1,32,27]{2,1,3,0:T(1,128)}, u32[]{:S(2)}) %copy-start.5) | copy-done | bytes 3480
  12.4 0.0 copy-start
  12.4 0.0 copy-start.1
  12.4 2.0 %shard_map.138 = (f32[48,4096]{1,0:T(8,128)S(1)}, bf16[8,4096]{1,0:T(8,128)(2,1)S(1)}, bf16[8,4096]{1,0:T(8,128)(2,1)S(1)}, bf16[256,512]{1,0:T(8,128)(2,1)S(1)}...) custom-call(bf16[32,4096]{1,0:T(8,128)(2,1)S(1)} %bitcast.37, ...), custom_call_target="tpu_custom_call" | custom-call | flops 1811939328 | bytes 1785728 | tf_op jit(solution)/shard_map/pallas_call | solution.py:50
  14.4 3.0 %all-to-all-done = bf16[16,8,512]{2,1,0:T(8,128)(2,1)S(1)} async-done(((bf16[16,8,512]{2,1,0:T(8,128)(2,1)}), bf16[16,8,512]{2,1,0:T(8,128)(2,1)S(1)}, u32[]{:S(2)}, u32[]{:S(2)}) %all-to-all-start) | async-done | bytes 131104 | tf_op jit(solution)/shard_map/all_to_all | solution.py:509
  17.4 0.0 copy-done
  17.4 0.0 copy-done.1
  17.4 0.6 shard_map.139
  18.0 0.7 %collective-permute-start = (bf16[8,5120]{1,0:T(8,128)(2,1)S(1)}, bf16[8,5120]{1,0:T(8,128)(2,1)S(1)}, u32[]{:S(2)}, u32[]{:S(2)}) collective-permute-start(bf16[8,5120]{1,0:T(8,128)(2,1)S(1)} %get-tuple-element.35), channel_id=1, source_target_pairs={{0,1},{2,3},{1,0},{3,2},{4,5},{6,7},{5,4},{7,6},{8,9},{10,11},{9,8... | collective-permute-start | bytes 245768 | tf_op jit(solution)/shard_map/ppermute | solution.py:498
  18.8 0.7 collective-permute-start.1
  19.4 0.1 collective-permute-start.4
  19.5 0.7 %collective-permute-start.5 = (bf16[8,4096]{1,0:T(8,128)(2,1)S(1)}, bf16[8,4096]{1,0:T(8,128)(2,1)S(1)}, u32[]{:S(2)}, u32[]{:S(2)}) collective-permute-start(bf16[8,4096]{1,0:T(8,128)(2,1)S(1)} %get-tuple-element.40), channel_id=1, source_target_pairs={{4,8},{8,4},{5,9},{9,5},{6,10},{10,6},{7,11},{11,7},{20,24},{24,20... | collective-permute-start | bytes 196616 | tf_op jit(solution)/shard_map/ppermute | solution.py:498
  20.2 2.4 %collective-permute-done.even_ref.even_side_ref = bf16[8,5120]{1,0:T(8,128)(2,1)S(1)} collective-permute-done((bf16[8,5120]{1,0:T(8,128)(2,1)S(1)}, bf16[8,5120]{1,0:T(8,128)(2,1)S(1)}, u32[]{:S(2)}, u32[]{:S(2)}) %collective-permute-start) | collective-permute-done | bytes 81952 | tf_op jit(solution)/shard_map/ppermute | solution.py:498
  22.6 0.0 collective-permute-done.1.odd_ref.odd_side_ref
  22.6 0.4 shard_map.140
  22.9 0.1 collective-permute-start.2
  23.0 0.7 %collective-permute-start.3 = (bf16[8,4096]{1,0:T(8,128)(2,1)S(1)}, bf16[8,4096]{1,0:T(8,128)(2,1)S(1)}, u32[]{:S(2)}, u32[]{:S(2)}) collective-permute-start(bf16[8,4096]{1,0:T(8,128)(2,1)S(1)} %get-tuple-element.38), channel_id=1, source_target_pairs={{4,8},{8,4},{5,9},{9,5},{6,10},{10,6},{7,11},{11,7},{20,24},{24,20... | collective-permute-start | bytes 196616 | tf_op jit(solution)/shard_map/ppermute | solution.py:498
  23.7 0.0 collective-permute-done.4.even_grad_ref
  23.7 0.0 collective-permute-done.5.odd_grad_ref
  23.7 0.5 collective-permute-done.2.even_cross_ref
  24.3 0.0 collective-permute-done.3.odd_cross_ref
  24.3 2.3 %shard_map.141 = (f32[64,1408]{1,0:T(8,128)S(1)}, bf16[64,1408]{1,0:T(8,128)(2,1)S(1)}, bf16[6,6,32,384]{3,2,1,0:T(8,128)(2,1)S(1)}, f32[32,4096]{1,0:T(8,128)S(...) custom-call(bf16[32,4096]{1,0:T(8,128)(2,1)S(1)} %get-tuple-element.34.merged_ref, ...), custom_call_target="tpu_custom_call" | custom-call | flops 905969664 | bytes 3997696 | tf_op jit(solution)/shard_map/pallas_call | solution.py:50
  26.6 4.9 %collective-permute-start.8 = (bf16[64,1408]{1,0:T(8,128)(2,1)S(1)}, bf16[64,1408]{1,0:T(8,128)(2,1)S(1)}, u32[]{:S(2)}, u32[]{:S(2)}) collective-permute-start(bf16[64,1408]{1,0:T(8,128)(2,1)S(1)} %get-tuple-element.52), channel_id=1, source_target_pairs={{0,4},{4,0},{1,5},{5,1},{2,6},{6,2},{3,7},{7,3},{8,12},{12,8},{9,1... | collective-permute-start | bytes 540680 | tf_op jit(solution)/shard_map/ppermute | solution.py:498
  31.5 1.0 %collective-permute-done.8.given_ref = bf16[64,1408]{1,0:T(8,128)(2,1)S(1)} collective-permute-done((bf16[64,1408]{1,0:T(8,128)(2,1)S(1)}, bf16[64,1408]{1,0:T(8,128)(2,1)S(1)}, u32[]{:S(2)}, u32[]{:S(2)}) %collective-permute-start.8) | collective-permute-done | bytes 180256 | tf_op jit(solution)/shard_map/ppermute | solution.py:498
  32.6 0.7 %shard_map.144 = bf16[64,1408]{1,0:T(8,128)(2,1)} custom-call(f32[64,1408]{1,0:T(8,128)S(1)} %get-tuple-element.51.kept_ref, bf16[64,1408]{1,0:T(8,128)(2,1)S(1)} %collective-permute-done.8.given_ref), custom_call_target="tpu_custom_call" | custom-call | bytes 720896 | tf_op jit(solution)/shard_map/pallas_call | solution.py:50
  33.3 5.7 %all-to-all-start.1 = ((bf16[8,8,1408]{2,1,0:T(8,128)(2,1)}), bf16[8,8,1408]{2,1,0:T(8,128)(2,1)S(1)}, u32[]{:S(2)}, u32[]{:S(2)}) async-start(bf16[8,8,1408]{2,1,0:T(8,128)(2,1)} %bitcast.17), calls=%async_computation.1 | async-start | bytes 360448 | tf_op jit(solution)/shard_map/all_to_all | solution.py:509
  38.9 2.0 %collective-permute-start.6 = (bf16[8,4096]{1,0:T(8,128)(2,1)S(1)}, bf16[8,4096]{1,0:T(8,128)(2,1)S(1)}, u32[]{:S(2)}, u32[]{:S(2)}) collective-permute-start(bf16[8,4096]{1,0:T(8,128)(2,1)S(1)} %get-tuple-element.48), channel_id=1, source_target_pairs={{0,1},{2,3},{1,0},{3,2},{4,5},{6,7},{5,4},{7,6},{8,9},{10,11},{9,8... | collective-permute-start | bytes 196616 | tf_op jit(solution)/shard_map/ppermute | solution.py:498
  40.9 0.7 collective-permute-start.7
  41.6 4.0 %collective-permute-done.6.even_ref = bf16[8,4096]{1,0:T(8,128)(2,1)S(1)} collective-permute-done((bf16[8,4096]{1,0:T(8,128)(2,1)S(1)}, bf16[8,4096]{1,0:T(8,128)(2,1)S(1)}, u32[]{:S(2)}, u32[]{:S(2)}) %collective-permute-start.6) | collective-permute-done | bytes 65568 | tf_op jit(solution)/shard_map/ppermute | solution.py:498
  45.6 0.0 collective-permute-done.7.odd_ref
  45.6 1.1 %shard_map.143 = (bf16[32,4096]{1,0:T(8,128)(2,1)}, bf16[64,1024]{1,0:T(8,128)(2,1)S(1)}) custom-call(f32[32,4096]{1,0:T(8,128)S(1)} %get-tuple-element.47.part_ref, s32[8,128]{1,0:T(8,128)S(1)} %get-tuple-element.33.lists_ref, bf16[8,4096]{1,0:T(8,128)(2,1)S(1)} %collective-permute-done.6.even_ref, bf16[8,4096]{1,0:T(8,128)(2,1)S(1)} %collective-permute-done.7.odd_ref, ...), custom_call_target="tpu_custom_call" | custom-call | bytes 1183744 | tf_op jit(solution)/shard_map/pallas_call | solution.py:50
  46.7 1.2 %all-to-all-done.1 = bf16[8,8,1408]{2,1,0:T(8,128)(2,1)S(1)} async-done(((bf16[8,8,1408]{2,1,0:T(8,128)(2,1)}), bf16[8,8,1408]{2,1,0:T(8,128)(2,1)S(1)}, u32[]{:S(2)}, u32[]{:S(2)}) %all-to-all-start.1) | async-done | bytes 180256 | tf_op jit(solution)/shard_map/all_to_all | solution.py:509
  47.9 0.2 shard_map.145
  48.1 14.1 %all_to_all.15 = bf16[8,8,2432]{2,1,0:T(8,128)(2,1)S(1)} all-to-all(bf16[8,8,2432]{2,1,0:T(8,128)(2,1)S(1)} %bitcast.29), channel_id=1, replica_groups=mesh['groups'=2,'x'=2,'core'=2,'gy'=4] {'x','gy'}, dimensions={0} | all-to-all | bytes 622592 | tf_op jit(solution)/shard_map/all_to_all | solution.py:509
  62.2 0.0 collective-permute-start.9
  62.3 2.2 %shard_map.142 = bf16[32,4096]{1,0:T(8,128)(2,1)} custom-call(bf16[6,6,32,384]{3,2,1,0:T(8,128)(2,1)S(1)} %get-tuple-element.46.pad_ref, bf16[27,64,64]{2,1,0:T(8,128)(2,1)S(1)} %copy-done.3), custom_call_target="tpu_custom_call" | custom-call | flops 905969664 | bytes 1368064 | tf_op jit(solution)/shard_map/pallas_call | solution.py:50
  64.5 0.0 collective-permute-done.9.given_ref
  64.5 0.0 copy-done.2
  64.5 1.4 %shard_map.146 = (f32[27,64,64]{2,1,0:T(8,128)}, f32[512,128]{1,0:T(8,128)}, bf16[64,1024]{1,0:T(8,128)(2,1)}) custom-call(bf16[64,2432]{1,0:T(8,128)(2,1)S(1)} %bitcast.28, bf16[64,2432]{1,0:T(8,128)(2,1)S(1)} %collective-permute-done.9.given_ref, s32[4,16]{1,0:T(4,128)S(1)} %bitcast.36, s32[8,128]{1,0:T(8,128)S(1)} %get-tuple-element.33.lists_ref), custom_call_target="tpu_custom_call" | custom-call | bytes 1462528 | tf_op jit(solution)/shard_map/pallas_call | solution.py:50
  (2 shorter events, 0.0 us)
Async XLA Ops:
  0.6 9.5 %copy-start.3 = (bf16[27,64,64]{2,1,0:T(8,128)(2,1)S(1)}, bf16[27,64,64]{2,1,0:T(8,128)(2,1)}, u32[]{:S(2)}) copy-start(bf16[27,64,64]{2,1,0:T(8,128)(2,1)} %weight_ref.3) | copy-start | bytes 663556
  2.7 14.7 %all-to-all-start = ((bf16[16,8,512]{2,1,0:T(8,128)(2,1)}), bf16[16,8,512]{2,1,0:T(8,128)(2,1)S(1)}, u32[]{:S(2)}, u32[]{:S(2)}) async-start(bf16[16,8,512]{2,1,0:T(8,128)(2,1)} %bitcast.40), calls=%async_computation | async-start | bytes 262144 | tf_op jit(solution)/shard_map/all_to_all | solution.py:509
  10.1 0.7 %copy-start.6 = (s32[8,128]{1,0:T(8,128)S(1)}, s32[8,128]{1,0:T(8,128)}, u32[]{:S(2)}) copy-start(s32[8,128]{1,0:T(8,128)} %get-tuple-element.32.lists_ref) | copy-start | bytes 12292
  10.8 0.9 %copy-start.4 = (bf16[1,1,32,4096]{3,2,1,0:T(8,128)(2,1)S(1)}, bf16[1,1,32,4096]{3,2,1,0:T(8,128)(2,1)}, u32[]{:S(2)}) copy-start(bf16[1,1,32,4096]{3,2,1,0:T(8,128)(2,1)} %param.19) | copy-start | bytes 786436
  11.7 0.7 %copy-start.5 = (s32[1,1,32,27]{2,1,3,0:T(1,128)S(1)}, s32[1,1,32,27]{2,1,3,0:T(1,128)}, u32[]{:S(2)}) copy-start(s32[1,1,32,27]{2,1,3,0:T(1,128)} %param.14) | copy-start | bytes 10372
  12.4 5.0 %copy-start = (bf16[8,128,64]{1,2,0:T(8,128)(2,1)S(1)}, bf16[8,128,64]{1,2,0:T(8,128)(2,1)}, u32[]{:S(2)}) copy-start(bf16[8,128,64]{1,2,0:T(8,128)(2,1)} %param.13) | copy-start | bytes 393220
  12.4 5.0 %copy-start.1 = (bf16[1,1,32,4096]{3,2,1,0:T(8,128)(2,1)S(1)}, bf16[1,1,32,4096]{3,2,1,0:T(8,128)(2,1)}, u32[]{:S(2)}) copy-start(bf16[1,1,32,4096]{3,2,1,0:T(8,128)(2,1)} %param.10) | copy-start | bytes 786436
  18.0 4.5 %collective-permute-start = (bf16[8,5120]{1,0:T(8,128)(2,1)S(1)}, bf16[8,5120]{1,0:T(8,128)(2,1)S(1)}, u32[]{:S(2)}, u32[]{:S(2)}) collective-permute-start(bf16[8,5120]{1,0:T(8,128)(2,1)S(1)} %get-tuple-element.35), channel_id=1, source_target_pairs={{0,1},{2,3},{1,0},{3,2},{4,5},{6,7},{5,4},{7,6},{8,9},{10,11},{9,8... | collective-permute-start | bytes 245768 | tf_op jit(solution)/shard_map/ppermute | solution.py:498
  18.8 3.8 %collective-permute-start.1 = (bf16[8,5120]{1,0:T(8,128)(2,1)S(1)}, bf16[8,5120]{1,0:T(8,128)(2,1)S(1)}, u32[]{:S(2)}, u32[]{:S(2)}) collective-permute-start(bf16[8,5120]{1,0:T(8,128)(2,1)S(1)} %get-tuple-element.36), channel_id=1, source_target_pairs={{1,2},{2,1},{5,6},{6,5},{9,10},{10,9},{13,14},{14,13},{17,18},{18,... | collective-permute-start | bytes 245768 | tf_op jit(solution)/shard_map/ppermute | solution.py:498
  19.4 4.3 %collective-permute-start.4 = (bf16[8,4096]{1,0:T(8,128)(2,1)S(1)}, bf16[8,4096]{1,0:T(8,128)(2,1)S(1)}, u32[]{:S(2)}, u32[]{:S(2)}) collective-permute-start(bf16[8,4096]{1,0:T(8,128)(2,1)S(1)} %get-tuple-element.39), channel_id=1, source_target_pairs={{0,4},{8,12},{4,0},{12,8},{1,5},{9,13},{5,1},{13,9},{2,6},{10,14},... | collective-permute-start | bytes 196616 | tf_op jit(solution)/shard_map/ppermute | solution.py:498
  19.5 4.2 %collective-permute-start.5 = (bf16[8,4096]{1,0:T(8,128)(2,1)S(1)}, bf16[8,4096]{1,0:T(8,128)(2,1)S(1)}, u32[]{:S(2)}, u32[]{:S(2)}) collective-permute-start(bf16[8,4096]{1,0:T(8,128)(2,1)S(1)} %get-tuple-element.40), channel_id=1, source_target_pairs={{4,8},{8,4},{5,9},{9,5},{6,10},{10,6},{7,11},{11,7},{20,24},{24,20... | collective-permute-start | bytes 196616 | tf_op jit(solution)/shard_map/ppermute | solution.py:498
  22.9 1.3 %collective-permute-start.2 = (bf16[8,4096]{1,0:T(8,128)(2,1)S(1)}, bf16[8,4096]{1,0:T(8,128)(2,1)S(1)}, u32[]{:S(2)}, u32[]{:S(2)}) collective-permute-start(bf16[8,4096]{1,0:T(8,128)(2,1)S(1)} %get-tuple-element.37), channel_id=1, source_target_pairs={{0,4},{8,12},{4,0},{12,8},{1,5},{9,13},{5,1},{13,9},{2,6},{10,14},... | collective-permute-start | bytes 196616 | tf_op jit(solution)/shard_map/ppermute | solution.py:498
  23.0 1.2 %collective-permute-start.3 = (bf16[8,4096]{1,0:T(8,128)(2,1)S(1)}, bf16[8,4096]{1,0:T(8,128)(2,1)S(1)}, u32[]{:S(2)}, u32[]{:S(2)}) collective-permute-start(bf16[8,4096]{1,0:T(8,128)(2,1)S(1)} %get-tuple-element.38), channel_id=1, source_target_pairs={{4,8},{8,4},{5,9},{9,5},{6,10},{10,6},{7,11},{11,7},{20,24},{24,20... | collective-permute-start | bytes 196616 | tf_op jit(solution)/shard_map/ppermute | solution.py:498
  26.6 5.9 %collective-permute-start.8 = (bf16[64,1408]{1,0:T(8,128)(2,1)S(1)}, bf16[64,1408]{1,0:T(8,128)(2,1)S(1)}, u32[]{:S(2)}, u32[]{:S(2)}) collective-permute-start(bf16[64,1408]{1,0:T(8,128)(2,1)S(1)} %get-tuple-element.52), channel_id=1, source_target_pairs={{0,4},{4,0},{1,5},{5,1},{2,6},{6,2},{3,7},{7,3},{8,12},{12,8},{9,1... | collective-permute-start | bytes 540680 | tf_op jit(solution)/shard_map/ppermute | solution.py:498
  33.3 14.7 %all-to-all-start.1 = ((bf16[8,8,1408]{2,1,0:T(8,128)(2,1)}), bf16[8,8,1408]{2,1,0:T(8,128)(2,1)S(1)}, u32[]{:S(2)}, u32[]{:S(2)}) async-start(bf16[8,8,1408]{2,1,0:T(8,128)(2,1)} %bitcast.17), calls=%async_computation.1 | async-start | bytes 360448 | tf_op jit(solution)/shard_map/all_to_all | solution.py:509
  38.9 6.7 %collective-permute-start.6 = (bf16[8,4096]{1,0:T(8,128)(2,1)S(1)}, bf16[8,4096]{1,0:T(8,128)(2,1)S(1)}, u32[]{:S(2)}, u32[]{:S(2)}) collective-permute-start(bf16[8,4096]{1,0:T(8,128)(2,1)S(1)} %get-tuple-element.48), channel_id=1, source_target_pairs={{0,1},{2,3},{1,0},{3,2},{4,5},{6,7},{5,4},{7,6},{8,9},{10,11},{9,8... | collective-permute-start | bytes 196616 | tf_op jit(solution)/shard_map/ppermute | solution.py:498
  40.9 4.7 %collective-permute-start.7 = (bf16[8,4096]{1,0:T(8,128)(2,1)S(1)}, bf16[8,4096]{1,0:T(8,128)(2,1)S(1)}, u32[]{:S(2)}, u32[]{:S(2)}) collective-permute-start(bf16[8,4096]{1,0:T(8,128)(2,1)S(1)} %get-tuple-element.49), channel_id=1, source_target_pairs={{1,2},{2,1},{5,6},{6,5},{9,10},{10,9},{13,14},{14,13},{17,18},{18,... | collective-permute-start | bytes 196616 | tf_op jit(solution)/shard_map/ppermute | solution.py:498
  62.2 2.2 %collective-permute-start.9 = (bf16[64,2432]{1,0:T(8,128)(2,1)S(1)}, bf16[64,2432]{1,0:T(8,128)(2,1)S(1)}, u32[]{:S(2)}, u32[]{:S(2)}) collective-permute-start(bf16[64,2432]{1,0:T(8,128)(2,1)S(1)} %bitcast.27), channel_id=1, source_target_pairs={{0,4},{4,0},{1,5},{5,1},{2,6},{6,2},{3,7},{7,3},{8,12},{12,8},{9,1... | collective-permute-start | bytes 933896 | tf_op jit(solution)/shard_map/ppermute | solution.py:498
  62.2 2.2 %copy-start.2 = (s32[1,1,16,4]{2,3,1,0:T(4,128)S(1)}, s32[1,1,16,4]{2,3,1,0:T(4,128)}, u32[]{:S(2)}) copy-start(s32[1,1,16,4]{2,3,1,0:T(4,128)} %param.18) | copy-start | bytes 772

commit v9 on v8

--- a/solution.py
+++ b/solution.py
@@ -61,31 +61,38 @@
     return jax.ShapeDtypeStruct(dims, dtype)
 
 
-def items_out(sends_ref, items_ref, out_ref):
+def items_out(sends_ref, items_ref, out_ref, across):
     capacity, devices = sends_ref.shape
     count, width = items_ref.shape
     half = width // 2
     group = 2 * capacity
-    lanes = devices * group
-    spread = ones_where(iota((lanes, devices), 0) // group == iota((lanes, devices), 1))
+    lanes = out_ref.shape[0]
+    chip = iota((lanes, devices), 0) // group
     slot = iota((lanes, capacity), 0) % group // 2
-    values = dot_nt(spread, sends_ref[...].astype(F32).astype(BF))
-    item = jnp.sum(jnp.where(slot == iota((lanes, capacity), 1), values, 0.0), axis=1, keepdims=True).astype(I32)
-    place = jnp.where(item < count, item + iota((lanes, 1), 0) % 2 * count, -1)
-    chosen = ones_where(iota((lanes, 2 * count), 1) == place)
-    out_ref[...] = dot(chosen, jnp.concatenate([items_ref[:, :half], items_ref[:, half:]], axis=0)).astype(BF)
-
-
-def merge(received_ref, slots, up_ref, fine_ref, merged_ref, parents_ref):
+    sends = sends_ref[...].astype(F32).astype(BF)
+    items = jnp.concatenate([items_ref[:, :half], items_ref[:, half:]], axis=0)
+    for core in range(2):
+        device = (chip // across[1] * 2 + core) * across[1] + chip % across[1]
+        values = dot_nt(ones_where(device == iota((lanes, devices), 1)), sends)
+        item = jnp.sum(jnp.where(slot == iota((lanes, capacity), 1), values, 0.0), axis=1, keepdims=True).astype(I32)
+        place = jnp.where(item < count, item + iota((lanes, 1), 0) % 2 * count, -1)
+        chosen = ones_where(iota((lanes, 2 * count), 1) == place)
+        out_ref[:, core * half : (core + 1) * half] = dot(chosen, items).astype(BF)
+
+
+def merge(arrived_ref, given_ref, lists_ref, up_ref, fine_ref, merged_ref, parents_ref, across):
     bricks = fine_ref.shape[0]
-    lanes, half = received_ref.shape
-    slot = column_of(slots)
-    place = iota((bricks, lanes), 1)
-    named = place // 2 == slot
-    received = received_ref[...]
-    parents = jnp.concatenate(
-        [dot(ones_where(named & (place % 2 == h)), received) for h in (0, 1)], axis=1
-    ).astype(BF)
+    lanes = arrived_ref.shape[0]
+    half = arrived_ref.shape[1] // 2
+    own = [by_pair(lists_ref, GX, r[:, :half].astype(F32), r[:, half:].astype(F32))[0] for r in (arrived_ref, given_ref)]
+    received = jnp.concatenate(own, axis=0).astype(BF)
+    slot = column_of(slots_of(lists_ref, bricks))
+    capacity, group = chip_slots(lanes, 1, across)
+    row = iota((bricks, lanes), 1)
+    sources = [device_of(row // group, lists_ref, other, across) for other in range(2)]
+    named = slot == jnp.concatenate([source * capacity + row % group // 2 for source in sources], axis=1)
+    odd = iota((bricks, 2 * lanes), 1) % 2
+    parents = jnp.concatenate([dot(ones_where(named & (odd == h)), received) for h in (0, 1)], axis=1).astype(BF)
     coarse = 2 * half // 8
     stacked = jnp.concatenate([parents[:, v * coarse : (v + 1) * coarse] for v in range(8)], axis=0)
     parents_ref[...] = stacked
@@ -271,7 +278,7 @@
 
 def first_body(
     sends_hbm, items_hbm, sides_hbm, crosses_hbm, slots_hbm, out_ref, lists_ref,
-    sends_ref, items_ref, sides_ref, crosses_ref, slots_ref, arrived,
+    sends_ref, items_ref, sides_ref, crosses_ref, slots_ref, arrived, across,
 ):
     sources = (sends_hbm, items_hbm, sides_hbm, crosses_hbm, slots_hbm)
     places = (sends_ref, items_ref, sides_ref, crosses_ref, slots_ref)
@@ -285,35 +292,47 @@
     lists_ref[0:2, :face] = sides_ref[...]
     lists_ref[2:4, :face] = crosses_ref[...]
     lists_ref[4:5, :bricks] = slots_ref[...]
-    items_out(sends_ref, items_ref, out_ref)
-
-
-def weight_grad_body(
-    merged_ref, even_side_ref, odd_side_ref, even_cross_ref, odd_cross_ref, even_grad_ref, odd_grad_ref,
-    turned_ref, mains_ref, ends_ref, lists_ref, ext_ref, parents_ref,
-    kept_ref, given_ref, pad_ref, part_ref, to_even_ref, to_odd_ref, table_ref, sums_ref,
+    items_out(sends_ref, items_ref, out_ref, across)
+
+
+def side_grad_body(
+    ext_ref, lists_ref, even_grad_ref, odd_grad_ref, even_side_ref, odd_side_ref, parents_ref,
+    part_ref, to_even_ref, to_odd_ref, up_sums_ref,
 ):
-    bricks, width = merged_ref.shape
-    face = even_side_ref.shape[0]
-    rows = bricks + 4 * face
-    high, low = from_pairs(lists_ref, GY, even_side_ref, odd_side_ref)
-    above, below = from_pairs(lists_ref, GX, even_cross_ref, odd_cross_ref)
-    table_ref[:bricks] = merged_ref[...]
-    table_ref[bricks:] = stack_rows(low[:, :width], high[:, :width], below, above)
+    bricks, width = part_ref.shape
+    face = to_even_ref.shape[0]
     from_next, from_prev = from_pairs(lists_ref, GX, even_grad_ref, odd_grad_ref)
     total = add_rows(ext_ref[...], crosses_of(lists_ref, face), from_next, from_prev)
     part_ref[...] = total[:bricks]
     to_even, to_odd = by_pair(lists_ref, GY, total[bricks + face :], total[bricks : bricks + face])
     to_even_ref[...] = to_even.astype(BF)
     to_odd_ref[...] = to_odd.astype(BF)
-    side_parents = stack_lanes(stack_rows(low[:, width:], high[:, width:]), parents_ref.shape[1])
+    high, low = by_pair(
+        lists_ref, GY, even_side_ref[:, width:].astype(F32), odd_side_ref[:, width:].astype(F32)
+    )
+    side_parents = stack_lanes(stack_rows(low, high), parents_ref.shape[1])
     grads = [stack_parities(total[:bricks].astype(BF)), stack_parities(total[bricks:].astype(BF))]
     up_sum = dot_tn(jnp.concatenate(grads, axis=0), jnp.concatenate([parents_ref[...], side_parents], axis=0))
     coarse = up_sum.shape[1]
+    count = up_sums_ref.shape[0]
+    for q in range(up_sum.shape[0] // count):
+        up_sums_ref[:, q * coarse : (q + 1) * coarse] = up_sum[q * count : (q + 1) * count]
+
+
+def weight_grad_body(
+    merged_ref, even_side_ref, odd_side_ref, even_cross_ref, odd_cross_ref, turned_ref, mains_ref, ends_ref, lists_ref,
+    up_sums_ref, kept_ref, given_ref, pad_ref, table_ref, sums_ref,
+):
+    bricks, width = merged_ref.shape
+    face = even_side_ref.shape[0]
+    rows = bricks + 4 * face
+    high, low = by_pair(lists_ref, GY, even_side_ref[:, :width].astype(F32), odd_side_ref[:, :width].astype(F32))
+    above, below = from_pairs(lists_ref, GX, even_cross_ref, odd_cross_ref)
+    table_ref[:bricks] = merged_ref[...]
+    table_ref[bricks:] = stack_rows(low, high, below, above)
     count = sums_ref.shape[0]
-    parts = up_sum.shape[0] // count
-    for q in range(parts):
-        sums_ref[:, q * coarse : (q + 1) * coarse] = up_sum[q * count : (q + 1) * count]
+    up_lanes = up_sums_ref.shape[1]
+    sums_ref[:, :up_lanes] = up_sums_ref[...]
     lower_half = iota((rows, 2 * C), 1) < C
     zero = jnp.zeros((rows, 2 * C), BF)
     for x in range(4):
@@ -352,7 +371,7 @@
     sums.append(jnp.zeros((C, 2 * C), F32))
     for pair in range(7):
         both = [jnp.where(lanes_low, sums[14 * h + 2 * pair], sums[14 * h + 2 * pair + 1]) for h in range(2)]
-        at = parts * coarse + pair * 2 * C
+        at = up_lanes + pair * 2 * C
         sums_ref[:, at : at + 2 * C] = jnp.concatenate(both, axis=0)
     kept, given = by_pair(lists_ref, GX, sums_ref[: count // 2], sums_ref[count // 2 :])
     kept_ref[...] = kept
@@ -369,7 +388,8 @@
     return pad_ref[ex : ex + 4, ey : ey + 4].reshape(16 * bricks, WIDE)
 
 
-def conv_body(pad_ref, weight_ref, out_ref, band_ref):
+def conv_body(pad_ref, weight_ref, lists_ref, out_ref, again_ref, band_ref):
+    again_ref[...] = lists_ref[...]
     bricks = pad_ref.shape[2]
     build_bands(weight_ref, band_ref)
     total = None
@@ -387,10 +407,12 @@
     return base + dot(chosen, stack_rows(first, second))
 
 
-def merge_body(received_ref, up_ref, fine_ref, lists_ref, merged_ref, parents_ref, a_ref, b_ref):
+def merge_body(
+    arrived_ref, given_ref, up_ref, fine_ref, lists_ref, merged_ref, parents_ref, a_ref, b_ref, across
+):
     bricks, width = fine_ref.shape
     face = a_ref.shape[0]
-    parents = merge(received_ref, slots_of(lists_ref, bricks), up_ref, fine_ref, merged_ref, parents_ref)
+    parents = merge(arrived_ref, given_ref, lists_ref, up_ref, fine_ref, merged_ref, parents_ref, across)
     lists = sides_of(lists_ref, face)
     lists = by_pair(lists_ref, GY, lists[0:1], lists[1:2])
     for out_ref, rows, owners in zip((a_ref, b_ref), pick_rows(lists, merged_ref[...]), pick_rows(lists, parents)):
@@ -434,7 +456,8 @@
     return (chip // across[1] * 2 + core) * across[1] + chip % across[1]
 
 
-def share_body(sums_ref, replies_ref, out_ref, across):
+def share_body(sums_ref, replies_ref, lists_ref, out_ref, again_ref, across):
+    again_ref[...] = lists_ref[...]
     count, item_lanes = replies_ref.shape
     share = count // (across[0] * across[1] // 2)
     same = iota((count, count), 0) % share == iota((count, count), 1) % share
@@ -543,11 +566,12 @@
 
     listed = (sends, items, sides, crosses, slots)
     outgoing, lists = call(
-        first_body, [shape((2 * capacity * devices, half)), lists_shape], *listed,
+        functools.partial(first_body, across=across), [shape((capacity * devices, item_width)), lists_shape], *listed,
         scratch=[pltpu.VMEM(a.shape, a.dtype) for a in listed] + [pltpu.SemaphoreType.DMA((len(listed),))],
         in_hbm=True,
     )
-    received = trade_rows(outgoing, ("x", "core", "gy"))
+    arrived = trade_rows(outgoing, ("x", "gy"))
+    arrived = (arrived, swap(arrived, "core", 0))
     lane = jnp.arange(128, dtype=I32)[None]
     parity = jnp.where(lane == GX, lax.axis_index("core"), lax.axis_index("gy") % 2).astype(I32)
     table_rows = start + 2 * face
@@ -562,33 +586,37 @@
     )
     cross_grads = swap_pairs(to_even, to_odd, GX_AXES)
     merged, parents, to_even, to_odd = call(
-        merge_body, [rows, shape((8 * bricks, coarse)), faces_and_parents, faces_and_parents],
-        received, up_turned, fine, lists,
+        functools.partial(merge_body, across=across), [rows, shape((8 * bricks, coarse)), faces_and_parents, faces_and_parents],
+        *arrived, up_turned, fine, lists,
     )
     sides = swap_pairs(to_even, to_odd, "gy")
     to_even, to_odd = call(cross_body, [face_rows, face_rows], merged, *sides, lists)
     crosses = swap_pairs(to_even, to_odd, GX_AXES)
     half_sums = (count // 2, sums_width)
-    kept, given, pad, fine_part, to_even, to_odd = call(
-        weight_grad_body,
-        [
-            shape(half_sums, F32), shape(half_sums), shape((6, 6, bricks, WIDE)), shape((bricks, width), F32),
-            face_rows, face_rows,
-        ],
-        merged, *sides, *crosses, *cross_grads, turned, mains, ends, lists, ext_grad, parents,
+    fine_part, to_even, to_odd, up_sums = call(
+        side_grad_body,
+        [shape((bricks, width), F32), face_rows, face_rows, shape((count, sums_width - 14 * C), F32)],
+        ext_grad, lists, *cross_grads, *sides, parents,
+    )
+    side_grads = swap_pairs(to_even, to_odd, "gy")
+    kept, given, pad = call(
+        weight_grad_body, [shape(half_sums, F32), shape(half_sums), shape((6, 6, bricks, WIDE))],
+        merged, *sides, *crosses, turned, mains, ends, lists, up_sums,
         scratch=[pltpu.VMEM((table_rows, width), BF), pltpu.VMEM((count, sums_width), F32)], flops=conv_flops,
     )
     given = swap(given, "core", 0)
     (sums,) = call(pair_sum_body, [shape(half_sums)], kept, given)
     sums = trade_rows(sums, ("x", "gy"))
-    side_grads = swap_pairs(to_even, to_odd, "gy")
     grad_fine, replies = call(
         functools.partial(fine_grad_body, across=across), [rows, shape((count // 2, 2 * item_lanes))],
         fine_part, lists, *side_grads, up_turned,
     )
-    (output,) = call(conv_body, [rows], pad, conv_weight, scratch=[band], flops=conv_flops)
-    (back,) = call(
-        functools.partial(share_body, across=across), [shape((count // 2, 2 * item_lanes + sums_width))], sums, replies
+    output, lists = call(
+        conv_body, [rows, lists_shape], pad, conv_weight, lists, scratch=[band], flops=conv_flops
+    )
+    back, lists = call(
+        functools.partial(share_body, across=across),
+        [shape((count // 2, 2 * item_lanes + sums_width)), lists_shape], sums, replies, lists,
     )
     back = trade_rows(back, ("x", "gy"))
     given = swap(back, "core", 0)

time: 66.4 us -> 71.6 us (1.078)
  waiting for transfers between devices: 12.2 us -> 17.3 us
  blocking collectives: 14.1 us -> 15.1 us
    all_to_all x2, waiting for transfers between devices: 4.19 us -> 7.5 us  [trade_rows(): lax.all_to_all(grid_view, axes, split_axis=0, concat_axis=0, tiled=True)]
    ppermute x10 -> x11, waiting for transfers between devices: 8.03 us -> 9.82 us  [swap(): lax.ppermute(value, axis, [(i, i + 1) for i in lower] + [(i + 1, i) for i...]
    all_to_all x1, blocking collectives: 14.1 us -> 15.1 us  [trade_rows(): lax.all_to_all(grid_view, axes, split_axis=0, concat_axis=0, tiled=True)]
    pallas_call x10 -> x11, Pallas kernels: 12.9 us -> 13.4 us  [call(): pl.pallas_call(body, out_shape=tuple(outs), in_specs=[pl.BlockSpec(memory...]
    ppermute x10 -> x11, starting transfers between devices: 10.4 us -> 10.2 us  [swap(): lax.ppermute(value, axis, [(i, i + 1) for i in lower] + [(i + 1, i) for i...]
  transfers between devices with their start and end apart: 12 -> 13, of which waited for: 6 -> 5; matrix products, arithmetic and copies ran while one was open for 0% -> 0% of each run, Pallas kernels for 9% -> 9%
where the time goes in v9:
time: 71.6 us; the launch traced here: 71.1 us
  starting transfers between devices  22.7 us (32%)
  waiting for transfers between devices  17.3 us (24%)
  blocking collectives  15.1 us (21%)
  Pallas kernels  13.4 us (19%)
  local copies, waits for them, and re-layouts  1.68 us (2%)
  between operations  0.81 us (1%)
    all_to_all x1, blocking collectives, trade_rows(): lax.all_to_all(grid_view, axes, split_axis=0, concat_axis=0, tiled=True)  15.1 us
    pallas_call x11, Pallas kernels, call(): pl.pallas_call(body, out_shape=tuple(outs), in_specs=[pl.BlockSpec(memory...  13.4 us
    all_to_all x2, starting transfers between devices, trade_rows(): lax.all_to_all(grid_view, axes, split_axis=0, concat_axis=0, tiled=True)  12.5 us
    ppermute x11, starting transfers between devices, swap(): lax.ppermute(value, axis, [(i, i + 1) for i in lower] + [(i + 1, i) for i...  10.2 us
    ppermute x11, waiting for transfers between devices, swap(): lax.ppermute(value, axis, [(i, i + 1) for i in lower] + [(i + 1, i) for i...  9.82 us
    all_to_all x2, waiting for transfers between devices, trade_rows(): lax.all_to_all(grid_view, axes, split_axis=0, concat_axis=0, tiled=True)  7.5 us
    unnamed x14, local copies, waits for them, and re-layouts  1.68 us
  transfers between devices with their start and end apart: 13, of which 5 were waited for; matrix products, arithmetic and copies ran while one was open for 0% of the time, Pallas kernels for 9%

profile of v9, /device:TPU:0, one launch (start us, length us, event | category | flops | bytes accessed | tf_op | source)
XLA Modules:
  0.0 71.1 jit_solution(15748229559674136161)
XLA Ops:
  0.6 0.0 copy-start.3
  0.6 2.3 %shard_map.137 = (bf16[64,1024]{1,0:T(8,128)(2,1)}, s32[8,128]{1,0:T(8,128)}) custom-call(s32[4,16]{1,0:T(4,128)} %bitcast.36, bf16[64,1024]{1,0:T(8,128)(2,1)} %bitcast.40, s32[2,8]{1,0:T(2,128)} %bitcast.42, s32[2,8]{1,0:T(2,128)} %bitcast.43, s32[1,32]{1,0:T(1,128)} %bitcast.44), custom_call_target="tpu_custom_call" | custom-call | bytes 266752 | tf_op jit(solution)/shard_map/pallas_call | solution.py:50
  2.9 7.3 %all-to-all-start = ((bf16[8,8,1024]{2,1,0:T(8,128)(2,1)}), bf16[8,8,1024]{2,1,0:T(8,128)(2,1)S(1)}, u32[]{:S(2)}, u32[]{:S(2)}) async-start(bf16[8,8,1024]{2,1,0:T(8,128)(2,1)} %bitcast.41), calls=%async_computation | async-start | bytes 262144 | tf_op jit(solution)/shard_map/all_to_all | solution.py:532
  10.2 0.0 copy-start.6
  10.2 7.5 %all-to-all-done = bf16[8,8,1024]{2,1,0:T(8,128)(2,1)S(1)} async-done(((bf16[8,8,1024]{2,1,0:T(8,128)(2,1)}), bf16[8,8,1024]{2,1,0:T(8,128)(2,1)S(1)}, u32[]{:S(2)}, u32[]{:S(2)}) %all-to-all-start) | async-done | bytes 131104 | tf_op jit(solution)/shard_map/all_to_all | solution.py:532
  17.7 0.0 collective-permute-start
  17.7 0.0 copy-done.3
  17.7 0.0 copy-done.6
  17.7 0.0 copy-start.4
  17.7 0.9 %copy-done.4 = bf16[1,1,32,4096]{3,2,1,0:T(8,128)(2,1)S(1)} copy-done((bf16[1,1,32,4096]{3,2,1,0:T(8,128)(2,1)S(1)}, bf16[1,1,32,4096]{3,2,1,0:T(8,128)(2,1)}, u32[]{:S(2)}) %copy-start.4) | copy-done | bytes 262168
  18.7 0.7 copy-done.5
  19.4 2.0 %shard_map.138 = (f32[48,4096]{1,0:T(8,128)S(1)}, bf16[8,4096]{1,0:T(8,128)(2,1)S(1)}, bf16[8,4096]{1,0:T(8,128)(2,1)S(1)}, bf16[256,512]{1,0:T(8,128)(2,1)S(1)}...) custom-call(bf16[32,4096]{1,0:T(8,128)(2,1)S(1)} %bitcast.38, ...), custom_call_target="tpu_custom_call" | custom-call | flops 1811939328 | bytes 1785728 | tf_op jit(solution)/shard_map/pallas_call | solution.py:50
  21.3 0.0 collective-permute-done.given_ref
  21.4 0.0 copy-done
  21.4 0.0 copy-done.1
  21.4 0.6 shard_map.139
  22.0 0.3 collective-permute-start.1
  22.3 0.7 collective-permute-start.2
  23.0 0.4 collective-permute-start.5
  23.3 0.7 collective-permute-start.6
  24.0 2.9 %collective-permute-done.1.even_ref.even_side_ref = bf16[8,5120]{1,0:T(8,128)(2,1)S(1)} collective-permute-done((bf16[8,5120]{1,0:T(8,128)(2,1)S(1)}, bf16[8,5120]{1,0:T(8,128)(2,1)S(1)}, u32[]{:S(2)}, u32[]{:S(2)}) %collective-permute-start.1) | collective-permute-done | bytes 81952 | tf_op jit(solution)/shard_map/ppermute | solution.py:521
  26.9 0.0 collective-permute-done.2.odd_ref.odd_side_ref
  26.9 0.4 shard_map.140
  27.3 0.1 collective-permute-start.3
  27.4 0.7 collective-permute-start.4
  28.1 0.0 collective-permute-done.5.even_grad_ref
  28.1 0.0 collective-permute-done.6.odd_grad_ref
  28.1 0.6 shard_map.141
  28.7 0.0 collective-permute-done.3.even_cross_ref
  28.7 0.0 collective-permute-done.4.odd_cross_ref
  28.7 2.0 %shard_map.142 = (f32[64,1408]{1,0:T(8,128)S(1)}, bf16[64,1408]{1,0:T(8,128)(2,1)S(1)}, bf16[6,6,32,384]{3,2,1,0:T(8,128)(2,1)S(1)}) custom-call(bf16[32,4096]{1,0:T(8,128)(2,1)S(1)} %get-tuple-element.39.merged_ref, bf16[8,5120]{1,0:T(8,128)(2,1)S(1)} %collective-permute-done.1.even_ref.even_side_ref, ...), custom_call_target="tpu_custom_call" | custom-call | flops 905969664 | bytes 2621440 | tf_op jit(solution)/shard_map/pallas_call | solution.py:50
  30.7 4.8 %collective-permute-start.9 = (bf16[64,1408]{1,0:T(8,128)(2,1)S(1)}, bf16[64,1408]{1,0:T(8,128)(2,1)S(1)}, u32[]{:S(2)}, u32[]{:S(2)}) collective-permute-start(bf16[64,1408]{1,0:T(8,128)(2,1)S(1)} %get-tuple-element.59), channel_id=1, source_target_pairs={{0,4},{4,0},{1,5},{5,1},{2,6},{6,2},{3,7},{7,3},{8,12},{12,8},{9,1... | collective-permute-start | bytes 540680 | tf_op jit(solution)/shard_map/ppermute | solution.py:521
  35.5 1.0 %collective-permute-done.9.given_ref = bf16[64,1408]{1,0:T(8,128)(2,1)S(1)} collective-permute-done((bf16[64,1408]{1,0:T(8,128)(2,1)S(1)}, bf16[64,1408]{1,0:T(8,128)(2,1)S(1)}, u32[]{:S(2)}, u32[]{:S(2)}) %collective-permute-start.9) | collective-permute-done | bytes 180256 | tf_op jit(solution)/shard_map/ppermute | solution.py:521
  36.6 0.7 shard_map.145
  37.3 5.3 %all-to-all-start.1 = ((bf16[8,8,1408]{2,1,0:T(8,128)(2,1)}), bf16[8,8,1408]{2,1,0:T(8,128)(2,1)S(1)}, u32[]{:S(2)}, u32[]{:S(2)}) async-start(bf16[8,8,1408]{2,1,0:T(8,128)(2,1)} %bitcast.17), calls=%async_computation.1 | async-start | bytes 360448 | tf_op jit(solution)/shard_map/all_to_all | solution.py:532
  42.5 2.0 %collective-permute-start.7 = (bf16[8,4096]{1,0:T(8,128)(2,1)S(1)}, bf16[8,4096]{1,0:T(8,128)(2,1)S(1)}, u32[]{:S(2)}, u32[]{:S(2)}) collective-permute-start(bf16[8,4096]{1,0:T(8,128)(2,1)S(1)} %get-tuple-element.55), channel_id=1, source_target_pairs={{0,1},{2,3},{1,0},{3,2},{4,5},{6,7},{5,4},{7,6},{8,9},{10,11},{9,8... | collective-permute-start | bytes 196616 | tf_op jit(solution)/shard_map/ppermute | solution.py:521
  44.6 0.7 collective-permute-start.8
  45.2 4.2 %collective-permute-done.7.even_ref = bf16[8,4096]{1,0:T(8,128)(2,1)S(1)} collective-permute-done((bf16[8,4096]{1,0:T(8,128)(2,1)S(1)}, bf16[8,4096]{1,0:T(8,128)(2,1)S(1)}, u32[]{:S(2)}, u32[]{:S(2)}) %collective-permute-start.7) | collective-permute-done | bytes 65568 | tf_op jit(solution)/shard_map/ppermute | solution.py:521
  49.4 0.0 collective-permute-done.8.odd_ref
  49.4 1.1 %shard_map.144 = (bf16[32,4096]{1,0:T(8,128)(2,1)}, bf16[64,1024]{1,0:T(8,128)(2,1)S(1)}) custom-call(f32[32,4096]{1,0:T(8,128)S(1)} %get-tuple-element.54.part_ref, s32[8,128]{1,0:T(8,128)S(1)} %get-tuple-element.38.lists_ref, bf16[8,4096]{1,0:T(8,128)(2,1)S(1)} %collective-permute-done.7.even_ref, bf16[8,4096]{1,0:T(8,128)(2,1)S(1)} %collective-permute-done.8.odd_ref, ...), custom_call_target="tpu_custom_call" | custom-call | bytes 1183744 | tf_op jit(solution)/shard_map/pallas_call | solution.py:50
  50.5 2.2 %shard_map.143 = (bf16[32,4096]{1,0:T(8,128)(2,1)}, s32[8,128]{1,0:T(8,128)S(1)}) custom-call(bf16[6,6,32,384]{3,2,1,0:T(8,128)(2,1)S(1)} %get-tuple-element.52.pad_ref, bf16[27,64,64]{2,1,0:T(8,128)(2,1)S(1)} %copy-done.3, s32[8,128]{1,0:T(8,128)S(1)} %get-tuple-element.38.lists_ref), custom_call_target="tpu_custom_call" | custom-call | flops 905969664 | bytes 1376256 | tf_op jit(solution)/shard_map/pallas_call | solution.py:50
  52.8 0.0 all-to-all-done.1
  52.8 0.2 shard_map.146
  52.9 15.1 %all_to_all.15 = bf16[8,8,2432]{2,1,0:T(8,128)(2,1)S(1)} all-to-all(bf16[8,8,2432]{2,1,0:T(8,128)(2,1)S(1)} %bitcast.34), channel_id=1, replica_groups=mesh['groups'=2,'x'=2,'core'=2,'gy'=4] {'x','gy'}, dimensions={0} | all-to-all | bytes 622592 | tf_op jit(solution)/shard_map/all_to_all | solution.py:532
  68.1 0.0 collective-permute-start.10
  68.1 1.6 %collective-permute-done.10.given_ref = bf16[64,2432]{1,0:T(8,128)(2,1)S(1)} collective-permute-done((bf16[64,2432]{1,0:T(8,128)(2,1)S(1)}, bf16[64,2432]{1,0:T(8,128)(2,1)S(1)}, u32[]{:S(2)}, u32[]{:S(2)}) %collective-permute-start.10) | collective-permute-done | bytes 311328 | tf_op jit(solution)/shard_map/ppermute | solution.py:521
  69.7 0.0 copy-done.2
  69.7 1.4 %shard_map.147 = (f32[27,64,64]{2,1,0:T(8,128)}, f32[512,128]{1,0:T(8,128)}, bf16[64,1024]{1,0:T(8,128)(2,1)}) custom-call(bf16[64,2432]{1,0:T(8,128)(2,1)S(1)} %bitcast.28, bf16[64,2432]{1,0:T(8,128)(2,1)S(1)} %collective-permute-done.10.given_ref, s32[4,16]{1,0:T(4,128)S(1)} %bitcast.37, s32[8,128]{1,0:T(8,128)S(1)} %get-tuple-element.63.lists_ref), custom_call_target="tpu_custom_call" | custom-call | bytes 1462528 | tf_op jit(solution)/shard_map/pallas_call | solution.py:50
  (5 shorter events, 0.0 us)
Async XLA Ops:
  0.6 17.1 %copy-start.3 = (bf16[27,64,64]{2,1,0:T(8,128)(2,1)S(1)}, bf16[27,64,64]{2,1,0:T(8,128)(2,1)}, u32[]{:S(2)}) copy-start(bf16[27,64,64]{2,1,0:T(8,128)(2,1)} %weight_ref.3) | copy-start | bytes 663556
  2.9 14.8 %all-to-all-start = ((bf16[8,8,1024]{2,1,0:T(8,128)(2,1)}), bf16[8,8,1024]{2,1,0:T(8,128)(2,1)S(1)}, u32[]{:S(2)}, u32[]{:S(2)}) async-start(bf16[8,8,1024]{2,1,0:T(8,128)(2,1)} %bitcast.41), calls=%async_computation | async-start | bytes 262144 | tf_op jit(solution)/shard_map/all_to_all | solution.py:532
  10.2 7.5 %copy-start.6 = (s32[8,128]{1,0:T(8,128)S(1)}, s32[8,128]{1,0:T(8,128)}, u32[]{:S(2)}) copy-start(s32[8,128]{1,0:T(8,128)} %get-tuple-element.37.lists_ref) | copy-start | bytes 12292
  17.7 3.7 %collective-permute-start = (bf16[64,1024]{1,0:T(8,128)(2,1)S(1)}, bf16[64,1024]{1,0:T(8,128)(2,1)S(1)}, u32[]{:S(2)}, u32[]{:S(2)}) collective-permute-start(bf16[64,1024]{1,0:T(8,128)(2,1)S(1)} %bitcast.30), channel_id=1, source_target_pairs={{0,4},{4,0},{1,5},{5,1},{2,6},{6,2},{3,7},{7,3},{8,12},{12,8},{9,1... | collective-permute-start | bytes 393224 | tf_op jit(solution)/shard_map/ppermute | solution.py:521
  17.7 1.0 %copy-start.4 = (bf16[1,1,32,4096]{3,2,1,0:T(8,128)(2,1)S(1)}, bf16[1,1,32,4096]{3,2,1,0:T(8,128)(2,1)}, u32[]{:S(2)}) copy-start(bf16[1,1,32,4096]{3,2,1,0:T(8,128)(2,1)} %param.19) | copy-start | bytes 786436
  18.7 0.7 %copy-start.5 = (s32[1,1,32,27]{2,1,3,0:T(1,128)S(1)}, s32[1,1,32,27]{2,1,3,0:T(1,128)}, u32[]{:S(2)}) copy-start(s32[1,1,32,27]{2,1,3,0:T(1,128)} %param.14) | copy-start | bytes 10372
  19.4 2.0 %copy-start = (bf16[8,128,64]{1,2,0:T(8,128)(2,1)S(1)}, bf16[8,128,64]{1,2,0:T(8,128)(2,1)}, u32[]{:S(2)}) copy-start(bf16[8,128,64]{1,2,0:T(8,128)(2,1)} %param.13) | copy-start | bytes 393220
  19.4 2.0 %copy-start.1 = (bf16[1,1,32,4096]{3,2,1,0:T(8,128)(2,1)S(1)}, bf16[1,1,32,4096]{3,2,1,0:T(8,128)(2,1)}, u32[]{:S(2)}) copy-start(bf16[1,1,32,4096]{3,2,1,0:T(8,128)(2,1)} %param.10) | copy-start | bytes 786436
  22.0 4.9 %collective-permute-start.1 = (bf16[8,5120]{1,0:T(8,128)(2,1)S(1)}, bf16[8,5120]{1,0:T(8,128)(2,1)S(1)}, u32[]{:S(2)}, u32[]{:S(2)}) collective-permute-start(bf16[8,5120]{1,0:T(8,128)(2,1)S(1)} %get-tuple-element.40), channel_id=1, source_target_pairs={{0,1},{2,3},{1,0},{3,2},{4,5},{6,7},{5,4},{7,6},{8,9},{10,11},{9,8... | collective-permute-start | bytes 245768 | tf_op jit(solution)/shard_map/ppermute | solution.py:521
  22.3 4.6 %collective-permute-start.2 = (bf16[8,5120]{1,0:T(8,128)(2,1)S(1)}, bf16[8,5120]{1,0:T(8,128)(2,1)S(1)}, u32[]{:S(2)}, u32[]{:S(2)}) collective-permute-start(bf16[8,5120]{1,0:T(8,128)(2,1)S(1)} %get-tuple-element.41), channel_id=1, source_target_pairs={{1,2},{2,1},{5,6},{6,5},{9,10},{10,9},{13,14},{14,13},{17,18},{18,... | collective-permute-start | bytes 245768 | tf_op jit(solution)/shard_map/ppermute | solution.py:521
  23.0 5.1 %collective-permute-start.5 = (bf16[8,4096]{1,0:T(8,128)(2,1)S(1)}, bf16[8,4096]{1,0:T(8,128)(2,1)S(1)}, u32[]{:S(2)}, u32[]{:S(2)}) collective-permute-start(bf16[8,4096]{1,0:T(8,128)(2,1)S(1)} %get-tuple-element.48), channel_id=1, source_target_pairs={{0,4},{8,12},{4,0},{12,8},{1,5},{9,13},{5,1},{13,9},{2,6},{10,14},... | collective-permute-start | bytes 196616 | tf_op jit(solution)/shard_map/ppermute | solution.py:521
  23.3 4.7 %collective-permute-start.6 = (bf16[8,4096]{1,0:T(8,128)(2,1)S(1)}, bf16[8,4096]{1,0:T(8,128)(2,1)S(1)}, u32[]{:S(2)}, u32[]{:S(2)}) collective-permute-start(bf16[8,4096]{1,0:T(8,128)(2,1)S(1)} %get-tuple-element.49), channel_id=1, source_target_pairs={{4,8},{8,4},{5,9},{9,5},{6,10},{10,6},{7,11},{11,7},{20,24},{24,20... | collective-permute-start | bytes 196616 | tf_op jit(solution)/shard_map/ppermute | solution.py:521
  27.3 1.4 %collective-permute-start.3 = (bf16[8,4096]{1,0:T(8,128)(2,1)S(1)}, bf16[8,4096]{1,0:T(8,128)(2,1)S(1)}, u32[]{:S(2)}, u32[]{:S(2)}) collective-permute-start(bf16[8,4096]{1,0:T(8,128)(2,1)S(1)} %get-tuple-element.42), channel_id=1, source_target_pairs={{0,4},{8,12},{4,0},{12,8},{1,5},{9,13},{5,1},{13,9},{2,6},{10,14},... | collective-permute-start | bytes 196616 | tf_op jit(solution)/shard_map/ppermute | solution.py:521
  27.4 1.3 %collective-permute-start.4 = (bf16[8,4096]{1,0:T(8,128)(2,1)S(1)}, bf16[8,4096]{1,0:T(8,128)(2,1)S(1)}, u32[]{:S(2)}, u32[]{:S(2)}) collective-permute-start(bf16[8,4096]{1,0:T(8,128)(2,1)S(1)} %get-tuple-element.43), channel_id=1, source_target_pairs={{4,8},{8,4},{5,9},{9,5},{6,10},{10,6},{7,11},{11,7},{20,24},{24,20... | collective-permute-start | bytes 196616 | tf_op jit(solution)/shard_map/ppermute | solution.py:521
  30.7 5.9 %collective-permute-start.9 = (bf16[64,1408]{1,0:T(8,128)(2,1)S(1)}, bf16[64,1408]{1,0:T(8,128)(2,1)S(1)}, u32[]{:S(2)}, u32[]{:S(2)}) collective-permute-start(bf16[64,1408]{1,0:T(8,128)(2,1)S(1)} %get-tuple-element.59), channel_id=1, source_target_pairs={{0,4},{4,0},{1,5},{5,1},{2,6},{6,2},{3,7},{7,3},{8,12},{12,8},{9,1... | collective-permute-start | bytes 540680 | tf_op jit(solution)/shard_map/ppermute | solution.py:521
  37.3 15.5 %all-to-all-start.1 = ((bf16[8,8,1408]{2,1,0:T(8,128)(2,1)}), bf16[8,8,1408]{2,1,0:T(8,128)(2,1)S(1)}, u32[]{:S(2)}, u32[]{:S(2)}) async-start(bf16[8,8,1408]{2,1,0:T(8,128)(2,1)} %bitcast.17), calls=%async_computation.1 | async-start | bytes 360448 | tf_op jit(solution)/shard_map/all_to_all | solution.py:532
  42.5 6.9 %collective-permute-start.7 = (bf16[8,4096]{1,0:T(8,128)(2,1)S(1)}, bf16[8,4096]{1,0:T(8,128)(2,1)S(1)}, u32[]{:S(2)}, u32[]{:S(2)}) collective-permute-start(bf16[8,4096]{1,0:T(8,128)(2,1)S(1)} %get-tuple-element.55), channel_id=1, source_target_pairs={{0,1},{2,3},{1,0},{3,2},{4,5},{6,7},{5,4},{7,6},{8,9},{10,11},{9,8... | collective-permute-start | bytes 196616 | tf_op jit(solution)/shard_map/ppermute | solution.py:521
  44.6 4.9 %collective-permute-start.8 = (bf16[8,4096]{1,0:T(8,128)(2,1)S(1)}, bf16[8,4096]{1,0:T(8,128)(2,1)S(1)}, u32[]{:S(2)}, u32[]{:S(2)}) collective-permute-start(bf16[8,4096]{1,0:T(8,128)(2,1)S(1)} %get-tuple-element.56), channel_id=1, source_target_pairs={{1,2},{2,1},{5,6},{6,5},{9,10},{10,9},{13,14},{14,13},{17,18},{18,... | collective-permute-start | bytes 196616 | tf_op jit(solution)/shard_map/ppermute | solution.py:521
  68.1 1.6 %copy-start.2 = (s32[1,1,16,4]{2,3,1,0:T(4,128)S(1)}, s32[1,1,16,4]{2,3,1,0:T(4,128)}, u32[]{:S(2)}) copy-start(s32[1,1,16,4]{2,3,1,0:T(4,128)} %param.18) | copy-start | bytes 772
  68.1 1.6 %collective-permute-start.10 = (bf16[64,2432]{1,0:T(8,128)(2,1)S(1)}, bf16[64,2432]{1,0:T(8,128)(2,1)S(1)}, u32[]{:S(2)}, u32[]{:S(2)}) collective-permute-start(bf16[64,2432]{1,0:T(8,128)(2,1)S(1)} %bitcast.27), channel_id=1, source_target_pairs={{0,4},{4,0},{1,5},{5,1},{2,6},{6,2},{3,7},{7,3},{8,12},{12,8},{9,1... | collective-permute-start | bytes 933896 | tf_op jit(solution)/shard_map/ppermute | solution.py:521

commit v10 on v9

--- a/solution.py
+++ b/solution.py
@@ -61,38 +61,31 @@
     return jax.ShapeDtypeStruct(dims, dtype)
 
 
-def items_out(sends_ref, items_ref, out_ref, across):
+def items_out(sends_ref, items_ref, out_ref):
     capacity, devices = sends_ref.shape
     count, width = items_ref.shape
     half = width // 2
     group = 2 * capacity
-    lanes = out_ref.shape[0]
-    chip = iota((lanes, devices), 0) // group
+    lanes = devices * group
+    spread = ones_where(iota((lanes, devices), 0) // group == iota((lanes, devices), 1))
     slot = iota((lanes, capacity), 0) % group // 2
-    sends = sends_ref[...].astype(F32).astype(BF)
-    items = jnp.concatenate([items_ref[:, :half], items_ref[:, half:]], axis=0)
-    for core in range(2):
-        device = (chip // across[1] * 2 + core) * across[1] + chip % across[1]
-        values = dot_nt(ones_where(device == iota((lanes, devices), 1)), sends)
-        item = jnp.sum(jnp.where(slot == iota((lanes, capacity), 1), values, 0.0), axis=1, keepdims=True).astype(I32)
-        place = jnp.where(item < count, item + iota((lanes, 1), 0) % 2 * count, -1)
-        chosen = ones_where(iota((lanes, 2 * count), 1) == place)
-        out_ref[:, core * half : (core + 1) * half] = dot(chosen, items).astype(BF)
-
-
-def merge(arrived_ref, given_ref, lists_ref, up_ref, fine_ref, merged_ref, parents_ref, across):
+    values = dot_nt(spread, sends_ref[...].astype(F32).astype(BF))
+    item = jnp.sum(jnp.where(slot == iota((lanes, capacity), 1), values, 0.0), axis=1, keepdims=True).astype(I32)
+    place = jnp.where(item < count, item + iota((lanes, 1), 0) % 2 * count, -1)
+    chosen = ones_where(iota((lanes, 2 * count), 1) == place)
+    out_ref[...] = dot(chosen, jnp.concatenate([items_ref[:, :half], items_ref[:, half:]], axis=0)).astype(BF)
+
+
+def merge(received_ref, slots, up_ref, fine_ref, merged_ref, parents_ref):
     bricks = fine_ref.shape[0]
-    lanes = arrived_ref.shape[0]
-    half = arrived_ref.shape[1] // 2
-    own = [by_pair(lists_ref, GX, r[:, :half].astype(F32), r[:, half:].astype(F32))[0] for r in (arrived_ref, given_ref)]
-    received = jnp.concatenate(own, axis=0).astype(BF)
-    slot = column_of(slots_of(lists_ref, bricks))
-    capacity, group = chip_slots(lanes, 1, across)
-    row = iota((bricks, lanes), 1)
-    sources = [device_of(row // group, lists_ref, other, across) for other in range(2)]
-    named = slot == jnp.concatenate([source * capacity + row % group // 2 for source in sources], axis=1)
-    odd = iota((bricks, 2 * lanes), 1) % 2
-    parents = jnp.concatenate([dot(ones_where(named & (odd == h)), received) for h in (0, 1)], axis=1).astype(BF)
+    lanes, half = received_ref.shape
+    slot = column_of(slots)
+    place = iota((bricks, lanes), 1)
+    named = place // 2 == slot
+    received = received_ref[...]
+    parents = jnp.concatenate(
+        [dot(ones_where(named & (place % 2 == h)), received) for h in (0, 1)], axis=1
+    ).astype(BF)
     coarse = 2 * half // 8
     stacked = jnp.concatenate([parents[:, v * coarse : (v + 1) * coarse] for v in range(8)], axis=0)
     parents_ref[...] = stacked
@@ -278,7 +271,7 @@
 
 def first_body(
     sends_hbm, items_hbm, sides_hbm, crosses_hbm, slots_hbm, out_ref, lists_ref,
-    sends_ref, items_ref, sides_ref, crosses_ref, slots_ref, arrived, across,
+    sends_ref, items_ref, sides_ref, crosses_ref, slots_ref, arrived,
 ):
     sources = (sends_hbm, items_hbm, sides_hbm, crosses_hbm, slots_hbm)
     places = (sends_ref, items_ref, sides_ref, crosses_ref, slots_ref)
@@ -292,7 +285,7 @@
     lists_ref[0:2, :face] = sides_ref[...]
     lists_ref[2:4, :face] = crosses_ref[...]
     lists_ref[4:5, :bricks] = slots_ref[...]
-    items_out(sends_ref, items_ref, out_ref, across)
+    items_out(sends_ref, items_ref, out_ref)
 
 
 def side_grad_body(
@@ -378,8 +371,10 @@
     given_ref[...] = given.astype(BF)
 
 
-def pair_sum_body(kept_ref, given_ref, out_ref):
-    out_ref[...] = (kept_ref[...] + given_ref[...].astype(F32)).astype(BF)
+def pair_sum_body(kept_ref, given_ref, replies_ref, out_ref):
+    at = replies_ref.shape[1]
+    out_ref[:, :at] = replies_ref[...]
+    out_ref[:, at:] = (kept_ref[...] + given_ref[...].astype(F32)).astype(BF)
 
 
 def inputs_at(pad_ref, e):
@@ -407,12 +402,10 @@
     return base + dot(chosen, stack_rows(first, second))
 
 
-def merge_body(
-    arrived_ref, given_ref, up_ref, fine_ref, lists_ref, merged_ref, parents_ref, a_ref, b_ref, across
-):
+def merge_body(received_ref, up_ref, fine_ref, lists_ref, merged_ref, parents_ref, a_ref, b_ref):
     bricks, width = fine_ref.shape
     face = a_ref.shape[0]
-    parents = merge(arrived_ref, given_ref, lists_ref, up_ref, fine_ref, merged_ref, parents_ref, across)
+    parents = merge(received_ref, slots_of(lists_ref, bricks), up_ref, fine_ref, merged_ref, parents_ref)
     lists = sides_of(lists_ref, face)
     lists = by_pair(lists_ref, GY, lists[0:1], lists[1:2])
     for out_ref, rows, owners in zip((a_ref, b_ref), pick_rows(lists, merged_ref[...]), pick_rows(lists, parents)):
@@ -456,16 +449,16 @@
     return (chip // across[1] * 2 + core) * across[1] + chip % across[1]
 
 
-def share_body(sums_ref, replies_ref, lists_ref, out_ref, again_ref, across):
-    again_ref[...] = lists_ref[...]
-    count, item_lanes = replies_ref.shape
+def share_body(back_ref, lists_ref, out_ref, given_ref, across):
+    count, item_lanes = given_ref.shape
+    given_ref[...] = back_ref[:, item_lanes : 2 * item_lanes]
     share = count // (across[0] * across[1] // 2)
     same = iota((count, count), 0) % share == iota((count, count), 1) % share
-    out_ref[:, :item_lanes] = replies_ref[...]
-    out_ref[:, item_lanes:] = dot(ones_where(same), sums_ref[...]).astype(BF)
-
-
-def coarse_grad(arrivals, sends_ref, lists_ref, out_ref, across):
+    out_ref[...] = dot(ones_where(same), back_ref[:, 2 * item_lanes :]).astype(BF)
+
+
+def coarse_grad_body(back_ref, given_ref, sends_ref, lists_ref, out_ref, across):
+    arrivals = (back_ref[:, : given_ref.shape[1]], given_ref[...])
     capacity, devices = sends_ref.shape
     count, item_width = out_ref.shape
     half = item_width // 2
@@ -490,16 +483,12 @@
         out_ref[:, h * half : (h + 1) * half] = totals[h].astype(BF)
 
 
-def last_body(back_ref, given_ref, sends_ref, lists_ref, conv_ref, up_ref, out_ref, item_lanes, across, scale):
-    half_count = back_ref.shape[0]
-    items = (back_ref[:, :item_lanes], given_ref[:, item_lanes : 2 * item_lanes])
-    coarse_grad(items, sends_ref, lists_ref, out_ref, across)
+def last_body(own_ref, other_ref, lists_ref, conv_ref, up_ref, scale):
+    half_count = own_ref.shape[0]
     coarse = up_ref.shape[1]
     count = 2 * half_count
     parts = up_ref.shape[0] // count
-    own = back_ref[:, 2 * item_lanes :].astype(F32) * scale
-    others = given_ref[:, 2 * item_lanes :].astype(F32) * scale
-    first, second = by_pair(lists_ref, GX, own, others)
+    first, second = (half * scale for half in from_pairs(lists_ref, GX, own_ref, other_ref))
     at = 0
     for q in range(parts):
         up_ref[q * count : q * count + half_count] = first[:, at : at + coarse]
@@ -566,12 +555,11 @@
 
     listed = (sends, items, sides, crosses, slots)
     outgoing, lists = call(
-        functools.partial(first_body, across=across), [shape((capacity * devices, item_width)), lists_shape], *listed,
+        first_body, [shape((2 * capacity * devices, half)), lists_shape], *listed,
         scratch=[pltpu.VMEM(a.shape, a.dtype) for a in listed] + [pltpu.SemaphoreType.DMA((len(listed),))],
         in_hbm=True,
     )
-    arrived = trade_rows(outgoing, ("x", "gy"))
-    arrived = (arrived, swap(arrived, "core", 0))
+    received = trade_rows(outgoing, ("x", "core", "gy"))
     lane = jnp.arange(128, dtype=I32)[None]
     parity = jnp.where(lane == GX, lax.axis_index("core"), lax.axis_index("gy") % 2).astype(I32)
     table_rows = start + 2 * face
@@ -586,8 +574,8 @@
     )
     cross_grads = swap_pairs(to_even, to_odd, GX_AXES)
     merged, parents, to_even, to_odd = call(
-        functools.partial(merge_body, across=across), [rows, shape((8 * bricks, coarse)), faces_and_parents, faces_and_parents],
-        *arrived, up_turned, fine, lists,
+        merge_body, [rows, shape((8 * bricks, coarse)), faces_and_parents, faces_and_parents],
+        received, up_turned, fine, lists,
     )
     sides = swap_pairs(to_even, to_odd, "gy")
     to_even, to_odd = call(cross_body, [face_rows, face_rows], merged, *sides, lists)
@@ -605,26 +593,28 @@
         scratch=[pltpu.VMEM((table_rows, width), BF), pltpu.VMEM((count, sums_width), F32)], flops=conv_flops,
     )
     given = swap(given, "core", 0)
-    (sums,) = call(pair_sum_body, [shape(half_sums)], kept, given)
-    sums = trade_rows(sums, ("x", "gy"))
     grad_fine, replies = call(
         functools.partial(fine_grad_body, across=across), [rows, shape((count // 2, 2 * item_lanes))],
         fine_part, lists, *side_grads, up_turned,
     )
+    (sums,) = call(pair_sum_body, [shape((count // 2, 2 * item_lanes + sums_width))], kept, given, replies)
+    back = trade_rows(sums, ("x", "gy"))
     output, lists = call(
         conv_body, [rows, lists_shape], pad, conv_weight, lists, scratch=[band], flops=conv_flops
     )
-    back, lists = call(
-        functools.partial(share_body, across=across),
-        [shape((count // 2, 2 * item_lanes + sums_width)), lists_shape], sums, replies, lists,
-    )
-    back = trade_rows(back, ("x", "gy"))
-    given = swap(back, "core", 0)
+    sums, given = call(
+        functools.partial(share_body, across=across), [shape(half_sums), shape((count // 2, item_lanes))], back, lists
+    )
+    sums = trade_rows(sums, ("x", "gy"))
+    other_sums = swap(sums, "core", 0)
+    given = swap(given, "core", 0)
+    (coarse_grad,) = call(
+        functools.partial(coarse_grad_body, across=across), [shape((item_count, item_width))], back, given, sends, lists
+    )
     scale = 1.0 / math.sqrt(64 * bricks * devices)
-    grad_conv, grad_up, coarse_grad = call(
-        functools.partial(last_body, item_lanes=item_lanes, across=across, scale=scale),
-        [shape((27, C, C), F32), shape((8 * C, coarse), F32), shape((item_count, item_width))],
-        back, given, sends, lists,
+    grad_conv, grad_up = call(
+        functools.partial(last_body, scale=scale),
+        [shape((27, C, C), F32), shape((8 * C, coarse), F32)], sums, other_sums, lists,
     )
     return (
         output.reshape(1, 1, bricks, width),

time: 71.6 us -> 70.3 us (0.982)
  blocking collectives: 15.1 us -> 10.3 us
  starting transfers between devices: 22.7 us -> 25.6 us
  waiting for transfers between devices: 17.3 us -> 16.5 us
  Pallas kernels: 13.4 us -> 14.2 us
    all_to_all x1, blocking collectives: 15.1 us -> 10.3 us  [trade_rows(): lax.all_to_all(grid_view, axes, split_axis=0, concat_axis=0, tiled=True)]
    ppermute x11, waiting for transfers between devices: 9.82 us -> 5.08 us  [swap(): lax.ppermute(value, axis, [(i, i + 1) for i in lower] + [(i + 1, i) for i...]
    all_to_all x2, waiting for transfers between devices: 7.5 us -> 11.4 us  [trade_rows(): lax.all_to_all(grid_view, axes, split_axis=0, concat_axis=0, tiled=True)]
    ppermute x11, starting transfers between devices: 10.2 us -> 12.7 us  [swap(): lax.ppermute(value, axis, [(i, i + 1) for i in lower] + [(i + 1, i) for i...]
    pallas_call x11 -> x12, Pallas kernels: 13.4 us -> 14.2 us  [call(): pl.pallas_call(body, out_shape=tuple(outs), in_specs=[pl.BlockSpec(memory...]
  transfers between devices with their start and end apart: 13 -> 13, of which waited for: 5 -> 5; matrix products, arithmetic and copies ran while one was open for 0% -> 0% of each run, Pallas kernels for 9% -> 10%
where the time goes in v10:
time: 70.3 us; the launch traced here: 69.8 us
  starting transfers between devices  25.6 us (36%)
  waiting for transfers between devices  16.5 us (23%)
  Pallas kernels  14.2 us (20%)
  blocking collectives  10.3 us (15%)
  local copies, waits for them, and re-layouts  2.33 us (3%)
  between operations  0.82 us (1%)
    pallas_call x12, Pallas kernels, call(): pl.pallas_call(body, out_shape=tuple(outs), in_specs=[pl.BlockSpec(memory...  14.2 us
    all_to_all x2, starting transfers between devices, trade_rows(): lax.all_to_all(grid_view, axes, split_axis=0, concat_axis=0, tiled=True)  12.9 us
    ppermute x11, starting transfers between devices, swap(): lax.ppermute(value, axis, [(i, i + 1) for i in lower] + [(i + 1, i) for i...  12.7 us
    all_to_all x2, waiting for transfers between devices, trade_rows(): lax.all_to_all(grid_view, axes, split_axis=0, concat_axis=0, tiled=True)  11.4 us
    all_to_all x1, blocking collectives, trade_rows(): lax.all_to_all(grid_view, axes, split_axis=0, concat_axis=0, tiled=True)  10.3 us
    ppermute x11, waiting for transfers between devices, swap(): lax.ppermute(value, axis, [(i, i + 1) for i in lower] + [(i + 1, i) for i...  5.08 us
    unnamed x14, local copies, waits for them, and re-layouts  2.33 us
  transfers between devices with their start and end apart: 13, of which 5 were waited for; matrix products, arithmetic and copies ran while one was open for 0% of the time, Pallas kernels for 10%

profile of v10, /device:TPU:0, one launch (start us, length us, event | category | flops | bytes accessed | tf_op | source)
XLA Modules:
  0.0 69.8 jit_solution(2221589670912267038)
XLA Ops:
  0.6 0.0 copy-start.3
  0.6 2.0 %shard_map.137 = (bf16[128,512]{1,0:T(8,128)(2,1)}, s32[8,128]{1,0:T(8,128)}) custom-call(s32[4,16]{1,0:T(4,128)} %bitcast.36, bf16[64,1024]{1,0:T(8,128)(2,1)} %bitcast.40, s32[2,8]{1,0:T(2,128)} %bitcast.43, s32[2,8]{1,0:T(2,128)} %bitcast.44, s32[1,32]{1,0:T(1,128)} %bitcast.45), custom_call_target="tpu_custom_call" | custom-call | bytes 266752 | tf_op jit(solution)/shard_map/pallas_call | solution.py:50
  2.7 7.4 %all-to-all-start = ((bf16[16,8,512]{2,1,0:T(8,128)(2,1)}), bf16[16,8,512]{2,1,0:T(8,128)(2,1)S(1)}, u32[]{:S(2)}, u32[]{:S(2)}) async-start(bf16[16,8,512]{2,1,0:T(8,128)(2,1)} %bitcast.41), calls=%async_computation | async-start | bytes 262144 | tf_op jit(solution)/shard_map/all_to_all | solution.py:521
  10.1 0.0 copy-start.6
  10.1 0.0 copy-done.3
  10.1 0.7 copy-done.6
  10.8 0.9 %copy-done.4 = bf16[1,1,32,4096]{3,2,1,0:T(8,128)(2,1)S(1)} copy-done((bf16[1,1,32,4096]{3,2,1,0:T(8,128)(2,1)S(1)}, bf16[1,1,32,4096]{3,2,1,0:T(8,128)(2,1)}, u32[]{:S(2)}) %copy-start.4) | copy-done | bytes 262168
  11.7 0.7 %copy-done.5 = s32[1,1,32,27]{2,1,3,0:T(1,128)S(1)} copy-done((s32[1,1,32,27]{2,1,3,0:T(1,128)S(1)}, s32[1,1,32,27]{2,1,3,0:T(1,128)}, u32[]{:S(2)}) %copy-start.5) | copy-done | bytes 3480
  12.4 2.0 %shard_map.138 = (f32[48,4096]{1,0:T(8,128)S(1)}, bf16[8,4096]{1,0:T(8,128)(2,1)S(1)}, bf16[8,4096]{1,0:T(8,128)(2,1)S(1)}, bf16[256,512]{1,0:T(8,128)(2,1)S(1)}...) custom-call(bf16[32,4096]{1,0:T(8,128)(2,1)S(1)} %bitcast.38, ...), custom_call_target="tpu_custom_call" | custom-call | flops 1811939328 | bytes 1785728 | tf_op jit(solution)/shard_map/pallas_call | solution.py:50
  14.4 3.0 %all-to-all-done = bf16[16,8,512]{2,1,0:T(8,128)(2,1)S(1)} async-done(((bf16[16,8,512]{2,1,0:T(8,128)(2,1)}), bf16[16,8,512]{2,1,0:T(8,128)(2,1)S(1)}, u32[]{:S(2)}, u32[]{:S(2)}) %all-to-all-start) | async-done | bytes 131104 | tf_op jit(solution)/shard_map/all_to_all | solution.py:521
  17.4 0.0 copy-done
  17.4 0.0 copy-done.1
  17.4 0.6 shard_map.139
  18.0 0.7 %collective-permute-start = (bf16[8,5120]{1,0:T(8,128)(2,1)S(1)}, bf16[8,5120]{1,0:T(8,128)(2,1)S(1)}, u32[]{:S(2)}, u32[]{:S(2)}) collective-permute-start(bf16[8,5120]{1,0:T(8,128)(2,1)S(1)} %get-tuple-element.39), channel_id=1, source_target_pairs={{0,1},{2,3},{1,0},{3,2},{4,5},{6,7},{5,4},{7,6},{8,9},{10,11},{9,8... | collective-permute-start | bytes 245768 | tf_op jit(solution)/shard_map/ppermute | solution.py:510
  18.8 0.7 collective-permute-start.1
  19.4 0.1 collective-permute-start.4
  19.5 0.7 collective-permute-start.5
  20.2 2.4 %collective-permute-done.even_ref.even_side_ref = bf16[8,5120]{1,0:T(8,128)(2,1)S(1)} collective-permute-done((bf16[8,5120]{1,0:T(8,128)(2,1)S(1)}, bf16[8,5120]{1,0:T(8,128)(2,1)S(1)}, u32[]{:S(2)}, u32[]{:S(2)}) %collective-permute-start) | collective-permute-done | bytes 81952 | tf_op jit(solution)/shard_map/ppermute | solution.py:510
  22.6 0.0 collective-permute-done.1.odd_ref.odd_side_ref
  22.6 0.4 shard_map.140
  22.9 0.1 collective-permute-start.2
  23.0 0.7 collective-permute-start.3
  23.7 0.0 collective-permute-done.4.even_grad_ref
  23.7 0.0 collective-permute-done.5.odd_grad_ref
  23.7 0.6 shard_map.141
  24.3 0.0 collective-permute-done.2.even_cross_ref
  24.3 0.0 collective-permute-done.3.odd_cross_ref
  24.3 2.0 %shard_map.142 = (f32[64,1408]{1,0:T(8,128)S(1)}, bf16[64,1408]{1,0:T(8,128)(2,1)S(1)}, bf16[6,6,32,384]{3,2,1,0:T(8,128)(2,1)S(1)}) custom-call(bf16[32,4096]{1,0:T(8,128)(2,1)S(1)} %get-tuple-element.38.merged_ref, bf16[8,5120]{1,0:T(8,128)(2,1)S(1)} %collective-permute-done.even_ref.even_side_ref, ...), custom_call_target="tpu_custom_call" | custom-call | flops 905969664 | bytes 2621440 | tf_op jit(solution)/shard_map/pallas_call | solution.py:50
  26.3 4.8 %collective-permute-start.8 = (bf16[64,1408]{1,0:T(8,128)(2,1)S(1)}, bf16[64,1408]{1,0:T(8,128)(2,1)S(1)}, u32[]{:S(2)}, u32[]{:S(2)}) collective-permute-start(bf16[64,1408]{1,0:T(8,128)(2,1)S(1)} %get-tuple-element.58), channel_id=1, source_target_pairs={{0,4},{4,0},{1,5},{5,1},{2,6},{6,2},{3,7},{7,3},{8,12},{12,8},{9,1... | collective-permute-start | bytes 540680 | tf_op jit(solution)/shard_map/ppermute | solution.py:510
  31.1 3.9 %collective-permute-start.6 = (bf16[8,4096]{1,0:T(8,128)(2,1)S(1)}, bf16[8,4096]{1,0:T(8,128)(2,1)S(1)}, u32[]{:S(2)}, u32[]{:S(2)}) collective-permute-start(bf16[8,4096]{1,0:T(8,128)(2,1)S(1)} %get-tuple-element.54), channel_id=1, source_target_pairs={{0,1},{2,3},{1,0},{3,2},{4,5},{6,7},{5,4},{7,6},{8,9},{10,11},{9,8... | collective-permute-start | bytes 196616 | tf_op jit(solution)/shard_map/ppermute | solution.py:510
  35.0 0.7 collective-permute-start.7
  35.7 1.7 %collective-permute-done.6.even_ref = bf16[8,4096]{1,0:T(8,128)(2,1)S(1)} collective-permute-done((bf16[8,4096]{1,0:T(8,128)(2,1)S(1)}, bf16[8,4096]{1,0:T(8,128)(2,1)S(1)}, u32[]{:S(2)}, u32[]{:S(2)}) %collective-permute-start.6) | collective-permute-done | bytes 65568 | tf_op jit(solution)/shard_map/ppermute | solution.py:510
  37.3 0.0 collective-permute-done.7.odd_ref
  37.3 1.1 %shard_map.144 = (bf16[32,4096]{1,0:T(8,128)(2,1)}, bf16[64,1024]{1,0:T(8,128)(2,1)S(1)}) custom-call(f32[32,4096]{1,0:T(8,128)S(1)} %get-tuple-element.53.part_ref, s32[8,128]{1,0:T(8,128)S(1)} %get-tuple-element.37.lists_ref, bf16[8,4096]{1,0:T(8,128)(2,1)S(1)} %collective-permute-done.6.even_ref, bf16[8,4096]{1,0:T(8,128)(2,1)S(1)} %collective-permute-done.7.odd_ref, ...), custom_call_target="tpu_custom_call" | custom-call | bytes 1183744 | tf_op jit(solution)/shard_map/pallas_call | solution.py:50
  38.4 0.0 collective-permute-done.8.given_ref
  38.4 0.8 %shard_map.145 = bf16[64,2432]{1,0:T(8,128)(2,1)} custom-call(f32[64,1408]{1,0:T(8,128)S(1)} %get-tuple-element.57.kept_ref, bf16[64,1408]{1,0:T(8,128)(2,1)S(1)} %collective-permute-done.8.given_ref, bf16[64,1024]{1,0:T(8,128)(2,1)S(1)} %get-tuple-element.59.replies_ref), custom_call_target="tpu_custom_call" | custom-call | bytes 983040 | tf_op jit(solution)/shard_map/pallas_call | solution.py:50
  39.2 5.5 %all-to-all-start.1 = ((bf16[8,8,2432]{2,1,0:T(8,128)(2,1)}), bf16[8,8,2432]{2,1,0:T(8,128)(2,1)S(1)}, u32[]{:S(2)}, u32[]{:S(2)}) async-start(bf16[8,8,2432]{2,1,0:T(8,128)(2,1)} %bitcast.17), calls=%async_computation.1 | async-start | bytes 622592 | tf_op jit(solution)/shard_map/all_to_all | solution.py:521
  44.7 2.2 %shard_map.143 = (bf16[32,4096]{1,0:T(8,128)(2,1)}, s32[8,128]{1,0:T(8,128)S(1)}) custom-call(bf16[6,6,32,384]{3,2,1,0:T(8,128)(2,1)S(1)} %get-tuple-element.51.pad_ref, bf16[27,64,64]{2,1,0:T(8,128)(2,1)S(1)} %copy-done.3, s32[8,128]{1,0:T(8,128)S(1)} %get-tuple-element.37.lists_ref), custom_call_target="tpu_custom_call" | custom-call | flops 905969664 | bytes 1376256 | tf_op jit(solution)/shard_map/pallas_call | solution.py:50
  46.9 8.4 %all-to-all-done.1 = bf16[8,8,2432]{2,1,0:T(8,128)(2,1)S(1)} async-done(((bf16[8,8,2432]{2,1,0:T(8,128)(2,1)}), bf16[8,8,2432]{2,1,0:T(8,128)(2,1)S(1)}, u32[]{:S(2)}, u32[]{:S(2)}) %all-to-all-start.1) | async-done | bytes 311328 | tf_op jit(solution)/shard_map/all_to_all | solution.py:521
  55.3 0.2 shard_map.146
  55.5 10.3 %all_to_all.15 = bf16[8,8,1408]{2,1,0:T(8,128)(2,1)S(1)} all-to-all(bf16[8,8,1408]{2,1,0:T(8,128)(2,1)S(1)} %bitcast.35), channel_id=1, replica_groups=mesh['groups'=2,'x'=2,'core'=2,'gy'=4] {'x','gy'}, dimensions={0} | all-to-all | bytes 360448 | tf_op jit(solution)/shard_map/all_to_all | solution.py:521
  65.8 0.0 collective-permute-start.10
  65.8 0.5 collective-permute-start.9
  66.3 1.0 %collective-permute-done.9.given_ref = bf16[64,512]{1,0:T(8,128)(2,1)S(1)} collective-permute-done((bf16[64,512]{1,0:T(8,128)(2,1)S(1)}, bf16[64,512]{1,0:T(8,128)(2,1)S(1)}, u32[]{:S(2)}, u32[]{:S(2)}) %collective-permute-start.9) | collective-permute-done | bytes 65568 | tf_op jit(solution)/shard_map/ppermute | solution.py:510
  67.3 0.0 copy-done.2
  67.3 1.0 %shard_map.147 = bf16[64,1024]{1,0:T(8,128)(2,1)} custom-call(bf16[64,2432]{1,0:T(8,128)(2,1)S(1)} %bitcast.28, bf16[64,512]{1,0:T(8,128)(2,1)S(1)} %collective-permute-done.9.given_ref, s32[4,16]{1,0:T(4,128)S(1)} %bitcast.37, s32[8,128]{1,0:T(8,128)S(1)} %get-tuple-element.60.lists_ref), custom_call_target="tpu_custom_call" | custom-call | bytes 512256 | tf_op jit(solution)/shard_map/pallas_call | solution.py:50
  68.4 0.0 collective-permute-done.10.other_ref
  68.4 1.4 %shard_map.148 = (f32[27,64,64]{2,1,0:T(8,128)}, f32[512,128]{1,0:T(8,128)}) custom-call(bf16[64,1408]{1,0:T(8,128)(2,1)S(1)} %bitcast.30, bf16[64,1408]{1,0:T(8,128)(2,1)S(1)} %collective-permute-done.10.other_ref, s32[8,128]{1,0:T(8,128)S(1)} %get-tuple-element.60.lists_ref), custom_call_target="tpu_custom_call" | custom-call | bytes 1069056 | tf_op jit(solution)/shard_map/pallas_call | solution.py:50
  (6 shorter events, 0.0 us)
Async XLA Ops:
  0.6 9.5 %copy-start.3 = (bf16[27,64,64]{2,1,0:T(8,128)(2,1)S(1)}, bf16[27,64,64]{2,1,0:T(8,128)(2,1)}, u32[]{:S(2)}) copy-start(bf16[27,64,64]{2,1,0:T(8,128)(2,1)} %weight_ref.3) | copy-start | bytes 663556
  2.7 14.7 %all-to-all-start = ((bf16[16,8,512]{2,1,0:T(8,128)(2,1)}), bf16[16,8,512]{2,1,0:T(8,128)(2,1)S(1)}, u32[]{:S(2)}, u32[]{:S(2)}) async-start(bf16[16,8,512]{2,1,0:T(8,128)(2,1)} %bitcast.41), calls=%async_computation | async-start | bytes 262144 | tf_op jit(solution)/shard_map/all_to_all | solution.py:521
  10.1 0.7 copy-start.6
  10.8 0.9 %copy-start.4 = (bf16[1,1,32,4096]{3,2,1,0:T(8,128)(2,1)S(1)}, bf16[1,1,32,4096]{3,2,1,0:T(8,128)(2,1)}, u32[]{:S(2)}) copy-start(bf16[1,1,32,4096]{3,2,1,0:T(8,128)(2,1)} %param.19) | copy-start | bytes 786436
  11.7 0.7 %copy-start.5 = (s32[1,1,32,27]{2,1,3,0:T(1,128)S(1)}, s32[1,1,32,27]{2,1,3,0:T(1,128)}, u32[]{:S(2)}) copy-start(s32[1,1,32,27]{2,1,3,0:T(1,128)} %param.14) | copy-start | bytes 10372
  12.4 5.0 %copy-start = (bf16[8,128,64]{1,2,0:T(8,128)(2,1)S(1)}, bf16[8,128,64]{1,2,0:T(8,128)(2,1)}, u32[]{:S(2)}) copy-start(bf16[8,128,64]{1,2,0:T(8,128)(2,1)} %param.13) | copy-start | bytes 393220
  12.4 5.0 %copy-start.1 = (bf16[1,1,32,4096]{3,2,1,0:T(8,128)(2,1)S(1)}, bf16[1,1,32,4096]{3,2,1,0:T(8,128)(2,1)}, u32[]{:S(2)}) copy-start(bf16[1,1,32,4096]{3,2,1,0:T(8,128)(2,1)} %param.10) | copy-start | bytes 786436
  18.0 4.5 %collective-permute-start = (bf16[8,5120]{1,0:T(8,128)(2,1)S(1)}, bf16[8,5120]{1,0:T(8,128)(2,1)S(1)}, u32[]{:S(2)}, u32[]{:S(2)}) collective-permute-start(bf16[8,5120]{1,0:T(8,128)(2,1)S(1)} %get-tuple-element.39), channel_id=1, source_target_pairs={{0,1},{2,3},{1,0},{3,2},{4,5},{6,7},{5,4},{7,6},{8,9},{10,11},{9,8... | collective-permute-start | bytes 245768 | tf_op jit(solution)/shard_map/ppermute | solution.py:510
  18.8 3.8 %collective-permute-start.1 = (bf16[8,5120]{1,0:T(8,128)(2,1)S(1)}, bf16[8,5120]{1,0:T(8,128)(2,1)S(1)}, u32[]{:S(2)}, u32[]{:S(2)}) collective-permute-start(bf16[8,5120]{1,0:T(8,128)(2,1)S(1)} %get-tuple-element.40), channel_id=1, source_target_pairs={{1,2},{2,1},{5,6},{6,5},{9,10},{10,9},{13,14},{14,13},{17,18},{18,... | collective-permute-start | bytes 245768 | tf_op jit(solution)/shard_map/ppermute | solution.py:510
  19.4 4.3 %collective-permute-start.4 = (bf16[8,4096]{1,0:T(8,128)(2,1)S(1)}, bf16[8,4096]{1,0:T(8,128)(2,1)S(1)}, u32[]{:S(2)}, u32[]{:S(2)}) collective-permute-start(bf16[8,4096]{1,0:T(8,128)(2,1)S(1)} %get-tuple-element.47), channel_id=1, source_target_pairs={{0,4},{8,12},{4,0},{12,8},{1,5},{9,13},{5,1},{13,9},{2,6},{10,14},... | collective-permute-start | bytes 196616 | tf_op jit(solution)/shard_map/ppermute | solution.py:510
  19.5 4.2 %collective-permute-start.5 = (bf16[8,4096]{1,0:T(8,128)(2,1)S(1)}, bf16[8,4096]{1,0:T(8,128)(2,1)S(1)}, u32[]{:S(2)}, u32[]{:S(2)}) collective-permute-start(bf16[8,4096]{1,0:T(8,128)(2,1)S(1)} %get-tuple-element.48), channel_id=1, source_target_pairs={{4,8},{8,4},{5,9},{9,5},{6,10},{10,6},{7,11},{11,7},{20,24},{24,20... | collective-permute-start | bytes 196616 | tf_op jit(solution)/shard_map/ppermute | solution.py:510
  22.9 1.4 %collective-permute-start.2 = (bf16[8,4096]{1,0:T(8,128)(2,1)S(1)}, bf16[8,4096]{1,0:T(8,128)(2,1)S(1)}, u32[]{:S(2)}, u32[]{:S(2)}) collective-permute-start(bf16[8,4096]{1,0:T(8,128)(2,1)S(1)} %get-tuple-element.41), channel_id=1, source_target_pairs={{0,4},{8,12},{4,0},{12,8},{1,5},{9,13},{5,1},{13,9},{2,6},{10,14},... | collective-permute-start | bytes 196616 | tf_op jit(solution)/shard_map/ppermute | solution.py:510
  23.0 1.3 %collective-permute-start.3 = (bf16[8,4096]{1,0:T(8,128)(2,1)S(1)}, bf16[8,4096]{1,0:T(8,128)(2,1)S(1)}, u32[]{:S(2)}, u32[]{:S(2)}) collective-permute-start(bf16[8,4096]{1,0:T(8,128)(2,1)S(1)} %get-tuple-element.42), channel_id=1, source_target_pairs={{4,8},{8,4},{5,9},{9,5},{6,10},{10,6},{7,11},{11,7},{20,24},{24,20... | collective-permute-start | bytes 196616 | tf_op jit(solution)/shard_map/ppermute | solution.py:510
  26.3 12.1 %collective-permute-start.8 = (bf16[64,1408]{1,0:T(8,128)(2,1)S(1)}, bf16[64,1408]{1,0:T(8,128)(2,1)S(1)}, u32[]{:S(2)}, u32[]{:S(2)}) collective-permute-start(bf16[64,1408]{1,0:T(8,128)(2,1)S(1)} %get-tuple-element.58), channel_id=1, source_target_pairs={{0,4},{4,0},{1,5},{5,1},{2,6},{6,2},{3,7},{7,3},{8,12},{12,8},{9,1... | collective-permute-start | bytes 540680 | tf_op jit(solution)/shard_map/ppermute | solution.py:510
  31.1 6.2 %collective-permute-start.6 = (bf16[8,4096]{1,0:T(8,128)(2,1)S(1)}, bf16[8,4096]{1,0:T(8,128)(2,1)S(1)}, u32[]{:S(2)}, u32[]{:S(2)}) collective-permute-start(bf16[8,4096]{1,0:T(8,128)(2,1)S(1)} %get-tuple-element.54), channel_id=1, source_target_pairs={{0,1},{2,3},{1,0},{3,2},{4,5},{6,7},{5,4},{7,6},{8,9},{10,11},{9,8... | collective-permute-start | bytes 196616 | tf_op jit(solution)/shard_map/ppermute | solution.py:510
  35.0 2.3 %collective-permute-start.7 = (bf16[8,4096]{1,0:T(8,128)(2,1)S(1)}, bf16[8,4096]{1,0:T(8,128)(2,1)S(1)}, u32[]{:S(2)}, u32[]{:S(2)}) collective-permute-start(bf16[8,4096]{1,0:T(8,128)(2,1)S(1)} %get-tuple-element.55), channel_id=1, source_target_pairs={{1,2},{2,1},{5,6},{6,5},{9,10},{10,9},{13,14},{14,13},{17,18},{18,... | collective-permute-start | bytes 196616 | tf_op jit(solution)/shard_map/ppermute | solution.py:510
  39.2 16.1 %all-to-all-start.1 = ((bf16[8,8,2432]{2,1,0:T(8,128)(2,1)}), bf16[8,8,2432]{2,1,0:T(8,128)(2,1)S(1)}, u32[]{:S(2)}, u32[]{:S(2)}) async-start(bf16[8,8,2432]{2,1,0:T(8,128)(2,1)} %bitcast.17), calls=%async_computation.1 | async-start | bytes 622592 | tf_op jit(solution)/shard_map/all_to_all | solution.py:521
  65.8 1.5 %copy-start.2 = (s32[1,1,16,4]{2,3,1,0:T(4,128)S(1)}, s32[1,1,16,4]{2,3,1,0:T(4,128)}, u32[]{:S(2)}) copy-start(s32[1,1,16,4]{2,3,1,0:T(4,128)} %param.18) | copy-start | bytes 772
  65.8 2.6 %collective-permute-start.10 = (bf16[64,1408]{1,0:T(8,128)(2,1)S(1)}, bf16[64,1408]{1,0:T(8,128)(2,1)S(1)}, u32[]{:S(2)}, u32[]{:S(2)}) collective-permute-start(bf16[64,1408]{1,0:T(8,128)(2,1)S(1)} %bitcast.29), channel_id=1, source_target_pairs={{0,4},{4,0},{1,5},{5,1},{2,6},{6,2},{3,7},{7,3},{8,12},{12,8},{9,1... | collective-permute-start | bytes 540680 | tf_op jit(solution)/shard_map/ppermute | solution.py:510
  65.8 1.5 %collective-permute-start.9 = (bf16[64,512]{1,0:T(8,128)(2,1)S(1)}, bf16[64,512]{1,0:T(8,128)(2,1)S(1)}, u32[]{:S(2)}, u32[]{:S(2)}) collective-permute-start(bf16[64,512]{1,0:T(8,128)(2,1)S(1)} %get-tuple-element.61), channel_id=1, source_target_pairs={{0,4},{4,0},{1,5},{5,1},{2,6},{6,2},{3,7},{7,3},{8,12},{12,8},{9,1... | collective-permute-start | bytes 196616 | tf_op jit(solution)/shard_map/ppermute | solution.py:510

commit v11 on v10

--- a/solution.py
+++ b/solution.py
@@ -371,10 +371,8 @@
     given_ref[...] = given.astype(BF)
 
 
-def pair_sum_body(kept_ref, given_ref, replies_ref, out_ref):
-    at = replies_ref.shape[1]
-    out_ref[:, :at] = replies_ref[...]
-    out_ref[:, at:] = (kept_ref[...] + given_ref[...].astype(F32)).astype(BF)
+def pair_sum_body(kept_ref, given_ref, out_ref):
+    out_ref[...] = (kept_ref[...] + given_ref[...].astype(F32)).astype(BF)
 
 
 def inputs_at(pad_ref, e):
@@ -449,16 +447,15 @@
     return (chip // across[1] * 2 + core) * across[1] + chip % across[1]
 
 
-def share_body(back_ref, lists_ref, out_ref, given_ref, across):
-    count, item_lanes = given_ref.shape
-    given_ref[...] = back_ref[:, item_lanes : 2 * item_lanes]
+def share_body(sums_ref, replies_ref, out_ref, across):
+    count, item_lanes = replies_ref.shape
     share = count // (across[0] * across[1] // 2)
     same = iota((count, count), 0) % share == iota((count, count), 1) % share
-    out_ref[...] = dot(ones_where(same), back_ref[:, 2 * item_lanes :]).astype(BF)
-
-
-def coarse_grad_body(back_ref, given_ref, sends_ref, lists_ref, out_ref, across):
-    arrivals = (back_ref[:, : given_ref.shape[1]], given_ref[...])
+    out_ref[:, :item_lanes] = replies_ref[...]
+    out_ref[:, item_lanes:] = dot(ones_where(same), sums_ref[...]).astype(BF)
+
+
+def coarse_grad(arrivals, sends_ref, lists_ref, out_ref, across):
     capacity, devices = sends_ref.shape
     count, item_width = out_ref.shape
     half = item_width // 2
@@ -483,12 +480,16 @@
         out_ref[:, h * half : (h + 1) * half] = totals[h].astype(BF)
 
 
-def last_body(own_ref, other_ref, lists_ref, conv_ref, up_ref, scale):
-    half_count = own_ref.shape[0]
+def last_body(back_ref, given_ref, sends_ref, lists_ref, conv_ref, up_ref, out_ref, item_lanes, across, scale):
+    half_count = back_ref.shape[0]
+    items = (back_ref[:, :item_lanes], given_ref[:, item_lanes : 2 * item_lanes])
+    coarse_grad(items, sends_ref, lists_ref, out_ref, across)
     coarse = up_ref.shape[1]
     count = 2 * half_count
     parts = up_ref.shape[0] // count
-    first, second = (half * scale for half in from_pairs(lists_ref, GX, own_ref, other_ref))
+    own = back_ref[:, 2 * item_lanes :].astype(F32) * scale
+    others = given_ref[:, 2 * item_lanes :].astype(F32) * scale
+    first, second = by_pair(lists_ref, GX, own, others)
     at = 0
     for q in range(parts):
         up_ref[q * count : q * count + half_count] = first[:, at : at + coarse]
@@ -593,28 +594,25 @@
         scratch=[pltpu.VMEM((table_rows, width), BF), pltpu.VMEM((count, sums_width), F32)], flops=conv_flops,
     )
     given = swap(given, "core", 0)
+    (sums,) = call(pair_sum_body, [shape(half_sums)], kept, given)
+    sums = trade_rows(sums, ("x", "gy"))
+    output, lists = call(
+        conv_body, [rows, lists_shape], pad, conv_weight, lists, scratch=[band], flops=conv_flops
+    )
     grad_fine, replies = call(
         functools.partial(fine_grad_body, across=across), [rows, shape((count // 2, 2 * item_lanes))],
         fine_part, lists, *side_grads, up_turned,
     )
-    (sums,) = call(pair_sum_body, [shape((count // 2, 2 * item_lanes + sums_width))], kept, given, replies)
-    back = trade_rows(sums, ("x", "gy"))
-    output, lists = call(
-        conv_body, [rows, lists_shape], pad, conv_weight, lists, scratch=[band], flops=conv_flops
-    )
-    sums, given = call(
-        functools.partial(share_body, across=across), [shape(half_sums), shape((count // 2, item_lanes))], back, lists
-    )
-    sums = trade_rows(sums, ("x", "gy"))
-    other_sums = swap(sums, "core", 0)
-    given = swap(given, "core", 0)
-    (coarse_grad,) = call(
-        functools.partial(coarse_grad_body, across=across), [shape((item_count, item_width))], back, given, sends, lists
-    )
+    (back,) = call(
+        functools.partial(share_body, across=across), [shape((count // 2, 2 * item_lanes + sums_width))], sums, replies
+    )
+    back = trade_rows(back, ("x", "gy"))
+    given = swap(back, "core", 0)
     scale = 1.0 / math.sqrt(64 * bricks * devices)
-    grad_conv, grad_up = call(
-        functools.partial(last_body, scale=scale),
-        [shape((27, C, C), F32), shape((8 * C, coarse), F32)], sums, other_sums, lists,
+    grad_conv, grad_up, coarse_grad = call(
+        functools.partial(last_body, item_lanes=item_lanes, across=across, scale=scale),
+        [shape((27, C, C), F32), shape((8 * C, coarse), F32), shape((item_count, item_width))],
+        back, given, sends, lists,
     )
     return (
         output.reshape(1, 1, bricks, width),

time: 70.3 us -> 65.4 us (0.930)
  waiting for transfers between devices: 16.5 us -> 11.1 us
  blocking collectives: 10.3 us -> 14.1 us
  starting transfers between devices: 25.6 us -> 23.4 us
  Pallas kernels: 14.2 us -> 13.1 us
    all_to_all x2, waiting for transfers between devices: 11.4 us -> 4.18 us  [trade_rows(): lax.all_to_all(grid_view, axes, split_axis=0, concat_axis=0, tiled=True)]
    all_to_all x1, blocking collectives: 10.3 us -> 14.1 us  [trade_rows(): lax.all_to_all(grid_view, axes, split_axis=0, concat_axis=0, tiled=True)]
    ppermute x11 -> x10, starting transfers between devices: 12.7 us -> 10.4 us  [swap(): lax.ppermute(value, axis, [(i, i + 1) for i in lower] + [(i + 1, i) for i...]
    ppermute x11 -> x10, waiting for transfers between devices: 5.08 us -> 6.87 us  [swap(): lax.ppermute(value, axis, [(i, i + 1) for i in lower] + [(i + 1, i) for i...]
    pallas_call x12 -> x11, Pallas kernels: 14.2 us -> 13.1 us  [call(): pl.pallas_call(body, out_shape=tuple(outs), in_specs=[pl.BlockSpec(memory...]
  transfers between devices with their start and end apart: 13 -> 12, of which waited for: 5 -> 6; matrix products, arithmetic and copies ran while one was open for 0% -> 0% of each run, Pallas kernels for 10% -> 10%
where the time goes in v11:
time: 65.4 us; the launch traced here: 64.9 us
  starting transfers between devices  23.4 us (36%)
  blocking collectives  14.1 us (22%)
  Pallas kernels  13.1 us (20%)
  waiting for transfers between devices  11.1 us (17%)
  local copies, waits for them, and re-layouts  2.34 us (4%)
  between operations  0.82 us (1%)
    all_to_all x1, blocking collectives, trade_rows(): lax.all_to_all(grid_view, axes, split_axis=0, concat_axis=0, tiled=True)  14.1 us
    pallas_call x11, Pallas kernels, call(): pl.pallas_call(body, out_shape=tuple(outs), in_specs=[pl.BlockSpec(memory...  13.1 us
    all_to_all x2, starting transfers between devices, trade_rows(): lax.all_to_all(grid_view, axes, split_axis=0, concat_axis=0, tiled=True)  13 us
    ppermute x10, starting transfers between devices, swap(): lax.ppermute(value, axis, [(i, i + 1) for i in lower] + [(i + 1, i) for i...  10.4 us
    ppermute x10, waiting for transfers between devices, swap(): lax.ppermute(value, axis, [(i, i + 1) for i in lower] + [(i + 1, i) for i...  6.87 us
    all_to_all x2, waiting for transfers between devices, trade_rows(): lax.all_to_all(grid_view, axes, split_axis=0, concat_axis=0, tiled=True)  4.18 us
    unnamed x14, local copies, waits for them, and re-layouts  2.34 us
  transfers between devices with their start and end apart: 12, of which 6 were waited for; matrix products, arithmetic and copies ran while one was open for 0% of the time, Pallas kernels for 10%

profile of v11, /device:TPU:0, one launch (start us, length us, event | category | flops | bytes accessed | tf_op | source)
XLA Modules:
  0.0 64.9 jit_solution(15250998782539730864)
XLA Ops:
  0.6 0.0 copy-start.3
  0.6 2.0 %shard_map.137 = (bf16[128,512]{1,0:T(8,128)(2,1)}, s32[8,128]{1,0:T(8,128)}) custom-call(s32[4,16]{1,0:T(4,128)} %bitcast.35, bf16[64,1024]{1,0:T(8,128)(2,1)} %bitcast.39, s32[2,8]{1,0:T(2,128)} %bitcast.41, s32[2,8]{1,0:T(2,128)} %bitcast.42, s32[1,32]{1,0:T(1,128)} %bitcast.43), custom_call_target="tpu_custom_call" | custom-call | bytes 266752 | tf_op jit(solution)/shard_map/pallas_call | solution.py:50
  2.7 7.4 %all-to-all-start = ((bf16[16,8,512]{2,1,0:T(8,128)(2,1)}), bf16[16,8,512]{2,1,0:T(8,128)(2,1)S(1)}, u32[]{:S(2)}, u32[]{:S(2)}) async-start(bf16[16,8,512]{2,1,0:T(8,128)(2,1)} %bitcast.40), calls=%async_computation | async-start | bytes 262144 | tf_op jit(solution)/shard_map/all_to_all | solution.py:522
  10.1 0.0 copy-start.6
  10.1 0.0 copy-done.3
  10.1 0.7 %copy-done.6 = s32[8,128]{1,0:T(8,128)S(1)} copy-done((s32[8,128]{1,0:T(8,128)S(1)}, s32[8,128]{1,0:T(8,128)}, u32[]{:S(2)}) %copy-start.6) | copy-done | bytes 4120
  10.8 0.0 copy-start.4
  10.8 0.9 %copy-done.4 = bf16[1,1,32,4096]{3,2,1,0:T(8,128)(2,1)S(1)} copy-done((bf16[1,1,32,4096]{3,2,1,0:T(8,128)(2,1)S(1)}, bf16[1,1,32,4096]{3,2,1,0:T(8,128)(2,1)}, u32[]{:S(2)}) %copy-start.4) | copy-done | bytes 262168
  11.7 0.0 copy-start.5
  11.7 0.7 %copy-done.5 = s32[1,1,32,27]{2,1,3,0:T(1,128)S(1)} copy-done((s32[1,1,32,27]{2,1,3,0:T(1,128)S(1)}, s32[1,1,32,27]{2,1,3,0:T(1,128)}, u32[]{:S(2)}) %copy-start.5) | copy-done | bytes 3480
  12.4 2.0 %shard_map.138 = (f32[48,4096]{1,0:T(8,128)S(1)}, bf16[8,4096]{1,0:T(8,128)(2,1)S(1)}, bf16[8,4096]{1,0:T(8,128)(2,1)S(1)}, bf16[256,512]{1,0:T(8,128)(2,1)S(1)}...) custom-call(bf16[32,4096]{1,0:T(8,128)(2,1)S(1)} %bitcast.37, ...), custom_call_target="tpu_custom_call" | custom-call | flops 1811939328 | bytes 1785728 | tf_op jit(solution)/shard_map/pallas_call | solution.py:50
  14.4 3.0 %all-to-all-done = bf16[16,8,512]{2,1,0:T(8,128)(2,1)S(1)} async-done(((bf16[16,8,512]{2,1,0:T(8,128)(2,1)}), bf16[16,8,512]{2,1,0:T(8,128)(2,1)S(1)}, u32[]{:S(2)}, u32[]{:S(2)}) %all-to-all-start) | async-done | bytes 131104 | tf_op jit(solution)/shard_map/all_to_all | solution.py:522
  17.4 0.0 copy-done
  17.4 0.0 copy-done.1
  17.4 0.6 shard_map.139
  18.0 0.7 %collective-permute-start = (bf16[8,5120]{1,0:T(8,128)(2,1)S(1)}, bf16[8,5120]{1,0:T(8,128)(2,1)S(1)}, u32[]{:S(2)}, u32[]{:S(2)}) collective-permute-start(bf16[8,5120]{1,0:T(8,128)(2,1)S(1)} %get-tuple-element.38), channel_id=1, source_target_pairs={{0,1},{2,3},{1,0},{3,2},{4,5},{6,7},{5,4},{7,6},{8,9},{10,11},{9,8... | collective-permute-start | bytes 245768 | tf_op jit(solution)/shard_map/ppermute | solution.py:511
  18.8 0.7 %collective-permute-start.1 = (bf16[8,5120]{1,0:T(8,128)(2,1)S(1)}, bf16[8,5120]{1,0:T(8,128)(2,1)S(1)}, u32[]{:S(2)}, u32[]{:S(2)}) collective-permute-start(bf16[8,5120]{1,0:T(8,128)(2,1)S(1)} %get-tuple-element.39), channel_id=1, source_target_pairs={{1,2},{2,1},{5,6},{6,5},{9,10},{10,9},{13,14},{14,13},{17,18},{18,... | collective-permute-start | bytes 245768 | tf_op jit(solution)/shard_map/ppermute | solution.py:511
  19.4 0.1 collective-permute-start.4
  19.5 0.7 %collective-permute-start.5 = (bf16[8,4096]{1,0:T(8,128)(2,1)S(1)}, bf16[8,4096]{1,0:T(8,128)(2,1)S(1)}, u32[]{:S(2)}, u32[]{:S(2)}) collective-permute-start(bf16[8,4096]{1,0:T(8,128)(2,1)S(1)} %get-tuple-element.47), channel_id=1, source_target_pairs={{4,8},{8,4},{5,9},{9,5},{6,10},{10,6},{7,11},{11,7},{20,24},{24,20... | collective-permute-start | bytes 196616 | tf_op jit(solution)/shard_map/ppermute | solution.py:511
  20.2 2.4 %collective-permute-done.even_ref.even_side_ref = bf16[8,5120]{1,0:T(8,128)(2,1)S(1)} collective-permute-done((bf16[8,5120]{1,0:T(8,128)(2,1)S(1)}, bf16[8,5120]{1,0:T(8,128)(2,1)S(1)}, u32[]{:S(2)}, u32[]{:S(2)}) %collective-permute-start) | collective-permute-done | bytes 81952 | tf_op jit(solution)/shard_map/ppermute | solution.py:511
  22.6 0.0 collective-permute-done.1.odd_ref.odd_side_ref
  22.6 0.4 shard_map.140
  22.9 0.1 collective-permute-start.2
  23.0 0.7 %collective-permute-start.3 = (bf16[8,4096]{1,0:T(8,128)(2,1)S(1)}, bf16[8,4096]{1,0:T(8,128)(2,1)S(1)}, u32[]{:S(2)}, u32[]{:S(2)}) collective-permute-start(bf16[8,4096]{1,0:T(8,128)(2,1)S(1)} %get-tuple-element.41), channel_id=1, source_target_pairs={{4,8},{8,4},{5,9},{9,5},{6,10},{10,6},{7,11},{11,7},{20,24},{24,20... | collective-permute-start | bytes 196616 | tf_op jit(solution)/shard_map/ppermute | solution.py:511
  23.7 0.0 collective-permute-done.4.even_grad_ref
  23.7 0.0 collective-permute-done.5.odd_grad_ref
  23.7 0.6 shard_map.141
  24.3 0.0 collective-permute-done.2.even_cross_ref
  24.3 0.0 collective-permute-done.3.odd_cross_ref
  24.3 2.0 %shard_map.142 = (f32[64,1408]{1,0:T(8,128)S(1)}, bf16[64,1408]{1,0:T(8,128)(2,1)S(1)}, bf16[6,6,32,384]{3,2,1,0:T(8,128)(2,1)S(1)}) custom-call(bf16[32,4096]{1,0:T(8,128)(2,1)S(1)} %get-tuple-element.37.merged_ref, bf16[8,5120]{1,0:T(8,128)(2,1)S(1)} %collective-permute-done.even_ref.even_side_ref, ...), custom_call_target="tpu_custom_call" | custom-call | flops 905969664 | bytes 2621440 | tf_op jit(solution)/shard_map/pallas_call | solution.py:50
  26.3 4.8 %collective-permute-start.8 = (bf16[64,1408]{1,0:T(8,128)(2,1)S(1)}, bf16[64,1408]{1,0:T(8,128)(2,1)S(1)}, u32[]{:S(2)}, u32[]{:S(2)}) collective-permute-start(bf16[64,1408]{1,0:T(8,128)(2,1)S(1)} %get-tuple-element.58), channel_id=1, source_target_pairs={{0,4},{4,0},{1,5},{5,1},{2,6},{6,2},{3,7},{7,3},{8,12},{12,8},{9,1... | collective-permute-start | bytes 540680 | tf_op jit(solution)/shard_map/ppermute | solution.py:511
  31.1 1.0 %collective-permute-done.8.given_ref = bf16[64,1408]{1,0:T(8,128)(2,1)S(1)} collective-permute-done((bf16[64,1408]{1,0:T(8,128)(2,1)S(1)}, bf16[64,1408]{1,0:T(8,128)(2,1)S(1)}, u32[]{:S(2)}, u32[]{:S(2)}) %collective-permute-start.8) | collective-permute-done | bytes 180256 | tf_op jit(solution)/shard_map/ppermute | solution.py:511
  32.2 0.7 %shard_map.145 = bf16[64,1408]{1,0:T(8,128)(2,1)} custom-call(f32[64,1408]{1,0:T(8,128)S(1)} %get-tuple-element.57.kept_ref, bf16[64,1408]{1,0:T(8,128)(2,1)S(1)} %collective-permute-done.8.given_ref), custom_call_target="tpu_custom_call" | custom-call | bytes 720896 | tf_op jit(solution)/shard_map/pallas_call | solution.py:50
  32.9 5.7 %all-to-all-start.1 = ((bf16[8,8,1408]{2,1,0:T(8,128)(2,1)}), bf16[8,8,1408]{2,1,0:T(8,128)(2,1)S(1)}, u32[]{:S(2)}, u32[]{:S(2)}) async-start(bf16[8,8,1408]{2,1,0:T(8,128)(2,1)} %bitcast.17), calls=%async_computation.1 | async-start | bytes 360448 | tf_op jit(solution)/shard_map/all_to_all | solution.py:522
  38.5 2.0 %collective-permute-start.6 = (bf16[8,4096]{1,0:T(8,128)(2,1)S(1)}, bf16[8,4096]{1,0:T(8,128)(2,1)S(1)}, u32[]{:S(2)}, u32[]{:S(2)}) collective-permute-start(bf16[8,4096]{1,0:T(8,128)(2,1)S(1)} %get-tuple-element.54), channel_id=1, source_target_pairs={{0,1},{2,3},{1,0},{3,2},{4,5},{6,7},{5,4},{7,6},{8,9},{10,11},{9,8... | collective-permute-start | bytes 196616 | tf_op jit(solution)/shard_map/ppermute | solution.py:511
  40.6 0.7 %collective-permute-start.7 = (bf16[8,4096]{1,0:T(8,128)(2,1)S(1)}, bf16[8,4096]{1,0:T(8,128)(2,1)S(1)}, u32[]{:S(2)}, u32[]{:S(2)}) collective-permute-start(bf16[8,4096]{1,0:T(8,128)(2,1)S(1)} %get-tuple-element.55), channel_id=1, source_target_pairs={{1,2},{2,1},{5,6},{6,5},{9,10},{10,9},{13,14},{14,13},{17,18},{18,... | collective-permute-start | bytes 196616 | tf_op jit(solution)/shard_map/ppermute | solution.py:511
  41.2 2.2 %shard_map.143 = (bf16[32,4096]{1,0:T(8,128)(2,1)}, s32[8,128]{1,0:T(8,128)S(1)}) custom-call(bf16[6,6,32,384]{3,2,1,0:T(8,128)(2,1)S(1)} %get-tuple-element.50.pad_ref, bf16[27,64,64]{2,1,0:T(8,128)(2,1)S(1)} %copy-done.3, s32[8,128]{1,0:T(8,128)S(1)} %get-tuple-element.36.lists_ref), custom_call_target="tpu_custom_call" | custom-call | flops 905969664 | bytes 1376256 | tf_op jit(solution)/shard_map/pallas_call | solution.py:50
  43.4 1.8 %collective-permute-done.6.even_ref = bf16[8,4096]{1,0:T(8,128)(2,1)S(1)} collective-permute-done((bf16[8,4096]{1,0:T(8,128)(2,1)S(1)}, bf16[8,4096]{1,0:T(8,128)(2,1)S(1)}, u32[]{:S(2)}, u32[]{:S(2)}) %collective-permute-start.6) | collective-permute-done | bytes 65568 | tf_op jit(solution)/shard_map/ppermute | solution.py:511
  45.3 0.0 collective-permute-done.7.odd_ref
  45.3 1.1 %shard_map.144 = (bf16[32,4096]{1,0:T(8,128)(2,1)}, bf16[64,1024]{1,0:T(8,128)(2,1)S(1)}) custom-call(f32[32,4096]{1,0:T(8,128)S(1)} %get-tuple-element.52.part_ref, s32[8,128]{1,0:T(8,128)S(1)} %get-tuple-element.53.lists_ref, bf16[8,4096]{1,0:T(8,128)(2,1)S(1)} %collective-permute-done.6.even_ref, bf16[8,4096]{1,0:T(8,128)(2,1)S(1)} %collective-permute-done.7.odd_ref, ...), custom_call_target="tpu_custom_call" | custom-call | bytes 1183744 | tf_op jit(solution)/shard_map/pallas_call | solution.py:50
  46.4 1.2 %all-to-all-done.1 = bf16[8,8,1408]{2,1,0:T(8,128)(2,1)S(1)} async-done(((bf16[8,8,1408]{2,1,0:T(8,128)(2,1)}), bf16[8,8,1408]{2,1,0:T(8,128)(2,1)S(1)}, u32[]{:S(2)}, u32[]{:S(2)}) %all-to-all-start.1) | async-done | bytes 180256 | tf_op jit(solution)/shard_map/all_to_all | solution.py:522
  47.5 0.2 shard_map.146
  47.7 0.0 copy-start.2
  47.7 14.1 %all_to_all.15 = bf16[8,8,2432]{2,1,0:T(8,128)(2,1)S(1)} all-to-all(bf16[8,8,2432]{2,1,0:T(8,128)(2,1)S(1)} %bitcast.29), channel_id=1, replica_groups=mesh['groups'=2,'x'=2,'core'=2,'gy'=4] {'x','gy'}, dimensions={0} | all-to-all | bytes 622592 | tf_op jit(solution)/shard_map/all_to_all | solution.py:522
  61.9 0.0 collective-permute-start.9
  61.9 1.6 %collective-permute-done.9.given_ref = bf16[64,2432]{1,0:T(8,128)(2,1)S(1)} collective-permute-done((bf16[64,2432]{1,0:T(8,128)(2,1)S(1)}, bf16[64,2432]{1,0:T(8,128)(2,1)S(1)}, u32[]{:S(2)}, u32[]{:S(2)}) %collective-permute-start.9) | collective-permute-done | bytes 311328 | tf_op jit(solution)/shard_map/ppermute | solution.py:511
  63.5 0.0 copy-done.2
  63.5 1.4 %shard_map.147 = (f32[27,64,64]{2,1,0:T(8,128)}, f32[512,128]{1,0:T(8,128)}, bf16[64,1024]{1,0:T(8,128)(2,1)}) custom-call(bf16[64,2432]{1,0:T(8,128)(2,1)S(1)} %bitcast.28, bf16[64,2432]{1,0:T(8,128)(2,1)S(1)} %collective-permute-done.9.given_ref, s32[4,16]{1,0:T(4,128)S(1)} %bitcast.36, s32[8,128]{1,0:T(8,128)S(1)} %get-tuple-element.53.lists_ref), custom_call_target="tpu_custom_call" | custom-call | bytes 1462528 | tf_op jit(solution)/shard_map/pallas_call | solution.py:50
  (3 shorter events, 0.0 us)
Async XLA Ops:
  0.6 9.5 %copy-start.3 = (bf16[27,64,64]{2,1,0:T(8,128)(2,1)S(1)}, bf16[27,64,64]{2,1,0:T(8,128)(2,1)}, u32[]{:S(2)}) copy-start(bf16[27,64,64]{2,1,0:T(8,128)(2,1)} %weight_ref.3) | copy-start | bytes 663556
  2.7 14.7 %all-to-all-start = ((bf16[16,8,512]{2,1,0:T(8,128)(2,1)}), bf16[16,8,512]{2,1,0:T(8,128)(2,1)S(1)}, u32[]{:S(2)}, u32[]{:S(2)}) async-start(bf16[16,8,512]{2,1,0:T(8,128)(2,1)} %bitcast.40), calls=%async_computation | async-start | bytes 262144 | tf_op jit(solution)/shard_map/all_to_all | solution.py:522
  10.1 0.7 %copy-start.6 = (s32[8,128]{1,0:T(8,128)S(1)}, s32[8,128]{1,0:T(8,128)}, u32[]{:S(2)}) copy-start(s32[8,128]{1,0:T(8,128)} %get-tuple-element.35.lists_ref) | copy-start | bytes 12292
  10.8 0.9 %copy-start.4 = (bf16[1,1,32,4096]{3,2,1,0:T(8,128)(2,1)S(1)}, bf16[1,1,32,4096]{3,2,1,0:T(8,128)(2,1)}, u32[]{:S(2)}) copy-start(bf16[1,1,32,4096]{3,2,1,0:T(8,128)(2,1)} %param.19) | copy-start | bytes 786436
  11.7 0.7 %copy-start.5 = (s32[1,1,32,27]{2,1,3,0:T(1,128)S(1)}, s32[1,1,32,27]{2,1,3,0:T(1,128)}, u32[]{:S(2)}) copy-start(s32[1,1,32,27]{2,1,3,0:T(1,128)} %param.14) | copy-start | bytes 10372
  12.4 5.0 %copy-start = (bf16[8,128,64]{1,2,0:T(8,128)(2,1)S(1)}, bf16[8,128,64]{1,2,0:T(8,128)(2,1)}, u32[]{:S(2)}) copy-start(bf16[8,128,64]{1,2,0:T(8,128)(2,1)} %param.13) | copy-start | bytes 393220
  12.4 5.0 %copy-start.1 = (bf16[1,1,32,4096]{3,2,1,0:T(8,128)(2,1)S(1)}, bf16[1,1,32,4096]{3,2,1,0:T(8,128)(2,1)}, u32[]{:S(2)}) copy-start(bf16[1,1,32,4096]{3,2,1,0:T(8,128)(2,1)} %param.10) | copy-start | bytes 786436
  18.0 4.5 %collective-permute-start = (bf16[8,5120]{1,0:T(8,128)(2,1)S(1)}, bf16[8,5120]{1,0:T(8,128)(2,1)S(1)}, u32[]{:S(2)}, u32[]{:S(2)}) collective-permute-start(bf16[8,5120]{1,0:T(8,128)(2,1)S(1)} %get-tuple-element.38), channel_id=1, source_target_pairs={{0,1},{2,3},{1,0},{3,2},{4,5},{6,7},{5,4},{7,6},{8,9},{10,11},{9,8... | collective-permute-start | bytes 245768 | tf_op jit(solution)/shard_map/ppermute | solution.py:511
  18.8 3.8 %collective-permute-start.1 = (bf16[8,5120]{1,0:T(8,128)(2,1)S(1)}, bf16[8,5120]{1,0:T(8,128)(2,1)S(1)}, u32[]{:S(2)}, u32[]{:S(2)}) collective-permute-start(bf16[8,5120]{1,0:T(8,128)(2,1)S(1)} %get-tuple-element.39), channel_id=1, source_target_pairs={{1,2},{2,1},{5,6},{6,5},{9,10},{10,9},{13,14},{14,13},{17,18},{18,... | collective-permute-start | bytes 245768 | tf_op jit(solution)/shard_map/ppermute | solution.py:511
  19.4 4.3 %collective-permute-start.4 = (bf16[8,4096]{1,0:T(8,128)(2,1)S(1)}, bf16[8,4096]{1,0:T(8,128)(2,1)S(1)}, u32[]{:S(2)}, u32[]{:S(2)}) collective-permute-start(bf16[8,4096]{1,0:T(8,128)(2,1)S(1)} %get-tuple-element.46), channel_id=1, source_target_pairs={{0,4},{8,12},{4,0},{12,8},{1,5},{9,13},{5,1},{13,9},{2,6},{10,14},... | collective-permute-start | bytes 196616 | tf_op jit(solution)/shard_map/ppermute | solution.py:511
  19.5 4.2 %collective-permute-start.5 = (bf16[8,4096]{1,0:T(8,128)(2,1)S(1)}, bf16[8,4096]{1,0:T(8,128)(2,1)S(1)}, u32[]{:S(2)}, u32[]{:S(2)}) collective-permute-start(bf16[8,4096]{1,0:T(8,128)(2,1)S(1)} %get-tuple-element.47), channel_id=1, source_target_pairs={{4,8},{8,4},{5,9},{9,5},{6,10},{10,6},{7,11},{11,7},{20,24},{24,20... | collective-permute-start | bytes 196616 | tf_op jit(solution)/shard_map/ppermute | solution.py:511
  22.9 1.4 %collective-permute-start.2 = (bf16[8,4096]{1,0:T(8,128)(2,1)S(1)}, bf16[8,4096]{1,0:T(8,128)(2,1)S(1)}, u32[]{:S(2)}, u32[]{:S(2)}) collective-permute-start(bf16[8,4096]{1,0:T(8,128)(2,1)S(1)} %get-tuple-element.40), channel_id=1, source_target_pairs={{0,4},{8,12},{4,0},{12,8},{1,5},{9,13},{5,1},{13,9},{2,6},{10,14},... | collective-permute-start | bytes 196616 | tf_op jit(solution)/shard_map/ppermute | solution.py:511
  23.0 1.3 %collective-permute-start.3 = (bf16[8,4096]{1,0:T(8,128)(2,1)S(1)}, bf16[8,4096]{1,0:T(8,128)(2,1)S(1)}, u32[]{:S(2)}, u32[]{:S(2)}) collective-permute-start(bf16[8,4096]{1,0:T(8,128)(2,1)S(1)} %get-tuple-element.41), channel_id=1, source_target_pairs={{4,8},{8,4},{5,9},{9,5},{6,10},{10,6},{7,11},{11,7},{20,24},{24,20... | collective-permute-start | bytes 196616 | tf_op jit(solution)/shard_map/ppermute | solution.py:511
  26.3 5.9 %collective-permute-start.8 = (bf16[64,1408]{1,0:T(8,128)(2,1)S(1)}, bf16[64,1408]{1,0:T(8,128)(2,1)S(1)}, u32[]{:S(2)}, u32[]{:S(2)}) collective-permute-start(bf16[64,1408]{1,0:T(8,128)(2,1)S(1)} %get-tuple-element.58), channel_id=1, source_target_pairs={{0,4},{4,0},{1,5},{5,1},{2,6},{6,2},{3,7},{7,3},{8,12},{12,8},{9,1... | collective-permute-start | bytes 540680 | tf_op jit(solution)/shard_map/ppermute | solution.py:511
  32.9 14.7 %all-to-all-start.1 = ((bf16[8,8,1408]{2,1,0:T(8,128)(2,1)}), bf16[8,8,1408]{2,1,0:T(8,128)(2,1)S(1)}, u32[]{:S(2)}, u32[]{:S(2)}) async-start(bf16[8,8,1408]{2,1,0:T(8,128)(2,1)} %bitcast.17), calls=%async_computation.1 | async-start | bytes 360448 | tf_op jit(solution)/shard_map/all_to_all | solution.py:522
  38.5 6.7 %collective-permute-start.6 = (bf16[8,4096]{1,0:T(8,128)(2,1)S(1)}, bf16[8,4096]{1,0:T(8,128)(2,1)S(1)}, u32[]{:S(2)}, u32[]{:S(2)}) collective-permute-start(bf16[8,4096]{1,0:T(8,128)(2,1)S(1)} %get-tuple-element.54), channel_id=1, source_target_pairs={{0,1},{2,3},{1,0},{3,2},{4,5},{6,7},{5,4},{7,6},{8,9},{10,11},{9,8... | collective-permute-start | bytes 196616 | tf_op jit(solution)/shard_map/ppermute | solution.py:511
  40.6 4.7 %collective-permute-start.7 = (bf16[8,4096]{1,0:T(8,128)(2,1)S(1)}, bf16[8,4096]{1,0:T(8,128)(2,1)S(1)}, u32[]{:S(2)}, u32[]{:S(2)}) collective-permute-start(bf16[8,4096]{1,0:T(8,128)(2,1)S(1)} %get-tuple-element.55), channel_id=1, source_target_pairs={{1,2},{2,1},{5,6},{6,5},{9,10},{10,9},{13,14},{14,13},{17,18},{18,... | collective-permute-start | bytes 196616 | tf_op jit(solution)/shard_map/ppermute | solution.py:511
  47.7 15.8 %copy-start.2 = (s32[1,1,16,4]{2,3,1,0:T(4,128)S(1)}, s32[1,1,16,4]{2,3,1,0:T(4,128)}, u32[]{:S(2)}) copy-start(s32[1,1,16,4]{2,3,1,0:T(4,128)} %param.18) | copy-start | bytes 772
  61.9 1.6 %collective-permute-start.9 = (bf16[64,2432]{1,0:T(8,128)(2,1)S(1)}, bf16[64,2432]{1,0:T(8,128)(2,1)S(1)}, u32[]{:S(2)}, u32[]{:S(2)}) collective-permute-start(bf16[64,2432]{1,0:T(8,128)(2,1)S(1)} %bitcast.27), channel_id=1, source_target_pairs={{0,4},{4,0},{1,5},{5,1},{2,6},{6,2},{3,7},{7,3},{8,12},{12,8},{9,1... | collective-permute-start | bytes 933896 | tf_op jit(solution)/shard_map/ppermute | solution.py:511

commit v12 on v10

--- a/solution.py
+++ b/solution.py
@@ -314,7 +314,7 @@
 
 def weight_grad_body(
     merged_ref, even_side_ref, odd_side_ref, even_cross_ref, odd_cross_ref, turned_ref, mains_ref, ends_ref, lists_ref,
-    up_sums_ref, kept_ref, given_ref, pad_ref, table_ref, sums_ref,
+    up_sums_ref, sums_ref, pad_ref, table_ref,
 ):
     bricks, width = merged_ref.shape
     face = even_side_ref.shape[0]
@@ -366,9 +366,6 @@
         both = [jnp.where(lanes_low, sums[14 * h + 2 * pair], sums[14 * h + 2 * pair + 1]) for h in range(2)]
         at = up_lanes + pair * 2 * C
         sums_ref[:, at : at + 2 * C] = jnp.concatenate(both, axis=0)
-    kept, given = by_pair(lists_ref, GX, sums_ref[: count // 2], sums_ref[count // 2 :])
-    kept_ref[...] = kept
-    given_ref[...] = given.astype(BF)
 
 
 def pair_sum_body(kept_ref, given_ref, replies_ref, out_ref):
@@ -413,7 +410,13 @@
         out_ref[:, width:] = owners.astype(BF)
 
 
-def fine_grad_body(part_ref, lists_ref, even_ref, odd_ref, up_ref, grad_ref, replies_ref, across):
+def fine_grad_body(
+    part_ref, lists_ref, even_ref, odd_ref, up_ref, sums_ref, grad_ref, replies_ref, kept_ref, given_ref, across
+):
+    half_count = kept_ref.shape[0]
+    kept, given = by_pair(lists_ref, GX, sums_ref[:half_count], sums_ref[half_count:])
+    kept_ref[...] = kept
+    given_ref[...] = given.astype(BF)
     bricks = part_ref.shape[0]
     face = even_ref.shape[0]
     from_next, from_prev = from_pairs(lists_ref, GY, even_ref, odd_ref)
@@ -457,7 +460,7 @@
     out_ref[...] = dot(ones_where(same), back_ref[:, 2 * item_lanes :]).astype(BF)
 
 
-def coarse_grad_body(back_ref, given_ref, sends_ref, lists_ref, out_ref, across):
+def coarse_grad(back_ref, given_ref, sends_ref, lists_ref, out_ref, across):
     arrivals = (back_ref[:, : given_ref.shape[1]], given_ref[...])
     capacity, devices = sends_ref.shape
     count, item_width = out_ref.shape
@@ -483,7 +486,10 @@
         out_ref[:, h * half : (h + 1) * half] = totals[h].astype(BF)
 
 
-def last_body(own_ref, other_ref, lists_ref, conv_ref, up_ref, scale):
+def last_body(
+    own_ref, other_ref, back_ref, given_ref, sends_ref, lists_ref, conv_ref, up_ref, out_ref, across, scale
+):
+    coarse_grad(back_ref, given_ref, sends_ref, lists_ref, out_ref, across)
     half_count = own_ref.shape[0]
     coarse = up_ref.shape[1]
     count = 2 * half_count
@@ -587,16 +593,17 @@
         ext_grad, lists, *cross_grads, *sides, parents,
     )
     side_grads = swap_pairs(to_even, to_odd, "gy")
-    kept, given, pad = call(
-        weight_grad_body, [shape(half_sums, F32), shape(half_sums), shape((6, 6, bricks, WIDE))],
+    sums, pad = call(
+        weight_grad_body, [shape((count, sums_width), F32), shape((6, 6, bricks, WIDE))],
         merged, *sides, *crosses, turned, mains, ends, lists, up_sums,
-        scratch=[pltpu.VMEM((table_rows, width), BF), pltpu.VMEM((count, sums_width), F32)], flops=conv_flops,
+        scratch=[pltpu.VMEM((table_rows, width), BF)], flops=conv_flops,
+    )
+    grad_fine, replies, kept, given = call(
+        functools.partial(fine_grad_body, across=across),
+        [rows, shape((count // 2, 2 * item_lanes)), shape(half_sums, F32), shape(half_sums)],
+        fine_part, lists, *side_grads, up_turned, sums,
     )
     given = swap(given, "core", 0)
-    grad_fine, replies = call(
-        functools.partial(fine_grad_body, across=across), [rows, shape((count // 2, 2 * item_lanes))],
-        fine_part, lists, *side_grads, up_turned,
-    )
     (sums,) = call(pair_sum_body, [shape((count // 2, 2 * item_lanes + sums_width))], kept, given, replies)
     back = trade_rows(sums, ("x", "gy"))
     output, lists = call(
@@ -608,13 +615,11 @@
     sums = trade_rows(sums, ("x", "gy"))
     other_sums = swap(sums, "core", 0)
     given = swap(given, "core", 0)
-    (coarse_grad,) = call(
-        functools.partial(coarse_grad_body, across=across), [shape((item_count, item_width))], back, given, sends, lists
-    )
     scale = 1.0 / math.sqrt(64 * bricks * devices)
-    grad_conv, grad_up = call(
-        functools.partial(last_body, scale=scale),
-        [shape((27, C, C), F32), shape((8 * C, coarse), F32)], sums, other_sums, lists,
+    grad_conv, grad_up, coarse_grad = call(
+        functools.partial(last_body, across=across, scale=scale),
+        [shape((27, C, C), F32), shape((8 * C, coarse), F32), shape((item_count, item_width))],
+        sums, other_sums, back, given, sends, lists,
     )
     return (
         output.reshape(1, 1, bricks, width),

time: 70.3 us -> 66.9 us (0.952)
  starting transfers between devices: 25.6 us -> 23.3 us
  Pallas kernels: 14.2 us -> 13.2 us
    ppermute x11, starting transfers between devices: 12.7 us -> 10 us  [swap(): lax.ppermute(value, axis, [(i, i + 1) for i in lower] + [(i + 1, i) for i...]
    pallas_call x12 -> x11, Pallas kernels: 14.2 us -> 13.2 us  [call(): pl.pallas_call(body, out_shape=tuple(outs), in_specs=[pl.BlockSpec(memory...]
  transfers between devices with their start and end apart: 13 -> 13, of which waited for: 5 -> 5; matrix products, arithmetic and copies ran while one was open for 0% -> 0% of each run, Pallas kernels for 10% -> 11%
where the time goes in v12:
time: 66.9 us; the launch traced here: 66.3 us
  starting transfers between devices  23.3 us (35%)
  waiting for transfers between devices  16.4 us (25%)
  Pallas kernels  13.2 us (20%)
  blocking collectives  10.3 us (15%)
  local copies, waits for them, and re-layouts  2.33 us (3%)
  between operations  0.83 us (1%)
    all_to_all x2, starting transfers between devices, trade_rows(): lax.all_to_all(grid_view, axes, split_axis=0, concat_axis=0, tiled=True)  13.3 us
    pallas_call x11, Pallas kernels, call(): pl.pallas_call(body, out_shape=tuple(outs), in_specs=[pl.BlockSpec(memory...  13.2 us
    all_to_all x2, waiting for transfers between devices, trade_rows(): lax.all_to_all(grid_view, axes, split_axis=0, concat_axis=0, tiled=True)  11.9 us
    all_to_all x1, blocking collectives, trade_rows(): lax.all_to_all(grid_view, axes, split_axis=0, concat_axis=0, tiled=True)  10.3 us
    ppermute x11, starting transfers between devices, swap(): lax.ppermute(value, axis, [(i, i + 1) for i in lower] + [(i + 1, i) for i...  10 us
    ppermute x11, waiting for transfers between devices, swap(): lax.ppermute(value, axis, [(i, i + 1) for i in lower] + [(i + 1, i) for i...  4.45 us
    unnamed x14, local copies, waits for them, and re-layouts  2.33 us
  transfers between devices with their start and end apart: 13, of which 5 were waited for; matrix products, arithmetic and copies ran while one was open for 0% of the time, Pallas kernels for 11%

profile of v12, /device:TPU:0, one launch (start us, length us, event | category | flops | bytes accessed | tf_op | source)
XLA Modules:
  0.0 66.3 jit_solution(7266877668617646874)
XLA Ops:
  0.6 0.0 copy-start.3
  0.6 2.0 %shard_map.137 = (bf16[128,512]{1,0:T(8,128)(2,1)}, s32[8,128]{1,0:T(8,128)}) custom-call(s32[4,16]{1,0:T(4,128)} %bitcast.36, bf16[64,1024]{1,0:T(8,128)(2,1)} %bitcast.40, s32[2,8]{1,0:T(2,128)} %bitcast.42, s32[2,8]{1,0:T(2,128)} %bitcast.43, s32[1,32]{1,0:T(1,128)} %bitcast.44), custom_call_target="tpu_custom_call" | custom-call | bytes 266752 | tf_op jit(solution)/shard_map/pallas_call | solution.py:50
  2.7 7.4 %all-to-all-start = ((bf16[16,8,512]{2,1,0:T(8,128)(2,1)}), bf16[16,8,512]{2,1,0:T(8,128)(2,1)S(1)}, u32[]{:S(2)}, u32[]{:S(2)}) async-start(bf16[16,8,512]{2,1,0:T(8,128)(2,1)} %bitcast.41), calls=%async_computation | async-start | bytes 262144 | tf_op jit(solution)/shard_map/all_to_all | solution.py:527
  10.1 0.0 copy-start.6
  10.1 0.0 copy-done.3
  10.1 0.7 copy-done.6
  10.8 0.0 copy-start.4
  10.8 0.9 %copy-done.4 = bf16[1,1,32,4096]{3,2,1,0:T(8,128)(2,1)S(1)} copy-done((bf16[1,1,32,4096]{3,2,1,0:T(8,128)(2,1)S(1)}, bf16[1,1,32,4096]{3,2,1,0:T(8,128)(2,1)}, u32[]{:S(2)}) %copy-start.4) | copy-done | bytes 262168
  11.7 0.7 %copy-done.5 = s32[1,1,32,27]{2,1,3,0:T(1,128)S(1)} copy-done((s32[1,1,32,27]{2,1,3,0:T(1,128)S(1)}, s32[1,1,32,27]{2,1,3,0:T(1,128)}, u32[]{:S(2)}) %copy-start.5) | copy-done | bytes 3480
  12.4 2.0 %shard_map.138 = (f32[48,4096]{1,0:T(8,128)S(1)}, bf16[8,4096]{1,0:T(8,128)(2,1)S(1)}, bf16[8,4096]{1,0:T(8,128)(2,1)S(1)}, bf16[256,512]{1,0:T(8,128)(2,1)S(1)}...) custom-call(bf16[32,4096]{1,0:T(8,128)(2,1)S(1)} %bitcast.38, ...), custom_call_target="tpu_custom_call" | custom-call | flops 1811939328 | bytes 1785728 | tf_op jit(solution)/shard_map/pallas_call | solution.py:50
  14.4 3.0 %all-to-all-done = bf16[16,8,512]{2,1,0:T(8,128)(2,1)S(1)} async-done(((bf16[16,8,512]{2,1,0:T(8,128)(2,1)}), bf16[16,8,512]{2,1,0:T(8,128)(2,1)S(1)}, u32[]{:S(2)}, u32[]{:S(2)}) %all-to-all-start) | async-done | bytes 131104 | tf_op jit(solution)/shard_map/all_to_all | solution.py:527
  17.4 0.0 copy-done
  17.4 0.0 copy-done.1
  17.4 0.6 shard_map.139
  18.0 0.7 %collective-permute-start = (bf16[8,5120]{1,0:T(8,128)(2,1)S(1)}, bf16[8,5120]{1,0:T(8,128)(2,1)S(1)}, u32[]{:S(2)}, u32[]{:S(2)}) collective-permute-start(bf16[8,5120]{1,0:T(8,128)(2,1)S(1)} %get-tuple-element.41), channel_id=1, source_target_pairs={{0,1},{2,3},{1,0},{3,2},{4,5},{6,7},{5,4},{7,6},{8,9},{10,11},{9,8... | collective-permute-start | bytes 245768 | tf_op jit(solution)/shard_map/ppermute | solution.py:516
  18.8 0.7 collective-permute-start.1
  19.4 0.1 collective-permute-start.4
  19.5 0.7 %collective-permute-start.5 = (bf16[8,4096]{1,0:T(8,128)(2,1)S(1)}, bf16[8,4096]{1,0:T(8,128)(2,1)S(1)}, u32[]{:S(2)}, u32[]{:S(2)}) collective-permute-start(bf16[8,4096]{1,0:T(8,128)(2,1)S(1)} %get-tuple-element.50), channel_id=1, source_target_pairs={{4,8},{8,4},{5,9},{9,5},{6,10},{10,6},{7,11},{11,7},{20,24},{24,20... | collective-permute-start | bytes 196616 | tf_op jit(solution)/shard_map/ppermute | solution.py:516
  20.2 2.4 %collective-permute-done.even_ref.even_side_ref = bf16[8,5120]{1,0:T(8,128)(2,1)S(1)} collective-permute-done((bf16[8,5120]{1,0:T(8,128)(2,1)S(1)}, bf16[8,5120]{1,0:T(8,128)(2,1)S(1)}, u32[]{:S(2)}, u32[]{:S(2)}) %collective-permute-start) | collective-permute-done | bytes 81952 | tf_op jit(solution)/shard_map/ppermute | solution.py:516
  22.6 0.0 collective-permute-done.1.odd_ref.odd_side_ref
  22.6 0.4 shard_map.140
  22.9 0.1 collective-permute-start.2
  23.0 0.7 %collective-permute-start.3 = (bf16[8,4096]{1,0:T(8,128)(2,1)S(1)}, bf16[8,4096]{1,0:T(8,128)(2,1)S(1)}, u32[]{:S(2)}, u32[]{:S(2)}) collective-permute-start(bf16[8,4096]{1,0:T(8,128)(2,1)S(1)} %get-tuple-element.44), channel_id=1, source_target_pairs={{4,8},{8,4},{5,9},{9,5},{6,10},{10,6},{7,11},{11,7},{20,24},{24,20... | collective-permute-start | bytes 196616 | tf_op jit(solution)/shard_map/ppermute | solution.py:516
  23.7 0.0 collective-permute-done.4.even_grad_ref
  23.7 0.0 collective-permute-done.5.odd_grad_ref
  23.7 0.6 shard_map.141
  24.3 3.9 %collective-permute-start.6 = (bf16[8,4096]{1,0:T(8,128)(2,1)S(1)}, bf16[8,4096]{1,0:T(8,128)(2,1)S(1)}, u32[]{:S(2)}, u32[]{:S(2)}) collective-permute-start(bf16[8,4096]{1,0:T(8,128)(2,1)S(1)} %get-tuple-element.56), channel_id=1, source_target_pairs={{0,1},{2,3},{1,0},{3,2},{4,5},{6,7},{5,4},{7,6},{8,9},{10,11},{9,8... | collective-permute-start | bytes 196616 | tf_op jit(solution)/shard_map/ppermute | solution.py:516
  28.2 0.7 collective-permute-start.7
  28.9 0.0 collective-permute-done.2.even_cross_ref
  28.9 0.0 collective-permute-done.3.odd_cross_ref
  28.9 2.0 %shard_map.142 = (f32[128,1408]{1,0:T(8,128)S(1)}, bf16[6,6,32,384]{3,2,1,0:T(8,128)(2,1)S(1)}) custom-call(bf16[32,4096]{1,0:T(8,128)(2,1)S(1)} %get-tuple-element.40.merged_ref, bf16[8,5120]{1,0:T(8,128)(2,1)S(1)} %collective-permute-done.even_ref.even_side_ref, bf16[8,5120]{1,0:T(8,128)(2,1)S(1)} %collective-permute-done.1.odd_ref.odd_side_ref, ...), custom_call_target="tpu_custom_call" | custom-call | flops 905969664 | bytes 2801664 | tf_op jit(solution)/shard_map/pallas_call | solution.py:50
  30.9 0.0 collective-permute-done.6.even_ref
  30.9 0.0 collective-permute-done.7.odd_ref
  30.9 1.1 %shard_map.144 = (bf16[32,4096]{1,0:T(8,128)(2,1)}, bf16[64,1024]{1,0:T(8,128)(2,1)S(1)}, f32[64,1408]{1,0:T(8,128)S(1)}, bf16[64,1408]{1,0:T(8,128)(2,1)S(1)}) custom-call(f32[32,4096]{1,0:T(8,128)S(1)} %get-tuple-element.55.part_ref, s32[8,128]{1,0:T(8,128)S(1)} %get-tuple-element.39.lists_ref, bf16[8,4096]{1,0:T(8,128)(2,1)S(1)} %collective-permute-done.6.even_ref, ...), custom_call_target="tpu_custom_call" | custom-call | bytes 2445312 | tf_op jit(solution)/shard_map/pallas_call | solution.py:50
  32.1 2.1 %collective-permute-start.8 = (bf16[64,1408]{1,0:T(8,128)(2,1)S(1)}, bf16[64,1408]{1,0:T(8,128)(2,1)S(1)}, u32[]{:S(2)}, u32[]{:S(2)}) collective-permute-start(bf16[64,1408]{1,0:T(8,128)(2,1)S(1)} %get-tuple-element.61), channel_id=1, source_target_pairs={{0,4},{4,0},{1,5},{5,1},{2,6},{6,2},{3,7},{7,3},{8,12},{12,8},{9,1... | collective-permute-start | bytes 540680 | tf_op jit(solution)/shard_map/ppermute | solution.py:516
  34.1 1.0 %collective-permute-done.8.given_ref = bf16[64,1408]{1,0:T(8,128)(2,1)S(1)} collective-permute-done((bf16[64,1408]{1,0:T(8,128)(2,1)S(1)}, bf16[64,1408]{1,0:T(8,128)(2,1)S(1)}, u32[]{:S(2)}, u32[]{:S(2)}) %collective-permute-start.8) | collective-permute-done | bytes 180256 | tf_op jit(solution)/shard_map/ppermute | solution.py:516
  35.2 0.8 %shard_map.145 = bf16[64,2432]{1,0:T(8,128)(2,1)} custom-call(f32[64,1408]{1,0:T(8,128)S(1)} %get-tuple-element.60.kept_ref, bf16[64,1408]{1,0:T(8,128)(2,1)S(1)} %collective-permute-done.8.given_ref, bf16[64,1024]{1,0:T(8,128)(2,1)S(1)} %get-tuple-element.62.replies_ref), custom_call_target="tpu_custom_call" | custom-call | bytes 983040 | tf_op jit(solution)/shard_map/pallas_call | solution.py:50
  35.9 5.9 %all-to-all-start.1 = ((bf16[8,8,2432]{2,1,0:T(8,128)(2,1)}), bf16[8,8,2432]{2,1,0:T(8,128)(2,1)S(1)}, u32[]{:S(2)}, u32[]{:S(2)}) async-start(bf16[8,8,2432]{2,1,0:T(8,128)(2,1)} %bitcast.17), calls=%async_computation.1 | async-start | bytes 622592 | tf_op jit(solution)/shard_map/all_to_all | solution.py:527
  41.8 2.2 %shard_map.143 = (bf16[32,4096]{1,0:T(8,128)(2,1)}, s32[8,128]{1,0:T(8,128)S(1)}) custom-call(bf16[6,6,32,384]{3,2,1,0:T(8,128)(2,1)S(1)} %get-tuple-element.53.pad_ref, bf16[27,64,64]{2,1,0:T(8,128)(2,1)S(1)} %copy-done.3, s32[8,128]{1,0:T(8,128)S(1)} %get-tuple-element.39.lists_ref), custom_call_target="tpu_custom_call" | custom-call | flops 905969664 | bytes 1376256 | tf_op jit(solution)/shard_map/pallas_call | solution.py:50
  44.0 8.9 %all-to-all-done.1 = bf16[8,8,2432]{2,1,0:T(8,128)(2,1)S(1)} async-done(((bf16[8,8,2432]{2,1,0:T(8,128)(2,1)}), bf16[8,8,2432]{2,1,0:T(8,128)(2,1)S(1)}, u32[]{:S(2)}, u32[]{:S(2)}) %all-to-all-start.1) | async-done | bytes 311328 | tf_op jit(solution)/shard_map/all_to_all | solution.py:527
  52.9 0.2 shard_map.146
  53.1 10.3 %all_to_all.15 = bf16[8,8,1408]{2,1,0:T(8,128)(2,1)S(1)} all-to-all(bf16[8,8,1408]{2,1,0:T(8,128)(2,1)S(1)} %bitcast.35), channel_id=1, replica_groups=mesh['groups'=2,'x'=2,'core'=2,'gy'=4] {'x','gy'}, dimensions={0} | all-to-all | bytes 360448 | tf_op jit(solution)/shard_map/all_to_all | solution.py:527
  63.5 0.0 collective-permute-start.9
  63.5 0.5 collective-permute-start.10
  64.0 1.0 %collective-permute-done.10.given_ref = bf16[64,512]{1,0:T(8,128)(2,1)S(1)} collective-permute-done((bf16[64,512]{1,0:T(8,128)(2,1)S(1)}, bf16[64,512]{1,0:T(8,128)(2,1)S(1)}, u32[]{:S(2)}, u32[]{:S(2)}) %collective-permute-start.10) | collective-permute-done | bytes 65568 | tf_op jit(solution)/shard_map/ppermute | solution.py:516
  65.0 0.0 collective-permute-done.9.other_ref
  65.0 0.0 copy-done.2
  65.0 1.4 %shard_map.147 = (f32[27,64,64]{2,1,0:T(8,128)}, f32[512,128]{1,0:T(8,128)}, bf16[64,1024]{1,0:T(8,128)(2,1)}) custom-call(bf16[64,1408]{1,0:T(8,128)(2,1)S(1)} %bitcast.30, bf16[64,1408]{1,0:T(8,128)(2,1)S(1)} %collective-permute-done.9.other_ref, bf16[64,2432]{1,0:T(8,128)(2,1)S(1)} %bitcast.28, bf16[64,512]{1,0:T(8,128)(2,1)S(1)} %collective-permute-done.10.given_ref, ...), custom_call_target="tpu_custom_call" | custom-call | bytes 1577216 | tf_op jit(solution)/shard_map/pallas_call | solution.py:50
  (5 shorter events, 0.0 us)
Async XLA Ops:
  0.6 9.5 %copy-start.3 = (bf16[27,64,64]{2,1,0:T(8,128)(2,1)S(1)}, bf16[27,64,64]{2,1,0:T(8,128)(2,1)}, u32[]{:S(2)}) copy-start(bf16[27,64,64]{2,1,0:T(8,128)(2,1)} %weight_ref.3) | copy-start | bytes 663556
  2.7 14.7 %all-to-all-start = ((bf16[16,8,512]{2,1,0:T(8,128)(2,1)}), bf16[16,8,512]{2,1,0:T(8,128)(2,1)S(1)}, u32[]{:S(2)}, u32[]{:S(2)}) async-start(bf16[16,8,512]{2,1,0:T(8,128)(2,1)} %bitcast.41), calls=%async_computation | async-start | bytes 262144 | tf_op jit(solution)/shard_map/all_to_all | solution.py:527
  10.1 0.7 %copy-start.6 = (s32[8,128]{1,0:T(8,128)S(1)}, s32[8,128]{1,0:T(8,128)}, u32[]{:S(2)}) copy-start(s32[8,128]{1,0:T(8,128)} %get-tuple-element.38.lists_ref) | copy-start | bytes 12292
  10.8 0.9 %copy-start.4 = (bf16[1,1,32,4096]{3,2,1,0:T(8,128)(2,1)S(1)}, bf16[1,1,32,4096]{3,2,1,0:T(8,128)(2,1)}, u32[]{:S(2)}) copy-start(bf16[1,1,32,4096]{3,2,1,0:T(8,128)(2,1)} %param.19) | copy-start | bytes 786436
  11.7 0.7 %copy-start.5 = (s32[1,1,32,27]{2,1,3,0:T(1,128)S(1)}, s32[1,1,32,27]{2,1,3,0:T(1,128)}, u32[]{:S(2)}) copy-start(s32[1,1,32,27]{2,1,3,0:T(1,128)} %param.14) | copy-start | bytes 10372
  12.4 5.0 %copy-start = (bf16[8,128,64]{1,2,0:T(8,128)(2,1)S(1)}, bf16[8,128,64]{1,2,0:T(8,128)(2,1)}, u32[]{:S(2)}) copy-start(bf16[8,128,64]{1,2,0:T(8,128)(2,1)} %param.13) | copy-start | bytes 393220
  12.4 5.0 %copy-start.1 = (bf16[1,1,32,4096]{3,2,1,0:T(8,128)(2,1)S(1)}, bf16[1,1,32,4096]{3,2,1,0:T(8,128)(2,1)}, u32[]{:S(2)}) copy-start(bf16[1,1,32,4096]{3,2,1,0:T(8,128)(2,1)} %param.10) | copy-start | bytes 786436
  18.0 4.5 %collective-permute-start = (bf16[8,5120]{1,0:T(8,128)(2,1)S(1)}, bf16[8,5120]{1,0:T(8,128)(2,1)S(1)}, u32[]{:S(2)}, u32[]{:S(2)}) collective-permute-start(bf16[8,5120]{1,0:T(8,128)(2,1)S(1)} %get-tuple-element.41), channel_id=1, source_target_pairs={{0,1},{2,3},{1,0},{3,2},{4,5},{6,7},{5,4},{7,6},{8,9},{10,11},{9,8... | collective-permute-start | bytes 245768 | tf_op jit(solution)/shard_map/ppermute | solution.py:516
  18.8 3.8 %collective-permute-start.1 = (bf16[8,5120]{1,0:T(8,128)(2,1)S(1)}, bf16[8,5120]{1,0:T(8,128)(2,1)S(1)}, u32[]{:S(2)}, u32[]{:S(2)}) collective-permute-start(bf16[8,5120]{1,0:T(8,128)(2,1)S(1)} %get-tuple-element.42), channel_id=1, source_target_pairs={{1,2},{2,1},{5,6},{6,5},{9,10},{10,9},{13,14},{14,13},{17,18},{18,... | collective-permute-start | bytes 245768 | tf_op jit(solution)/shard_map/ppermute | solution.py:516
  19.4 4.3 %collective-permute-start.4 = (bf16[8,4096]{1,0:T(8,128)(2,1)S(1)}, bf16[8,4096]{1,0:T(8,128)(2,1)S(1)}, u32[]{:S(2)}, u32[]{:S(2)}) collective-permute-start(bf16[8,4096]{1,0:T(8,128)(2,1)S(1)} %get-tuple-element.49), channel_id=1, source_target_pairs={{0,4},{8,12},{4,0},{12,8},{1,5},{9,13},{5,1},{13,9},{2,6},{10,14},... | collective-permute-start | bytes 196616 | tf_op jit(solution)/shard_map/ppermute | solution.py:516
  19.5 4.2 %collective-permute-start.5 = (bf16[8,4096]{1,0:T(8,128)(2,1)S(1)}, bf16[8,4096]{1,0:T(8,128)(2,1)S(1)}, u32[]{:S(2)}, u32[]{:S(2)}) collective-permute-start(bf16[8,4096]{1,0:T(8,128)(2,1)S(1)} %get-tuple-element.50), channel_id=1, source_target_pairs={{4,8},{8,4},{5,9},{9,5},{6,10},{10,6},{7,11},{11,7},{20,24},{24,20... | collective-permute-start | bytes 196616 | tf_op jit(solution)/shard_map/ppermute | solution.py:516
  22.9 6.0 %collective-permute-start.2 = (bf16[8,4096]{1,0:T(8,128)(2,1)S(1)}, bf16[8,4096]{1,0:T(8,128)(2,1)S(1)}, u32[]{:S(2)}, u32[]{:S(2)}) collective-permute-start(bf16[8,4096]{1,0:T(8,128)(2,1)S(1)} %get-tuple-element.43), channel_id=1, source_target_pairs={{0,4},{8,12},{4,0},{12,8},{1,5},{9,13},{5,1},{13,9},{2,6},{10,14},... | collective-permute-start | bytes 196616 | tf_op jit(solution)/shard_map/ppermute | solution.py:516
  23.0 5.9 %collective-permute-start.3 = (bf16[8,4096]{1,0:T(8,128)(2,1)S(1)}, bf16[8,4096]{1,0:T(8,128)(2,1)S(1)}, u32[]{:S(2)}, u32[]{:S(2)}) collective-permute-start(bf16[8,4096]{1,0:T(8,128)(2,1)S(1)} %get-tuple-element.44), channel_id=1, source_target_pairs={{4,8},{8,4},{5,9},{9,5},{6,10},{10,6},{7,11},{11,7},{20,24},{24,20... | collective-permute-start | bytes 196616 | tf_op jit(solution)/shard_map/ppermute | solution.py:516
  24.3 6.6 %collective-permute-start.6 = (bf16[8,4096]{1,0:T(8,128)(2,1)S(1)}, bf16[8,4096]{1,0:T(8,128)(2,1)S(1)}, u32[]{:S(2)}, u32[]{:S(2)}) collective-permute-start(bf16[8,4096]{1,0:T(8,128)(2,1)S(1)} %get-tuple-element.56), channel_id=1, source_target_pairs={{0,1},{2,3},{1,0},{3,2},{4,5},{6,7},{5,4},{7,6},{8,9},{10,11},{9,8... | collective-permute-start | bytes 196616 | tf_op jit(solution)/shard_map/ppermute | solution.py:516
  28.2 2.7 %collective-permute-start.7 = (bf16[8,4096]{1,0:T(8,128)(2,1)S(1)}, bf16[8,4096]{1,0:T(8,128)(2,1)S(1)}, u32[]{:S(2)}, u32[]{:S(2)}) collective-permute-start(bf16[8,4096]{1,0:T(8,128)(2,1)S(1)} %get-tuple-element.57), channel_id=1, source_target_pairs={{1,2},{2,1},{5,6},{6,5},{9,10},{10,9},{13,14},{14,13},{17,18},{18,... | collective-permute-start | bytes 196616 | tf_op jit(solution)/shard_map/ppermute | solution.py:516
  32.1 3.1 %collective-permute-start.8 = (bf16[64,1408]{1,0:T(8,128)(2,1)S(1)}, bf16[64,1408]{1,0:T(8,128)(2,1)S(1)}, u32[]{:S(2)}, u32[]{:S(2)}) collective-permute-start(bf16[64,1408]{1,0:T(8,128)(2,1)S(1)} %get-tuple-element.61), channel_id=1, source_target_pairs={{0,4},{4,0},{1,5},{5,1},{2,6},{6,2},{3,7},{7,3},{8,12},{12,8},{9,1... | collective-permute-start | bytes 540680 | tf_op jit(solution)/shard_map/ppermute | solution.py:516
  35.9 17.0 %all-to-all-start.1 = ((bf16[8,8,2432]{2,1,0:T(8,128)(2,1)}), bf16[8,8,2432]{2,1,0:T(8,128)(2,1)S(1)}, u32[]{:S(2)}, u32[]{:S(2)}) async-start(bf16[8,8,2432]{2,1,0:T(8,128)(2,1)} %bitcast.17), calls=%async_computation.1 | async-start | bytes 622592 | tf_op jit(solution)/shard_map/all_to_all | solution.py:527
  63.4 1.5 %copy-start.2 = (s32[1,1,16,4]{2,3,1,0:T(4,128)S(1)}, s32[1,1,16,4]{2,3,1,0:T(4,128)}, u32[]{:S(2)}) copy-start(s32[1,1,16,4]{2,3,1,0:T(4,128)} %param.18) | copy-start | bytes 772
  63.5 1.5 %collective-permute-start.9 = (bf16[64,1408]{1,0:T(8,128)(2,1)S(1)}, bf16[64,1408]{1,0:T(8,128)(2,1)S(1)}, u32[]{:S(2)}, u32[]{:S(2)}) collective-permute-start(bf16[64,1408]{1,0:T(8,128)(2,1)S(1)} %bitcast.29), channel_id=1, source_target_pairs={{0,4},{4,0},{1,5},{5,1},{2,6},{6,2},{3,7},{7,3},{8,12},{12,8},{9,1... | collective-permute-start | bytes 540680 | tf_op jit(solution)/shard_map/ppermute | solution.py:516
  63.5 1.5 %collective-permute-start.10 = (bf16[64,512]{1,0:T(8,128)(2,1)S(1)}, bf16[64,512]{1,0:T(8,128)(2,1)S(1)}, u32[]{:S(2)}, u32[]{:S(2)}) collective-permute-start(bf16[64,512]{1,0:T(8,128)(2,1)S(1)} %get-tuple-element.65), channel_id=1, source_target_pairs={{0,4},{4,0},{1,5},{5,1},{2,6},{6,2},{3,7},{7,3},{8,12},{12,8},{9,1... | collective-permute-start | bytes 196616 | tf_op jit(solution)/shard_map/ppermute | solution.py:516

commit v13 on v11

--- a/solution.py
+++ b/solution.py
@@ -61,10 +61,8 @@
     return jax.ShapeDtypeStruct(dims, dtype)
 
 
-def items_out(sends_ref, items_ref, out_ref):
+def items_named(sends_ref, count):
     capacity, devices = sends_ref.shape
-    count, width = items_ref.shape
-    half = width // 2
     group = 2 * capacity
     lanes = devices * group
     spread = ones_where(iota((lanes, devices), 0) // group == iota((lanes, devices), 1))
@@ -72,8 +70,7 @@
     values = dot_nt(spread, sends_ref[...].astype(F32).astype(BF))
     item = jnp.sum(jnp.where(slot == iota((lanes, capacity), 1), values, 0.0), axis=1, keepdims=True).astype(I32)
     place = jnp.where(item < count, item + iota((lanes, 1), 0) % 2 * count, -1)
-    chosen = ones_where(iota((lanes, 2 * count), 1) == place)
-    out_ref[...] = dot(chosen, jnp.concatenate([items_ref[:, :half], items_ref[:, half:]], axis=0)).astype(BF)
+    return ones_where(iota((lanes, 2 * count), 1) == place)
 
 
 def merge(received_ref, slots, up_ref, fine_ref, merged_ref, parents_ref):
@@ -278,14 +275,19 @@
     copies = [pltpu.make_async_copy(s, p, arrived.at[i]) for i, (s, p) in enumerate(zip(sources, places))]
     for copy in copies:
         copy.start()
-    for copy in copies:
+    copies[0].wait()
+    chosen = items_named(sends_ref, items_ref.shape[0])
+    copies[1].wait()
+    half = out_ref.shape[1]
+    items = jnp.concatenate([items_ref[:, :half], items_ref[:, half:]], axis=0)
+    out_ref[...] = dot(chosen, items).astype(BF)
+    for copy in copies[2:]:
         copy.wait()
     face, bricks = (sides_ref.shape[1], slots_ref.shape[1])
     lists_ref[...] = jnp.zeros(lists_ref.shape, I32)
     lists_ref[0:2, :face] = sides_ref[...]
     lists_ref[2:4, :face] = crosses_ref[...]
     lists_ref[4:5, :bricks] = slots_ref[...]
-    items_out(sends_ref, items_ref, out_ref)
 
 
 def side_grad_body(
@@ -313,7 +315,7 @@
 
 
 def weight_grad_body(
-    merged_ref, even_side_ref, odd_side_ref, even_cross_ref, odd_cross_ref, turned_ref, mains_ref, ends_ref, lists_ref,
+    odd_cross_ref, even_cross_ref, merged_ref, even_side_ref, odd_side_ref, turned_ref, mains_ref, ends_ref, lists_ref,
     up_sums_ref, kept_ref, given_ref, pad_ref, table_ref, sums_ref,
 ):
     bricks, width = merged_ref.shape
@@ -590,7 +592,7 @@
     side_grads = swap_pairs(to_even, to_odd, "gy")
     kept, given, pad = call(
         weight_grad_body, [shape(half_sums, F32), shape(half_sums), shape((6, 6, bricks, WIDE))],
-        merged, *sides, *crosses, turned, mains, ends, lists, up_sums,
+        *crosses[::-1], merged, *sides, turned, mains, ends, lists, up_sums,
         scratch=[pltpu.VMEM((table_rows, width), BF), pltpu.VMEM((count, sums_width), F32)], flops=conv_flops,
     )
     given = swap(given, "core", 0)

time: 65.4 us -> 65.1 us (level)
    ppermute x10, starting transfers between devices: 10.4 us -> 9.1 us  [swap(): lax.ppermute(value, axis, [(i, i + 1) for i in lower] + [(i + 1, i) for i...]
    all_to_all x2, waiting for transfers between devices: 4.18 us -> 5.4 us  [trade_rows(): lax.all_to_all(grid_view, axes, split_axis=0, concat_axis=0, tiled=True)]
    ppermute x10, waiting for transfers between devices: 6.87 us -> 5.94 us  [swap(): lax.ppermute(value, axis, [(i, i + 1) for i in lower] + [(i + 1, i) for i...]
    all_to_all x2, starting transfers between devices: 13 us -> 13.9 us  [trade_rows(): lax.all_to_all(grid_view, axes, split_axis=0, concat_axis=0, tiled=True)]
  transfers between devices with their start and end apart: 12 -> 12, of which waited for: 6 -> 7; matrix products, arithmetic and copies ran while one was open for 0% -> 0% of each run, Pallas kernels for 10% -> 10%
where the time goes in v13:
time: 65.1 us; the launch traced here: 64.6 us
  starting transfers between devices  23 us (35%)
  blocking collectives  14.1 us (22%)
  Pallas kernels  12.9 us (20%)
  waiting for transfers between devices  11.3 us (17%)
  local copies, waits for them, and re-layouts  2.34 us (4%)
  between operations  0.8 us (1%)
    all_to_all x1, blocking collectives, trade_rows(): lax.all_to_all(grid_view, axes, split_axis=0, concat_axis=0, tiled=True)  14.1 us
    all_to_all x2, starting transfers between devices, trade_rows(): lax.all_to_all(grid_view, axes, split_axis=0, concat_axis=0, tiled=True)  13.9 us
    pallas_call x11, Pallas kernels, call(): pl.pallas_call(body, out_shape=tuple(outs), in_specs=[pl.BlockSpec(memory...  12.9 us
    ppermute x10, starting transfers between devices, swap(): lax.ppermute(value, axis, [(i, i + 1) for i in lower] + [(i + 1, i) for i...  9.1 us
    ppermute x10, waiting for transfers between devices, swap(): lax.ppermute(value, axis, [(i, i + 1) for i in lower] + [(i + 1, i) for i...  5.94 us
    all_to_all x2, waiting for transfers between devices, trade_rows(): lax.all_to_all(grid_view, axes, split_axis=0, concat_axis=0, tiled=True)  5.4 us
    unnamed x14, local copies, waits for them, and re-layouts  2.34 us
  transfers between devices with their start and end apart: 12, of which 7 were waited for; matrix products, arithmetic and copies ran while one was open for 0% of the time, Pallas kernels for 10%

profile of v13, /device:TPU:0, one launch (start us, length us, event | category | flops | bytes accessed | tf_op | source)
XLA Modules:
  0.0 64.6 jit_solution(12890906299298691634)
XLA Ops:
  0.6 0.0 copy-start.3
  0.6 1.9 %shard_map.137 = (bf16[128,512]{1,0:T(8,128)(2,1)}, s32[8,128]{1,0:T(8,128)}) custom-call(s32[4,16]{1,0:T(4,128)} %bitcast.35, bf16[64,1024]{1,0:T(8,128)(2,1)} %bitcast.39, s32[2,8]{1,0:T(2,128)} %bitcast.41, s32[2,8]{1,0:T(2,128)} %bitcast.42, s32[1,32]{1,0:T(1,128)} %bitcast.43), custom_call_target="tpu_custom_call" | custom-call | bytes 266752 | tf_op jit(solution)/shard_map/pallas_call | solution.py:50
  2.5 7.4 %all-to-all-start = ((bf16[16,8,512]{2,1,0:T(8,128)(2,1)}), bf16[16,8,512]{2,1,0:T(8,128)(2,1)S(1)}, u32[]{:S(2)}, u32[]{:S(2)}) async-start(bf16[16,8,512]{2,1,0:T(8,128)(2,1)} %bitcast.40), calls=%async_computation | async-start | bytes 262144 | tf_op jit(solution)/shard_map/all_to_all | solution.py:524
  9.9 0.0 copy-start.6
  9.9 0.0 copy-done.3
  9.9 0.7 %copy-done.6 = s32[8,128]{1,0:T(8,128)S(1)} copy-done((s32[8,128]{1,0:T(8,128)S(1)}, s32[8,128]{1,0:T(8,128)}, u32[]{:S(2)}) %copy-start.6) | copy-done | bytes 4120
  10.6 0.0 copy-start.4
  10.6 0.9 %copy-done.4 = bf16[1,1,32,4096]{3,2,1,0:T(8,128)(2,1)S(1)} copy-done((bf16[1,1,32,4096]{3,2,1,0:T(8,128)(2,1)S(1)}, bf16[1,1,32,4096]{3,2,1,0:T(8,128)(2,1)}, u32[]{:S(2)}) %copy-start.4) | copy-done | bytes 262168
  11.5 0.0 copy-start.5
  11.5 0.7 %copy-done.5 = s32[1,1,32,27]{2,1,3,0:T(1,128)S(1)} copy-done((s32[1,1,32,27]{2,1,3,0:T(1,128)S(1)}, s32[1,1,32,27]{2,1,3,0:T(1,128)}, u32[]{:S(2)}) %copy-start.5) | copy-done | bytes 3480
  12.2 2.0 %shard_map.138 = (f32[48,4096]{1,0:T(8,128)S(1)}, bf16[8,4096]{1,0:T(8,128)(2,1)S(1)}, bf16[8,4096]{1,0:T(8,128)(2,1)S(1)}, bf16[256,512]{1,0:T(8,128)(2,1)S(1)}...) custom-call(bf16[32,4096]{1,0:T(8,128)(2,1)S(1)} %bitcast.37, ...), custom_call_target="tpu_custom_call" | custom-call | flops 1811939328 | bytes 1785728 | tf_op jit(solution)/shard_map/pallas_call | solution.py:50
  14.2 3.0 %all-to-all-done = bf16[16,8,512]{2,1,0:T(8,128)(2,1)S(1)} async-done(((bf16[16,8,512]{2,1,0:T(8,128)(2,1)}), bf16[16,8,512]{2,1,0:T(8,128)(2,1)S(1)}, u32[]{:S(2)}, u32[]{:S(2)}) %all-to-all-start) | async-done | bytes 131104 | tf_op jit(solution)/shard_map/all_to_all | solution.py:524
  17.2 0.0 copy-done
  17.2 0.0 copy-done.1
  17.2 0.6 shard_map.139
  17.9 0.7 %collective-permute-start = (bf16[8,5120]{1,0:T(8,128)(2,1)S(1)}, bf16[8,5120]{1,0:T(8,128)(2,1)S(1)}, u32[]{:S(2)}, u32[]{:S(2)}) collective-permute-start(bf16[8,5120]{1,0:T(8,128)(2,1)S(1)} %get-tuple-element.38), channel_id=1, source_target_pairs={{0,1},{2,3},{1,0},{3,2},{4,5},{6,7},{5,4},{7,6},{8,9},{10,11},{9,8... | collective-permute-start | bytes 245768 | tf_op jit(solution)/shard_map/ppermute | solution.py:513
  18.6 0.7 %collective-permute-start.1 = (bf16[8,5120]{1,0:T(8,128)(2,1)S(1)}, bf16[8,5120]{1,0:T(8,128)(2,1)S(1)}, u32[]{:S(2)}, u32[]{:S(2)}) collective-permute-start(bf16[8,5120]{1,0:T(8,128)(2,1)S(1)} %get-tuple-element.39), channel_id=1, source_target_pairs={{1,2},{2,1},{5,6},{6,5},{9,10},{10,9},{13,14},{14,13},{17,18},{18,... | collective-permute-start | bytes 245768 | tf_op jit(solution)/shard_map/ppermute | solution.py:513
  19.2 0.1 collective-permute-start.4
  19.3 0.7 %collective-permute-start.5 = (bf16[8,4096]{1,0:T(8,128)(2,1)S(1)}, bf16[8,4096]{1,0:T(8,128)(2,1)S(1)}, u32[]{:S(2)}, u32[]{:S(2)}) collective-permute-start(bf16[8,4096]{1,0:T(8,128)(2,1)S(1)} %get-tuple-element.47), channel_id=1, source_target_pairs={{4,8},{8,4},{5,9},{9,5},{6,10},{10,6},{7,11},{11,7},{20,24},{24,20... | collective-permute-start | bytes 196616 | tf_op jit(solution)/shard_map/ppermute | solution.py:513
  20.0 2.4 %collective-permute-done.even_ref.even_side_ref = bf16[8,5120]{1,0:T(8,128)(2,1)S(1)} collective-permute-done((bf16[8,5120]{1,0:T(8,128)(2,1)S(1)}, bf16[8,5120]{1,0:T(8,128)(2,1)S(1)}, u32[]{:S(2)}, u32[]{:S(2)}) %collective-permute-start) | collective-permute-done | bytes 81952 | tf_op jit(solution)/shard_map/ppermute | solution.py:513
  22.4 0.0 collective-permute-done.1.odd_ref.odd_side_ref
  22.4 0.3 shard_map.140
  22.7 0.7 %collective-permute-start.2 = (bf16[8,4096]{1,0:T(8,128)(2,1)S(1)}, bf16[8,4096]{1,0:T(8,128)(2,1)S(1)}, u32[]{:S(2)}, u32[]{:S(2)}) collective-permute-start(bf16[8,4096]{1,0:T(8,128)(2,1)S(1)} %get-tuple-element.40), channel_id=1, source_target_pairs={{4,8},{8,4},{5,9},{9,5},{6,10},{10,6},{7,11},{11,7},{20,24},{24,20... | collective-permute-start | bytes 196616 | tf_op jit(solution)/shard_map/ppermute | solution.py:513
  23.4 2.4 %collective-permute-start.3 = (bf16[8,4096]{1,0:T(8,128)(2,1)S(1)}, bf16[8,4096]{1,0:T(8,128)(2,1)S(1)}, u32[]{:S(2)}, u32[]{:S(2)}) collective-permute-start(bf16[8,4096]{1,0:T(8,128)(2,1)S(1)} %get-tuple-element.41), channel_id=1, source_target_pairs={{0,4},{8,12},{4,0},{12,8},{1,5},{9,13},{5,1},{13,9},{2,6},{10,14},... | collective-permute-start | bytes 196616 | tf_op jit(solution)/shard_map/ppermute | solution.py:513
  25.8 0.0 collective-permute-done.4.even_grad_ref
  25.8 0.0 collective-permute-done.5.odd_grad_ref
  25.8 0.6 shard_map.141
  26.4 0.0 collective-permute-done.2.odd_cross_ref
  26.4 0.3 collective-permute-done.3.even_cross_ref
  26.7 2.0 %shard_map.142 = (f32[64,1408]{1,0:T(8,128)S(1)}, bf16[64,1408]{1,0:T(8,128)(2,1)S(1)}, bf16[6,6,32,384]{3,2,1,0:T(8,128)(2,1)S(1)}) custom-call(bf16[8,4096]{1,0:T(8,128)(2,1)S(1)} %collective-permute-done.2.odd_cross_ref, bf16[8,4096]{1,0:T(8,128)(2,1)S(1)} %collective-permute-done.3.even_cross_ref, bf16[32,4096]{1,0:T(8,128)(2,1)S(1)} %get-tuple-element.37.merged_ref, ...), custom_call_target="tpu_custom_call" | custom-call | flops 905969664 | bytes 2621440 | tf_op jit(solution)/shard_map/pallas_call | solution.py:50
  28.7 1.2 %collective-permute-start.8 = (bf16[64,1408]{1,0:T(8,128)(2,1)S(1)}, bf16[64,1408]{1,0:T(8,128)(2,1)S(1)}, u32[]{:S(2)}, u32[]{:S(2)}) collective-permute-start(bf16[64,1408]{1,0:T(8,128)(2,1)S(1)} %get-tuple-element.58), channel_id=1, source_target_pairs={{0,4},{4,0},{1,5},{5,1},{2,6},{6,2},{3,7},{7,3},{8,12},{12,8},{9,1... | collective-permute-start | bytes 540680 | tf_op jit(solution)/shard_map/ppermute | solution.py:513
  29.9 1.0 %collective-permute-done.8.given_ref = bf16[64,1408]{1,0:T(8,128)(2,1)S(1)} collective-permute-done((bf16[64,1408]{1,0:T(8,128)(2,1)S(1)}, bf16[64,1408]{1,0:T(8,128)(2,1)S(1)}, u32[]{:S(2)}, u32[]{:S(2)}) %collective-permute-start.8) | collective-permute-done | bytes 180256 | tf_op jit(solution)/shard_map/ppermute | solution.py:513
  31.0 0.7 %shard_map.145 = bf16[64,1408]{1,0:T(8,128)(2,1)} custom-call(f32[64,1408]{1,0:T(8,128)S(1)} %get-tuple-element.57.kept_ref, bf16[64,1408]{1,0:T(8,128)(2,1)S(1)} %collective-permute-done.8.given_ref), custom_call_target="tpu_custom_call" | custom-call | bytes 720896 | tf_op jit(solution)/shard_map/pallas_call | solution.py:50
  31.7 6.6 %all-to-all-start.1 = ((bf16[8,8,1408]{2,1,0:T(8,128)(2,1)}), bf16[8,8,1408]{2,1,0:T(8,128)(2,1)S(1)}, u32[]{:S(2)}, u32[]{:S(2)}) async-start(bf16[8,8,1408]{2,1,0:T(8,128)(2,1)} %bitcast.17), calls=%async_computation.1 | async-start | bytes 360448 | tf_op jit(solution)/shard_map/all_to_all | solution.py:524
  38.3 2.0 %collective-permute-start.6 = (bf16[8,4096]{1,0:T(8,128)(2,1)S(1)}, bf16[8,4096]{1,0:T(8,128)(2,1)S(1)}, u32[]{:S(2)}, u32[]{:S(2)}) collective-permute-start(bf16[8,4096]{1,0:T(8,128)(2,1)S(1)} %get-tuple-element.54), channel_id=1, source_target_pairs={{0,1},{2,3},{1,0},{3,2},{4,5},{6,7},{5,4},{7,6},{8,9},{10,11},{9,8... | collective-permute-start | bytes 196616 | tf_op jit(solution)/shard_map/ppermute | solution.py:513
  40.3 0.7 %collective-permute-start.7 = (bf16[8,4096]{1,0:T(8,128)(2,1)S(1)}, bf16[8,4096]{1,0:T(8,128)(2,1)S(1)}, u32[]{:S(2)}, u32[]{:S(2)}) collective-permute-start(bf16[8,4096]{1,0:T(8,128)(2,1)S(1)} %get-tuple-element.55), channel_id=1, source_target_pairs={{1,2},{2,1},{5,6},{6,5},{9,10},{10,9},{13,14},{14,13},{17,18},{18,... | collective-permute-start | bytes 196616 | tf_op jit(solution)/shard_map/ppermute | solution.py:513
  40.9 2.2 %shard_map.143 = (bf16[32,4096]{1,0:T(8,128)(2,1)}, s32[8,128]{1,0:T(8,128)S(1)}) custom-call(bf16[6,6,32,384]{3,2,1,0:T(8,128)(2,1)S(1)} %get-tuple-element.50.pad_ref, bf16[27,64,64]{2,1,0:T(8,128)(2,1)S(1)} %copy-done.3, s32[8,128]{1,0:T(8,128)S(1)} %get-tuple-element.36.lists_ref), custom_call_target="tpu_custom_call" | custom-call | flops 905969664 | bytes 1376256 | tf_op jit(solution)/shard_map/pallas_call | solution.py:50
  43.2 0.6 collective-permute-done.6.even_ref
  43.8 0.0 collective-permute-done.7.odd_ref
  43.8 1.1 %shard_map.144 = (bf16[32,4096]{1,0:T(8,128)(2,1)}, bf16[64,1024]{1,0:T(8,128)(2,1)S(1)}) custom-call(f32[32,4096]{1,0:T(8,128)S(1)} %get-tuple-element.52.part_ref, s32[8,128]{1,0:T(8,128)S(1)} %get-tuple-element.53.lists_ref, bf16[8,4096]{1,0:T(8,128)(2,1)S(1)} %collective-permute-done.6.even_ref, bf16[8,4096]{1,0:T(8,128)(2,1)S(1)} %collective-permute-done.7.odd_ref, ...), custom_call_target="tpu_custom_call" | custom-call | bytes 1183744 | tf_op jit(solution)/shard_map/pallas_call | solution.py:50
  44.9 2.4 %all-to-all-done.1 = bf16[8,8,1408]{2,1,0:T(8,128)(2,1)S(1)} async-done(((bf16[8,8,1408]{2,1,0:T(8,128)(2,1)}), bf16[8,8,1408]{2,1,0:T(8,128)(2,1)S(1)}, u32[]{:S(2)}, u32[]{:S(2)}) %all-to-all-start.1) | async-done | bytes 180256 | tf_op jit(solution)/shard_map/all_to_all | solution.py:524
  47.3 0.2 shard_map.146
  47.5 0.0 copy-start.2
  47.5 14.1 %all_to_all.15 = bf16[8,8,2432]{2,1,0:T(8,128)(2,1)S(1)} all-to-all(bf16[8,8,2432]{2,1,0:T(8,128)(2,1)S(1)} %bitcast.29), channel_id=1, replica_groups=mesh['groups'=2,'x'=2,'core'=2,'gy'=4] {'x','gy'}, dimensions={0} | all-to-all | bytes 622592 | tf_op jit(solution)/shard_map/all_to_all | solution.py:524
  61.6 0.0 collective-permute-start.9
  61.6 1.6 %collective-permute-done.9.given_ref = bf16[64,2432]{1,0:T(8,128)(2,1)S(1)} collective-permute-done((bf16[64,2432]{1,0:T(8,128)(2,1)S(1)}, bf16[64,2432]{1,0:T(8,128)(2,1)S(1)}, u32[]{:S(2)}, u32[]{:S(2)}) %collective-permute-start.9) | collective-permute-done | bytes 311328 | tf_op jit(solution)/shard_map/ppermute | solution.py:513
  63.2 0.0 copy-done.2
  63.2 1.4 %shard_map.147 = (f32[27,64,64]{2,1,0:T(8,128)}, f32[512,128]{1,0:T(8,128)}, bf16[64,1024]{1,0:T(8,128)(2,1)}) custom-call(bf16[64,2432]{1,0:T(8,128)(2,1)S(1)} %bitcast.28, bf16[64,2432]{1,0:T(8,128)(2,1)S(1)} %collective-permute-done.9.given_ref, s32[4,16]{1,0:T(4,128)S(1)} %bitcast.36, s32[8,128]{1,0:T(8,128)S(1)} %get-tuple-element.53.lists_ref), custom_call_target="tpu_custom_call" | custom-call | bytes 1462528 | tf_op jit(solution)/shard_map/pallas_call | solution.py:50
  (3 shorter events, 0.0 us)
Async XLA Ops:
  0.6 9.3 %copy-start.3 = (bf16[27,64,64]{2,1,0:T(8,128)(2,1)S(1)}, bf16[27,64,64]{2,1,0:T(8,128)(2,1)}, u32[]{:S(2)}) copy-start(bf16[27,64,64]{2,1,0:T(8,128)(2,1)} %weight_ref.3) | copy-start | bytes 663556
  2.5 14.7 %all-to-all-start = ((bf16[16,8,512]{2,1,0:T(8,128)(2,1)}), bf16[16,8,512]{2,1,0:T(8,128)(2,1)S(1)}, u32[]{:S(2)}, u32[]{:S(2)}) async-start(bf16[16,8,512]{2,1,0:T(8,128)(2,1)} %bitcast.40), calls=%async_computation | async-start | bytes 262144 | tf_op jit(solution)/shard_map/all_to_all | solution.py:524
  9.9 0.7 %copy-start.6 = (s32[8,128]{1,0:T(8,128)S(1)}, s32[8,128]{1,0:T(8,128)}, u32[]{:S(2)}) copy-start(s32[8,128]{1,0:T(8,128)} %get-tuple-element.35.lists_ref) | copy-start | bytes 12292
  10.6 0.9 %copy-start.4 = (bf16[1,1,32,4096]{3,2,1,0:T(8,128)(2,1)S(1)}, bf16[1,1,32,4096]{3,2,1,0:T(8,128)(2,1)}, u32[]{:S(2)}) copy-start(bf16[1,1,32,4096]{3,2,1,0:T(8,128)(2,1)} %param.19) | copy-start | bytes 786436
  11.5 0.7 %copy-start.5 = (s32[1,1,32,27]{2,1,3,0:T(1,128)S(1)}, s32[1,1,32,27]{2,1,3,0:T(1,128)}, u32[]{:S(2)}) copy-start(s32[1,1,32,27]{2,1,3,0:T(1,128)} %param.14) | copy-start | bytes 10372
  12.2 5.0 %copy-start = (bf16[8,128,64]{1,2,0:T(8,128)(2,1)S(1)}, bf16[8,128,64]{1,2,0:T(8,128)(2,1)}, u32[]{:S(2)}) copy-start(bf16[8,128,64]{1,2,0:T(8,128)(2,1)} %param.13) | copy-start | bytes 393220
  12.2 5.0 %copy-start.1 = (bf16[1,1,32,4096]{3,2,1,0:T(8,128)(2,1)S(1)}, bf16[1,1,32,4096]{3,2,1,0:T(8,128)(2,1)}, u32[]{:S(2)}) copy-start(bf16[1,1,32,4096]{3,2,1,0:T(8,128)(2,1)} %param.10) | copy-start | bytes 786436
  17.9 4.5 %collective-permute-start = (bf16[8,5120]{1,0:T(8,128)(2,1)S(1)}, bf16[8,5120]{1,0:T(8,128)(2,1)S(1)}, u32[]{:S(2)}, u32[]{:S(2)}) collective-permute-start(bf16[8,5120]{1,0:T(8,128)(2,1)S(1)} %get-tuple-element.38), channel_id=1, source_target_pairs={{0,1},{2,3},{1,0},{3,2},{4,5},{6,7},{5,4},{7,6},{8,9},{10,11},{9,8... | collective-permute-start | bytes 245768 | tf_op jit(solution)/shard_map/ppermute | solution.py:513
  18.6 3.8 %collective-permute-start.1 = (bf16[8,5120]{1,0:T(8,128)(2,1)S(1)}, bf16[8,5120]{1,0:T(8,128)(2,1)S(1)}, u32[]{:S(2)}, u32[]{:S(2)}) collective-permute-start(bf16[8,5120]{1,0:T(8,128)(2,1)S(1)} %get-tuple-element.39), channel_id=1, source_target_pairs={{1,2},{2,1},{5,6},{6,5},{9,10},{10,9},{13,14},{14,13},{17,18},{18,... | collective-permute-start | bytes 245768 | tf_op jit(solution)/shard_map/ppermute | solution.py:513
  19.2 6.6 %collective-permute-start.4 = (bf16[8,4096]{1,0:T(8,128)(2,1)S(1)}, bf16[8,4096]{1,0:T(8,128)(2,1)S(1)}, u32[]{:S(2)}, u32[]{:S(2)}) collective-permute-start(bf16[8,4096]{1,0:T(8,128)(2,1)S(1)} %get-tuple-element.46), channel_id=1, source_target_pairs={{0,4},{8,12},{4,0},{12,8},{1,5},{9,13},{5,1},{13,9},{2,6},{10,14},... | collective-permute-start | bytes 196616 | tf_op jit(solution)/shard_map/ppermute | solution.py:513
  19.3 6.5 %collective-permute-start.5 = (bf16[8,4096]{1,0:T(8,128)(2,1)S(1)}, bf16[8,4096]{1,0:T(8,128)(2,1)S(1)}, u32[]{:S(2)}, u32[]{:S(2)}) collective-permute-start(bf16[8,4096]{1,0:T(8,128)(2,1)S(1)} %get-tuple-element.47), channel_id=1, source_target_pairs={{4,8},{8,4},{5,9},{9,5},{6,10},{10,6},{7,11},{11,7},{20,24},{24,20... | collective-permute-start | bytes 196616 | tf_op jit(solution)/shard_map/ppermute | solution.py:513
  22.7 3.7 %collective-permute-start.2 = (bf16[8,4096]{1,0:T(8,128)(2,1)S(1)}, bf16[8,4096]{1,0:T(8,128)(2,1)S(1)}, u32[]{:S(2)}, u32[]{:S(2)}) collective-permute-start(bf16[8,4096]{1,0:T(8,128)(2,1)S(1)} %get-tuple-element.40), channel_id=1, source_target_pairs={{4,8},{8,4},{5,9},{9,5},{6,10},{10,6},{7,11},{11,7},{20,24},{24,20... | collective-permute-start | bytes 196616 | tf_op jit(solution)/shard_map/ppermute | solution.py:513
  23.4 3.3 %collective-permute-start.3 = (bf16[8,4096]{1,0:T(8,128)(2,1)S(1)}, bf16[8,4096]{1,0:T(8,128)(2,1)S(1)}, u32[]{:S(2)}, u32[]{:S(2)}) collective-permute-start(bf16[8,4096]{1,0:T(8,128)(2,1)S(1)} %get-tuple-element.41), channel_id=1, source_target_pairs={{0,4},{8,12},{4,0},{12,8},{1,5},{9,13},{5,1},{13,9},{2,6},{10,14},... | collective-permute-start | bytes 196616 | tf_op jit(solution)/shard_map/ppermute | solution.py:513
  28.7 2.3 %collective-permute-start.8 = (bf16[64,1408]{1,0:T(8,128)(2,1)S(1)}, bf16[64,1408]{1,0:T(8,128)(2,1)S(1)}, u32[]{:S(2)}, u32[]{:S(2)}) collective-permute-start(bf16[64,1408]{1,0:T(8,128)(2,1)S(1)} %get-tuple-element.58), channel_id=1, source_target_pairs={{0,4},{4,0},{1,5},{5,1},{2,6},{6,2},{3,7},{7,3},{8,12},{12,8},{9,1... | collective-permute-start | bytes 540680 | tf_op jit(solution)/shard_map/ppermute | solution.py:513
  31.7 15.6 %all-to-all-start.1 = ((bf16[8,8,1408]{2,1,0:T(8,128)(2,1)}), bf16[8,8,1408]{2,1,0:T(8,128)(2,1)S(1)}, u32[]{:S(2)}, u32[]{:S(2)}) async-start(bf16[8,8,1408]{2,1,0:T(8,128)(2,1)} %bitcast.17), calls=%async_computation.1 | async-start | bytes 360448 | tf_op jit(solution)/shard_map/all_to_all | solution.py:524
  38.3 5.5 %collective-permute-start.6 = (bf16[8,4096]{1,0:T(8,128)(2,1)S(1)}, bf16[8,4096]{1,0:T(8,128)(2,1)S(1)}, u32[]{:S(2)}, u32[]{:S(2)}) collective-permute-start(bf16[8,4096]{1,0:T(8,128)(2,1)S(1)} %get-tuple-element.54), channel_id=1, source_target_pairs={{0,1},{2,3},{1,0},{3,2},{4,5},{6,7},{5,4},{7,6},{8,9},{10,11},{9,8... | collective-permute-start | bytes 196616 | tf_op jit(solution)/shard_map/ppermute | solution.py:513
  40.3 3.5 %collective-permute-start.7 = (bf16[8,4096]{1,0:T(8,128)(2,1)S(1)}, bf16[8,4096]{1,0:T(8,128)(2,1)S(1)}, u32[]{:S(2)}, u32[]{:S(2)}) collective-permute-start(bf16[8,4096]{1,0:T(8,128)(2,1)S(1)} %get-tuple-element.55), channel_id=1, source_target_pairs={{1,2},{2,1},{5,6},{6,5},{9,10},{10,9},{13,14},{14,13},{17,18},{18,... | collective-permute-start | bytes 196616 | tf_op jit(solution)/shard_map/ppermute | solution.py:513
  47.5 15.8 %copy-start.2 = (s32[1,1,16,4]{2,3,1,0:T(4,128)S(1)}, s32[1,1,16,4]{2,3,1,0:T(4,128)}, u32[]{:S(2)}) copy-start(s32[1,1,16,4]{2,3,1,0:T(4,128)} %param.18) | copy-start | bytes 772
  61.6 1.6 %collective-permute-start.9 = (bf16[64,2432]{1,0:T(8,128)(2,1)S(1)}, bf16[64,2432]{1,0:T(8,128)(2,1)S(1)}, u32[]{:S(2)}, u32[]{:S(2)}) collective-permute-start(bf16[64,2432]{1,0:T(8,128)(2,1)S(1)} %bitcast.27), channel_id=1, source_target_pairs={{0,4},{4,0},{1,5},{5,1},{2,6},{6,2},{3,7},{7,3},{8,12},{12,8},{9,1... | collective-permute-start | bytes 933896 | tf_op jit(solution)/shard_map/ppermute | solution.py:513

commit v14 on v13

--- a/solution.py
+++ b/solution.py
@@ -130,7 +130,7 @@
     return lists_ref[4:5, :bricks]
 
 
-def cross_body(merged_ref, even_ref, odd_ref, lists_ref, a_ref, b_ref):
+def cross_body(odd_ref, even_ref, merged_ref, lists_ref, a_ref, b_ref):
     face, width = a_ref.shape
     high, low = from_pairs(lists_ref, GY, even_ref, odd_ref)
     rows = jnp.concatenate([merged_ref[...], stack_rows(low[:, :width], high[:, :width])], axis=0)
@@ -413,7 +413,7 @@
         out_ref[:, width:] = owners.astype(BF)
 
 
-def fine_grad_body(part_ref, lists_ref, even_ref, odd_ref, up_ref, grad_ref, replies_ref, across):
+def fine_grad_body(odd_ref, even_ref, part_ref, lists_ref, up_ref, grad_ref, replies_ref, across):
     bricks = part_ref.shape[0]
     face = even_ref.shape[0]
     from_next, from_prev = from_pairs(lists_ref, GY, even_ref, odd_ref)
@@ -581,7 +581,7 @@
         received, up_turned, fine, lists,
     )
     sides = swap_pairs(to_even, to_odd, "gy")
-    to_even, to_odd = call(cross_body, [face_rows, face_rows], merged, *sides, lists)
+    to_even, to_odd = call(cross_body, [face_rows, face_rows], *sides[::-1], merged, lists)
     crosses = swap_pairs(to_even, to_odd, GX_AXES)
     half_sums = (count // 2, sums_width)
     fine_part, to_even, to_odd, up_sums = call(
@@ -603,7 +603,7 @@
     )
     grad_fine, replies = call(
         functools.partial(fine_grad_body, across=across), [rows, shape((count // 2, 2 * item_lanes))],
-        fine_part, lists, *side_grads, up_turned,
+        *side_grads[::-1], fine_part, lists, up_turned,
     )
     (back,) = call(
         functools.partial(share_body, across=across), [shape((count // 2, 2 * item_lanes + sums_width))], sums, replies

time: 65.1 us -> 65.1 us (level)
  starting transfers between devices: 23 us -> 26.5 us
  waiting for transfers between devices: 11.3 us -> 8.59 us
    ppermute x10, starting transfers between devices: 9.1 us -> 14.6 us  [swap(): lax.ppermute(value, axis, [(i, i + 1) for i in lower] + [(i + 1, i) for i...]
    all_to_all x2, waiting for transfers between devices: 5.4 us -> 3.02 us  [trade_rows(): lax.all_to_all(grid_view, axes, split_axis=0, concat_axis=0, tiled=True)]
    all_to_all x2, starting transfers between devices: 13.9 us -> 11.9 us  [trade_rows(): lax.all_to_all(grid_view, axes, split_axis=0, concat_axis=0, tiled=True)]
  transfers between devices with their start and end apart: 12 -> 12, of which waited for: 7 -> 6; matrix products, arithmetic and copies ran while one was open for 0% -> 0% of each run, Pallas kernels for 10% -> 10%
where the time goes in v14:
time: 65.1 us; the launch traced here: 64.6 us
  starting transfers between devices  26.5 us (41%)
  blocking collectives  13.5 us (21%)
  Pallas kernels  12.9 us (20%)
  waiting for transfers between devices  8.59 us (13%)
  local copies, waits for them, and re-layouts  2.34 us (4%)
  between operations  0.8 us (1%)
    ppermute x10, starting transfers between devices, swap(): lax.ppermute(value, axis, [(i, i + 1) for i in lower] + [(i + 1, i) for i...  14.6 us
    all_to_all x1, blocking collectives, trade_rows(): lax.all_to_all(grid_view, axes, split_axis=0, concat_axis=0, tiled=True)  13.5 us
    pallas_call x11, Pallas kernels, call(): pl.pallas_call(body, out_shape=tuple(outs), in_specs=[pl.BlockSpec(memory...  12.9 us
    all_to_all x2, starting transfers between devices, trade_rows(): lax.all_to_all(grid_view, axes, split_axis=0, concat_axis=0, tiled=True)  11.9 us
    ppermute x10, waiting for transfers between devices, swap(): lax.ppermute(value, axis, [(i, i + 1) for i in lower] + [(i + 1, i) for i...  5.57 us
    all_to_all x2, waiting for transfers between devices, trade_rows(): lax.all_to_all(grid_view, axes, split_axis=0, concat_axis=0, tiled=True)  3.02 us
    unnamed x14, local copies, waits for them, and re-layouts  2.34 us
  transfers between devices with their start and end apart: 12, of which 6 were waited for; matrix products, arithmetic and copies ran while one was open for 0% of the time, Pallas kernels for 10%

profile of v14, /device:TPU:0, one launch (start us, length us, event | category | flops | bytes accessed | tf_op | source)
XLA Modules:
  0.0 64.6 jit_solution(8093124115096726648)
XLA Ops:
  0.6 0.0 copy-start.3
  0.6 1.9 %shard_map.137 = (bf16[128,512]{1,0:T(8,128)(2,1)}, s32[8,128]{1,0:T(8,128)}) custom-call(s32[4,16]{1,0:T(4,128)} %bitcast.35, bf16[64,1024]{1,0:T(8,128)(2,1)} %bitcast.39, s32[2,8]{1,0:T(2,128)} %bitcast.41, s32[2,8]{1,0:T(2,128)} %bitcast.42, s32[1,32]{1,0:T(1,128)} %bitcast.43), custom_call_target="tpu_custom_call" | custom-call | bytes 266752 | tf_op jit(solution)/shard_map/pallas_call | solution.py:50
  2.5 7.4 %all-to-all-start = ((bf16[16,8,512]{2,1,0:T(8,128)(2,1)}), bf16[16,8,512]{2,1,0:T(8,128)(2,1)S(1)}, u32[]{:S(2)}, u32[]{:S(2)}) async-start(bf16[16,8,512]{2,1,0:T(8,128)(2,1)} %bitcast.40), calls=%async_computation | async-start | bytes 262144 | tf_op jit(solution)/shard_map/all_to_all | solution.py:524
  9.9 0.0 copy-start.6
  9.9 0.0 copy-done.3
  9.9 0.7 %copy-done.6 = s32[8,128]{1,0:T(8,128)S(1)} copy-done((s32[8,128]{1,0:T(8,128)S(1)}, s32[8,128]{1,0:T(8,128)}, u32[]{:S(2)}) %copy-start.6) | copy-done | bytes 4120
  10.6 0.0 copy-start.4
  10.6 0.9 %copy-done.4 = bf16[1,1,32,4096]{3,2,1,0:T(8,128)(2,1)S(1)} copy-done((bf16[1,1,32,4096]{3,2,1,0:T(8,128)(2,1)S(1)}, bf16[1,1,32,4096]{3,2,1,0:T(8,128)(2,1)}, u32[]{:S(2)}) %copy-start.4) | copy-done | bytes 262168
  11.5 0.0 copy-start.5
  11.5 0.7 %copy-done.5 = s32[1,1,32,27]{2,1,3,0:T(1,128)S(1)} copy-done((s32[1,1,32,27]{2,1,3,0:T(1,128)S(1)}, s32[1,1,32,27]{2,1,3,0:T(1,128)}, u32[]{:S(2)}) %copy-start.5) | copy-done | bytes 3480
  12.2 2.0 %shard_map.138 = (f32[48,4096]{1,0:T(8,128)S(1)}, bf16[8,4096]{1,0:T(8,128)(2,1)S(1)}, bf16[8,4096]{1,0:T(8,128)(2,1)S(1)}, bf16[256,512]{1,0:T(8,128)(2,1)S(1)}...) custom-call(bf16[32,4096]{1,0:T(8,128)(2,1)S(1)} %bitcast.37, ...), custom_call_target="tpu_custom_call" | custom-call | flops 1811939328 | bytes 1785728 | tf_op jit(solution)/shard_map/pallas_call | solution.py:50
  14.2 3.0 %all-to-all-done = bf16[16,8,512]{2,1,0:T(8,128)(2,1)S(1)} async-done(((bf16[16,8,512]{2,1,0:T(8,128)(2,1)}), bf16[16,8,512]{2,1,0:T(8,128)(2,1)S(1)}, u32[]{:S(2)}, u32[]{:S(2)}) %all-to-all-start) | async-done | bytes 131104 | tf_op jit(solution)/shard_map/all_to_all | solution.py:524
  17.2 0.0 copy-done
  17.2 0.0 copy-done.1
  17.2 0.6 shard_map.139
  17.9 0.7 %collective-permute-start = (bf16[8,5120]{1,0:T(8,128)(2,1)S(1)}, bf16[8,5120]{1,0:T(8,128)(2,1)S(1)}, u32[]{:S(2)}, u32[]{:S(2)}) collective-permute-start(bf16[8,5120]{1,0:T(8,128)(2,1)S(1)} %get-tuple-element.37), channel_id=1, source_target_pairs={{1,2},{2,1},{5,6},{6,5},{9,10},{10,9},{13,14},{14,13},{17,18},{18,... | collective-permute-start | bytes 245768 | tf_op jit(solution)/shard_map/ppermute | solution.py:513
  18.5 2.6 %collective-permute-start.1 = (bf16[8,5120]{1,0:T(8,128)(2,1)S(1)}, bf16[8,5120]{1,0:T(8,128)(2,1)S(1)}, u32[]{:S(2)}, u32[]{:S(2)}) collective-permute-start(bf16[8,5120]{1,0:T(8,128)(2,1)S(1)} %get-tuple-element.38), channel_id=1, source_target_pairs={{0,1},{2,3},{1,0},{3,2},{4,5},{6,7},{5,4},{7,6},{8,9},{10,11},{9,8... | collective-permute-start | bytes 245768 | tf_op jit(solution)/shard_map/ppermute | solution.py:513
  21.2 0.0 collective-permute-start.4
  21.2 0.7 %collective-permute-start.5 = (bf16[8,4096]{1,0:T(8,128)(2,1)S(1)}, bf16[8,4096]{1,0:T(8,128)(2,1)S(1)}, u32[]{:S(2)}, u32[]{:S(2)}) collective-permute-start(bf16[8,4096]{1,0:T(8,128)(2,1)S(1)} %get-tuple-element.47), channel_id=1, source_target_pairs={{4,8},{8,4},{5,9},{9,5},{6,10},{10,6},{7,11},{11,7},{20,24},{24,20... | collective-permute-start | bytes 196616 | tf_op jit(solution)/shard_map/ppermute | solution.py:513
  21.8 0.0 collective-permute-done.odd_ref.odd_side_ref
  21.8 1.8 %collective-permute-done.1.even_ref.even_side_ref = bf16[8,5120]{1,0:T(8,128)(2,1)S(1)} collective-permute-done((bf16[8,5120]{1,0:T(8,128)(2,1)S(1)}, bf16[8,5120]{1,0:T(8,128)(2,1)S(1)}, u32[]{:S(2)}, u32[]{:S(2)}) %collective-permute-start.1) | collective-permute-done | bytes 81952 | tf_op jit(solution)/shard_map/ppermute | solution.py:513
  23.6 0.3 shard_map.140
  24.0 0.7 %collective-permute-start.2 = (bf16[8,4096]{1,0:T(8,128)(2,1)S(1)}, bf16[8,4096]{1,0:T(8,128)(2,1)S(1)}, u32[]{:S(2)}, u32[]{:S(2)}) collective-permute-start(bf16[8,4096]{1,0:T(8,128)(2,1)S(1)} %get-tuple-element.40), channel_id=1, source_target_pairs={{4,8},{8,4},{5,9},{9,5},{6,10},{10,6},{7,11},{11,7},{20,24},{24,20... | collective-permute-start | bytes 196616 | tf_op jit(solution)/shard_map/ppermute | solution.py:513
  24.6 3.0 %collective-permute-start.3 = (bf16[8,4096]{1,0:T(8,128)(2,1)S(1)}, bf16[8,4096]{1,0:T(8,128)(2,1)S(1)}, u32[]{:S(2)}, u32[]{:S(2)}) collective-permute-start(bf16[8,4096]{1,0:T(8,128)(2,1)S(1)} %get-tuple-element.41), channel_id=1, source_target_pairs={{0,4},{8,12},{4,0},{12,8},{1,5},{9,13},{5,1},{13,9},{2,6},{10,14},... | collective-permute-start | bytes 196616 | tf_op jit(solution)/shard_map/ppermute | solution.py:513
  27.7 0.0 collective-permute-done.4.even_grad_ref
  27.7 0.0 collective-permute-done.5.odd_grad_ref
  27.7 0.6 shard_map.141
  28.3 0.0 collective-permute-done.2.odd_cross_ref
  28.3 0.3 collective-permute-done.3.even_cross_ref
  28.6 2.0 %shard_map.142 = (f32[64,1408]{1,0:T(8,128)S(1)}, bf16[64,1408]{1,0:T(8,128)(2,1)S(1)}, bf16[6,6,32,384]{3,2,1,0:T(8,128)(2,1)S(1)}) custom-call(bf16[8,4096]{1,0:T(8,128)(2,1)S(1)} %collective-permute-done.2.odd_cross_ref, bf16[8,4096]{1,0:T(8,128)(2,1)S(1)} %collective-permute-done.3.even_cross_ref, bf16[32,4096]{1,0:T(8,128)(2,1)S(1)} %get-tuple-element.39.merged_ref, ...), custom_call_target="tpu_custom_call" | custom-call | flops 905969664 | bytes 2621440 | tf_op jit(solution)/shard_map/pallas_call | solution.py:50
  30.6 1.5 %collective-permute-start.8 = (bf16[64,1408]{1,0:T(8,128)(2,1)S(1)}, bf16[64,1408]{1,0:T(8,128)(2,1)S(1)}, u32[]{:S(2)}, u32[]{:S(2)}) collective-permute-start(bf16[64,1408]{1,0:T(8,128)(2,1)S(1)} %get-tuple-element.58), channel_id=1, source_target_pairs={{0,4},{4,0},{1,5},{5,1},{2,6},{6,2},{3,7},{7,3},{8,12},{12,8},{9,1... | collective-permute-start | bytes 540680 | tf_op jit(solution)/shard_map/ppermute | solution.py:513
  32.1 1.0 %collective-permute-done.8.given_ref = bf16[64,1408]{1,0:T(8,128)(2,1)S(1)} collective-permute-done((bf16[64,1408]{1,0:T(8,128)(2,1)S(1)}, bf16[64,1408]{1,0:T(8,128)(2,1)S(1)}, u32[]{:S(2)}, u32[]{:S(2)}) %collective-permute-start.8) | collective-permute-done | bytes 180256 | tf_op jit(solution)/shard_map/ppermute | solution.py:513
  33.1 0.7 %shard_map.145 = bf16[64,1408]{1,0:T(8,128)(2,1)} custom-call(f32[64,1408]{1,0:T(8,128)S(1)} %get-tuple-element.57.kept_ref, bf16[64,1408]{1,0:T(8,128)(2,1)S(1)} %collective-permute-done.8.given_ref), custom_call_target="tpu_custom_call" | custom-call | bytes 720896 | tf_op jit(solution)/shard_map/pallas_call | solution.py:50
  33.8 4.5 %all-to-all-start.1 = ((bf16[8,8,1408]{2,1,0:T(8,128)(2,1)}), bf16[8,8,1408]{2,1,0:T(8,128)(2,1)S(1)}, u32[]{:S(2)}, u32[]{:S(2)}) async-start(bf16[8,8,1408]{2,1,0:T(8,128)(2,1)} %bitcast.17), calls=%async_computation.1 | async-start | bytes 360448 | tf_op jit(solution)/shard_map/all_to_all | solution.py:524
  38.3 0.7 %collective-permute-start.6 = (bf16[8,4096]{1,0:T(8,128)(2,1)S(1)}, bf16[8,4096]{1,0:T(8,128)(2,1)S(1)}, u32[]{:S(2)}, u32[]{:S(2)}) collective-permute-start(bf16[8,4096]{1,0:T(8,128)(2,1)S(1)} %get-tuple-element.52), channel_id=1, source_target_pairs={{1,2},{2,1},{5,6},{6,5},{9,10},{10,9},{13,14},{14,13},{17,18},{18,... | collective-permute-start | bytes 196616 | tf_op jit(solution)/shard_map/ppermute | solution.py:513
  39.0 4.8 %collective-permute-start.7 = (bf16[8,4096]{1,0:T(8,128)(2,1)S(1)}, bf16[8,4096]{1,0:T(8,128)(2,1)S(1)}, u32[]{:S(2)}, u32[]{:S(2)}) collective-permute-start(bf16[8,4096]{1,0:T(8,128)(2,1)S(1)} %get-tuple-element.53), channel_id=1, source_target_pairs={{0,1},{2,3},{1,0},{3,2},{4,5},{6,7},{5,4},{7,6},{8,9},{10,11},{9,8... | collective-permute-start | bytes 196616 | tf_op jit(solution)/shard_map/ppermute | solution.py:513
  43.8 2.2 %shard_map.143 = (bf16[32,4096]{1,0:T(8,128)(2,1)}, s32[8,128]{1,0:T(8,128)S(1)}) custom-call(bf16[6,6,32,384]{3,2,1,0:T(8,128)(2,1)S(1)} %get-tuple-element.50.pad_ref, bf16[27,64,64]{2,1,0:T(8,128)(2,1)S(1)} %copy-done.3, s32[8,128]{1,0:T(8,128)S(1)} %get-tuple-element.36.lists_ref), custom_call_target="tpu_custom_call" | custom-call | flops 905969664 | bytes 1376256 | tf_op jit(solution)/shard_map/pallas_call | solution.py:50
  46.0 0.0 collective-permute-done.6.odd_ref
  46.0 0.8 %collective-permute-done.7.even_ref = bf16[8,4096]{1,0:T(8,128)(2,1)S(1)} collective-permute-done((bf16[8,4096]{1,0:T(8,128)(2,1)S(1)}, bf16[8,4096]{1,0:T(8,128)(2,1)S(1)}, u32[]{:S(2)}, u32[]{:S(2)}) %collective-permute-start.7) | collective-permute-done | bytes 65568 | tf_op jit(solution)/shard_map/ppermute | solution.py:513
  46.8 1.1 %shard_map.144 = (bf16[32,4096]{1,0:T(8,128)(2,1)}, bf16[64,1024]{1,0:T(8,128)(2,1)S(1)}) custom-call(bf16[8,4096]{1,0:T(8,128)(2,1)S(1)} %collective-permute-done.6.odd_ref, bf16[8,4096]{1,0:T(8,128)(2,1)S(1)} %collective-permute-done.7.even_ref, f32[32,4096]{1,0:T(8,128)S(1)} %get-tuple-element.54.part_ref, s32[8,128]{1,0:T(8,128)S(1)} %get-tuple-element.55.lists_ref, ...), custom_call_target="tpu_custom_call" | custom-call | bytes 1183744 | tf_op jit(solution)/shard_map/pallas_call | solution.py:50
  47.9 0.0 all-to-all-done.1
  47.9 0.2 shard_map.146
  48.1 0.0 copy-start.2
  48.1 13.5 %all_to_all.15 = bf16[8,8,2432]{2,1,0:T(8,128)(2,1)S(1)} all-to-all(bf16[8,8,2432]{2,1,0:T(8,128)(2,1)S(1)} %bitcast.29), channel_id=1, replica_groups=mesh['groups'=2,'x'=2,'core'=2,'gy'=4] {'x','gy'}, dimensions={0} | all-to-all | bytes 622592 | tf_op jit(solution)/shard_map/all_to_all | solution.py:524
  61.6 0.0 collective-permute-start.9
  61.6 1.6 %collective-permute-done.9.given_ref = bf16[64,2432]{1,0:T(8,128)(2,1)S(1)} collective-permute-done((bf16[64,2432]{1,0:T(8,128)(2,1)S(1)}, bf16[64,2432]{1,0:T(8,128)(2,1)S(1)}, u32[]{:S(2)}, u32[]{:S(2)}) %collective-permute-start.9) | collective-permute-done | bytes 311328 | tf_op jit(solution)/shard_map/ppermute | solution.py:513
  63.2 0.0 copy-done.2
  63.2 1.4 %shard_map.147 = (f32[27,64,64]{2,1,0:T(8,128)}, f32[512,128]{1,0:T(8,128)}, bf16[64,1024]{1,0:T(8,128)(2,1)}) custom-call(bf16[64,2432]{1,0:T(8,128)(2,1)S(1)} %bitcast.28, bf16[64,2432]{1,0:T(8,128)(2,1)S(1)} %collective-permute-done.9.given_ref, s32[4,16]{1,0:T(4,128)S(1)} %bitcast.36, s32[8,128]{1,0:T(8,128)S(1)} %get-tuple-element.55.lists_ref), custom_call_target="tpu_custom_call" | custom-call | bytes 1462528 | tf_op jit(solution)/shard_map/pallas_call | solution.py:50
  (3 shorter events, 0.0 us)
Async XLA Ops:
  0.6 9.3 %copy-start.3 = (bf16[27,64,64]{2,1,0:T(8,128)(2,1)S(1)}, bf16[27,64,64]{2,1,0:T(8,128)(2,1)}, u32[]{:S(2)}) copy-start(bf16[27,64,64]{2,1,0:T(8,128)(2,1)} %weight_ref.3) | copy-start | bytes 663556
  2.5 14.7 %all-to-all-start = ((bf16[16,8,512]{2,1,0:T(8,128)(2,1)}), bf16[16,8,512]{2,1,0:T(8,128)(2,1)S(1)}, u32[]{:S(2)}, u32[]{:S(2)}) async-start(bf16[16,8,512]{2,1,0:T(8,128)(2,1)} %bitcast.40), calls=%async_computation | async-start | bytes 262144 | tf_op jit(solution)/shard_map/all_to_all | solution.py:524
  9.9 0.7 %copy-start.6 = (s32[8,128]{1,0:T(8,128)S(1)}, s32[8,128]{1,0:T(8,128)}, u32[]{:S(2)}) copy-start(s32[8,128]{1,0:T(8,128)} %get-tuple-element.35.lists_ref) | copy-start | bytes 12292
  10.6 0.9 %copy-start.4 = (bf16[1,1,32,4096]{3,2,1,0:T(8,128)(2,1)S(1)}, bf16[1,1,32,4096]{3,2,1,0:T(8,128)(2,1)}, u32[]{:S(2)}) copy-start(bf16[1,1,32,4096]{3,2,1,0:T(8,128)(2,1)} %param.19) | copy-start | bytes 786436
  11.5 0.7 %copy-start.5 = (s32[1,1,32,27]{2,1,3,0:T(1,128)S(1)}, s32[1,1,32,27]{2,1,3,0:T(1,128)}, u32[]{:S(2)}) copy-start(s32[1,1,32,27]{2,1,3,0:T(1,128)} %param.14) | copy-start | bytes 10372
  12.2 5.0 %copy-start = (bf16[8,128,64]{1,2,0:T(8,128)(2,1)S(1)}, bf16[8,128,64]{1,2,0:T(8,128)(2,1)}, u32[]{:S(2)}) copy-start(bf16[8,128,64]{1,2,0:T(8,128)(2,1)} %param.13) | copy-start | bytes 393220
  12.2 5.0 %copy-start.1 = (bf16[1,1,32,4096]{3,2,1,0:T(8,128)(2,1)S(1)}, bf16[1,1,32,4096]{3,2,1,0:T(8,128)(2,1)}, u32[]{:S(2)}) copy-start(bf16[1,1,32,4096]{3,2,1,0:T(8,128)(2,1)} %param.10) | copy-start | bytes 786436
  17.9 4.0 %collective-permute-start = (bf16[8,5120]{1,0:T(8,128)(2,1)S(1)}, bf16[8,5120]{1,0:T(8,128)(2,1)S(1)}, u32[]{:S(2)}, u32[]{:S(2)}) collective-permute-start(bf16[8,5120]{1,0:T(8,128)(2,1)S(1)} %get-tuple-element.37), channel_id=1, source_target_pairs={{1,2},{2,1},{5,6},{6,5},{9,10},{10,9},{13,14},{14,13},{17,18},{18,... | collective-permute-start | bytes 245768 | tf_op jit(solution)/shard_map/ppermute | solution.py:513
  18.5 5.1 %collective-permute-start.1 = (bf16[8,5120]{1,0:T(8,128)(2,1)S(1)}, bf16[8,5120]{1,0:T(8,128)(2,1)S(1)}, u32[]{:S(2)}, u32[]{:S(2)}) collective-permute-start(bf16[8,5120]{1,0:T(8,128)(2,1)S(1)} %get-tuple-element.38), channel_id=1, source_target_pairs={{0,1},{2,3},{1,0},{3,2},{4,5},{6,7},{5,4},{7,6},{8,9},{10,11},{9,8... | collective-permute-start | bytes 245768 | tf_op jit(solution)/shard_map/ppermute | solution.py:513
  21.2 6.5 %collective-permute-start.4 = (bf16[8,4096]{1,0:T(8,128)(2,1)S(1)}, bf16[8,4096]{1,0:T(8,128)(2,1)S(1)}, u32[]{:S(2)}, u32[]{:S(2)}) collective-permute-start(bf16[8,4096]{1,0:T(8,128)(2,1)S(1)} %get-tuple-element.46), channel_id=1, source_target_pairs={{0,4},{8,12},{4,0},{12,8},{1,5},{9,13},{5,1},{13,9},{2,6},{10,14},... | collective-permute-start | bytes 196616 | tf_op jit(solution)/shard_map/ppermute | solution.py:513
  21.2 6.5 %collective-permute-start.5 = (bf16[8,4096]{1,0:T(8,128)(2,1)S(1)}, bf16[8,4096]{1,0:T(8,128)(2,1)S(1)}, u32[]{:S(2)}, u32[]{:S(2)}) collective-permute-start(bf16[8,4096]{1,0:T(8,128)(2,1)S(1)} %get-tuple-element.47), channel_id=1, source_target_pairs={{4,8},{8,4},{5,9},{9,5},{6,10},{10,6},{7,11},{11,7},{20,24},{24,20... | collective-permute-start | bytes 196616 | tf_op jit(solution)/shard_map/ppermute | solution.py:513
  24.0 4.3 %collective-permute-start.2 = (bf16[8,4096]{1,0:T(8,128)(2,1)S(1)}, bf16[8,4096]{1,0:T(8,128)(2,1)S(1)}, u32[]{:S(2)}, u32[]{:S(2)}) collective-permute-start(bf16[8,4096]{1,0:T(8,128)(2,1)S(1)} %get-tuple-element.40), channel_id=1, source_target_pairs={{4,8},{8,4},{5,9},{9,5},{6,10},{10,6},{7,11},{11,7},{20,24},{24,20... | collective-permute-start | bytes 196616 | tf_op jit(solution)/shard_map/ppermute | solution.py:513
  24.6 3.9 %collective-permute-start.3 = (bf16[8,4096]{1,0:T(8,128)(2,1)S(1)}, bf16[8,4096]{1,0:T(8,128)(2,1)S(1)}, u32[]{:S(2)}, u32[]{:S(2)}) collective-permute-start(bf16[8,4096]{1,0:T(8,128)(2,1)S(1)} %get-tuple-element.41), channel_id=1, source_target_pairs={{0,4},{8,12},{4,0},{12,8},{1,5},{9,13},{5,1},{13,9},{2,6},{10,14},... | collective-permute-start | bytes 196616 | tf_op jit(solution)/shard_map/ppermute | solution.py:513
  30.6 2.6 %collective-permute-start.8 = (bf16[64,1408]{1,0:T(8,128)(2,1)S(1)}, bf16[64,1408]{1,0:T(8,128)(2,1)S(1)}, u32[]{:S(2)}, u32[]{:S(2)}) collective-permute-start(bf16[64,1408]{1,0:T(8,128)(2,1)S(1)} %get-tuple-element.58), channel_id=1, source_target_pairs={{0,4},{4,0},{1,5},{5,1},{2,6},{6,2},{3,7},{7,3},{8,12},{12,8},{9,1... | collective-permute-start | bytes 540680 | tf_op jit(solution)/shard_map/ppermute | solution.py:513
  33.8 14.1 %all-to-all-start.1 = ((bf16[8,8,1408]{2,1,0:T(8,128)(2,1)}), bf16[8,8,1408]{2,1,0:T(8,128)(2,1)S(1)}, u32[]{:S(2)}, u32[]{:S(2)}) async-start(bf16[8,8,1408]{2,1,0:T(8,128)(2,1)} %bitcast.17), calls=%async_computation.1 | async-start | bytes 360448 | tf_op jit(solution)/shard_map/all_to_all | solution.py:524
  38.3 7.7 %collective-permute-start.6 = (bf16[8,4096]{1,0:T(8,128)(2,1)S(1)}, bf16[8,4096]{1,0:T(8,128)(2,1)S(1)}, u32[]{:S(2)}, u32[]{:S(2)}) collective-permute-start(bf16[8,4096]{1,0:T(8,128)(2,1)S(1)} %get-tuple-element.52), channel_id=1, source_target_pairs={{1,2},{2,1},{5,6},{6,5},{9,10},{10,9},{13,14},{14,13},{17,18},{18,... | collective-permute-start | bytes 196616 | tf_op jit(solution)/shard_map/ppermute | solution.py:513
  39.0 7.9 %collective-permute-start.7 = (bf16[8,4096]{1,0:T(8,128)(2,1)S(1)}, bf16[8,4096]{1,0:T(8,128)(2,1)S(1)}, u32[]{:S(2)}, u32[]{:S(2)}) collective-permute-start(bf16[8,4096]{1,0:T(8,128)(2,1)S(1)} %get-tuple-element.53), channel_id=1, source_target_pairs={{0,1},{2,3},{1,0},{3,2},{4,5},{6,7},{5,4},{7,6},{8,9},{10,11},{9,8... | collective-permute-start | bytes 196616 | tf_op jit(solution)/shard_map/ppermute | solution.py:513
  48.1 15.1 %copy-start.2 = (s32[1,1,16,4]{2,3,1,0:T(4,128)S(1)}, s32[1,1,16,4]{2,3,1,0:T(4,128)}, u32[]{:S(2)}) copy-start(s32[1,1,16,4]{2,3,1,0:T(4,128)} %param.18) | copy-start | bytes 772
  61.6 1.6 %collective-permute-start.9 = (bf16[64,2432]{1,0:T(8,128)(2,1)S(1)}, bf16[64,2432]{1,0:T(8,128)(2,1)S(1)}, u32[]{:S(2)}, u32[]{:S(2)}) collective-permute-start(bf16[64,2432]{1,0:T(8,128)(2,1)S(1)} %bitcast.27), channel_id=1, source_target_pairs={{0,4},{4,0},{1,5},{5,1},{2,6},{6,2},{3,7},{7,3},{8,12},{12,8},{9,1... | collective-permute-start | bytes 933896 | tf_op jit(solution)/shard_map/ppermute | solution.py:513

commit v15 on v13

--- a/solution.py
+++ b/solution.py
@@ -45,13 +45,17 @@
     return jnp.sum(jnp.where(diagonal, spread, 0.0), axis=1, keepdims=True).astype(I32)
 
 
-def call(body, outs, *args, scratch=(), flops=0, in_hbm=False):
+def call(body, outs, *args, scratch=(), flops=0, in_hbm=False, results_in_hbm=0, aliases={}):
     moved = sum(a.size * a.dtype.itemsize for a in list(args) + list(outs))
+    in_place = [pltpu.HBM if in_hbm else pl.ANY if i in aliases else None for i in range(len(args))]
+    out_place = [pl.ANY if i < results_in_hbm else None for i in range(len(outs))]
     return pl.pallas_call(
         body,
         out_shape=tuple(outs),
-        in_specs=[pl.BlockSpec(memory_space=pltpu.HBM) if in_hbm else pl.BlockSpec() for _ in args],
+        in_specs=[pl.BlockSpec(memory_space=place) for place in in_place],
+        out_specs=tuple(pl.BlockSpec(memory_space=place) for place in out_place),
         scratch_shapes=tuple(scratch),
+        input_output_aliases=aliases,
         cost_estimate=pl.CostEstimate(flops=flops, bytes_accessed=moved, transcendentals=0),
         compiler_params=pltpu.CompilerParams(vmem_limit_bytes=None if in_hbm else 28 * 2**20),
     )(*args)
@@ -314,9 +318,9 @@
         up_sums_ref[:, q * coarse : (q + 1) * coarse] = up_sum[q * count : (q + 1) * count]
 
 
-def weight_grad_body(
+def given_sums_body(
     odd_cross_ref, even_cross_ref, merged_ref, even_side_ref, odd_side_ref, turned_ref, mains_ref, ends_ref, lists_ref,
-    up_sums_ref, kept_ref, given_ref, pad_ref, table_ref, sums_ref,
+    up_sums_ref, given_ref, pad_ref, table_ref,
 ):
     bricks, width = merged_ref.shape
     face = even_side_ref.shape[0]
@@ -325,9 +329,6 @@
     above, below = from_pairs(lists_ref, GX, even_cross_ref, odd_cross_ref)
     table_ref[:bricks] = merged_ref[...]
     table_ref[bricks:] = stack_rows(low, high, below, above)
-    count = sums_ref.shape[0]
-    up_lanes = up_sums_ref.shape[1]
-    sums_ref[:, :up_lanes] = up_sums_ref[...]
     lower_half = iota((rows, 2 * C), 1) < C
     zero = jnp.zeros((rows, 2 * C), BF)
     for x in range(4):
@@ -349,11 +350,21 @@
                 for i, (X, Y, _, _) in enumerate(moved):
                     pad_ref[X, Y, :, :RUN] = got[i * bricks : (i + 1) * bricks]
 
+    half_sums(1 - lists_ref[5, GX], pad_ref, turned_ref, up_sums_ref, given_ref)
+
+
+def half_sums(group, pad_ref, turned_ref, up_sums_ref, out_ref):
     turned = turned_ref[...]
+    half_count = out_ref.shape[0]
+    up_lanes = up_sums_ref.shape[1]
+    up_half = jnp.where(group == 0, up_sums_ref[:half_count], up_sums_ref[half_count:])
+    out_ref[:, :up_lanes] = up_half.astype(out_ref.dtype)
+    bricks = pad_ref.shape[2]
     lanes_low = iota((C, 2 * C), 1) < C
     sums = []
-    for e in range(9):
-        wide = dot(turned, inputs_at(pad_ref, e))
+    for i in range(5):
+        ex, ey = (jnp.where(group == 0, i // 3, (i + 4) // 3), jnp.where(group == 0, i % 3, (i + 4) % 3))
+        wide = dot(turned, pad_ref[pl.ds(ex, 4), pl.ds(ey, 4)].reshape(16 * bricks, WIDE))
 
         def block(z, s):
             return wide[z * C : (z + 1) * C, s * 2 * C : (s + 1) * 2 * C]
@@ -364,13 +375,14 @@
         for value in (low, mid, high):
             sums.append(value + pltpu.roll(value, C, 1))
     sums.append(jnp.zeros((C, 2 * C), F32))
-    for pair in range(7):
-        both = [jnp.where(lanes_low, sums[14 * h + 2 * pair], sums[14 * h + 2 * pair + 1]) for h in range(2)]
-        at = up_lanes + pair * 2 * C
-        sums_ref[:, at : at + 2 * C] = jnp.concatenate(both, axis=0)
-    kept, given = by_pair(lists_ref, GX, sums_ref[: count // 2], sums_ref[count // 2 :])
-    kept_ref[...] = kept
-    given_ref[...] = given.astype(BF)
+    pairs = [jnp.where(lanes_low, sums[2 * k], sums[2 * k + 1]) for k in range(8)]
+    for p in range(7):
+        at = up_lanes + p * 2 * C
+        out_ref[:, at : at + 2 * C] = jnp.where(group == 0, pairs[p], pairs[p + 1]).astype(out_ref.dtype)
+
+
+def kept_sums_body(pad_ref, turned_ref, up_sums_ref, lists_ref, kept_ref):
+    half_sums(lists_ref[5, GX], pad_ref, turned_ref, up_sums_ref, kept_ref)
 
 
 def pair_sum_body(kept_ref, given_ref, out_ref):
@@ -457,54 +469,84 @@
     out_ref[:, item_lanes:] = dot(ones_where(same), sums_ref[...]).astype(BF)
 
 
-def coarse_grad(arrivals, sends_ref, lists_ref, out_ref, across):
+def coarse_part(arrived, sends_ref, lists_ref, other, out_dims, across):
     capacity, devices = sends_ref.shape
-    count, item_width = out_ref.shape
+    count, item_width = out_dims
     half = item_width // 2
-    lanes = arrivals[0].shape[0]
-    pieces = arrivals[0].shape[1] // half
+    lanes = arrived.shape[0]
+    pieces = arrived.shape[1] // half
     _, group = chip_slots(lanes, pieces, across)
     sends = sends_ref[...].astype(F32).astype(BF)
     lane = iota((1, lanes), 1)
+    source = device_of(lane // group, lists_ref, other, across)
+    rows = dot(sends, ones_where(source == iota((devices, lanes), 0)))
     totals = [None, None]
-    for other in range(2):
-        source = device_of(lane // group, lists_ref, other, across)
-        rows = dot(sends, ones_where(source == iota((devices, lanes), 0)))
-        for j in range(pieces):
-            piece = lane % group * pieces + j
-            picked = jnp.where(piece // 2 == iota((capacity, lanes), 0), rows, 0.0)
-            index = jnp.sum(picked, axis=0, keepdims=True).astype(I32)
-            named = iota((count, lanes), 0) == index
-            for h in range(2):
-                part = dot(ones_where(named & (piece % 2 == h)), arrivals[other][:, j * half : (j + 1) * half])
-                totals[h] = part if totals[h] is None else totals[h] + part
-    for h in range(2):
-        out_ref[:, h * half : (h + 1) * half] = totals[h].astype(BF)
-
-
-def last_body(back_ref, given_ref, sends_ref, lists_ref, conv_ref, up_ref, out_ref, item_lanes, across, scale):
-    half_count = back_ref.shape[0]
-    items = (back_ref[:, :item_lanes], given_ref[:, item_lanes : 2 * item_lanes])
-    coarse_grad(items, sends_ref, lists_ref, out_ref, across)
-    coarse = up_ref.shape[1]
-    count = 2 * half_count
-    parts = up_ref.shape[0] // count
-    own = back_ref[:, 2 * item_lanes :].astype(F32) * scale
-    others = given_ref[:, 2 * item_lanes :].astype(F32) * scale
-    first, second = by_pair(lists_ref, GX, own, others)
+    for j in range(pieces):
+        piece = lane % group * pieces + j
+        picked = jnp.where(piece // 2 == iota((capacity, lanes), 0), rows, 0.0)
+        index = jnp.sum(picked, axis=0, keepdims=True).astype(I32)
+        named = iota((count, lanes), 0) == index
+        for h in range(2):
+            part = dot(ones_where(named & (piece % 2 == h)), arrived[:, j * half : (j + 1) * half])
+            totals[h] = part if totals[h] is None else totals[h] + part
+    return jnp.concatenate(totals, axis=1)
+
+
+def write_half(group, half, conv_hbm, up_hbm, conv_ref, up_ref, done, scale):
+    half_count, coarse = up_ref.shape[1:]
+    parts = up_ref.shape[0]
     at = 0
+    copies = []
     for q in range(parts):
-        up_ref[q * count : q * count + half_count] = first[:, at : at + coarse]
-        up_ref[q * count + half_count : (q + 1) * count] = second[:, at : at + coarse]
+        up_ref[q] = half[:, at : at + coarse].astype(F32) * scale
         at += coarse
+        place = pl.ds(pl.multiple_of((2 * q + group) * half_count, half_count), half_count)
+        copies.append(pltpu.make_async_copy(up_ref.at[q], up_hbm.at[place], done.at[q]))
+        copies[-1].start()
     for pair in range(7):
-        turned = jnp.concatenate([first[:, at : at + 2 * C], second[:, at : at + 2 * C]], axis=0).T
+        turned = half[:, at : at + 2 * C].astype(F32).T * scale
         at += 2 * C
-        for h in range(2):
-            for s in range(2):
-                o = 14 * h + 2 * pair + s
-                if o < 27:
-                    conv_ref[o] = turned[s * C : (s + 1) * C, h * C : (h + 1) * C]
+        for s in range(2):
+            conv_ref[2 * pair + s] = turned[s * C : (s + 1) * C]
+    copies.append(pltpu.make_async_copy(conv_ref.at[pl.ds(0, 13)], conv_hbm.at[pl.ds(14 * group, 13)], done.at[parts]))
+    copies[-1].start()
+    last = pltpu.make_async_copy(conv_ref.at[13], conv_hbm.at[13], done.at[parts + 1])
+
+    @pl.when(group == 0)
+    def _():
+        last.start()
+
+    return copies, last
+
+
+def end_half(group, copies, last):
+    for copy in copies:
+        copy.wait()
+
+    @pl.when(group == 0)
+    def _():
+        last.wait()
+
+
+def own_half_body(
+    back_ref, sends_ref, lists_ref, conv_hbm, up_hbm, part_ref, conv_ref, up_ref, done, item_lanes, across, scale
+):
+    group = lists_ref[5, GX]
+    started = write_half(group, back_ref[:, 2 * item_lanes :], conv_hbm, up_hbm, conv_ref, up_ref, done, scale)
+    part_ref[...] = coarse_part(back_ref[:, :item_lanes], sends_ref, lists_ref, 0, part_ref.shape, across)
+    end_half(group, *started)
+
+
+def other_half_body(
+    given_ref, part_ref, sends_ref, lists_ref, conv_in, up_in,
+    conv_hbm, up_hbm, out_ref, conv_ref, up_ref, done, item_lanes, across, scale,
+):
+    group = 1 - lists_ref[5, GX]
+    started = write_half(group, given_ref[:, 2 * item_lanes :], conv_hbm, up_hbm, conv_ref, up_ref, done, scale)
+    came = given_ref[:, item_lanes : 2 * item_lanes]
+    other = coarse_part(came, sends_ref, lists_ref, 1, out_ref.shape, across)
+    out_ref[...] = (part_ref[...] + other).astype(BF)
+    end_half(group, *started)
 
 
 def swap(value, axis, first):
@@ -583,20 +625,21 @@
     sides = swap_pairs(to_even, to_odd, "gy")
     to_even, to_odd = call(cross_body, [face_rows, face_rows], merged, *sides, lists)
     crosses = swap_pairs(to_even, to_odd, GX_AXES)
-    half_sums = (count // 2, sums_width)
+    half_sums_dims = (count // 2, sums_width)
     fine_part, to_even, to_odd, up_sums = call(
         side_grad_body,
         [shape((bricks, width), F32), face_rows, face_rows, shape((count, sums_width - 14 * C), F32)],
         ext_grad, lists, *cross_grads, *sides, parents,
     )
     side_grads = swap_pairs(to_even, to_odd, "gy")
-    kept, given, pad = call(
-        weight_grad_body, [shape(half_sums, F32), shape(half_sums), shape((6, 6, bricks, WIDE))],
+    given, pad = call(
+        given_sums_body, [shape(half_sums_dims), shape((6, 6, bricks, WIDE))],
         *crosses[::-1], merged, *sides, turned, mains, ends, lists, up_sums,
-        scratch=[pltpu.VMEM((table_rows, width), BF), pltpu.VMEM((count, sums_width), F32)], flops=conv_flops,
-    )
+        scratch=[pltpu.VMEM((table_rows, width), BF)], flops=conv_flops,
+    )
+    (kept,) = call(kept_sums_body, [shape(half_sums_dims, F32)], pad, turned, up_sums, lists, flops=conv_flops)
     given = swap(given, "core", 0)
-    (sums,) = call(pair_sum_body, [shape(half_sums)], kept, given)
+    (sums,) = call(pair_sum_body, [shape(half_sums_dims)], kept, given)
     sums = trade_rows(sums, ("x", "gy"))
     output, lists = call(
         conv_body, [rows, lists_shape], pad, conv_weight, lists, scratch=[band], flops=conv_flops
@@ -611,10 +654,22 @@
     back = trade_rows(back, ("x", "gy"))
     given = swap(back, "core", 0)
     scale = 1.0 / math.sqrt(64 * bricks * devices)
+    results = [shape((27, C, C), F32), shape((8 * C, coarse), F32)]
+    halves = dict(
+        scratch=[
+            pltpu.VMEM((14, C, C), F32), pltpu.VMEM((8 * C // count, count // 2, coarse), F32),
+            pltpu.SemaphoreType.DMA((8 * C // count + 2,)),
+        ],
+        results_in_hbm=2,
+    )
+    sizes = dict(item_lanes=item_lanes, across=across, scale=scale)
+    grad_conv, grad_up, part = call(
+        functools.partial(own_half_body, **sizes), results + [shape((item_count, item_width), F32)],
+        back, sends, lists, **halves,
+    )
     grad_conv, grad_up, coarse_grad = call(
-        functools.partial(last_body, item_lanes=item_lanes, across=across, scale=scale),
-        [shape((27, C, C), F32), shape((8 * C, coarse), F32), shape((item_count, item_width))],
-        back, given, sends, lists,
+        functools.partial(other_half_body, **sizes), results + [shape((item_count, item_width))],
+        given, part, sends, lists, grad_conv, grad_up, aliases={4: 0, 5: 1}, **halves,
     )
     return (
         output.reshape(1, 1, bricks, width),

time: 65.1 us -> 65 us (level)
  waiting for transfers between devices: 11.3 us -> 9.25 us
  Pallas kernels: 12.9 us -> 14.8 us
    ppermute x10, waiting for transfers between devices: 5.94 us -> 3.85 us  [swap(): lax.ppermute(value, axis, [(i, i + 1) for i in lower] + [(i + 1, i) for i...]
    pallas_call x11 -> x13, Pallas kernels: 12.9 us -> 14.8 us  [call(): pl.pallas_call(body, out_shape=tuple(outs), in_specs=[pl.BlockSpec(memory...]
  transfers between devices with their start and end apart: 12 -> 12, of which waited for: 7 -> 7; matrix products, arithmetic and copies ran while one was open for 0% -> 0% of each run, Pallas kernels for 10% -> 13%
where the time goes in v15:
time: 65 us; the launch traced here: 64.4 us
  starting transfers between devices  23 us (35%)
  Pallas kernels  14.8 us (23%)
  blocking collectives  14.1 us (22%)
  waiting for transfers between devices  9.25 us (14%)
  local copies, waits for them, and re-layouts  2.34 us (4%)
  between operations  0.82 us (1%)
    pallas_call x13, Pallas kernels, call(): pl.pallas_call(body, out_shape=tuple(outs), in_specs=[pl.BlockSpec(memory...  14.8 us
    all_to_all x1, blocking collectives, trade_rows(): lax.all_to_all(grid_view, axes, split_axis=0, concat_axis=0, tiled=True)  14.1 us
    all_to_all x2, starting transfers between devices, trade_rows(): lax.all_to_all(grid_view, axes, split_axis=0, concat_axis=0, tiled=True)  13.9 us
    ppermute x10, starting transfers between devices, swap(): lax.ppermute(value, axis, [(i, i + 1) for i in lower] + [(i + 1, i) for i...  9.1 us
    all_to_all x2, waiting for transfers between devices, trade_rows(): lax.all_to_all(grid_view, axes, split_axis=0, concat_axis=0, tiled=True)  5.4 us
    ppermute x10, waiting for transfers between devices, swap(): lax.ppermute(value, axis, [(i, i + 1) for i in lower] + [(i + 1, i) for i...  3.85 us
    unnamed x14, local copies, waits for them, and re-layouts  2.34 us
  transfers between devices with their start and end apart: 12, of which 7 were waited for; matrix products, arithmetic and copies ran while one was open for 0% of the time, Pallas kernels for 13%

profile of v15, /device:TPU:0, one launch (start us, length us, event | category | flops | bytes accessed | tf_op | source)
XLA Modules:
  0.0 64.4 jit_solution(6010715824391884377)
XLA Ops:
  0.6 0.0 copy-start.3
  0.6 1.9 %shard_map.137 = (bf16[128,512]{1,0:T(8,128)(2,1)}, s32[8,128]{1,0:T(8,128)}) custom-call(s32[4,16]{1,0:T(4,128)} %bitcast.35, bf16[64,1024]{1,0:T(8,128)(2,1)} %bitcast.41, s32[2,8]{1,0:T(2,128)} %bitcast.43, s32[2,8]{1,0:T(2,128)} %bitcast.44, s32[1,32]{1,0:T(1,128)} %bitcast.45), custom_call_target="tpu_custom_call" | custom-call | bytes 266752 | tf_op jit(solution)/shard_map/pallas_call | solution.py:52
  2.5 7.4 %all-to-all-start = ((bf16[16,8,512]{2,1,0:T(8,128)(2,1)}), bf16[16,8,512]{2,1,0:T(8,128)(2,1)S(1)}, u32[]{:S(2)}, u32[]{:S(2)}) async-start(bf16[16,8,512]{2,1,0:T(8,128)(2,1)} %bitcast.42), calls=%async_computation | async-start | bytes 262144 | tf_op jit(solution)/shard_map/all_to_all | solution.py:566
  9.9 0.0 copy-start.6
  9.9 0.0 copy-done.3
  9.9 0.7 %copy-done.6 = s32[8,128]{1,0:T(8,128)S(1)} copy-done((s32[8,128]{1,0:T(8,128)S(1)}, s32[8,128]{1,0:T(8,128)}, u32[]{:S(2)}) %copy-start.6) | copy-done | bytes 4120
  10.6 0.9 %copy-done.4 = bf16[1,1,32,4096]{3,2,1,0:T(8,128)(2,1)S(1)} copy-done((bf16[1,1,32,4096]{3,2,1,0:T(8,128)(2,1)S(1)}, bf16[1,1,32,4096]{3,2,1,0:T(8,128)(2,1)}, u32[]{:S(2)}) %copy-start.4) | copy-done | bytes 262168
  11.5 0.7 %copy-done.5 = s32[1,1,32,27]{2,1,3,0:T(1,128)S(1)} copy-done((s32[1,1,32,27]{2,1,3,0:T(1,128)S(1)}, s32[1,1,32,27]{2,1,3,0:T(1,128)}, u32[]{:S(2)}) %copy-start.5) | copy-done | bytes 3480
  12.2 2.0 %shard_map.138 = (f32[48,4096]{1,0:T(8,128)S(1)}, bf16[8,4096]{1,0:T(8,128)(2,1)S(1)}, bf16[8,4096]{1,0:T(8,128)(2,1)S(1)}, bf16[256,512]{1,0:T(8,128)(2,1)S(1)}...) custom-call(bf16[32,4096]{1,0:T(8,128)(2,1)S(1)} %bitcast.38, ...), custom_call_target="tpu_custom_call" | custom-call | flops 1811939328 | bytes 1785728 | tf_op jit(solution)/shard_map/pallas_call | solution.py:52
  14.2 3.0 %all-to-all-done = bf16[16,8,512]{2,1,0:T(8,128)(2,1)S(1)} async-done(((bf16[16,8,512]{2,1,0:T(8,128)(2,1)}), bf16[16,8,512]{2,1,0:T(8,128)(2,1)S(1)}, u32[]{:S(2)}, u32[]{:S(2)}) %all-to-all-start) | async-done | bytes 131104 | tf_op jit(solution)/shard_map/all_to_all | solution.py:566
  17.2 0.0 copy-done
  17.2 0.0 copy-done.1
  17.2 0.6 shard_map.139
  17.9 0.7 %collective-permute-start = (bf16[8,5120]{1,0:T(8,128)(2,1)S(1)}, bf16[8,5120]{1,0:T(8,128)(2,1)S(1)}, u32[]{:S(2)}, u32[]{:S(2)}) collective-permute-start(bf16[8,5120]{1,0:T(8,128)(2,1)S(1)} %get-tuple-element.40), channel_id=1, source_target_pairs={{0,1},{2,3},{1,0},{3,2},{4,5},{6,7},{5,4},{7,6},{8,9},{10,11},{9,8... | collective-permute-start | bytes 245768 | tf_op jit(solution)/shard_map/ppermute | solution.py:555
  18.6 0.7 %collective-permute-start.1 = (bf16[8,5120]{1,0:T(8,128)(2,1)S(1)}, bf16[8,5120]{1,0:T(8,128)(2,1)S(1)}, u32[]{:S(2)}, u32[]{:S(2)}) collective-permute-start(bf16[8,5120]{1,0:T(8,128)(2,1)S(1)} %get-tuple-element.41), channel_id=1, source_target_pairs={{1,2},{2,1},{5,6},{6,5},{9,10},{10,9},{13,14},{14,13},{17,18},{18,... | collective-permute-start | bytes 245768 | tf_op jit(solution)/shard_map/ppermute | solution.py:555
  19.2 0.1 collective-permute-start.4
  19.3 0.7 %collective-permute-start.5 = (bf16[8,4096]{1,0:T(8,128)(2,1)S(1)}, bf16[8,4096]{1,0:T(8,128)(2,1)S(1)}, u32[]{:S(2)}, u32[]{:S(2)}) collective-permute-start(bf16[8,4096]{1,0:T(8,128)(2,1)S(1)} %get-tuple-element.49), channel_id=1, source_target_pairs={{4,8},{8,4},{5,9},{9,5},{6,10},{10,6},{7,11},{11,7},{20,24},{24,20... | collective-permute-start | bytes 196616 | tf_op jit(solution)/shard_map/ppermute | solution.py:555
  20.0 2.4 %collective-permute-done.even_ref.even_side_ref = bf16[8,5120]{1,0:T(8,128)(2,1)S(1)} collective-permute-done((bf16[8,5120]{1,0:T(8,128)(2,1)S(1)}, bf16[8,5120]{1,0:T(8,128)(2,1)S(1)}, u32[]{:S(2)}, u32[]{:S(2)}) %collective-permute-start) | collective-permute-done | bytes 81952 | tf_op jit(solution)/shard_map/ppermute | solution.py:555
  22.4 0.0 collective-permute-done.1.odd_ref.odd_side_ref
  22.4 0.3 shard_map.140
  22.7 0.7 %collective-permute-start.2 = (bf16[8,4096]{1,0:T(8,128)(2,1)S(1)}, bf16[8,4096]{1,0:T(8,128)(2,1)S(1)}, u32[]{:S(2)}, u32[]{:S(2)}) collective-permute-start(bf16[8,4096]{1,0:T(8,128)(2,1)S(1)} %get-tuple-element.42), channel_id=1, source_target_pairs={{4,8},{8,4},{5,9},{9,5},{6,10},{10,6},{7,11},{11,7},{20,24},{24,20... | collective-permute-start | bytes 196616 | tf_op jit(solution)/shard_map/ppermute | solution.py:555
  23.4 2.4 %collective-permute-start.3 = (bf16[8,4096]{1,0:T(8,128)(2,1)S(1)}, bf16[8,4096]{1,0:T(8,128)(2,1)S(1)}, u32[]{:S(2)}, u32[]{:S(2)}) collective-permute-start(bf16[8,4096]{1,0:T(8,128)(2,1)S(1)} %get-tuple-element.43), channel_id=1, source_target_pairs={{0,4},{8,12},{4,0},{12,8},{1,5},{9,13},{5,1},{13,9},{2,6},{10,14},... | collective-permute-start | bytes 196616 | tf_op jit(solution)/shard_map/ppermute | solution.py:555
  25.8 0.0 collective-permute-done.4.even_grad_ref
  25.8 0.0 collective-permute-done.5.odd_grad_ref
  25.8 0.6 shard_map.141
  26.4 0.0 collective-permute-done.2.odd_cross_ref
  26.4 0.3 collective-permute-done.3.even_cross_ref
  26.7 1.4 %shard_map.142 = (bf16[64,1408]{1,0:T(8,128)(2,1)S(1)}, bf16[6,6,32,384]{3,2,1,0:T(8,128)(2,1)S(1)}) custom-call(bf16[8,4096]{1,0:T(8,128)(2,1)S(1)} %collective-permute-done.2.odd_cross_ref, bf16[8,4096]{1,0:T(8,128)(2,1)S(1)} %collective-permute-done.3.even_cross_ref, bf16[32,4096]{1,0:T(8,128)(2,1)S(1)} %get-tuple-element.39.merged_ref, ...), custom_call_target="tpu_custom_call" | custom-call | flops 905969664 | bytes 2260992 | tf_op jit(solution)/shard_map/pallas_call | solution.py:52
  28.1 1.2 %collective-permute-start.8 = (bf16[64,1408]{1,0:T(8,128)(2,1)S(1)}, bf16[64,1408]{1,0:T(8,128)(2,1)S(1)}, u32[]{:S(2)}, u32[]{:S(2)}) collective-permute-start(bf16[64,1408]{1,0:T(8,128)(2,1)S(1)} %get-tuple-element.59), channel_id=1, source_target_pairs={{0,4},{4,0},{1,5},{5,1},{2,6},{6,2},{3,7},{7,3},{8,12},{12,8},{9,1... | collective-permute-start | bytes 540680 | tf_op jit(solution)/shard_map/ppermute | solution.py:555
  29.4 0.9 %shard_map.145.kept_ref = f32[64,1408]{1,0:T(8,128)S(1)} custom-call(bf16[6,6,32,384]{3,2,1,0:T(8,128)(2,1)S(1)} %get-tuple-element.52.pad_ref, bf16[256,512]{1,0:T(8,128)(2,1)S(1)} %get-tuple-element.44.turned_ref, f32[128,512]{1,0:T(8,128)S(1)} %get-tuple-element.51.up_sums_ref, s32[8,128]{1,0:T(8,128)S(1)} %get-tuple-element.38.lists_ref), custom_call_target="tpu_custom_call" | custom-call | flops 905969664 | bytes 1773568 | tf_op jit(solution)/shard_map/pallas_call | solution.py:52
  30.3 0.1 collective-permute-done.8.given_ref
  30.4 0.7 %shard_map.146 = bf16[64,1408]{1,0:T(8,128)(2,1)} custom-call(f32[64,1408]{1,0:T(8,128)S(1)} %shard_map.145.kept_ref, bf16[64,1408]{1,0:T(8,128)(2,1)S(1)} %collective-permute-done.8.given_ref), custom_call_target="tpu_custom_call" | custom-call | bytes 720896 | tf_op jit(solution)/shard_map/pallas_call | solution.py:52
  31.1 6.6 %all-to-all-start.1 = ((bf16[8,8,1408]{2,1,0:T(8,128)(2,1)}), bf16[8,8,1408]{2,1,0:T(8,128)(2,1)S(1)}, u32[]{:S(2)}, u32[]{:S(2)}) async-start(bf16[8,8,1408]{2,1,0:T(8,128)(2,1)} %bitcast.17), calls=%async_computation.1 | async-start | bytes 360448 | tf_op jit(solution)/shard_map/all_to_all | solution.py:566
  37.7 2.0 %collective-permute-start.6 = (bf16[8,4096]{1,0:T(8,128)(2,1)S(1)}, bf16[8,4096]{1,0:T(8,128)(2,1)S(1)}, u32[]{:S(2)}, u32[]{:S(2)}) collective-permute-start(bf16[8,4096]{1,0:T(8,128)(2,1)S(1)} %get-tuple-element.56), channel_id=1, source_target_pairs={{0,1},{2,3},{1,0},{3,2},{4,5},{6,7},{5,4},{7,6},{8,9},{10,11},{9,8... | collective-permute-start | bytes 196616 | tf_op jit(solution)/shard_map/ppermute | solution.py:555
  39.7 0.7 %collective-permute-start.7 = (bf16[8,4096]{1,0:T(8,128)(2,1)S(1)}, bf16[8,4096]{1,0:T(8,128)(2,1)S(1)}, u32[]{:S(2)}, u32[]{:S(2)}) collective-permute-start(bf16[8,4096]{1,0:T(8,128)(2,1)S(1)} %get-tuple-element.57), channel_id=1, source_target_pairs={{1,2},{2,1},{5,6},{6,5},{9,10},{10,9},{13,14},{14,13},{17,18},{18,... | collective-permute-start | bytes 196616 | tf_op jit(solution)/shard_map/ppermute | solution.py:555
  40.4 2.2 %shard_map.143 = (bf16[32,4096]{1,0:T(8,128)(2,1)}, s32[8,128]{1,0:T(8,128)S(1)}) custom-call(bf16[6,6,32,384]{3,2,1,0:T(8,128)(2,1)S(1)} %get-tuple-element.52.pad_ref, bf16[27,64,64]{2,1,0:T(8,128)(2,1)S(1)} %copy-done.3, s32[8,128]{1,0:T(8,128)S(1)} %get-tuple-element.38.lists_ref), custom_call_target="tpu_custom_call" | custom-call | flops 905969664 | bytes 1376256 | tf_op jit(solution)/shard_map/pallas_call | solution.py:52
  42.6 0.6 collective-permute-done.6.even_ref
  43.2 0.0 collective-permute-done.7.odd_ref
  43.2 1.1 %shard_map.144 = (bf16[32,4096]{1,0:T(8,128)(2,1)}, bf16[64,1024]{1,0:T(8,128)(2,1)S(1)}) custom-call(f32[32,4096]{1,0:T(8,128)S(1)} %get-tuple-element.54.part_ref, s32[8,128]{1,0:T(8,128)S(1)} %get-tuple-element.55.lists_ref, bf16[8,4096]{1,0:T(8,128)(2,1)S(1)} %collective-permute-done.6.even_ref, bf16[8,4096]{1,0:T(8,128)(2,1)S(1)} %collective-permute-done.7.odd_ref, ...), custom_call_target="tpu_custom_call" | custom-call | bytes 1183744 | tf_op jit(solution)/shard_map/pallas_call | solution.py:52
  44.3 2.4 %all-to-all-done.1 = bf16[8,8,1408]{2,1,0:T(8,128)(2,1)S(1)} async-done(((bf16[8,8,1408]{2,1,0:T(8,128)(2,1)}), bf16[8,8,1408]{2,1,0:T(8,128)(2,1)S(1)}, u32[]{:S(2)}, u32[]{:S(2)}) %all-to-all-start.1) | async-done | bytes 180256 | tf_op jit(solution)/shard_map/all_to_all | solution.py:566
  46.7 0.2 shard_map.147
  46.9 0.0 copy-start.2
  46.9 14.1 %all_to_all.15 = bf16[8,8,2432]{2,1,0:T(8,128)(2,1)S(1)} all-to-all(bf16[8,8,2432]{2,1,0:T(8,128)(2,1)S(1)} %bitcast.29), channel_id=1, replica_groups=mesh['groups'=2,'x'=2,'core'=2,'gy'=4] {'x','gy'}, dimensions={0} | all-to-all | bytes 622592 | tf_op jit(solution)/shard_map/all_to_all | solution.py:566
  61.1 0.0 collective-permute-start.9
  61.1 0.0 copy-done.2
  61.1 1.1 %shard_map.148 = (f32[27,64,64]{2,1,0:T(8,128)}, f32[512,128]{1,0:T(8,128)}, f32[64,1024]{1,0:T(8,128)S(1)}) custom-call(bf16[64,2432]{1,0:T(8,128)(2,1)S(1)} %bitcast.28, s32[4,16]{1,0:T(4,128)S(1)} %bitcast.36, s32[8,128]{1,0:T(8,128)S(1)} %get-tuple-element.55.lists_ref), custom_call_target="tpu_custom_call" | custom-call | bytes 1282304 | tf_op jit(solution)/shard_map/pallas_call | solution.py:52
  62.2 0.5 collective-permute-done.9.given_ref
  62.7 1.8 %shard_map.149 = (f32[27,64,64]{2,1,0:T(8,128)}, f32[512,128]{1,0:T(8,128)}, bf16[64,1024]{1,0:T(8,128)(2,1)}) custom-call(bf16[64,2432]{1,0:T(8,128)(2,1)S(1)} %collective-permute-done.9.given_ref, f32[64,1024]{1,0:T(8,128)S(1)} %get-tuple-element.61.part_ref, s32[4,16]{1,0:T(4,128)S(1)} %bitcast.37, ...), custom_call_target="tpu_custom_call", output_to_operand_aliasing={{0}: (4, {}), {1}: (5, {})} | custom-call | bytes 2117888 | tf_op jit(solution)/shard_map/pallas_call | solution.py:52
  (5 shorter events, 0.0 us)
Async XLA Ops:
  0.6 9.3 %copy-start.3 = (bf16[27,64,64]{2,1,0:T(8,128)(2,1)S(1)}, bf16[27,64,64]{2,1,0:T(8,128)(2,1)}, u32[]{:S(2)}) copy-start(bf16[27,64,64]{2,1,0:T(8,128)(2,1)} %weight_ref.3) | copy-start | bytes 663556
  2.5 14.7 %all-to-all-start = ((bf16[16,8,512]{2,1,0:T(8,128)(2,1)}), bf16[16,8,512]{2,1,0:T(8,128)(2,1)S(1)}, u32[]{:S(2)}, u32[]{:S(2)}) async-start(bf16[16,8,512]{2,1,0:T(8,128)(2,1)} %bitcast.42), calls=%async_computation | async-start | bytes 262144 | tf_op jit(solution)/shard_map/all_to_all | solution.py:566
  9.9 0.7 %copy-start.6 = (s32[8,128]{1,0:T(8,128)S(1)}, s32[8,128]{1,0:T(8,128)}, u32[]{:S(2)}) copy-start(s32[8,128]{1,0:T(8,128)} %get-tuple-element.37.lists_ref) | copy-start | bytes 12292
  10.6 0.9 %copy-start.4 = (bf16[1,1,32,4096]{3,2,1,0:T(8,128)(2,1)S(1)}, bf16[1,1,32,4096]{3,2,1,0:T(8,128)(2,1)}, u32[]{:S(2)}) copy-start(bf16[1,1,32,4096]{3,2,1,0:T(8,128)(2,1)} %param.19) | copy-start | bytes 786436
  11.5 0.7 %copy-start.5 = (s32[1,1,32,27]{2,1,3,0:T(1,128)S(1)}, s32[1,1,32,27]{2,1,3,0:T(1,128)}, u32[]{:S(2)}) copy-start(s32[1,1,32,27]{2,1,3,0:T(1,128)} %param.14) | copy-start | bytes 10372
  12.2 5.0 %copy-start = (bf16[8,128,64]{1,2,0:T(8,128)(2,1)S(1)}, bf16[8,128,64]{1,2,0:T(8,128)(2,1)}, u32[]{:S(2)}) copy-start(bf16[8,128,64]{1,2,0:T(8,128)(2,1)} %param.13) | copy-start | bytes 393220
  12.2 5.0 %copy-start.1 = (bf16[1,1,32,4096]{3,2,1,0:T(8,128)(2,1)S(1)}, bf16[1,1,32,4096]{3,2,1,0:T(8,128)(2,1)}, u32[]{:S(2)}) copy-start(bf16[1,1,32,4096]{3,2,1,0:T(8,128)(2,1)} %param.10) | copy-start | bytes 786436
  17.9 4.5 %collective-permute-start = (bf16[8,5120]{1,0:T(8,128)(2,1)S(1)}, bf16[8,5120]{1,0:T(8,128)(2,1)S(1)}, u32[]{:S(2)}, u32[]{:S(2)}) collective-permute-start(bf16[8,5120]{1,0:T(8,128)(2,1)S(1)} %get-tuple-element.40), channel_id=1, source_target_pairs={{0,1},{2,3},{1,0},{3,2},{4,5},{6,7},{5,4},{7,6},{8,9},{10,11},{9,8... | collective-permute-start | bytes 245768 | tf_op jit(solution)/shard_map/ppermute | solution.py:555
  18.6 3.8 %collective-permute-start.1 = (bf16[8,5120]{1,0:T(8,128)(2,1)S(1)}, bf16[8,5120]{1,0:T(8,128)(2,1)S(1)}, u32[]{:S(2)}, u32[]{:S(2)}) collective-permute-start(bf16[8,5120]{1,0:T(8,128)(2,1)S(1)} %get-tuple-element.41), channel_id=1, source_target_pairs={{1,2},{2,1},{5,6},{6,5},{9,10},{10,9},{13,14},{14,13},{17,18},{18,... | collective-permute-start | bytes 245768 | tf_op jit(solution)/shard_map/ppermute | solution.py:555
  19.2 6.6 %collective-permute-start.4 = (bf16[8,4096]{1,0:T(8,128)(2,1)S(1)}, bf16[8,4096]{1,0:T(8,128)(2,1)S(1)}, u32[]{:S(2)}, u32[]{:S(2)}) collective-permute-start(bf16[8,4096]{1,0:T(8,128)(2,1)S(1)} %get-tuple-element.48), channel_id=1, source_target_pairs={{0,4},{8,12},{4,0},{12,8},{1,5},{9,13},{5,1},{13,9},{2,6},{10,14},... | collective-permute-start | bytes 196616 | tf_op jit(solution)/shard_map/ppermute | solution.py:555
  19.3 6.5 %collective-permute-start.5 = (bf16[8,4096]{1,0:T(8,128)(2,1)S(1)}, bf16[8,4096]{1,0:T(8,128)(2,1)S(1)}, u32[]{:S(2)}, u32[]{:S(2)}) collective-permute-start(bf16[8,4096]{1,0:T(8,128)(2,1)S(1)} %get-tuple-element.49), channel_id=1, source_target_pairs={{4,8},{8,4},{5,9},{9,5},{6,10},{10,6},{7,11},{11,7},{20,24},{24,20... | collective-permute-start | bytes 196616 | tf_op jit(solution)/shard_map/ppermute | solution.py:555
  22.7 3.7 %collective-permute-start.2 = (bf16[8,4096]{1,0:T(8,128)(2,1)S(1)}, bf16[8,4096]{1,0:T(8,128)(2,1)S(1)}, u32[]{:S(2)}, u32[]{:S(2)}) collective-permute-start(bf16[8,4096]{1,0:T(8,128)(2,1)S(1)} %get-tuple-element.42), channel_id=1, source_target_pairs={{4,8},{8,4},{5,9},{9,5},{6,10},{10,6},{7,11},{11,7},{20,24},{24,20... | collective-permute-start | bytes 196616 | tf_op jit(solution)/shard_map/ppermute | solution.py:555
  23.4 3.3 %collective-permute-start.3 = (bf16[8,4096]{1,0:T(8,128)(2,1)S(1)}, bf16[8,4096]{1,0:T(8,128)(2,1)S(1)}, u32[]{:S(2)}, u32[]{:S(2)}) collective-permute-start(bf16[8,4096]{1,0:T(8,128)(2,1)S(1)} %get-tuple-element.43), channel_id=1, source_target_pairs={{0,4},{8,12},{4,0},{12,8},{1,5},{9,13},{5,1},{13,9},{2,6},{10,14},... | collective-permute-start | bytes 196616 | tf_op jit(solution)/shard_map/ppermute | solution.py:555
  28.1 2.3 %collective-permute-start.8 = (bf16[64,1408]{1,0:T(8,128)(2,1)S(1)}, bf16[64,1408]{1,0:T(8,128)(2,1)S(1)}, u32[]{:S(2)}, u32[]{:S(2)}) collective-permute-start(bf16[64,1408]{1,0:T(8,128)(2,1)S(1)} %get-tuple-element.59), channel_id=1, source_target_pairs={{0,4},{4,0},{1,5},{5,1},{2,6},{6,2},{3,7},{7,3},{8,12},{12,8},{9,1... | collective-permute-start | bytes 540680 | tf_op jit(solution)/shard_map/ppermute | solution.py:555
  31.1 15.6 %all-to-all-start.1 = ((bf16[8,8,1408]{2,1,0:T(8,128)(2,1)}), bf16[8,8,1408]{2,1,0:T(8,128)(2,1)S(1)}, u32[]{:S(2)}, u32[]{:S(2)}) async-start(bf16[8,8,1408]{2,1,0:T(8,128)(2,1)} %bitcast.17), calls=%async_computation.1 | async-start | bytes 360448 | tf_op jit(solution)/shard_map/all_to_all | solution.py:566
  37.7 5.5 %collective-permute-start.6 = (bf16[8,4096]{1,0:T(8,128)(2,1)S(1)}, bf16[8,4096]{1,0:T(8,128)(2,1)S(1)}, u32[]{:S(2)}, u32[]{:S(2)}) collective-permute-start(bf16[8,4096]{1,0:T(8,128)(2,1)S(1)} %get-tuple-element.56), channel_id=1, source_target_pairs={{0,1},{2,3},{1,0},{3,2},{4,5},{6,7},{5,4},{7,6},{8,9},{10,11},{9,8... | collective-permute-start | bytes 196616 | tf_op jit(solution)/shard_map/ppermute | solution.py:555
  39.7 3.5 %collective-permute-start.7 = (bf16[8,4096]{1,0:T(8,128)(2,1)S(1)}, bf16[8,4096]{1,0:T(8,128)(2,1)S(1)}, u32[]{:S(2)}, u32[]{:S(2)}) collective-permute-start(bf16[8,4096]{1,0:T(8,128)(2,1)S(1)} %get-tuple-element.57), channel_id=1, source_target_pairs={{1,2},{2,1},{5,6},{6,5},{9,10},{10,9},{13,14},{14,13},{17,18},{18,... | collective-permute-start | bytes 196616 | tf_op jit(solution)/shard_map/ppermute | solution.py:555
  46.9 14.2 %copy-start.2 = (s32[1,1,16,4]{2,3,1,0:T(4,128)S(1)}, s32[1,1,16,4]{2,3,1,0:T(4,128)}, u32[]{:S(2)}) copy-start(s32[1,1,16,4]{2,3,1,0:T(4,128)} %param.18) | copy-start | bytes 772
  61.1 1.6 %collective-permute-start.9 = (bf16[64,2432]{1,0:T(8,128)(2,1)S(1)}, bf16[64,2432]{1,0:T(8,128)(2,1)S(1)}, u32[]{:S(2)}, u32[]{:S(2)}) collective-permute-start(bf16[64,2432]{1,0:T(8,128)(2,1)S(1)} %bitcast.27), channel_id=1, source_target_pairs={{0,4},{4,0},{1,5},{5,1},{2,6},{6,2},{3,7},{7,3},{8,12},{12,8},{9,1... | collective-permute-start | bytes 933896 | tf_op jit(solution)/shard_map/ppermute | solution.py:555

commit v16 on v13

--- a/solution.py
+++ b/solution.py
@@ -314,9 +314,9 @@
         up_sums_ref[:, q * coarse : (q + 1) * coarse] = up_sum[q * count : (q + 1) * count]
 
 
-def weight_grad_body(
+def given_sums_body(
     odd_cross_ref, even_cross_ref, merged_ref, even_side_ref, odd_side_ref, turned_ref, mains_ref, ends_ref, lists_ref,
-    up_sums_ref, kept_ref, given_ref, pad_ref, table_ref, sums_ref,
+    up_sums_ref, given_ref, pad_ref, table_ref,
 ):
     bricks, width = merged_ref.shape
     face = even_side_ref.shape[0]
@@ -325,9 +325,6 @@
     above, below = from_pairs(lists_ref, GX, even_cross_ref, odd_cross_ref)
     table_ref[:bricks] = merged_ref[...]
     table_ref[bricks:] = stack_rows(low, high, below, above)
-    count = sums_ref.shape[0]
-    up_lanes = up_sums_ref.shape[1]
-    sums_ref[:, :up_lanes] = up_sums_ref[...]
     lower_half = iota((rows, 2 * C), 1) < C
     zero = jnp.zeros((rows, 2 * C), BF)
     for x in range(4):
@@ -349,11 +346,21 @@
                 for i, (X, Y, _, _) in enumerate(moved):
                     pad_ref[X, Y, :, :RUN] = got[i * bricks : (i + 1) * bricks]
 
+    half_sums(1 - lists_ref[5, GX], pad_ref, turned_ref, up_sums_ref, given_ref)
+
+
+def half_sums(group, pad_ref, turned_ref, up_sums_ref, out_ref):
     turned = turned_ref[...]
+    half_count = out_ref.shape[0]
+    up_lanes = up_sums_ref.shape[1]
+    up_half = jnp.where(group == 0, up_sums_ref[:half_count], up_sums_ref[half_count:])
+    out_ref[:, :up_lanes] = up_half.astype(out_ref.dtype)
+    bricks = pad_ref.shape[2]
     lanes_low = iota((C, 2 * C), 1) < C
     sums = []
-    for e in range(9):
-        wide = dot(turned, inputs_at(pad_ref, e))
+    for i in range(5):
+        ex, ey = (jnp.where(group == 0, i // 3, (i + 4) // 3), jnp.where(group == 0, i % 3, (i + 4) % 3))
+        wide = dot(turned, pad_ref[pl.ds(ex, 4), pl.ds(ey, 4)].reshape(16 * bricks, WIDE))
 
         def block(z, s):
             return wide[z * C : (z + 1) * C, s * 2 * C : (s + 1) * 2 * C]
@@ -364,13 +371,14 @@
         for value in (low, mid, high):
             sums.append(value + pltpu.roll(value, C, 1))
     sums.append(jnp.zeros((C, 2 * C), F32))
-    for pair in range(7):
-        both = [jnp.where(lanes_low, sums[14 * h + 2 * pair], sums[14 * h + 2 * pair + 1]) for h in range(2)]
-        at = up_lanes + pair * 2 * C
-        sums_ref[:, at : at + 2 * C] = jnp.concatenate(both, axis=0)
-    kept, given = by_pair(lists_ref, GX, sums_ref[: count // 2], sums_ref[count // 2 :])
-    kept_ref[...] = kept
-    given_ref[...] = given.astype(BF)
+    pairs = [jnp.where(lanes_low, sums[2 * k], sums[2 * k + 1]) for k in range(8)]
+    for p in range(7):
+        at = up_lanes + p * 2 * C
+        out_ref[:, at : at + 2 * C] = jnp.where(group == 0, pairs[p], pairs[p + 1]).astype(out_ref.dtype)
+
+
+def kept_sums_body(pad_ref, turned_ref, up_sums_ref, lists_ref, kept_ref):
+    half_sums(lists_ref[5, GX], pad_ref, turned_ref, up_sums_ref, kept_ref)
 
 
 def pair_sum_body(kept_ref, given_ref, out_ref):
@@ -583,20 +591,21 @@
     sides = swap_pairs(to_even, to_odd, "gy")
     to_even, to_odd = call(cross_body, [face_rows, face_rows], merged, *sides, lists)
     crosses = swap_pairs(to_even, to_odd, GX_AXES)
-    half_sums = (count // 2, sums_width)
+    half_sums_dims = (count // 2, sums_width)
     fine_part, to_even, to_odd, up_sums = call(
         side_grad_body,
         [shape((bricks, width), F32), face_rows, face_rows, shape((count, sums_width - 14 * C), F32)],
         ext_grad, lists, *cross_grads, *sides, parents,
     )
     side_grads = swap_pairs(to_even, to_odd, "gy")
-    kept, given, pad = call(
-        weight_grad_body, [shape(half_sums, F32), shape(half_sums), shape((6, 6, bricks, WIDE))],
+    given, pad = call(
+        given_sums_body, [shape(half_sums_dims), shape((6, 6, bricks, WIDE))],
         *crosses[::-1], merged, *sides, turned, mains, ends, lists, up_sums,
-        scratch=[pltpu.VMEM((table_rows, width), BF), pltpu.VMEM((count, sums_width), F32)], flops=conv_flops,
-    )
+        scratch=[pltpu.VMEM((table_rows, width), BF)], flops=conv_flops,
+    )
+    (kept,) = call(kept_sums_body, [shape(half_sums_dims, F32)], pad, turned, up_sums, lists, flops=conv_flops)
     given = swap(given, "core", 0)
-    (sums,) = call(pair_sum_body, [shape(half_sums)], kept, given)
+    (sums,) = call(pair_sum_body, [shape(half_sums_dims)], kept, given)
     sums = trade_rows(sums, ("x", "gy"))
     output, lists = call(
         conv_body, [rows, lists_shape], pad, conv_weight, lists, scratch=[band], flops=conv_flops

time: 65.1 us -> 64.6 us (level)
  waiting for transfers between devices: 11.3 us -> 10.4 us
    ppermute x10, waiting for transfers between devices: 5.94 us -> 4.99 us  [swap(): lax.ppermute(value, axis, [(i, i + 1) for i in lower] + [(i + 1, i) for i...]
    pallas_call x11 -> x12, Pallas kernels: 12.9 us -> 13.3 us  [call(): pl.pallas_call(body, out_shape=tuple(outs), in_specs=[pl.BlockSpec(memory...]
  transfers between devices with their start and end apart: 12 -> 12, of which waited for: 7 -> 7; matrix products, arithmetic and copies ran while one was open for 0% -> 0% of each run, Pallas kernels for 10% -> 11%
where the time goes in v16:
time: 64.6 us; the launch traced here: 64 us
  starting transfers between devices  23 us (36%)
  blocking collectives  14.1 us (22%)
  Pallas kernels  13.3 us (21%)
  waiting for transfers between devices  10.4 us (16%)
  local copies, waits for them, and re-layouts  2.34 us (4%)
  between operations  0.81 us (1%)
    all_to_all x1, blocking collectives, trade_rows(): lax.all_to_all(grid_view, axes, split_axis=0, concat_axis=0, tiled=True)  14.1 us
    all_to_all x2, starting transfers between devices, trade_rows(): lax.all_to_all(grid_view, axes, split_axis=0, concat_axis=0, tiled=True)  13.9 us
    pallas_call x12, Pallas kernels, call(): pl.pallas_call(body, out_shape=tuple(outs), in_specs=[pl.BlockSpec(memory...  13.3 us
    ppermute x10, starting transfers between devices, swap(): lax.ppermute(value, axis, [(i, i + 1) for i in lower] + [(i + 1, i) for i...  9.1 us
    all_to_all x2, waiting for transfers between devices, trade_rows(): lax.all_to_all(grid_view, axes, split_axis=0, concat_axis=0, tiled=True)  5.4 us
    ppermute x10, waiting for transfers between devices, swap(): lax.ppermute(value, axis, [(i, i + 1) for i in lower] + [(i + 1, i) for i...  4.99 us
    unnamed x14, local copies, waits for them, and re-layouts  2.34 us
  transfers between devices with their start and end apart: 12, of which 7 were waited for; matrix products, arithmetic and copies ran while one was open for 0% of the time, Pallas kernels for 11%

profile of v16, /device:TPU:0, one launch (start us, length us, event | category | flops | bytes accessed | tf_op | source)
XLA Modules:
  0.0 64.0 jit_solution(12974698016190376741)
XLA Ops:
  0.6 0.0 copy-start.3
  0.6 1.9 %shard_map.137 = (bf16[128,512]{1,0:T(8,128)(2,1)}, s32[8,128]{1,0:T(8,128)}) custom-call(s32[4,16]{1,0:T(4,128)} %bitcast.35, bf16[64,1024]{1,0:T(8,128)(2,1)} %bitcast.39, s32[2,8]{1,0:T(2,128)} %bitcast.41, s32[2,8]{1,0:T(2,128)} %bitcast.42, s32[1,32]{1,0:T(1,128)} %bitcast.43), custom_call_target="tpu_custom_call" | custom-call | bytes 266752 | tf_op jit(solution)/shard_map/pallas_call | solution.py:50
  2.5 7.4 %all-to-all-start = ((bf16[16,8,512]{2,1,0:T(8,128)(2,1)}), bf16[16,8,512]{2,1,0:T(8,128)(2,1)S(1)}, u32[]{:S(2)}, u32[]{:S(2)}) async-start(bf16[16,8,512]{2,1,0:T(8,128)(2,1)} %bitcast.40), calls=%async_computation | async-start | bytes 262144 | tf_op jit(solution)/shard_map/all_to_all | solution.py:532
  9.9 0.0 copy-start.6
  9.9 0.0 copy-done.3
  9.9 0.7 %copy-done.6 = s32[8,128]{1,0:T(8,128)S(1)} copy-done((s32[8,128]{1,0:T(8,128)S(1)}, s32[8,128]{1,0:T(8,128)}, u32[]{:S(2)}) %copy-start.6) | copy-done | bytes 4120
  10.6 0.0 copy-start.4
  10.6 0.9 %copy-done.4 = bf16[1,1,32,4096]{3,2,1,0:T(8,128)(2,1)S(1)} copy-done((bf16[1,1,32,4096]{3,2,1,0:T(8,128)(2,1)S(1)}, bf16[1,1,32,4096]{3,2,1,0:T(8,128)(2,1)}, u32[]{:S(2)}) %copy-start.4) | copy-done | bytes 262168
  11.5 0.7 %copy-done.5 = s32[1,1,32,27]{2,1,3,0:T(1,128)S(1)} copy-done((s32[1,1,32,27]{2,1,3,0:T(1,128)S(1)}, s32[1,1,32,27]{2,1,3,0:T(1,128)}, u32[]{:S(2)}) %copy-start.5) | copy-done | bytes 3480
  12.2 2.0 %shard_map.138 = (f32[48,4096]{1,0:T(8,128)S(1)}, bf16[8,4096]{1,0:T(8,128)(2,1)S(1)}, bf16[8,4096]{1,0:T(8,128)(2,1)S(1)}, bf16[256,512]{1,0:T(8,128)(2,1)S(1)}...) custom-call(bf16[32,4096]{1,0:T(8,128)(2,1)S(1)} %bitcast.37, ...), custom_call_target="tpu_custom_call" | custom-call | flops 1811939328 | bytes 1785728 | tf_op jit(solution)/shard_map/pallas_call | solution.py:50
  14.2 3.0 %all-to-all-done = bf16[16,8,512]{2,1,0:T(8,128)(2,1)S(1)} async-done(((bf16[16,8,512]{2,1,0:T(8,128)(2,1)}), bf16[16,8,512]{2,1,0:T(8,128)(2,1)S(1)}, u32[]{:S(2)}, u32[]{:S(2)}) %all-to-all-start) | async-done | bytes 131104 | tf_op jit(solution)/shard_map/all_to_all | solution.py:532
  17.2 0.0 copy-done
  17.2 0.0 copy-done.1
  17.2 0.6 shard_map.139
  17.9 0.7 %collective-permute-start = (bf16[8,5120]{1,0:T(8,128)(2,1)S(1)}, bf16[8,5120]{1,0:T(8,128)(2,1)S(1)}, u32[]{:S(2)}, u32[]{:S(2)}) collective-permute-start(bf16[8,5120]{1,0:T(8,128)(2,1)S(1)} %get-tuple-element.37), channel_id=1, source_target_pairs={{0,1},{2,3},{1,0},{3,2},{4,5},{6,7},{5,4},{7,6},{8,9},{10,11},{9,8... | collective-permute-start | bytes 245768 | tf_op jit(solution)/shard_map/ppermute | solution.py:521
  18.6 0.7 %collective-permute-start.1 = (bf16[8,5120]{1,0:T(8,128)(2,1)S(1)}, bf16[8,5120]{1,0:T(8,128)(2,1)S(1)}, u32[]{:S(2)}, u32[]{:S(2)}) collective-permute-start(bf16[8,5120]{1,0:T(8,128)(2,1)S(1)} %get-tuple-element.38), channel_id=1, source_target_pairs={{1,2},{2,1},{5,6},{6,5},{9,10},{10,9},{13,14},{14,13},{17,18},{18,... | collective-permute-start | bytes 245768 | tf_op jit(solution)/shard_map/ppermute | solution.py:521
  19.2 0.1 collective-permute-start.4
  19.3 0.7 %collective-permute-start.5 = (bf16[8,4096]{1,0:T(8,128)(2,1)S(1)}, bf16[8,4096]{1,0:T(8,128)(2,1)S(1)}, u32[]{:S(2)}, u32[]{:S(2)}) collective-permute-start(bf16[8,4096]{1,0:T(8,128)(2,1)S(1)} %get-tuple-element.46), channel_id=1, source_target_pairs={{4,8},{8,4},{5,9},{9,5},{6,10},{10,6},{7,11},{11,7},{20,24},{24,20... | collective-permute-start | bytes 196616 | tf_op jit(solution)/shard_map/ppermute | solution.py:521
  20.0 2.4 %collective-permute-done.even_ref.even_side_ref = bf16[8,5120]{1,0:T(8,128)(2,1)S(1)} collective-permute-done((bf16[8,5120]{1,0:T(8,128)(2,1)S(1)}, bf16[8,5120]{1,0:T(8,128)(2,1)S(1)}, u32[]{:S(2)}, u32[]{:S(2)}) %collective-permute-start) | collective-permute-done | bytes 81952 | tf_op jit(solution)/shard_map/ppermute | solution.py:521
  22.4 0.0 collective-permute-done.1.odd_ref.odd_side_ref
  22.4 0.3 shard_map.140
  22.7 0.7 %collective-permute-start.2 = (bf16[8,4096]{1,0:T(8,128)(2,1)S(1)}, bf16[8,4096]{1,0:T(8,128)(2,1)S(1)}, u32[]{:S(2)}, u32[]{:S(2)}) collective-permute-start(bf16[8,4096]{1,0:T(8,128)(2,1)S(1)} %get-tuple-element.39), channel_id=1, source_target_pairs={{4,8},{8,4},{5,9},{9,5},{6,10},{10,6},{7,11},{11,7},{20,24},{24,20... | collective-permute-start | bytes 196616 | tf_op jit(solution)/shard_map/ppermute | solution.py:521
  23.4 2.4 %collective-permute-start.3 = (bf16[8,4096]{1,0:T(8,128)(2,1)S(1)}, bf16[8,4096]{1,0:T(8,128)(2,1)S(1)}, u32[]{:S(2)}, u32[]{:S(2)}) collective-permute-start(bf16[8,4096]{1,0:T(8,128)(2,1)S(1)} %get-tuple-element.40), channel_id=1, source_target_pairs={{0,4},{8,12},{4,0},{12,8},{1,5},{9,13},{5,1},{13,9},{2,6},{10,14},... | collective-permute-start | bytes 196616 | tf_op jit(solution)/shard_map/ppermute | solution.py:521
  25.8 0.0 collective-permute-done.4.even_grad_ref
  25.8 0.0 collective-permute-done.5.odd_grad_ref
  25.8 0.6 shard_map.141
  26.4 0.0 collective-permute-done.2.odd_cross_ref
  26.4 0.3 collective-permute-done.3.even_cross_ref
  26.7 1.4 %shard_map.142 = (bf16[64,1408]{1,0:T(8,128)(2,1)S(1)}, bf16[6,6,32,384]{3,2,1,0:T(8,128)(2,1)S(1)}) custom-call(bf16[8,4096]{1,0:T(8,128)(2,1)S(1)} %collective-permute-done.2.odd_cross_ref, bf16[8,4096]{1,0:T(8,128)(2,1)S(1)} %collective-permute-done.3.even_cross_ref, bf16[32,4096]{1,0:T(8,128)(2,1)S(1)} %get-tuple-element.36.merged_ref, ...), custom_call_target="tpu_custom_call" | custom-call | flops 905969664 | bytes 2260992 | tf_op jit(solution)/shard_map/pallas_call | solution.py:50
  28.1 1.2 %collective-permute-start.8 = (bf16[64,1408]{1,0:T(8,128)(2,1)S(1)}, bf16[64,1408]{1,0:T(8,128)(2,1)S(1)}, u32[]{:S(2)}, u32[]{:S(2)}) collective-permute-start(bf16[64,1408]{1,0:T(8,128)(2,1)S(1)} %get-tuple-element.56), channel_id=1, source_target_pairs={{0,4},{4,0},{1,5},{5,1},{2,6},{6,2},{3,7},{7,3},{8,12},{12,8},{9,1... | collective-permute-start | bytes 540680 | tf_op jit(solution)/shard_map/ppermute | solution.py:521
  29.4 0.9 %shard_map.145.kept_ref = f32[64,1408]{1,0:T(8,128)S(1)} custom-call(bf16[6,6,32,384]{3,2,1,0:T(8,128)(2,1)S(1)} %get-tuple-element.49.pad_ref, bf16[256,512]{1,0:T(8,128)(2,1)S(1)} %get-tuple-element.41.turned_ref, f32[128,512]{1,0:T(8,128)S(1)} %get-tuple-element.48.up_sums_ref, s32[8,128]{1,0:T(8,128)S(1)} %get-tuple-element.35.lists_ref), custom_call_target="tpu_custom_call" | custom-call | flops 905969664 | bytes 1773568 | tf_op jit(solution)/shard_map/pallas_call | solution.py:50
  30.3 0.1 collective-permute-done.8.given_ref
  30.4 0.7 %shard_map.146 = bf16[64,1408]{1,0:T(8,128)(2,1)} custom-call(f32[64,1408]{1,0:T(8,128)S(1)} %shard_map.145.kept_ref, bf16[64,1408]{1,0:T(8,128)(2,1)S(1)} %collective-permute-done.8.given_ref), custom_call_target="tpu_custom_call" | custom-call | bytes 720896 | tf_op jit(solution)/shard_map/pallas_call | solution.py:50
  31.1 6.6 %all-to-all-start.1 = ((bf16[8,8,1408]{2,1,0:T(8,128)(2,1)}), bf16[8,8,1408]{2,1,0:T(8,128)(2,1)S(1)}, u32[]{:S(2)}, u32[]{:S(2)}) async-start(bf16[8,8,1408]{2,1,0:T(8,128)(2,1)} %bitcast.17), calls=%async_computation.1 | async-start | bytes 360448 | tf_op jit(solution)/shard_map/all_to_all | solution.py:532
  37.7 2.0 %collective-permute-start.6 = (bf16[8,4096]{1,0:T(8,128)(2,1)S(1)}, bf16[8,4096]{1,0:T(8,128)(2,1)S(1)}, u32[]{:S(2)}, u32[]{:S(2)}) collective-permute-start(bf16[8,4096]{1,0:T(8,128)(2,1)S(1)} %get-tuple-element.53), channel_id=1, source_target_pairs={{0,1},{2,3},{1,0},{3,2},{4,5},{6,7},{5,4},{7,6},{8,9},{10,11},{9,8... | collective-permute-start | bytes 196616 | tf_op jit(solution)/shard_map/ppermute | solution.py:521
  39.7 0.7 %collective-permute-start.7 = (bf16[8,4096]{1,0:T(8,128)(2,1)S(1)}, bf16[8,4096]{1,0:T(8,128)(2,1)S(1)}, u32[]{:S(2)}, u32[]{:S(2)}) collective-permute-start(bf16[8,4096]{1,0:T(8,128)(2,1)S(1)} %get-tuple-element.54), channel_id=1, source_target_pairs={{1,2},{2,1},{5,6},{6,5},{9,10},{10,9},{13,14},{14,13},{17,18},{18,... | collective-permute-start | bytes 196616 | tf_op jit(solution)/shard_map/ppermute | solution.py:521
  40.4 2.2 %shard_map.143 = (bf16[32,4096]{1,0:T(8,128)(2,1)}, s32[8,128]{1,0:T(8,128)S(1)}) custom-call(bf16[6,6,32,384]{3,2,1,0:T(8,128)(2,1)S(1)} %get-tuple-element.49.pad_ref, bf16[27,64,64]{2,1,0:T(8,128)(2,1)S(1)} %copy-done.3, s32[8,128]{1,0:T(8,128)S(1)} %get-tuple-element.35.lists_ref), custom_call_target="tpu_custom_call" | custom-call | flops 905969664 | bytes 1376256 | tf_op jit(solution)/shard_map/pallas_call | solution.py:50
  42.6 0.6 collective-permute-done.6.even_ref
  43.2 0.0 collective-permute-done.7.odd_ref
  43.2 1.1 %shard_map.144 = (bf16[32,4096]{1,0:T(8,128)(2,1)}, bf16[64,1024]{1,0:T(8,128)(2,1)S(1)}) custom-call(f32[32,4096]{1,0:T(8,128)S(1)} %get-tuple-element.51.part_ref, s32[8,128]{1,0:T(8,128)S(1)} %get-tuple-element.52.lists_ref, bf16[8,4096]{1,0:T(8,128)(2,1)S(1)} %collective-permute-done.6.even_ref, bf16[8,4096]{1,0:T(8,128)(2,1)S(1)} %collective-permute-done.7.odd_ref, ...), custom_call_target="tpu_custom_call" | custom-call | bytes 1183744 | tf_op jit(solution)/shard_map/pallas_call | solution.py:50
  44.3 2.4 %all-to-all-done.1 = bf16[8,8,1408]{2,1,0:T(8,128)(2,1)S(1)} async-done(((bf16[8,8,1408]{2,1,0:T(8,128)(2,1)}), bf16[8,8,1408]{2,1,0:T(8,128)(2,1)S(1)}, u32[]{:S(2)}, u32[]{:S(2)}) %all-to-all-start.1) | async-done | bytes 180256 | tf_op jit(solution)/shard_map/all_to_all | solution.py:532
  46.7 0.2 shard_map.147
  46.9 0.0 copy-start.2
  46.9 14.1 %all_to_all.15 = bf16[8,8,2432]{2,1,0:T(8,128)(2,1)S(1)} all-to-all(bf16[8,8,2432]{2,1,0:T(8,128)(2,1)S(1)} %bitcast.29), channel_id=1, replica_groups=mesh['groups'=2,'x'=2,'core'=2,'gy'=4] {'x','gy'}, dimensions={0} | all-to-all | bytes 622592 | tf_op jit(solution)/shard_map/all_to_all | solution.py:532
  61.1 0.0 collective-permute-start.9
  61.1 1.6 %collective-permute-done.9.given_ref = bf16[64,2432]{1,0:T(8,128)(2,1)S(1)} collective-permute-done((bf16[64,2432]{1,0:T(8,128)(2,1)S(1)}, bf16[64,2432]{1,0:T(8,128)(2,1)S(1)}, u32[]{:S(2)}, u32[]{:S(2)}) %collective-permute-start.9) | collective-permute-done | bytes 311328 | tf_op jit(solution)/shard_map/ppermute | solution.py:521
  62.7 0.0 copy-done.2
  62.7 1.4 %shard_map.148 = (f32[27,64,64]{2,1,0:T(8,128)}, f32[512,128]{1,0:T(8,128)}, bf16[64,1024]{1,0:T(8,128)(2,1)}) custom-call(bf16[64,2432]{1,0:T(8,128)(2,1)S(1)} %bitcast.28, bf16[64,2432]{1,0:T(8,128)(2,1)S(1)} %collective-permute-done.9.given_ref, s32[4,16]{1,0:T(4,128)S(1)} %bitcast.36, s32[8,128]{1,0:T(8,128)S(1)} %get-tuple-element.52.lists_ref), custom_call_target="tpu_custom_call" | custom-call | bytes 1462528 | tf_op jit(solution)/shard_map/pallas_call | solution.py:50
  (4 shorter events, 0.0 us)
Async XLA Ops:
  0.6 9.3 %copy-start.3 = (bf16[27,64,64]{2,1,0:T(8,128)(2,1)S(1)}, bf16[27,64,64]{2,1,0:T(8,128)(2,1)}, u32[]{:S(2)}) copy-start(bf16[27,64,64]{2,1,0:T(8,128)(2,1)} %weight_ref.3) | copy-start | bytes 663556
  2.5 14.7 %all-to-all-start = ((bf16[16,8,512]{2,1,0:T(8,128)(2,1)}), bf16[16,8,512]{2,1,0:T(8,128)(2,1)S(1)}, u32[]{:S(2)}, u32[]{:S(2)}) async-start(bf16[16,8,512]{2,1,0:T(8,128)(2,1)} %bitcast.40), calls=%async_computation | async-start | bytes 262144 | tf_op jit(solution)/shard_map/all_to_all | solution.py:532
  9.9 0.7 %copy-start.6 = (s32[8,128]{1,0:T(8,128)S(1)}, s32[8,128]{1,0:T(8,128)}, u32[]{:S(2)}) copy-start(s32[8,128]{1,0:T(8,128)} %get-tuple-element.34.lists_ref) | copy-start | bytes 12292
  10.6 0.9 %copy-start.4 = (bf16[1,1,32,4096]{3,2,1,0:T(8,128)(2,1)S(1)}, bf16[1,1,32,4096]{3,2,1,0:T(8,128)(2,1)}, u32[]{:S(2)}) copy-start(bf16[1,1,32,4096]{3,2,1,0:T(8,128)(2,1)} %param.19) | copy-start | bytes 786436
  11.5 0.7 %copy-start.5 = (s32[1,1,32,27]{2,1,3,0:T(1,128)S(1)}, s32[1,1,32,27]{2,1,3,0:T(1,128)}, u32[]{:S(2)}) copy-start(s32[1,1,32,27]{2,1,3,0:T(1,128)} %param.14) | copy-start | bytes 10372
  12.2 5.0 %copy-start = (bf16[8,128,64]{1,2,0:T(8,128)(2,1)S(1)}, bf16[8,128,64]{1,2,0:T(8,128)(2,1)}, u32[]{:S(2)}) copy-start(bf16[8,128,64]{1,2,0:T(8,128)(2,1)} %param.13) | copy-start | bytes 393220
  12.2 5.0 %copy-start.1 = (bf16[1,1,32,4096]{3,2,1,0:T(8,128)(2,1)S(1)}, bf16[1,1,32,4096]{3,2,1,0:T(8,128)(2,1)}, u32[]{:S(2)}) copy-start(bf16[1,1,32,4096]{3,2,1,0:T(8,128)(2,1)} %param.10) | copy-start | bytes 786436
  17.9 4.5 %collective-permute-start = (bf16[8,5120]{1,0:T(8,128)(2,1)S(1)}, bf16[8,5120]{1,0:T(8,128)(2,1)S(1)}, u32[]{:S(2)}, u32[]{:S(2)}) collective-permute-start(bf16[8,5120]{1,0:T(8,128)(2,1)S(1)} %get-tuple-element.37), channel_id=1, source_target_pairs={{0,1},{2,3},{1,0},{3,2},{4,5},{6,7},{5,4},{7,6},{8,9},{10,11},{9,8... | collective-permute-start | bytes 245768 | tf_op jit(solution)/shard_map/ppermute | solution.py:521
  18.6 3.8 %collective-permute-start.1 = (bf16[8,5120]{1,0:T(8,128)(2,1)S(1)}, bf16[8,5120]{1,0:T(8,128)(2,1)S(1)}, u32[]{:S(2)}, u32[]{:S(2)}) collective-permute-start(bf16[8,5120]{1,0:T(8,128)(2,1)S(1)} %get-tuple-element.38), channel_id=1, source_target_pairs={{1,2},{2,1},{5,6},{6,5},{9,10},{10,9},{13,14},{14,13},{17,18},{18,... | collective-permute-start | bytes 245768 | tf_op jit(solution)/shard_map/ppermute | solution.py:521
  19.2 6.6 %collective-permute-start.4 = (bf16[8,4096]{1,0:T(8,128)(2,1)S(1)}, bf16[8,4096]{1,0:T(8,128)(2,1)S(1)}, u32[]{:S(2)}, u32[]{:S(2)}) collective-permute-start(bf16[8,4096]{1,0:T(8,128)(2,1)S(1)} %get-tuple-element.45), channel_id=1, source_target_pairs={{0,4},{8,12},{4,0},{12,8},{1,5},{9,13},{5,1},{13,9},{2,6},{10,14},... | collective-permute-start | bytes 196616 | tf_op jit(solution)/shard_map/ppermute | solution.py:521
  19.3 6.5 %collective-permute-start.5 = (bf16[8,4096]{1,0:T(8,128)(2,1)S(1)}, bf16[8,4096]{1,0:T(8,128)(2,1)S(1)}, u32[]{:S(2)}, u32[]{:S(2)}) collective-permute-start(bf16[8,4096]{1,0:T(8,128)(2,1)S(1)} %get-tuple-element.46), channel_id=1, source_target_pairs={{4,8},{8,4},{5,9},{9,5},{6,10},{10,6},{7,11},{11,7},{20,24},{24,20... | collective-permute-start | bytes 196616 | tf_op jit(solution)/shard_map/ppermute | solution.py:521
  22.7 3.7 %collective-permute-start.2 = (bf16[8,4096]{1,0:T(8,128)(2,1)S(1)}, bf16[8,4096]{1,0:T(8,128)(2,1)S(1)}, u32[]{:S(2)}, u32[]{:S(2)}) collective-permute-start(bf16[8,4096]{1,0:T(8,128)(2,1)S(1)} %get-tuple-element.39), channel_id=1, source_target_pairs={{4,8},{8,4},{5,9},{9,5},{6,10},{10,6},{7,11},{11,7},{20,24},{24,20... | collective-permute-start | bytes 196616 | tf_op jit(solution)/shard_map/ppermute | solution.py:521
  23.4 3.3 %collective-permute-start.3 = (bf16[8,4096]{1,0:T(8,128)(2,1)S(1)}, bf16[8,4096]{1,0:T(8,128)(2,1)S(1)}, u32[]{:S(2)}, u32[]{:S(2)}) collective-permute-start(bf16[8,4096]{1,0:T(8,128)(2,1)S(1)} %get-tuple-element.40), channel_id=1, source_target_pairs={{0,4},{8,12},{4,0},{12,8},{1,5},{9,13},{5,1},{13,9},{2,6},{10,14},... | collective-permute-start | bytes 196616 | tf_op jit(solution)/shard_map/ppermute | solution.py:521
  28.1 2.3 %collective-permute-start.8 = (bf16[64,1408]{1,0:T(8,128)(2,1)S(1)}, bf16[64,1408]{1,0:T(8,128)(2,1)S(1)}, u32[]{:S(2)}, u32[]{:S(2)}) collective-permute-start(bf16[64,1408]{1,0:T(8,128)(2,1)S(1)} %get-tuple-element.56), channel_id=1, source_target_pairs={{0,4},{4,0},{1,5},{5,1},{2,6},{6,2},{3,7},{7,3},{8,12},{12,8},{9,1... | collective-permute-start | bytes 540680 | tf_op jit(solution)/shard_map/ppermute | solution.py:521
  31.1 15.6 %all-to-all-start.1 = ((bf16[8,8,1408]{2,1,0:T(8,128)(2,1)}), bf16[8,8,1408]{2,1,0:T(8,128)(2,1)S(1)}, u32[]{:S(2)}, u32[]{:S(2)}) async-start(bf16[8,8,1408]{2,1,0:T(8,128)(2,1)} %bitcast.17), calls=%async_computation.1 | async-start | bytes 360448 | tf_op jit(solution)/shard_map/all_to_all | solution.py:532
  37.7 5.5 %collective-permute-start.6 = (bf16[8,4096]{1,0:T(8,128)(2,1)S(1)}, bf16[8,4096]{1,0:T(8,128)(2,1)S(1)}, u32[]{:S(2)}, u32[]{:S(2)}) collective-permute-start(bf16[8,4096]{1,0:T(8,128)(2,1)S(1)} %get-tuple-element.53), channel_id=1, source_target_pairs={{0,1},{2,3},{1,0},{3,2},{4,5},{6,7},{5,4},{7,6},{8,9},{10,11},{9,8... | collective-permute-start | bytes 196616 | tf_op jit(solution)/shard_map/ppermute | solution.py:521
  39.7 3.5 %collective-permute-start.7 = (bf16[8,4096]{1,0:T(8,128)(2,1)S(1)}, bf16[8,4096]{1,0:T(8,128)(2,1)S(1)}, u32[]{:S(2)}, u32[]{:S(2)}) collective-permute-start(bf16[8,4096]{1,0:T(8,128)(2,1)S(1)} %get-tuple-element.54), channel_id=1, source_target_pairs={{1,2},{2,1},{5,6},{6,5},{9,10},{10,9},{13,14},{14,13},{17,18},{18,... | collective-permute-start | bytes 196616 | tf_op jit(solution)/shard_map/ppermute | solution.py:521
  46.9 15.8 %copy-start.2 = (s32[1,1,16,4]{2,3,1,0:T(4,128)S(1)}, s32[1,1,16,4]{2,3,1,0:T(4,128)}, u32[]{:S(2)}) copy-start(s32[1,1,16,4]{2,3,1,0:T(4,128)} %param.18) | copy-start | bytes 772
  61.1 1.6 %collective-permute-start.9 = (bf16[64,2432]{1,0:T(8,128)(2,1)S(1)}, bf16[64,2432]{1,0:T(8,128)(2,1)S(1)}, u32[]{:S(2)}, u32[]{:S(2)}) collective-permute-start(bf16[64,2432]{1,0:T(8,128)(2,1)S(1)} %bitcast.27), channel_id=1, source_target_pairs={{0,4},{4,0},{1,5},{5,1},{2,6},{6,2},{3,7},{7,3},{8,12},{12,8},{9,1... | collective-permute-start | bytes 933896 | tf_op jit(solution)/shard_map/ppermute | solution.py:521

commit v17 on v16

--- a/solution.py
+++ b/solution.py
@@ -291,7 +291,7 @@
 
 
 def side_grad_body(
-    ext_ref, lists_ref, even_grad_ref, odd_grad_ref, even_side_ref, odd_side_ref, parents_ref,
+    odd_grad_ref, even_grad_ref, ext_ref, lists_ref, even_side_ref, odd_side_ref, parents_ref,
     part_ref, to_even_ref, to_odd_ref, up_sums_ref,
 ):
     bricks, width = part_ref.shape
@@ -595,7 +595,7 @@
     fine_part, to_even, to_odd, up_sums = call(
         side_grad_body,
         [shape((bricks, width), F32), face_rows, face_rows, shape((count, sums_width - 14 * C), F32)],
-        ext_grad, lists, *cross_grads, *sides, parents,
+        *cross_grads[::-1], ext_grad, lists, *sides, parents,
     )
     side_grads = swap_pairs(to_even, to_odd, "gy")
     given, pad = call(
@@ -608,11 +608,11 @@
     (sums,) = call(pair_sum_body, [shape(half_sums_dims)], kept, given)
     sums = trade_rows(sums, ("x", "gy"))
     output, lists = call(
-        conv_body, [rows, lists_shape], pad, conv_weight, lists, scratch=[band], flops=conv_flops
+        conv_body, [rows, lists_shape], pad, conv_weight, lists, scratch=[band], flops=20 * conv_flops
     )
     grad_fine, replies = call(
         functools.partial(fine_grad_body, across=across), [rows, shape((count // 2, 2 * item_lanes))],
-        fine_part, lists, *side_grads, up_turned,
+        fine_part, lists, *side_grads, up_turned, flops=10 * conv_flops,
     )
     (back,) = call(
         functools.partial(share_body, across=across), [shape((count // 2, 2 * item_lanes + sums_width))], sums, replies

time: 64.6 us -> 65.5 us (1.014)
  waiting for transfers between devices: 10.4 us -> 12.7 us
  blocking collectives: 14.1 us -> 12.7 us
    all_to_all x2, waiting for transfers between devices: 5.4 us -> 10.6 us  [trade_rows(): lax.all_to_all(grid_view, axes, split_axis=0, concat_axis=0, tiled=True)]
    ppermute x10, waiting for transfers between devices: 4.99 us -> 2.1 us  [swap(): lax.ppermute(value, axis, [(i, i + 1) for i in lower] + [(i + 1, i) for i...]
    ppermute x10, starting transfers between devices: 9.1 us -> 11.8 us  [swap(): lax.ppermute(value, axis, [(i, i + 1) for i in lower] + [(i + 1, i) for i...]
    all_to_all x2, starting transfers between devices: 13.9 us -> 11.4 us  [trade_rows(): lax.all_to_all(grid_view, axes, split_axis=0, concat_axis=0, tiled=True)]
    all_to_all x1, blocking collectives: 14.1 us -> 12.7 us  [trade_rows(): lax.all_to_all(grid_view, axes, split_axis=0, concat_axis=0, tiled=True)]
  transfers between devices with their start and end apart: 12 -> 12, of which waited for: 7 -> 4; matrix products, arithmetic and copies ran while one was open for 0% -> 0% of each run, Pallas kernels for 11% -> 14%
where the time goes in v17:
time: 65.5 us; the launch traced here: 64.9 us
  starting transfers between devices  23.1 us (35%)
  Pallas kernels  13.3 us (20%)
  waiting for transfers between devices  12.7 us (19%)
  blocking collectives  12.7 us (19%)
  local copies, waits for them, and re-layouts  2.33 us (4%)
  between operations  0.82 us (1%)
    pallas_call x12, Pallas kernels, call(): pl.pallas_call(body, out_shape=tuple(outs), in_specs=[pl.BlockSpec(memory...  13.3 us
    all_to_all x1, blocking collectives, trade_rows(): lax.all_to_all(grid_view, axes, split_axis=0, concat_axis=0, tiled=True)  12.7 us
    ppermute x10, starting transfers between devices, swap(): lax.ppermute(value, axis, [(i, i + 1) for i in lower] + [(i + 1, i) for i...  11.8 us
    all_to_all x2, starting transfers between devices, trade_rows(): lax.all_to_all(grid_view, axes, split_axis=0, concat_axis=0, tiled=True)  11.4 us
    all_to_all x2, waiting for transfers between devices, trade_rows(): lax.all_to_all(grid_view, axes, split_axis=0, concat_axis=0, tiled=True)  10.6 us
    unnamed x14, local copies, waits for them, and re-layouts  2.33 us
    ppermute x10, waiting for transfers between devices, swap(): lax.ppermute(value, axis, [(i, i + 1) for i in lower] + [(i + 1, i) for i...  2.1 us
  transfers between devices with their start and end apart: 12, of which 4 were waited for; matrix products, arithmetic and copies ran while one was open for 0% of the time, Pallas kernels for 14%

profile of v17, /device:TPU:0, one launch (start us, length us, event | category | flops | bytes accessed | tf_op | source)
XLA Modules:
  0.0 64.9 jit_solution(8092312945822372767)
XLA Ops:
  0.6 0.0 copy-start.3
  0.6 1.9 %shard_map.137 = (bf16[128,512]{1,0:T(8,128)(2,1)}, s32[8,128]{1,0:T(8,128)}) custom-call(s32[4,16]{1,0:T(4,128)} %bitcast.35, bf16[64,1024]{1,0:T(8,128)(2,1)} %bitcast.39, s32[2,8]{1,0:T(2,128)} %bitcast.41, s32[2,8]{1,0:T(2,128)} %bitcast.42, s32[1,32]{1,0:T(1,128)} %bitcast.43), custom_call_target="tpu_custom_call" | custom-call | bytes 266752 | tf_op jit(solution)/shard_map/pallas_call | solution.py:50
  2.5 7.4 %all-to-all-start = ((bf16[16,8,512]{2,1,0:T(8,128)(2,1)}), bf16[16,8,512]{2,1,0:T(8,128)(2,1)S(1)}, u32[]{:S(2)}, u32[]{:S(2)}) async-start(bf16[16,8,512]{2,1,0:T(8,128)(2,1)} %bitcast.40), calls=%async_computation | async-start | bytes 262144 | tf_op jit(solution)/shard_map/all_to_all | solution.py:532
  9.9 0.0 copy-start.6
  9.9 0.0 copy-done.3
  9.9 0.7 %copy-done.6 = s32[8,128]{1,0:T(8,128)S(1)} copy-done((s32[8,128]{1,0:T(8,128)S(1)}, s32[8,128]{1,0:T(8,128)}, u32[]{:S(2)}) %copy-start.6) | copy-done | bytes 4120
  10.6 0.0 copy-start.4
  10.6 0.9 %copy-done.4 = bf16[1,1,32,4096]{3,2,1,0:T(8,128)(2,1)S(1)} copy-done((bf16[1,1,32,4096]{3,2,1,0:T(8,128)(2,1)S(1)}, bf16[1,1,32,4096]{3,2,1,0:T(8,128)(2,1)}, u32[]{:S(2)}) %copy-start.4) | copy-done | bytes 262168
  11.5 0.0 copy-start.5
  11.5 0.7 %copy-done.5 = s32[1,1,32,27]{2,1,3,0:T(1,128)S(1)} copy-done((s32[1,1,32,27]{2,1,3,0:T(1,128)S(1)}, s32[1,1,32,27]{2,1,3,0:T(1,128)}, u32[]{:S(2)}) %copy-start.5) | copy-done | bytes 3480
  12.2 2.0 %shard_map.138 = (f32[48,4096]{1,0:T(8,128)S(1)}, bf16[8,4096]{1,0:T(8,128)(2,1)S(1)}, bf16[8,4096]{1,0:T(8,128)(2,1)S(1)}, bf16[256,512]{1,0:T(8,128)(2,1)S(1)}...) custom-call(bf16[32,4096]{1,0:T(8,128)(2,1)S(1)} %bitcast.37, ...), custom_call_target="tpu_custom_call" | custom-call | flops 1811939328 | bytes 1785728 | tf_op jit(solution)/shard_map/pallas_call | solution.py:50
  14.2 3.0 %all-to-all-done = bf16[16,8,512]{2,1,0:T(8,128)(2,1)S(1)} async-done(((bf16[16,8,512]{2,1,0:T(8,128)(2,1)}), bf16[16,8,512]{2,1,0:T(8,128)(2,1)S(1)}, u32[]{:S(2)}, u32[]{:S(2)}) %all-to-all-start) | async-done | bytes 131104 | tf_op jit(solution)/shard_map/all_to_all | solution.py:532
  17.2 0.0 copy-done
  17.2 0.0 copy-done.1
  17.2 0.6 shard_map.139
  17.9 0.7 %collective-permute-start = (bf16[8,5120]{1,0:T(8,128)(2,1)S(1)}, bf16[8,5120]{1,0:T(8,128)(2,1)S(1)}, u32[]{:S(2)}, u32[]{:S(2)}) collective-permute-start(bf16[8,5120]{1,0:T(8,128)(2,1)S(1)} %get-tuple-element.37), channel_id=1, source_target_pairs={{0,1},{2,3},{1,0},{3,2},{4,5},{6,7},{5,4},{7,6},{8,9},{10,11},{9,8... | collective-permute-start | bytes 245768 | tf_op jit(solution)/shard_map/ppermute | solution.py:521
  18.6 0.7 %collective-permute-start.1 = (bf16[8,5120]{1,0:T(8,128)(2,1)S(1)}, bf16[8,5120]{1,0:T(8,128)(2,1)S(1)}, u32[]{:S(2)}, u32[]{:S(2)}) collective-permute-start(bf16[8,5120]{1,0:T(8,128)(2,1)S(1)} %get-tuple-element.38), channel_id=1, source_target_pairs={{1,2},{2,1},{5,6},{6,5},{9,10},{10,9},{13,14},{14,13},{17,18},{18,... | collective-permute-start | bytes 245768 | tf_op jit(solution)/shard_map/ppermute | solution.py:521
  19.2 0.7 %collective-permute-start.4 = (bf16[8,4096]{1,0:T(8,128)(2,1)S(1)}, bf16[8,4096]{1,0:T(8,128)(2,1)S(1)}, u32[]{:S(2)}, u32[]{:S(2)}) collective-permute-start(bf16[8,4096]{1,0:T(8,128)(2,1)S(1)} %get-tuple-element.44), channel_id=1, source_target_pairs={{4,8},{8,4},{5,9},{9,5},{6,10},{10,6},{7,11},{11,7},{20,24},{24,20... | collective-permute-start | bytes 196616 | tf_op jit(solution)/shard_map/ppermute | solution.py:521
  19.9 2.0 %collective-permute-start.5 = (bf16[8,4096]{1,0:T(8,128)(2,1)S(1)}, bf16[8,4096]{1,0:T(8,128)(2,1)S(1)}, u32[]{:S(2)}, u32[]{:S(2)}) collective-permute-start(bf16[8,4096]{1,0:T(8,128)(2,1)S(1)} %get-tuple-element.45), channel_id=1, source_target_pairs={{0,4},{8,12},{4,0},{12,8},{1,5},{9,13},{5,1},{13,9},{2,6},{10,14},... | collective-permute-start | bytes 196616 | tf_op jit(solution)/shard_map/ppermute | solution.py:521
  21.9 0.5 collective-permute-done.even_ref.even_side_ref
  22.4 0.0 collective-permute-done.1.odd_ref.odd_side_ref
  22.4 0.3 shard_map.140
  22.7 0.7 %collective-permute-start.2 = (bf16[8,4096]{1,0:T(8,128)(2,1)S(1)}, bf16[8,4096]{1,0:T(8,128)(2,1)S(1)}, u32[]{:S(2)}, u32[]{:S(2)}) collective-permute-start(bf16[8,4096]{1,0:T(8,128)(2,1)S(1)} %get-tuple-element.39), channel_id=1, source_target_pairs={{4,8},{8,4},{5,9},{9,5},{6,10},{10,6},{7,11},{11,7},{20,24},{24,20... | collective-permute-start | bytes 196616 | tf_op jit(solution)/shard_map/ppermute | solution.py:521
  23.4 2.4 %collective-permute-start.3 = (bf16[8,4096]{1,0:T(8,128)(2,1)S(1)}, bf16[8,4096]{1,0:T(8,128)(2,1)S(1)}, u32[]{:S(2)}, u32[]{:S(2)}) collective-permute-start(bf16[8,4096]{1,0:T(8,128)(2,1)S(1)} %get-tuple-element.40), channel_id=1, source_target_pairs={{0,4},{8,12},{4,0},{12,8},{1,5},{9,13},{5,1},{13,9},{2,6},{10,14},... | collective-permute-start | bytes 196616 | tf_op jit(solution)/shard_map/ppermute | solution.py:521
  25.8 0.0 collective-permute-done.4.odd_grad_ref
  25.8 0.0 collective-permute-done.5.even_grad_ref
  25.8 0.6 shard_map.141
  26.4 4.0 %collective-permute-start.6 = (bf16[8,4096]{1,0:T(8,128)(2,1)S(1)}, bf16[8,4096]{1,0:T(8,128)(2,1)S(1)}, u32[]{:S(2)}, u32[]{:S(2)}) collective-permute-start(bf16[8,4096]{1,0:T(8,128)(2,1)S(1)} %get-tuple-element.53), channel_id=1, source_target_pairs={{0,1},{2,3},{1,0},{3,2},{4,5},{6,7},{5,4},{7,6},{8,9},{10,11},{9,8... | collective-permute-start | bytes 196616 | tf_op jit(solution)/shard_map/ppermute | solution.py:521
  30.4 0.7 %collective-permute-start.7 = (bf16[8,4096]{1,0:T(8,128)(2,1)S(1)}, bf16[8,4096]{1,0:T(8,128)(2,1)S(1)}, u32[]{:S(2)}, u32[]{:S(2)}) collective-permute-start(bf16[8,4096]{1,0:T(8,128)(2,1)S(1)} %get-tuple-element.54), channel_id=1, source_target_pairs={{1,2},{2,1},{5,6},{6,5},{9,10},{10,9},{13,14},{14,13},{17,18},{18,... | collective-permute-start | bytes 196616 | tf_op jit(solution)/shard_map/ppermute | solution.py:521
  31.0 0.0 collective-permute-done.2.odd_cross_ref
  31.0 0.0 collective-permute-done.3.even_cross_ref
  31.0 1.4 %shard_map.142 = (bf16[64,1408]{1,0:T(8,128)(2,1)S(1)}, bf16[6,6,32,384]{3,2,1,0:T(8,128)(2,1)S(1)}) custom-call(bf16[8,4096]{1,0:T(8,128)(2,1)S(1)} %collective-permute-done.2.odd_cross_ref, bf16[8,4096]{1,0:T(8,128)(2,1)S(1)} %collective-permute-done.3.even_cross_ref, bf16[32,4096]{1,0:T(8,128)(2,1)S(1)} %get-tuple-element.36.merged_ref, ...), custom_call_target="tpu_custom_call" | custom-call | flops 905969664 | bytes 2260992 | tf_op jit(solution)/shard_map/pallas_call | solution.py:50
  32.5 0.1 collective-permute-start.8
  32.5 2.2 %shard_map.143 = (bf16[32,4096]{1,0:T(8,128)(2,1)}, s32[8,128]{1,0:T(8,128)S(1)}) custom-call(bf16[6,6,32,384]{3,2,1,0:T(8,128)(2,1)S(1)} %get-tuple-element.49.pad_ref, bf16[27,64,64]{2,1,0:T(8,128)(2,1)S(1)} %copy-done.3, s32[8,128]{1,0:T(8,128)S(1)} %get-tuple-element.35.lists_ref), custom_call_target="tpu_custom_call" | custom-call | flops 18119393280 | bytes 1376256 | tf_op jit(solution)/shard_map/pallas_call | solution.py:50
  34.8 0.9 %shard_map.145.kept_ref = f32[64,1408]{1,0:T(8,128)S(1)} custom-call(bf16[6,6,32,384]{3,2,1,0:T(8,128)(2,1)S(1)} %get-tuple-element.49.pad_ref, bf16[256,512]{1,0:T(8,128)(2,1)S(1)} %get-tuple-element.41.turned_ref, f32[128,512]{1,0:T(8,128)S(1)} %get-tuple-element.48.up_sums_ref, s32[8,128]{1,0:T(8,128)S(1)} %get-tuple-element.35.lists_ref), custom_call_target="tpu_custom_call" | custom-call | flops 905969664 | bytes 1773568 | tf_op jit(solution)/shard_map/pallas_call | solution.py:50
  35.7 0.0 collective-permute-done.8.given_ref
  35.7 0.7 %shard_map.146 = bf16[64,1408]{1,0:T(8,128)(2,1)} custom-call(f32[64,1408]{1,0:T(8,128)S(1)} %shard_map.145.kept_ref, bf16[64,1408]{1,0:T(8,128)(2,1)S(1)} %collective-permute-done.8.given_ref), custom_call_target="tpu_custom_call" | custom-call | bytes 720896 | tf_op jit(solution)/shard_map/pallas_call | solution.py:50
  36.4 4.0 %all-to-all-start.1 = ((bf16[8,8,1408]{2,1,0:T(8,128)(2,1)}), bf16[8,8,1408]{2,1,0:T(8,128)(2,1)S(1)}, u32[]{:S(2)}, u32[]{:S(2)}) async-start(bf16[8,8,1408]{2,1,0:T(8,128)(2,1)} %bitcast.17), calls=%async_computation.1 | async-start | bytes 360448 | tf_op jit(solution)/shard_map/all_to_all | solution.py:532
  40.4 0.0 collective-permute-done.6.even_ref
  40.4 0.0 collective-permute-done.7.odd_ref
  40.4 1.1 %shard_map.144 = (bf16[32,4096]{1,0:T(8,128)(2,1)}, bf16[64,1024]{1,0:T(8,128)(2,1)S(1)}) custom-call(f32[32,4096]{1,0:T(8,128)S(1)} %get-tuple-element.51.part_ref, s32[8,128]{1,0:T(8,128)S(1)} %get-tuple-element.52.lists_ref, bf16[8,4096]{1,0:T(8,128)(2,1)S(1)} %collective-permute-done.6.even_ref, bf16[8,4096]{1,0:T(8,128)(2,1)S(1)} %collective-permute-done.7.odd_ref, ...), custom_call_target="tpu_custom_call" | custom-call | flops 9059696640 | bytes 1183744 | tf_op jit(solution)/shard_map/pallas_call | solution.py:50
  41.5 7.6 %all-to-all-done.1 = bf16[8,8,1408]{2,1,0:T(8,128)(2,1)S(1)} async-done(((bf16[8,8,1408]{2,1,0:T(8,128)(2,1)}), bf16[8,8,1408]{2,1,0:T(8,128)(2,1)S(1)}, u32[]{:S(2)}, u32[]{:S(2)}) %all-to-all-start.1) | async-done | bytes 180256 | tf_op jit(solution)/shard_map/all_to_all | solution.py:532
  49.1 0.2 shard_map.147
  49.3 12.7 %all_to_all.15 = bf16[8,8,2432]{2,1,0:T(8,128)(2,1)S(1)} all-to-all(bf16[8,8,2432]{2,1,0:T(8,128)(2,1)S(1)} %bitcast.29), channel_id=1, replica_groups=mesh['groups'=2,'x'=2,'core'=2,'gy'=4] {'x','gy'}, dimensions={0} | all-to-all | bytes 622592 | tf_op jit(solution)/shard_map/all_to_all | solution.py:532
  62.0 0.0 collective-permute-start.9
  62.0 1.6 %collective-permute-done.9.given_ref = bf16[64,2432]{1,0:T(8,128)(2,1)S(1)} collective-permute-done((bf16[64,2432]{1,0:T(8,128)(2,1)S(1)}, bf16[64,2432]{1,0:T(8,128)(2,1)S(1)}, u32[]{:S(2)}, u32[]{:S(2)}) %collective-permute-start.9) | collective-permute-done | bytes 311328 | tf_op jit(solution)/shard_map/ppermute | solution.py:521
  63.6 0.0 copy-done.2
  63.6 1.4 %shard_map.148 = (f32[27,64,64]{2,1,0:T(8,128)}, f32[512,128]{1,0:T(8,128)}, bf16[64,1024]{1,0:T(8,128)(2,1)}) custom-call(bf16[64,2432]{1,0:T(8,128)(2,1)S(1)} %bitcast.28, bf16[64,2432]{1,0:T(8,128)(2,1)S(1)} %collective-permute-done.9.given_ref, s32[4,16]{1,0:T(4,128)S(1)} %bitcast.36, s32[8,128]{1,0:T(8,128)S(1)} %get-tuple-element.52.lists_ref), custom_call_target="tpu_custom_call" | custom-call | bytes 1462528 | tf_op jit(solution)/shard_map/pallas_call | solution.py:50
  (4 shorter events, 0.0 us)
Async XLA Ops:
  0.6 9.3 %copy-start.3 = (bf16[27,64,64]{2,1,0:T(8,128)(2,1)S(1)}, bf16[27,64,64]{2,1,0:T(8,128)(2,1)}, u32[]{:S(2)}) copy-start(bf16[27,64,64]{2,1,0:T(8,128)(2,1)} %weight_ref.3) | copy-start | bytes 663556
  2.5 14.7 %all-to-all-start = ((bf16[16,8,512]{2,1,0:T(8,128)(2,1)}), bf16[16,8,512]{2,1,0:T(8,128)(2,1)S(1)}, u32[]{:S(2)}, u32[]{:S(2)}) async-start(bf16[16,8,512]{2,1,0:T(8,128)(2,1)} %bitcast.40), calls=%async_computation | async-start | bytes 262144 | tf_op jit(solution)/shard_map/all_to_all | solution.py:532
  9.9 0.7 %copy-start.6 = (s32[8,128]{1,0:T(8,128)S(1)}, s32[8,128]{1,0:T(8,128)}, u32[]{:S(2)}) copy-start(s32[8,128]{1,0:T(8,128)} %get-tuple-element.34.lists_ref) | copy-start | bytes 12292
  10.6 0.9 %copy-start.4 = (bf16[1,1,32,4096]{3,2,1,0:T(8,128)(2,1)S(1)}, bf16[1,1,32,4096]{3,2,1,0:T(8,128)(2,1)}, u32[]{:S(2)}) copy-start(bf16[1,1,32,4096]{3,2,1,0:T(8,128)(2,1)} %param.19) | copy-start | bytes 786436
  11.5 0.7 %copy-start.5 = (s32[1,1,32,27]{2,1,3,0:T(1,128)S(1)}, s32[1,1,32,27]{2,1,3,0:T(1,128)}, u32[]{:S(2)}) copy-start(s32[1,1,32,27]{2,1,3,0:T(1,128)} %param.14) | copy-start | bytes 10372
  12.2 5.0 %copy-start = (bf16[1,1,32,4096]{3,2,1,0:T(8,128)(2,1)S(1)}, bf16[1,1,32,4096]{3,2,1,0:T(8,128)(2,1)}, u32[]{:S(2)}) copy-start(bf16[1,1,32,4096]{3,2,1,0:T(8,128)(2,1)} %param.10) | copy-start | bytes 786436
  12.2 5.0 %copy-start.1 = (bf16[8,128,64]{1,2,0:T(8,128)(2,1)S(1)}, bf16[8,128,64]{1,2,0:T(8,128)(2,1)}, u32[]{:S(2)}) copy-start(bf16[8,128,64]{1,2,0:T(8,128)(2,1)} %param.13) | copy-start | bytes 393220
  17.9 4.5 %collective-permute-start = (bf16[8,5120]{1,0:T(8,128)(2,1)S(1)}, bf16[8,5120]{1,0:T(8,128)(2,1)S(1)}, u32[]{:S(2)}, u32[]{:S(2)}) collective-permute-start(bf16[8,5120]{1,0:T(8,128)(2,1)S(1)} %get-tuple-element.37), channel_id=1, source_target_pairs={{0,1},{2,3},{1,0},{3,2},{4,5},{6,7},{5,4},{7,6},{8,9},{10,11},{9,8... | collective-permute-start | bytes 245768 | tf_op jit(solution)/shard_map/ppermute | solution.py:521
  18.6 3.8 %collective-permute-start.1 = (bf16[8,5120]{1,0:T(8,128)(2,1)S(1)}, bf16[8,5120]{1,0:T(8,128)(2,1)S(1)}, u32[]{:S(2)}, u32[]{:S(2)}) collective-permute-start(bf16[8,5120]{1,0:T(8,128)(2,1)S(1)} %get-tuple-element.38), channel_id=1, source_target_pairs={{1,2},{2,1},{5,6},{6,5},{9,10},{10,9},{13,14},{14,13},{17,18},{18,... | collective-permute-start | bytes 245768 | tf_op jit(solution)/shard_map/ppermute | solution.py:521
  19.2 6.5 %collective-permute-start.4 = (bf16[8,4096]{1,0:T(8,128)(2,1)S(1)}, bf16[8,4096]{1,0:T(8,128)(2,1)S(1)}, u32[]{:S(2)}, u32[]{:S(2)}) collective-permute-start(bf16[8,4096]{1,0:T(8,128)(2,1)S(1)} %get-tuple-element.44), channel_id=1, source_target_pairs={{4,8},{8,4},{5,9},{9,5},{6,10},{10,6},{7,11},{11,7},{20,24},{24,20... | collective-permute-start | bytes 196616 | tf_op jit(solution)/shard_map/ppermute | solution.py:521
  19.9 5.9 %collective-permute-start.5 = (bf16[8,4096]{1,0:T(8,128)(2,1)S(1)}, bf16[8,4096]{1,0:T(8,128)(2,1)S(1)}, u32[]{:S(2)}, u32[]{:S(2)}) collective-permute-start(bf16[8,4096]{1,0:T(8,128)(2,1)S(1)} %get-tuple-element.45), channel_id=1, source_target_pairs={{0,4},{8,12},{4,0},{12,8},{1,5},{9,13},{5,1},{13,9},{2,6},{10,14},... | collective-permute-start | bytes 196616 | tf_op jit(solution)/shard_map/ppermute | solution.py:521
  22.7 8.3 %collective-permute-start.2 = (bf16[8,4096]{1,0:T(8,128)(2,1)S(1)}, bf16[8,4096]{1,0:T(8,128)(2,1)S(1)}, u32[]{:S(2)}, u32[]{:S(2)}) collective-permute-start(bf16[8,4096]{1,0:T(8,128)(2,1)S(1)} %get-tuple-element.39), channel_id=1, source_target_pairs={{4,8},{8,4},{5,9},{9,5},{6,10},{10,6},{7,11},{11,7},{20,24},{24,20... | collective-permute-start | bytes 196616 | tf_op jit(solution)/shard_map/ppermute | solution.py:521
  23.4 7.6 %collective-permute-start.3 = (bf16[8,4096]{1,0:T(8,128)(2,1)S(1)}, bf16[8,4096]{1,0:T(8,128)(2,1)S(1)}, u32[]{:S(2)}, u32[]{:S(2)}) collective-permute-start(bf16[8,4096]{1,0:T(8,128)(2,1)S(1)} %get-tuple-element.40), channel_id=1, source_target_pairs={{0,4},{8,12},{4,0},{12,8},{1,5},{9,13},{5,1},{13,9},{2,6},{10,14},... | collective-permute-start | bytes 196616 | tf_op jit(solution)/shard_map/ppermute | solution.py:521
  26.4 14.0 %collective-permute-start.6 = (bf16[8,4096]{1,0:T(8,128)(2,1)S(1)}, bf16[8,4096]{1,0:T(8,128)(2,1)S(1)}, u32[]{:S(2)}, u32[]{:S(2)}) collective-permute-start(bf16[8,4096]{1,0:T(8,128)(2,1)S(1)} %get-tuple-element.53), channel_id=1, source_target_pairs={{0,1},{2,3},{1,0},{3,2},{4,5},{6,7},{5,4},{7,6},{8,9},{10,11},{9,8... | collective-permute-start | bytes 196616 | tf_op jit(solution)/shard_map/ppermute | solution.py:521
  30.4 10.1 %collective-permute-start.7 = (bf16[8,4096]{1,0:T(8,128)(2,1)S(1)}, bf16[8,4096]{1,0:T(8,128)(2,1)S(1)}, u32[]{:S(2)}, u32[]{:S(2)}) collective-permute-start(bf16[8,4096]{1,0:T(8,128)(2,1)S(1)} %get-tuple-element.54), channel_id=1, source_target_pairs={{1,2},{2,1},{5,6},{6,5},{9,10},{10,9},{13,14},{14,13},{17,18},{18,... | collective-permute-start | bytes 196616 | tf_op jit(solution)/shard_map/ppermute | solution.py:521
  32.5 3.2 %collective-permute-start.8 = (bf16[64,1408]{1,0:T(8,128)(2,1)S(1)}, bf16[64,1408]{1,0:T(8,128)(2,1)S(1)}, u32[]{:S(2)}, u32[]{:S(2)}) collective-permute-start(bf16[64,1408]{1,0:T(8,128)(2,1)S(1)} %get-tuple-element.56), channel_id=1, source_target_pairs={{0,4},{4,0},{1,5},{5,1},{2,6},{6,2},{3,7},{7,3},{8,12},{12,8},{9,1... | collective-permute-start | bytes 540680 | tf_op jit(solution)/shard_map/ppermute | solution.py:521
  36.4 12.7 %all-to-all-start.1 = ((bf16[8,8,1408]{2,1,0:T(8,128)(2,1)}), bf16[8,8,1408]{2,1,0:T(8,128)(2,1)S(1)}, u32[]{:S(2)}, u32[]{:S(2)}) async-start(bf16[8,8,1408]{2,1,0:T(8,128)(2,1)} %bitcast.17), calls=%async_computation.1 | async-start | bytes 360448 | tf_op jit(solution)/shard_map/all_to_all | solution.py:532
  49.1 14.5 %copy-start.2 = (s32[1,1,16,4]{2,3,1,0:T(4,128)S(1)}, s32[1,1,16,4]{2,3,1,0:T(4,128)}, u32[]{:S(2)}) copy-start(s32[1,1,16,4]{2,3,1,0:T(4,128)} %param.18) | copy-start | bytes 772
  62.0 1.6 %collective-permute-start.9 = (bf16[64,2432]{1,0:T(8,128)(2,1)S(1)}, bf16[64,2432]{1,0:T(8,128)(2,1)S(1)}, u32[]{:S(2)}, u32[]{:S(2)}) collective-permute-start(bf16[64,2432]{1,0:T(8,128)(2,1)S(1)} %bitcast.27), channel_id=1, source_target_pairs={{0,4},{4,0},{1,5},{5,1},{2,6},{6,2},{3,7},{7,3},{8,12},{12,8},{9,1... | collective-permute-start | bytes 933896 | tf_op jit(solution)/shard_map/ppermute | solution.py:521

commit v18 on v17

--- a/solution.py
+++ b/solution.py
@@ -381,7 +381,8 @@
     half_sums(lists_ref[5, GX], pad_ref, turned_ref, up_sums_ref, kept_ref)
 
 
-def pair_sum_body(kept_ref, given_ref, out_ref):
+def pair_sum_body(kept_ref, given_ref, lists_ref, out_ref, again_ref):
+    again_ref[...] = lists_ref[...]
     out_ref[...] = (kept_ref[...] + given_ref[...].astype(F32)).astype(BF)
 
 
@@ -457,7 +458,7 @@
     return (chip // across[1] * 2 + core) * across[1] + chip % across[1]
 
 
-def share_body(sums_ref, replies_ref, out_ref, across):
+def share_body(sums_ref, replies_ref, lists_ref, out_ref, across):
     count, item_lanes = replies_ref.shape
     share = count // (across[0] * across[1] // 2)
     same = iota((count, count), 0) % share == iota((count, count), 1) % share
@@ -605,17 +606,18 @@
     )
     (kept,) = call(kept_sums_body, [shape(half_sums_dims, F32)], pad, turned, up_sums, lists, flops=conv_flops)
     given = swap(given, "core", 0)
-    (sums,) = call(pair_sum_body, [shape(half_sums_dims)], kept, given)
+    sums, after_sums = call(pair_sum_body, [shape(half_sums_dims), lists_shape], kept, given, lists)
     sums = trade_rows(sums, ("x", "gy"))
-    output, lists = call(
-        conv_body, [rows, lists_shape], pad, conv_weight, lists, scratch=[band], flops=20 * conv_flops
+    output, after_conv = call(
+        conv_body, [rows, lists_shape], pad, conv_weight, after_sums, scratch=[band], flops=conv_flops
     )
     grad_fine, replies = call(
         functools.partial(fine_grad_body, across=across), [rows, shape((count // 2, 2 * item_lanes))],
-        fine_part, lists, *side_grads, up_turned, flops=10 * conv_flops,
+        fine_part, after_sums, *side_grads, up_turned, flops=10 * conv_flops,
     )
     (back,) = call(
-        functools.partial(share_body, across=across), [shape((count // 2, 2 * item_lanes + sums_width))], sums, replies
+        functools.partial(share_body, across=across), [shape((count // 2, 2 * item_lanes + sums_width))],
+        sums, replies, after_conv,
     )
     back = trade_rows(back, ("x", "gy"))
     given = swap(back, "core", 0)

time: 65.5 us -> 65.2 us (level)
  waiting for transfers between devices: 12.7 us -> 10.5 us
  starting transfers between devices: 23.1 us -> 25.2 us
    all_to_all x2, waiting for transfers between devices: 10.6 us -> 8.13 us  [trade_rows(): lax.all_to_all(grid_view, axes, split_axis=0, concat_axis=0, tiled=True)]
    all_to_all x2, starting transfers between devices: 11.4 us -> 12.5 us  [trade_rows(): lax.all_to_all(grid_view, axes, split_axis=0, concat_axis=0, tiled=True)]
    ppermute x10, starting transfers between devices: 11.8 us -> 12.7 us  [swap(): lax.ppermute(value, axis, [(i, i + 1) for i in lower] + [(i + 1, i) for i...]
    unnamed x14 -> x18, local copies, waits for them, and re-layouts: 2.33 us -> 2.35 us
  transfers between devices with their start and end apart: 12 -> 12, of which waited for: 4 -> 5; matrix products, arithmetic and copies ran while one was open for 0% -> 0% of each run, Pallas kernels for 14% -> 12%
where the time goes in v18:
time: 65.2 us; the launch traced here: 64.6 us
  starting transfers between devices  25.2 us (39%)
  Pallas kernels  13.3 us (20%)
  blocking collectives  12.5 us (19%)
  waiting for transfers between devices  10.5 us (16%)
  local copies, waits for them, and re-layouts  2.35 us (4%)
  between operations  0.84 us (1%)
    pallas_call x12, Pallas kernels, call(): pl.pallas_call(body, out_shape=tuple(outs), in_specs=[pl.BlockSpec(memory...  13.3 us
    ppermute x10, starting transfers between devices, swap(): lax.ppermute(value, axis, [(i, i + 1) for i in lower] + [(i + 1, i) for i...  12.7 us
    all_to_all x2, starting transfers between devices, trade_rows(): lax.all_to_all(grid_view, axes, split_axis=0, concat_axis=0, tiled=True)  12.5 us
    all_to_all x1, blocking collectives, trade_rows(): lax.all_to_all(grid_view, axes, split_axis=0, concat_axis=0, tiled=True)  12.5 us
    all_to_all x2, waiting for transfers between devices, trade_rows(): lax.all_to_all(grid_view, axes, split_axis=0, concat_axis=0, tiled=True)  8.13 us
    ppermute x10, waiting for transfers between devices, swap(): lax.ppermute(value, axis, [(i, i + 1) for i in lower] + [(i + 1, i) for i...  2.37 us
    unnamed x18, local copies, waits for them, and re-layouts  2.35 us
  transfers between devices with their start and end apart: 12, of which 5 were waited for; matrix products, arithmetic and copies ran while one was open for 0% of the time, Pallas kernels for 12%

profile of v18, /device:TPU:0, one launch (start us, length us, event | category | flops | bytes accessed | tf_op | source)
XLA Modules:
  0.0 64.6 jit_solution(6523053913830738406)
XLA Ops:
  0.6 0.0 copy-start.3
  0.6 1.9 %shard_map.137 = (bf16[128,512]{1,0:T(8,128)(2,1)}, s32[8,128]{1,0:T(8,128)}) custom-call(s32[4,16]{1,0:T(4,128)} %bitcast.35, bf16[64,1024]{1,0:T(8,128)(2,1)} %bitcast.39, s32[2,8]{1,0:T(2,128)} %bitcast.41, s32[2,8]{1,0:T(2,128)} %bitcast.42, s32[1,32]{1,0:T(1,128)} %bitcast.43), custom_call_target="tpu_custom_call" | custom-call | bytes 266752 | tf_op jit(solution)/shard_map/pallas_call | solution.py:50
  2.5 7.4 %all-to-all-start = ((bf16[16,8,512]{2,1,0:T(8,128)(2,1)}), bf16[16,8,512]{2,1,0:T(8,128)(2,1)S(1)}, u32[]{:S(2)}, u32[]{:S(2)}) async-start(bf16[16,8,512]{2,1,0:T(8,128)(2,1)} %bitcast.40), calls=%async_computation | async-start | bytes 262144 | tf_op jit(solution)/shard_map/all_to_all | solution.py:533
  9.9 0.0 copy-start.6
  9.9 0.0 copy-done.3
  9.9 0.7 %copy-done.6 = s32[8,128]{1,0:T(8,128)S(1)} copy-done((s32[8,128]{1,0:T(8,128)S(1)}, s32[8,128]{1,0:T(8,128)}, u32[]{:S(2)}) %copy-start.6) | copy-done | bytes 4120
  10.6 0.9 %copy-done.4 = bf16[1,1,32,4096]{3,2,1,0:T(8,128)(2,1)S(1)} copy-done((bf16[1,1,32,4096]{3,2,1,0:T(8,128)(2,1)S(1)}, bf16[1,1,32,4096]{3,2,1,0:T(8,128)(2,1)}, u32[]{:S(2)}) %copy-start.4) | copy-done | bytes 262168
  11.5 0.7 %copy-done.5 = s32[1,1,32,27]{2,1,3,0:T(1,128)S(1)} copy-done((s32[1,1,32,27]{2,1,3,0:T(1,128)S(1)}, s32[1,1,32,27]{2,1,3,0:T(1,128)}, u32[]{:S(2)}) %copy-start.5) | copy-done | bytes 3480
  12.2 2.0 %shard_map.138 = (f32[48,4096]{1,0:T(8,128)S(1)}, bf16[8,4096]{1,0:T(8,128)(2,1)S(1)}, bf16[8,4096]{1,0:T(8,128)(2,1)S(1)}, bf16[256,512]{1,0:T(8,128)(2,1)S(1)}...) custom-call(bf16[32,4096]{1,0:T(8,128)(2,1)S(1)} %bitcast.37, ...), custom_call_target="tpu_custom_call" | custom-call | flops 1811939328 | bytes 1785728 | tf_op jit(solution)/shard_map/pallas_call | solution.py:50
  14.2 0.0 copy-start.7
  14.2 3.0 %all-to-all-done = bf16[16,8,512]{2,1,0:T(8,128)(2,1)S(1)} async-done(((bf16[16,8,512]{2,1,0:T(8,128)(2,1)}), bf16[16,8,512]{2,1,0:T(8,128)(2,1)S(1)}, u32[]{:S(2)}, u32[]{:S(2)}) %all-to-all-start) | async-done | bytes 131104 | tf_op jit(solution)/shard_map/all_to_all | solution.py:533
  17.2 0.0 copy-done
  17.2 0.0 copy-done.1
  17.2 0.6 shard_map.139
  17.9 0.0 copy-done.7
  17.9 0.7 %collective-permute-start = (bf16[8,5120]{1,0:T(8,128)(2,1)S(1)}, bf16[8,5120]{1,0:T(8,128)(2,1)S(1)}, u32[]{:S(2)}, u32[]{:S(2)}) collective-permute-start(bf16[8,5120]{1,0:T(8,128)(2,1)S(1)} %get-tuple-element.39), channel_id=1, source_target_pairs={{0,1},{2,3},{1,0},{3,2},{4,5},{6,7},{5,4},{7,6},{8,9},{10,11},{9,8... | collective-permute-start | bytes 245768 | tf_op jit(solution)/shard_map/ppermute | solution.py:522
  18.6 0.7 %collective-permute-start.1 = (bf16[8,5120]{1,0:T(8,128)(2,1)S(1)}, bf16[8,5120]{1,0:T(8,128)(2,1)S(1)}, u32[]{:S(2)}, u32[]{:S(2)}) collective-permute-start(bf16[8,5120]{1,0:T(8,128)(2,1)S(1)} %get-tuple-element.40), channel_id=1, source_target_pairs={{1,2},{2,1},{5,6},{6,5},{9,10},{10,9},{13,14},{14,13},{17,18},{18,... | collective-permute-start | bytes 245768 | tf_op jit(solution)/shard_map/ppermute | solution.py:522
  19.3 0.7 %collective-permute-start.4 = (bf16[8,4096]{1,0:T(8,128)(2,1)S(1)}, bf16[8,4096]{1,0:T(8,128)(2,1)S(1)}, u32[]{:S(2)}, u32[]{:S(2)}) collective-permute-start(bf16[8,4096]{1,0:T(8,128)(2,1)S(1)} %get-tuple-element.46), channel_id=1, source_target_pairs={{4,8},{8,4},{5,9},{9,5},{6,10},{10,6},{7,11},{11,7},{20,24},{24,20... | collective-permute-start | bytes 196616 | tf_op jit(solution)/shard_map/ppermute | solution.py:522
  19.9 2.0 %collective-permute-start.5 = (bf16[8,4096]{1,0:T(8,128)(2,1)S(1)}, bf16[8,4096]{1,0:T(8,128)(2,1)S(1)}, u32[]{:S(2)}, u32[]{:S(2)}) collective-permute-start(bf16[8,4096]{1,0:T(8,128)(2,1)S(1)} %get-tuple-element.47), channel_id=1, source_target_pairs={{0,4},{8,12},{4,0},{12,8},{1,5},{9,13},{5,1},{13,9},{2,6},{10,14},... | collective-permute-start | bytes 196616 | tf_op jit(solution)/shard_map/ppermute | solution.py:522
  21.9 0.5 collective-permute-done.even_ref.even_side_ref
  22.4 0.0 collective-permute-done.1.odd_ref.odd_side_ref
  22.4 0.3 shard_map.140
  22.8 0.7 %collective-permute-start.2 = (bf16[8,4096]{1,0:T(8,128)(2,1)S(1)}, bf16[8,4096]{1,0:T(8,128)(2,1)S(1)}, u32[]{:S(2)}, u32[]{:S(2)}) collective-permute-start(bf16[8,4096]{1,0:T(8,128)(2,1)S(1)} %get-tuple-element.41), channel_id=1, source_target_pairs={{4,8},{8,4},{5,9},{9,5},{6,10},{10,6},{7,11},{11,7},{20,24},{24,20... | collective-permute-start | bytes 196616 | tf_op jit(solution)/shard_map/ppermute | solution.py:522
  23.4 2.4 %collective-permute-start.3 = (bf16[8,4096]{1,0:T(8,128)(2,1)S(1)}, bf16[8,4096]{1,0:T(8,128)(2,1)S(1)}, u32[]{:S(2)}, u32[]{:S(2)}) collective-permute-start(bf16[8,4096]{1,0:T(8,128)(2,1)S(1)} %get-tuple-element.42), channel_id=1, source_target_pairs={{0,4},{8,12},{4,0},{12,8},{1,5},{9,13},{5,1},{13,9},{2,6},{10,14},... | collective-permute-start | bytes 196616 | tf_op jit(solution)/shard_map/ppermute | solution.py:522
  25.8 0.0 collective-permute-done.4.odd_grad_ref
  25.8 0.0 collective-permute-done.5.even_grad_ref
  25.8 0.6 shard_map.141
  26.4 0.0 collective-permute-done.2.odd_cross_ref
  26.4 0.3 collective-permute-done.3.even_cross_ref
  26.7 1.4 %shard_map.142 = (bf16[64,1408]{1,0:T(8,128)(2,1)S(1)}, bf16[6,6,32,384]{3,2,1,0:T(8,128)(2,1)S(1)}) custom-call(bf16[8,4096]{1,0:T(8,128)(2,1)S(1)} %collective-permute-done.2.odd_cross_ref, bf16[8,4096]{1,0:T(8,128)(2,1)S(1)} %collective-permute-done.3.even_cross_ref, bf16[32,4096]{1,0:T(8,128)(2,1)S(1)} %get-tuple-element.38.merged_ref, ...), custom_call_target="tpu_custom_call" | custom-call | flops 905969664 | bytes 2260992 | tf_op jit(solution)/shard_map/pallas_call | solution.py:50
  28.1 1.3 %collective-permute-start.6 = (bf16[64,1408]{1,0:T(8,128)(2,1)S(1)}, bf16[64,1408]{1,0:T(8,128)(2,1)S(1)}, u32[]{:S(2)}, u32[]{:S(2)}) collective-permute-start(bf16[64,1408]{1,0:T(8,128)(2,1)S(1)} %get-tuple-element.52), channel_id=1, source_target_pairs={{0,4},{4,0},{1,5},{5,1},{2,6},{6,2},{3,7},{7,3},{8,12},{12,8},{9,1... | collective-permute-start | bytes 540680 | tf_op jit(solution)/shard_map/ppermute | solution.py:522
  29.4 3.7 %collective-permute-start.7 = (bf16[8,4096]{1,0:T(8,128)(2,1)S(1)}, bf16[8,4096]{1,0:T(8,128)(2,1)S(1)}, u32[]{:S(2)}, u32[]{:S(2)}) collective-permute-start(bf16[8,4096]{1,0:T(8,128)(2,1)S(1)} %get-tuple-element.56), channel_id=1, source_target_pairs={{0,1},{2,3},{1,0},{3,2},{4,5},{6,7},{5,4},{7,6},{8,9},{10,11},{9,8... | collective-permute-start | bytes 196616 | tf_op jit(solution)/shard_map/ppermute | solution.py:522
  33.1 0.7 %collective-permute-start.8 = (bf16[8,4096]{1,0:T(8,128)(2,1)S(1)}, bf16[8,4096]{1,0:T(8,128)(2,1)S(1)}, u32[]{:S(2)}, u32[]{:S(2)}) collective-permute-start(bf16[8,4096]{1,0:T(8,128)(2,1)S(1)} %get-tuple-element.57), channel_id=1, source_target_pairs={{1,2},{2,1},{5,6},{6,5},{9,10},{10,9},{13,14},{14,13},{17,18},{18,... | collective-permute-start | bytes 196616 | tf_op jit(solution)/shard_map/ppermute | solution.py:522
  33.7 0.9 %shard_map.143.kept_ref = f32[64,1408]{1,0:T(8,128)S(1)} custom-call(bf16[6,6,32,384]{3,2,1,0:T(8,128)(2,1)S(1)} %get-tuple-element.51.pad_ref, bf16[256,512]{1,0:T(8,128)(2,1)S(1)} %get-tuple-element.43.turned_ref, f32[128,512]{1,0:T(8,128)S(1)} %get-tuple-element.50.up_sums_ref, s32[8,128]{1,0:T(8,128)S(1)} %get-tuple-element.37.lists_ref), custom_call_target="tpu_custom_call" | custom-call | flops 905969664 | bytes 1773568 | tf_op jit(solution)/shard_map/pallas_call | solution.py:50
  34.7 0.0 collective-permute-done.6.given_ref
  34.7 0.7 %shard_map.144 = (bf16[64,1408]{1,0:T(8,128)(2,1)}, s32[8,128]{1,0:T(8,128)S(1)}) custom-call(f32[64,1408]{1,0:T(8,128)S(1)} %shard_map.143.kept_ref, bf16[64,1408]{1,0:T(8,128)(2,1)S(1)} %collective-permute-done.6.given_ref, s32[8,128]{1,0:T(8,128)S(1)} %get-tuple-element.37.lists_ref), custom_call_target="tpu_custom_call" | custom-call | bytes 729088 | tf_op jit(solution)/shard_map/pallas_call | solution.py:50
  35.4 5.1 %all-to-all-start.1 = ((bf16[8,8,1408]{2,1,0:T(8,128)(2,1)}), bf16[8,8,1408]{2,1,0:T(8,128)(2,1)S(1)}, u32[]{:S(2)}, u32[]{:S(2)}) async-start(bf16[8,8,1408]{2,1,0:T(8,128)(2,1)} %bitcast.17), calls=%async_computation.1 | async-start | bytes 360448 | tf_op jit(solution)/shard_map/all_to_all | solution.py:533
  40.5 0.0 collective-permute-done.7.even_ref
  40.6 0.0 collective-permute-done.8.odd_ref
  40.6 1.1 %shard_map.146 = (bf16[32,4096]{1,0:T(8,128)(2,1)}, bf16[64,1024]{1,0:T(8,128)(2,1)S(1)}) custom-call(f32[32,4096]{1,0:T(8,128)S(1)} %get-tuple-element.55.part_ref, s32[8,128]{1,0:T(8,128)S(1)} %get-tuple-element.53.lists_ref, bf16[8,4096]{1,0:T(8,128)(2,1)S(1)} %collective-permute-done.7.even_ref, bf16[8,4096]{1,0:T(8,128)(2,1)S(1)} %collective-permute-done.8.odd_ref, ...), custom_call_target="tpu_custom_call" | custom-call | flops 9059696640 | bytes 1183744 | tf_op jit(solution)/shard_map/pallas_call | solution.py:50
  41.7 2.2 %shard_map.145 = (bf16[32,4096]{1,0:T(8,128)(2,1)}, s32[8,128]{1,0:T(8,128)S(1)}) custom-call(bf16[6,6,32,384]{3,2,1,0:T(8,128)(2,1)S(1)} %get-tuple-element.51.pad_ref, bf16[27,64,64]{2,1,0:T(8,128)(2,1)S(1)} %copy-done.3, s32[8,128]{1,0:T(8,128)S(1)} %get-tuple-element.53.lists_ref), custom_call_target="tpu_custom_call" | custom-call | flops 905969664 | bytes 1376256 | tf_op jit(solution)/shard_map/pallas_call | solution.py:50
  43.9 5.1 %all-to-all-done.1 = bf16[8,8,1408]{2,1,0:T(8,128)(2,1)S(1)} async-done(((bf16[8,8,1408]{2,1,0:T(8,128)(2,1)}), bf16[8,8,1408]{2,1,0:T(8,128)(2,1)S(1)}, u32[]{:S(2)}, u32[]{:S(2)}) %all-to-all-start.1) | async-done | bytes 180256 | tf_op jit(solution)/shard_map/all_to_all | solution.py:533
  49.0 0.2 shard_map.147
  49.2 0.0 copy-start.2
  49.2 12.5 %all_to_all.15 = bf16[8,8,2432]{2,1,0:T(8,128)(2,1)S(1)} all-to-all(bf16[8,8,2432]{2,1,0:T(8,128)(2,1)S(1)} %bitcast.29), channel_id=1, replica_groups=mesh['groups'=2,'x'=2,'core'=2,'gy'=4] {'x','gy'}, dimensions={0} | all-to-all | bytes 622592 | tf_op jit(solution)/shard_map/all_to_all | solution.py:533
  61.7 0.0 collective-permute-start.9
  61.7 1.6 %collective-permute-done.9.given_ref = bf16[64,2432]{1,0:T(8,128)(2,1)S(1)} collective-permute-done((bf16[64,2432]{1,0:T(8,128)(2,1)S(1)}, bf16[64,2432]{1,0:T(8,128)(2,1)S(1)}, u32[]{:S(2)}, u32[]{:S(2)}) %collective-permute-start.9) | collective-permute-done | bytes 311328 | tf_op jit(solution)/shard_map/ppermute | solution.py:522
  63.3 1.4 %shard_map.148 = (f32[27,64,64]{2,1,0:T(8,128)}, f32[512,128]{1,0:T(8,128)}, bf16[64,1024]{1,0:T(8,128)(2,1)}) custom-call(bf16[64,2432]{1,0:T(8,128)(2,1)S(1)} %bitcast.28, bf16[64,2432]{1,0:T(8,128)(2,1)S(1)} %collective-permute-done.9.given_ref, s32[4,16]{1,0:T(4,128)S(1)} %bitcast.36, s32[8,128]{1,0:T(8,128)S(1)} %get-tuple-element.37.lists_ref), custom_call_target="tpu_custom_call" | custom-call | bytes 1462528 | tf_op jit(solution)/shard_map/pallas_call | solution.py:50
  (8 shorter events, 0.0 us)
Async XLA Ops:
  0.6 9.3 %copy-start.3 = (bf16[27,64,64]{2,1,0:T(8,128)(2,1)S(1)}, bf16[27,64,64]{2,1,0:T(8,128)(2,1)}, u32[]{:S(2)}) copy-start(bf16[27,64,64]{2,1,0:T(8,128)(2,1)} %weight_ref.3) | copy-start | bytes 663556
  2.5 14.7 %all-to-all-start = ((bf16[16,8,512]{2,1,0:T(8,128)(2,1)}), bf16[16,8,512]{2,1,0:T(8,128)(2,1)S(1)}, u32[]{:S(2)}, u32[]{:S(2)}) async-start(bf16[16,8,512]{2,1,0:T(8,128)(2,1)} %bitcast.40), calls=%async_computation | async-start | bytes 262144 | tf_op jit(solution)/shard_map/all_to_all | solution.py:533
  9.9 0.7 %copy-start.6 = (s32[8,128]{1,0:T(8,128)S(1)}, s32[8,128]{1,0:T(8,128)}, u32[]{:S(2)}) copy-start(s32[8,128]{1,0:T(8,128)} %get-tuple-element.36.lists_ref) | copy-start | bytes 12292
  10.6 0.9 %copy-start.4 = (bf16[1,1,32,4096]{3,2,1,0:T(8,128)(2,1)S(1)}, bf16[1,1,32,4096]{3,2,1,0:T(8,128)(2,1)}, u32[]{:S(2)}) copy-start(bf16[1,1,32,4096]{3,2,1,0:T(8,128)(2,1)} %param.19) | copy-start | bytes 786436
  11.5 0.7 %copy-start.5 = (s32[1,1,32,27]{2,1,3,0:T(1,128)S(1)}, s32[1,1,32,27]{2,1,3,0:T(1,128)}, u32[]{:S(2)}) copy-start(s32[1,1,32,27]{2,1,3,0:T(1,128)} %param.14) | copy-start | bytes 10372
  12.2 5.0 %copy-start = (bf16[1,1,32,4096]{3,2,1,0:T(8,128)(2,1)S(1)}, bf16[1,1,32,4096]{3,2,1,0:T(8,128)(2,1)}, u32[]{:S(2)}) copy-start(bf16[1,1,32,4096]{3,2,1,0:T(8,128)(2,1)} %param.10) | copy-start | bytes 786436
  12.2 5.0 %copy-start.1 = (bf16[8,128,64]{1,2,0:T(8,128)(2,1)S(1)}, bf16[8,128,64]{1,2,0:T(8,128)(2,1)}, u32[]{:S(2)}) copy-start(bf16[8,128,64]{1,2,0:T(8,128)(2,1)} %param.13) | copy-start | bytes 393220
  14.2 3.6 %copy-start.7 = (bf16[9,32,128]{2,1,0:T(8,128)(2,1)}, bf16[9,32,128]{2,1,0:T(8,128)(2,1)S(1)}, u32[]{:S(2)}) copy-start(bf16[9,32,128]{2,1,0:T(8,128)(2,1)S(1)} %get-tuple-element.45.ends_ref) | copy-start | bytes 221188
  17.9 4.5 %collective-permute-start = (bf16[8,5120]{1,0:T(8,128)(2,1)S(1)}, bf16[8,5120]{1,0:T(8,128)(2,1)S(1)}, u32[]{:S(2)}, u32[]{:S(2)}) collective-permute-start(bf16[8,5120]{1,0:T(8,128)(2,1)S(1)} %get-tuple-element.39), channel_id=1, source_target_pairs={{0,1},{2,3},{1,0},{3,2},{4,5},{6,7},{5,4},{7,6},{8,9},{10,11},{9,8... | collective-permute-start | bytes 245768 | tf_op jit(solution)/shard_map/ppermute | solution.py:522
  18.6 3.8 %collective-permute-start.1 = (bf16[8,5120]{1,0:T(8,128)(2,1)S(1)}, bf16[8,5120]{1,0:T(8,128)(2,1)S(1)}, u32[]{:S(2)}, u32[]{:S(2)}) collective-permute-start(bf16[8,5120]{1,0:T(8,128)(2,1)S(1)} %get-tuple-element.40), channel_id=1, source_target_pairs={{1,2},{2,1},{5,6},{6,5},{9,10},{10,9},{13,14},{14,13},{17,18},{18,... | collective-permute-start | bytes 245768 | tf_op jit(solution)/shard_map/ppermute | solution.py:522
  19.3 6.5 %collective-permute-start.4 = (bf16[8,4096]{1,0:T(8,128)(2,1)S(1)}, bf16[8,4096]{1,0:T(8,128)(2,1)S(1)}, u32[]{:S(2)}, u32[]{:S(2)}) collective-permute-start(bf16[8,4096]{1,0:T(8,128)(2,1)S(1)} %get-tuple-element.46), channel_id=1, source_target_pairs={{4,8},{8,4},{5,9},{9,5},{6,10},{10,6},{7,11},{11,7},{20,24},{24,20... | collective-permute-start | bytes 196616 | tf_op jit(solution)/shard_map/ppermute | solution.py:522
  19.9 5.9 %collective-permute-start.5 = (bf16[8,4096]{1,0:T(8,128)(2,1)S(1)}, bf16[8,4096]{1,0:T(8,128)(2,1)S(1)}, u32[]{:S(2)}, u32[]{:S(2)}) collective-permute-start(bf16[8,4096]{1,0:T(8,128)(2,1)S(1)} %get-tuple-element.47), channel_id=1, source_target_pairs={{0,4},{8,12},{4,0},{12,8},{1,5},{9,13},{5,1},{13,9},{2,6},{10,14},... | collective-permute-start | bytes 196616 | tf_op jit(solution)/shard_map/ppermute | solution.py:522
  22.8 3.7 %collective-permute-start.2 = (bf16[8,4096]{1,0:T(8,128)(2,1)S(1)}, bf16[8,4096]{1,0:T(8,128)(2,1)S(1)}, u32[]{:S(2)}, u32[]{:S(2)}) collective-permute-start(bf16[8,4096]{1,0:T(8,128)(2,1)S(1)} %get-tuple-element.41), channel_id=1, source_target_pairs={{4,8},{8,4},{5,9},{9,5},{6,10},{10,6},{7,11},{11,7},{20,24},{24,20... | collective-permute-start | bytes 196616 | tf_op jit(solution)/shard_map/ppermute | solution.py:522
  23.4 3.3 %collective-permute-start.3 = (bf16[8,4096]{1,0:T(8,128)(2,1)S(1)}, bf16[8,4096]{1,0:T(8,128)(2,1)S(1)}, u32[]{:S(2)}, u32[]{:S(2)}) collective-permute-start(bf16[8,4096]{1,0:T(8,128)(2,1)S(1)} %get-tuple-element.42), channel_id=1, source_target_pairs={{0,4},{8,12},{4,0},{12,8},{1,5},{9,13},{5,1},{13,9},{2,6},{10,14},... | collective-permute-start | bytes 196616 | tf_op jit(solution)/shard_map/ppermute | solution.py:522
  25.8 0.9 %copy-start.8 = (bf16[9,32,128]{2,1,0:T(8,128)(2,1)S(1)}, bf16[9,32,128]{2,1,0:T(8,128)(2,1)}, u32[]{:S(2)}) copy-start(bf16[9,32,128]{2,1,0:T(8,128)(2,1)} %copy-done.7) | copy-start | bytes 221188
  28.1 6.6 %collective-permute-start.6 = (bf16[64,1408]{1,0:T(8,128)(2,1)S(1)}, bf16[64,1408]{1,0:T(8,128)(2,1)S(1)}, u32[]{:S(2)}, u32[]{:S(2)}) collective-permute-start(bf16[64,1408]{1,0:T(8,128)(2,1)S(1)} %get-tuple-element.52), channel_id=1, source_target_pairs={{0,4},{4,0},{1,5},{5,1},{2,6},{6,2},{3,7},{7,3},{8,12},{12,8},{9,1... | collective-permute-start | bytes 540680 | tf_op jit(solution)/shard_map/ppermute | solution.py:522
  29.4 11.2 %collective-permute-start.7 = (bf16[8,4096]{1,0:T(8,128)(2,1)S(1)}, bf16[8,4096]{1,0:T(8,128)(2,1)S(1)}, u32[]{:S(2)}, u32[]{:S(2)}) collective-permute-start(bf16[8,4096]{1,0:T(8,128)(2,1)S(1)} %get-tuple-element.56), channel_id=1, source_target_pairs={{0,1},{2,3},{1,0},{3,2},{4,5},{6,7},{5,4},{7,6},{8,9},{10,11},{9,8... | collective-permute-start | bytes 196616 | tf_op jit(solution)/shard_map/ppermute | solution.py:522
  33.1 7.5 %collective-permute-start.8 = (bf16[8,4096]{1,0:T(8,128)(2,1)S(1)}, bf16[8,4096]{1,0:T(8,128)(2,1)S(1)}, u32[]{:S(2)}, u32[]{:S(2)}) collective-permute-start(bf16[8,4096]{1,0:T(8,128)(2,1)S(1)} %get-tuple-element.57), channel_id=1, source_target_pairs={{1,2},{2,1},{5,6},{6,5},{9,10},{10,9},{13,14},{14,13},{17,18},{18,... | collective-permute-start | bytes 196616 | tf_op jit(solution)/shard_map/ppermute | solution.py:522
  35.4 13.6 %all-to-all-start.1 = ((bf16[8,8,1408]{2,1,0:T(8,128)(2,1)}), bf16[8,8,1408]{2,1,0:T(8,128)(2,1)S(1)}, u32[]{:S(2)}, u32[]{:S(2)}) async-start(bf16[8,8,1408]{2,1,0:T(8,128)(2,1)} %bitcast.17), calls=%async_computation.1 | async-start | bytes 360448 | tf_op jit(solution)/shard_map/all_to_all | solution.py:533
  49.2 14.1 %copy-start.2 = (s32[1,1,16,4]{2,3,1,0:T(4,128)S(1)}, s32[1,1,16,4]{2,3,1,0:T(4,128)}, u32[]{:S(2)}) copy-start(s32[1,1,16,4]{2,3,1,0:T(4,128)} %param.18) | copy-start | bytes 772
  61.7 1.6 %collective-permute-start.9 = (bf16[64,2432]{1,0:T(8,128)(2,1)S(1)}, bf16[64,2432]{1,0:T(8,128)(2,1)S(1)}, u32[]{:S(2)}, u32[]{:S(2)}) collective-permute-start(bf16[64,2432]{1,0:T(8,128)(2,1)S(1)} %bitcast.27), channel_id=1, source_target_pairs={{0,4},{4,0},{1,5},{5,1},{2,6},{6,2},{3,7},{7,3},{8,12},{12,8},{9,1... | collective-permute-start | bytes 933896 | tf_op jit(solution)/shard_map/ppermute | solution.py:522

commit v19 on v15

--- a/solution.py
+++ b/solution.py
@@ -45,17 +45,13 @@
     return jnp.sum(jnp.where(diagonal, spread, 0.0), axis=1, keepdims=True).astype(I32)
 
 
-def call(body, outs, *args, scratch=(), flops=0, in_hbm=False, results_in_hbm=0, aliases={}):
+def call(body, outs, *args, scratch=(), flops=0, in_hbm=False):
     moved = sum(a.size * a.dtype.itemsize for a in list(args) + list(outs))
-    in_place = [pltpu.HBM if in_hbm else pl.ANY if i in aliases else None for i in range(len(args))]
-    out_place = [pl.ANY if i < results_in_hbm else None for i in range(len(outs))]
     return pl.pallas_call(
         body,
         out_shape=tuple(outs),
-        in_specs=[pl.BlockSpec(memory_space=place) for place in in_place],
-        out_specs=tuple(pl.BlockSpec(memory_space=place) for place in out_place),
+        in_specs=[pl.BlockSpec(memory_space=pltpu.HBM) if in_hbm else pl.BlockSpec() for _ in args],
         scratch_shapes=tuple(scratch),
-        input_output_aliases=aliases,
         cost_estimate=pl.CostEstimate(flops=flops, bytes_accessed=moved, transcendentals=0),
         compiler_params=pltpu.CompilerParams(vmem_limit_bytes=None if in_hbm else 28 * 2**20),
     )(*args)
@@ -492,61 +488,42 @@
     return jnp.concatenate(totals, axis=1)
 
 
-def write_half(group, half, conv_hbm, up_hbm, conv_ref, up_ref, done, scale):
-    half_count, coarse = up_ref.shape[1:]
-    parts = up_ref.shape[0]
+def finish_half(half, conv_ref, up_ref, scale):
+    coarse = up_ref.shape[2]
     at = 0
-    copies = []
-    for q in range(parts):
+    for q in range(up_ref.shape[0]):
         up_ref[q] = half[:, at : at + coarse].astype(F32) * scale
         at += coarse
-        place = pl.ds(pl.multiple_of((2 * q + group) * half_count, half_count), half_count)
-        copies.append(pltpu.make_async_copy(up_ref.at[q], up_hbm.at[place], done.at[q]))
-        copies[-1].start()
     for pair in range(7):
         turned = half[:, at : at + 2 * C].astype(F32).T * scale
         at += 2 * C
         for s in range(2):
             conv_ref[2 * pair + s] = turned[s * C : (s + 1) * C]
-    copies.append(pltpu.make_async_copy(conv_ref.at[pl.ds(0, 13)], conv_hbm.at[pl.ds(14 * group, 13)], done.at[parts]))
-    copies[-1].start()
-    last = pltpu.make_async_copy(conv_ref.at[13], conv_hbm.at[13], done.at[parts + 1])
-
-    @pl.when(group == 0)
-    def _():
-        last.start()
-
-    return copies, last
-
-
-def end_half(group, copies, last):
-    for copy in copies:
-        copy.wait()
-
-    @pl.when(group == 0)
-    def _():
-        last.wait()
-
-
-def own_half_body(
-    back_ref, sends_ref, lists_ref, conv_hbm, up_hbm, part_ref, conv_ref, up_ref, done, item_lanes, across, scale
+
+
+def own_half_body(back_ref, sends_ref, lists_ref, conv_ref, up_ref, part_ref, item_lanes, across, scale):
+    finish_half(back_ref[:, 2 * item_lanes :], conv_ref, up_ref, scale)
+    part_ref[...] = coarse_part(back_ref[:, :item_lanes], sends_ref, lists_ref, 0, part_ref.shape, across)
+
+
+def last_body(
+    given_ref, own_conv_ref, own_up_ref, part_ref, sends_ref, lists_ref,
+    conv_ref, up_ref, out_ref, other_conv_ref, other_up_ref, item_lanes, across, scale,
 ):
-    group = lists_ref[5, GX]
-    started = write_half(group, back_ref[:, 2 * item_lanes :], conv_hbm, up_hbm, conv_ref, up_ref, done, scale)
-    part_ref[...] = coarse_part(back_ref[:, :item_lanes], sends_ref, lists_ref, 0, part_ref.shape, across)
-    end_half(group, *started)
-
-
-def other_half_body(
-    given_ref, part_ref, sends_ref, lists_ref, conv_in, up_in,
-    conv_hbm, up_hbm, out_ref, conv_ref, up_ref, done, item_lanes, across, scale,
-):
-    group = 1 - lists_ref[5, GX]
-    started = write_half(group, given_ref[:, 2 * item_lanes :], conv_hbm, up_hbm, conv_ref, up_ref, done, scale)
+    finish_half(given_ref[:, 2 * item_lanes :], other_conv_ref, other_up_ref, scale)
+    for o in range(14):
+        first, second = by_pair(lists_ref, GX, own_conv_ref[o], other_conv_ref[o])
+        conv_ref[o] = first
+        if o < 13:
+            conv_ref[14 + o] = second
+    half_count = own_up_ref.shape[1]
+    for q in range(own_up_ref.shape[0]):
+        first, second = by_pair(lists_ref, GX, own_up_ref[q], other_up_ref[q])
+        up_ref[2 * q * half_count : (2 * q + 1) * half_count] = first
+        up_ref[(2 * q + 1) * half_count : (2 * q + 2) * half_count] = second
     came = given_ref[:, item_lanes : 2 * item_lanes]
     other = coarse_part(came, sends_ref, lists_ref, 1, out_ref.shape, across)
     out_ref[...] = (part_ref[...] + other).astype(BF)
-    end_half(group, *started)
 
 
 def swap(value, axis, first):
@@ -654,22 +631,17 @@
     back = trade_rows(back, ("x", "gy"))
     given = swap(back, "core", 0)
     scale = 1.0 / math.sqrt(64 * bricks * devices)
-    results = [shape((27, C, C), F32), shape((8 * C, coarse), F32)]
-    halves = dict(
-        scratch=[
-            pltpu.VMEM((14, C, C), F32), pltpu.VMEM((8 * C // count, count // 2, coarse), F32),
-            pltpu.SemaphoreType.DMA((8 * C // count + 2,)),
-        ],
-        results_in_hbm=2,
-    )
     sizes = dict(item_lanes=item_lanes, across=across, scale=scale)
-    grad_conv, grad_up, part = call(
-        functools.partial(own_half_body, **sizes), results + [shape((item_count, item_width), F32)],
-        back, sends, lists, **halves,
+    half_conv, half_up = ((14, C, C), (8 * C // count, count // 2, coarse))
+    own_conv, own_up, part = call(
+        functools.partial(own_half_body, **sizes),
+        [shape(half_conv, F32), shape(half_up, F32), shape((item_count, item_width), F32)], back, sends, lists,
     )
     grad_conv, grad_up, coarse_grad = call(
-        functools.partial(other_half_body, **sizes), results + [shape((item_count, item_width))],
-        given, part, sends, lists, grad_conv, grad_up, aliases={4: 0, 5: 1}, **halves,
+        functools.partial(last_body, **sizes),
+        [shape((27, C, C), F32), shape((8 * C, coarse), F32), shape((item_count, item_width))],
+        given, own_conv, own_up, part, sends, lists,
+        scratch=[pltpu.VMEM(half_conv, F32), pltpu.VMEM(half_up, F32)],
     )
     return (
         output.reshape(1, 1, bricks, width),

time: 65 us -> 64.6 us (level)
  Pallas kernels: 14.8 us -> 13.7 us
  waiting for transfers between devices: 9.25 us -> 10 us
    pallas_call x13, Pallas kernels: 14.8 us -> 13.7 us  [call(): pl.pallas_call(body, out_shape=tuple(outs), in_specs=[pl.BlockSpec(memory...]
    ppermute x10, waiting for transfers between devices: 3.85 us -> 4.64 us  [swap(): lax.ppermute(value, axis, [(i, i + 1) for i in lower] + [(i + 1, i) for i...]
  transfers between devices with their start and end apart: 12 -> 12, of which waited for: 7 -> 7; matrix products, arithmetic and copies ran while one was open for 0% -> 0% of each run, Pallas kernels for 13% -> 12%
where the time goes in v19:
time: 64.6 us; the launch traced here: 64.1 us
  starting transfers between devices  23 us (36%)
  blocking collectives  14.1 us (22%)
  Pallas kernels  13.7 us (21%)
  waiting for transfers between devices  10 us (15%)
  local copies, waits for them, and re-layouts  2.34 us (4%)
  between operations  0.81 us (1%)
    all_to_all x1, blocking collectives, trade_rows(): lax.all_to_all(grid_view, axes, split_axis=0, concat_axis=0, tiled=True)  14.1 us
    all_to_all x2, starting transfers between devices, trade_rows(): lax.all_to_all(grid_view, axes, split_axis=0, concat_axis=0, tiled=True)  13.9 us
    pallas_call x13, Pallas kernels, call(): pl.pallas_call(body, out_shape=tuple(outs), in_specs=[pl.BlockSpec(memory...  13.7 us
    ppermute x10, starting transfers between devices, swap(): lax.ppermute(value, axis, [(i, i + 1) for i in lower] + [(i + 1, i) for i...  9.1 us
    all_to_all x2, waiting for transfers between devices, trade_rows(): lax.all_to_all(grid_view, axes, split_axis=0, concat_axis=0, tiled=True)  5.4 us
    ppermute x10, waiting for transfers between devices, swap(): lax.ppermute(value, axis, [(i, i + 1) for i in lower] + [(i + 1, i) for i...  4.64 us
    unnamed x14, local copies, waits for them, and re-layouts  2.34 us
  transfers between devices with their start and end apart: 12, of which 7 were waited for; matrix products, arithmetic and copies ran while one was open for 0% of the time, Pallas kernels for 12%

profile of v19, /device:TPU:0, one launch (start us, length us, event | category | flops | bytes accessed | tf_op | source)
XLA Modules:
  0.0 64.1 jit_solution(15046449697876891442)
XLA Ops:
  0.6 0.0 copy-start.3
  0.6 1.9 %shard_map.137 = (bf16[128,512]{1,0:T(8,128)(2,1)}, s32[8,128]{1,0:T(8,128)}) custom-call(s32[4,16]{1,0:T(4,128)} %bitcast.35, bf16[64,1024]{1,0:T(8,128)(2,1)} %bitcast.40, s32[2,8]{1,0:T(2,128)} %bitcast.42, s32[2,8]{1,0:T(2,128)} %bitcast.43, s32[1,32]{1,0:T(1,128)} %bitcast.44), custom_call_target="tpu_custom_call" | custom-call | bytes 266752 | tf_op jit(solution)/shard_map/pallas_call | solution.py:50
  2.5 7.4 %all-to-all-start = ((bf16[16,8,512]{2,1,0:T(8,128)(2,1)}), bf16[16,8,512]{2,1,0:T(8,128)(2,1)S(1)}, u32[]{:S(2)}, u32[]{:S(2)}) async-start(bf16[16,8,512]{2,1,0:T(8,128)(2,1)} %bitcast.41), calls=%async_computation | async-start | bytes 262144 | tf_op jit(solution)/shard_map/all_to_all | solution.py:543
  9.9 0.0 copy-start.6
  9.9 0.0 copy-done.3
  9.9 0.7 %copy-done.6 = s32[8,128]{1,0:T(8,128)S(1)} copy-done((s32[8,128]{1,0:T(8,128)S(1)}, s32[8,128]{1,0:T(8,128)}, u32[]{:S(2)}) %copy-start.6) | copy-done | bytes 4120
  10.6 0.9 %copy-done.4 = bf16[1,1,32,4096]{3,2,1,0:T(8,128)(2,1)S(1)} copy-done((bf16[1,1,32,4096]{3,2,1,0:T(8,128)(2,1)S(1)}, bf16[1,1,32,4096]{3,2,1,0:T(8,128)(2,1)}, u32[]{:S(2)}) %copy-start.4) | copy-done | bytes 262168
  11.5 0.7 %copy-done.5 = s32[1,1,32,27]{2,1,3,0:T(1,128)S(1)} copy-done((s32[1,1,32,27]{2,1,3,0:T(1,128)S(1)}, s32[1,1,32,27]{2,1,3,0:T(1,128)}, u32[]{:S(2)}) %copy-start.5) | copy-done | bytes 3480
  12.2 2.0 %shard_map.138 = (f32[48,4096]{1,0:T(8,128)S(1)}, bf16[8,4096]{1,0:T(8,128)(2,1)S(1)}, bf16[8,4096]{1,0:T(8,128)(2,1)S(1)}, bf16[256,512]{1,0:T(8,128)(2,1)S(1)}...) custom-call(bf16[32,4096]{1,0:T(8,128)(2,1)S(1)} %bitcast.38, ...), custom_call_target="tpu_custom_call" | custom-call | flops 1811939328 | bytes 1785728 | tf_op jit(solution)/shard_map/pallas_call | solution.py:50
  14.2 3.0 %all-to-all-done = bf16[16,8,512]{2,1,0:T(8,128)(2,1)S(1)} async-done(((bf16[16,8,512]{2,1,0:T(8,128)(2,1)}), bf16[16,8,512]{2,1,0:T(8,128)(2,1)S(1)}, u32[]{:S(2)}, u32[]{:S(2)}) %all-to-all-start) | async-done | bytes 131104 | tf_op jit(solution)/shard_map/all_to_all | solution.py:543
  17.2 0.0 copy-done
  17.2 0.0 copy-done.1
  17.2 0.6 shard_map.139
  17.9 0.7 %collective-permute-start = (bf16[8,5120]{1,0:T(8,128)(2,1)S(1)}, bf16[8,5120]{1,0:T(8,128)(2,1)S(1)}, u32[]{:S(2)}, u32[]{:S(2)}) collective-permute-start(bf16[8,5120]{1,0:T(8,128)(2,1)S(1)} %get-tuple-element.40), channel_id=1, source_target_pairs={{0,1},{2,3},{1,0},{3,2},{4,5},{6,7},{5,4},{7,6},{8,9},{10,11},{9,8... | collective-permute-start | bytes 245768 | tf_op jit(solution)/shard_map/ppermute | solution.py:532
  18.6 0.7 %collective-permute-start.1 = (bf16[8,5120]{1,0:T(8,128)(2,1)S(1)}, bf16[8,5120]{1,0:T(8,128)(2,1)S(1)}, u32[]{:S(2)}, u32[]{:S(2)}) collective-permute-start(bf16[8,5120]{1,0:T(8,128)(2,1)S(1)} %get-tuple-element.41), channel_id=1, source_target_pairs={{1,2},{2,1},{5,6},{6,5},{9,10},{10,9},{13,14},{14,13},{17,18},{18,... | collective-permute-start | bytes 245768 | tf_op jit(solution)/shard_map/ppermute | solution.py:532
  19.2 0.1 collective-permute-start.4
  19.3 0.7 %collective-permute-start.5 = (bf16[8,4096]{1,0:T(8,128)(2,1)S(1)}, bf16[8,4096]{1,0:T(8,128)(2,1)S(1)}, u32[]{:S(2)}, u32[]{:S(2)}) collective-permute-start(bf16[8,4096]{1,0:T(8,128)(2,1)S(1)} %get-tuple-element.49), channel_id=1, source_target_pairs={{4,8},{8,4},{5,9},{9,5},{6,10},{10,6},{7,11},{11,7},{20,24},{24,20... | collective-permute-start | bytes 196616 | tf_op jit(solution)/shard_map/ppermute | solution.py:532
  20.0 2.4 %collective-permute-done.even_ref.even_side_ref = bf16[8,5120]{1,0:T(8,128)(2,1)S(1)} collective-permute-done((bf16[8,5120]{1,0:T(8,128)(2,1)S(1)}, bf16[8,5120]{1,0:T(8,128)(2,1)S(1)}, u32[]{:S(2)}, u32[]{:S(2)}) %collective-permute-start) | collective-permute-done | bytes 81952 | tf_op jit(solution)/shard_map/ppermute | solution.py:532
  22.4 0.0 collective-permute-done.1.odd_ref.odd_side_ref
  22.4 0.3 shard_map.140
  22.7 0.7 %collective-permute-start.2 = (bf16[8,4096]{1,0:T(8,128)(2,1)S(1)}, bf16[8,4096]{1,0:T(8,128)(2,1)S(1)}, u32[]{:S(2)}, u32[]{:S(2)}) collective-permute-start(bf16[8,4096]{1,0:T(8,128)(2,1)S(1)} %get-tuple-element.42), channel_id=1, source_target_pairs={{4,8},{8,4},{5,9},{9,5},{6,10},{10,6},{7,11},{11,7},{20,24},{24,20... | collective-permute-start | bytes 196616 | tf_op jit(solution)/shard_map/ppermute | solution.py:532
  23.4 2.4 %collective-permute-start.3 = (bf16[8,4096]{1,0:T(8,128)(2,1)S(1)}, bf16[8,4096]{1,0:T(8,128)(2,1)S(1)}, u32[]{:S(2)}, u32[]{:S(2)}) collective-permute-start(bf16[8,4096]{1,0:T(8,128)(2,1)S(1)} %get-tuple-element.43), channel_id=1, source_target_pairs={{0,4},{8,12},{4,0},{12,8},{1,5},{9,13},{5,1},{13,9},{2,6},{10,14},... | collective-permute-start | bytes 196616 | tf_op jit(solution)/shard_map/ppermute | solution.py:532
  25.8 0.0 collective-permute-done.4.even_grad_ref
  25.8 0.0 collective-permute-done.5.odd_grad_ref
  25.8 0.6 shard_map.141
  26.4 0.0 collective-permute-done.2.odd_cross_ref
  26.4 0.3 collective-permute-done.3.even_cross_ref
  26.7 1.4 %shard_map.142 = (bf16[64,1408]{1,0:T(8,128)(2,1)S(1)}, bf16[6,6,32,384]{3,2,1,0:T(8,128)(2,1)S(1)}) custom-call(bf16[8,4096]{1,0:T(8,128)(2,1)S(1)} %collective-permute-done.2.odd_cross_ref, bf16[8,4096]{1,0:T(8,128)(2,1)S(1)} %collective-permute-done.3.even_cross_ref, bf16[32,4096]{1,0:T(8,128)(2,1)S(1)} %get-tuple-element.39.merged_ref, ...), custom_call_target="tpu_custom_call" | custom-call | flops 905969664 | bytes 2260992 | tf_op jit(solution)/shard_map/pallas_call | solution.py:50
  28.1 1.2 %collective-permute-start.8 = (bf16[64,1408]{1,0:T(8,128)(2,1)S(1)}, bf16[64,1408]{1,0:T(8,128)(2,1)S(1)}, u32[]{:S(2)}, u32[]{:S(2)}) collective-permute-start(bf16[64,1408]{1,0:T(8,128)(2,1)S(1)} %get-tuple-element.59), channel_id=1, source_target_pairs={{0,4},{4,0},{1,5},{5,1},{2,6},{6,2},{3,7},{7,3},{8,12},{12,8},{9,1... | collective-permute-start | bytes 540680 | tf_op jit(solution)/shard_map/ppermute | solution.py:532
  29.4 0.9 %shard_map.145.kept_ref = f32[64,1408]{1,0:T(8,128)S(1)} custom-call(bf16[6,6,32,384]{3,2,1,0:T(8,128)(2,1)S(1)} %get-tuple-element.52.pad_ref, bf16[256,512]{1,0:T(8,128)(2,1)S(1)} %get-tuple-element.44.turned_ref, f32[128,512]{1,0:T(8,128)S(1)} %get-tuple-element.51.up_sums_ref, s32[8,128]{1,0:T(8,128)S(1)} %get-tuple-element.38.lists_ref), custom_call_target="tpu_custom_call" | custom-call | flops 905969664 | bytes 1773568 | tf_op jit(solution)/shard_map/pallas_call | solution.py:50
  30.3 0.1 collective-permute-done.8.given_ref
  30.4 0.7 %shard_map.146 = bf16[64,1408]{1,0:T(8,128)(2,1)} custom-call(f32[64,1408]{1,0:T(8,128)S(1)} %shard_map.145.kept_ref, bf16[64,1408]{1,0:T(8,128)(2,1)S(1)} %collective-permute-done.8.given_ref), custom_call_target="tpu_custom_call" | custom-call | bytes 720896 | tf_op jit(solution)/shard_map/pallas_call | solution.py:50
  31.1 6.6 %all-to-all-start.1 = ((bf16[8,8,1408]{2,1,0:T(8,128)(2,1)}), bf16[8,8,1408]{2,1,0:T(8,128)(2,1)S(1)}, u32[]{:S(2)}, u32[]{:S(2)}) async-start(bf16[8,8,1408]{2,1,0:T(8,128)(2,1)} %bitcast.17), calls=%async_computation.1 | async-start | bytes 360448 | tf_op jit(solution)/shard_map/all_to_all | solution.py:543
  37.7 2.0 %collective-permute-start.6 = (bf16[8,4096]{1,0:T(8,128)(2,1)S(1)}, bf16[8,4096]{1,0:T(8,128)(2,1)S(1)}, u32[]{:S(2)}, u32[]{:S(2)}) collective-permute-start(bf16[8,4096]{1,0:T(8,128)(2,1)S(1)} %get-tuple-element.56), channel_id=1, source_target_pairs={{0,1},{2,3},{1,0},{3,2},{4,5},{6,7},{5,4},{7,6},{8,9},{10,11},{9,8... | collective-permute-start | bytes 196616 | tf_op jit(solution)/shard_map/ppermute | solution.py:532
  39.7 0.7 %collective-permute-start.7 = (bf16[8,4096]{1,0:T(8,128)(2,1)S(1)}, bf16[8,4096]{1,0:T(8,128)(2,1)S(1)}, u32[]{:S(2)}, u32[]{:S(2)}) collective-permute-start(bf16[8,4096]{1,0:T(8,128)(2,1)S(1)} %get-tuple-element.57), channel_id=1, source_target_pairs={{1,2},{2,1},{5,6},{6,5},{9,10},{10,9},{13,14},{14,13},{17,18},{18,... | collective-permute-start | bytes 196616 | tf_op jit(solution)/shard_map/ppermute | solution.py:532
  40.4 2.2 %shard_map.143 = (bf16[32,4096]{1,0:T(8,128)(2,1)}, s32[8,128]{1,0:T(8,128)S(1)}) custom-call(bf16[6,6,32,384]{3,2,1,0:T(8,128)(2,1)S(1)} %get-tuple-element.52.pad_ref, bf16[27,64,64]{2,1,0:T(8,128)(2,1)S(1)} %copy-done.3, s32[8,128]{1,0:T(8,128)S(1)} %get-tuple-element.38.lists_ref), custom_call_target="tpu_custom_call" | custom-call | flops 905969664 | bytes 1376256 | tf_op jit(solution)/shard_map/pallas_call | solution.py:50
  42.6 0.6 collective-permute-done.6.even_ref
  43.2 0.0 collective-permute-done.7.odd_ref
  43.2 1.1 %shard_map.144 = (bf16[32,4096]{1,0:T(8,128)(2,1)}, bf16[64,1024]{1,0:T(8,128)(2,1)S(1)}) custom-call(f32[32,4096]{1,0:T(8,128)S(1)} %get-tuple-element.54.part_ref, s32[8,128]{1,0:T(8,128)S(1)} %get-tuple-element.55.lists_ref, bf16[8,4096]{1,0:T(8,128)(2,1)S(1)} %collective-permute-done.6.even_ref, bf16[8,4096]{1,0:T(8,128)(2,1)S(1)} %collective-permute-done.7.odd_ref, ...), custom_call_target="tpu_custom_call" | custom-call | bytes 1183744 | tf_op jit(solution)/shard_map/pallas_call | solution.py:50
  44.3 2.4 %all-to-all-done.1 = bf16[8,8,1408]{2,1,0:T(8,128)(2,1)S(1)} async-done(((bf16[8,8,1408]{2,1,0:T(8,128)(2,1)}), bf16[8,8,1408]{2,1,0:T(8,128)(2,1)S(1)}, u32[]{:S(2)}, u32[]{:S(2)}) %all-to-all-start.1) | async-done | bytes 180256 | tf_op jit(solution)/shard_map/all_to_all | solution.py:543
  46.7 0.2 shard_map.147
  46.9 0.0 copy-start.2
  46.9 14.1 %all_to_all.15 = bf16[8,8,2432]{2,1,0:T(8,128)(2,1)S(1)} all-to-all(bf16[8,8,2432]{2,1,0:T(8,128)(2,1)S(1)} %bitcast.29), channel_id=1, replica_groups=mesh['groups'=2,'x'=2,'core'=2,'gy'=4] {'x','gy'}, dimensions={0} | all-to-all | bytes 622592 | tf_op jit(solution)/shard_map/all_to_all | solution.py:543
  61.1 0.0 collective-permute-start.9
  61.1 0.0 copy-done.2
  61.1 0.4 shard_map.148
  61.4 1.2 %collective-permute-done.9.given_ref = bf16[64,2432]{1,0:T(8,128)(2,1)S(1)} collective-permute-done((bf16[64,2432]{1,0:T(8,128)(2,1)S(1)}, bf16[64,2432]{1,0:T(8,128)(2,1)S(1)}, u32[]{:S(2)}, u32[]{:S(2)}) %collective-permute-start.9) | collective-permute-done | bytes 311328 | tf_op jit(solution)/shard_map/ppermute | solution.py:532
  62.7 1.4 %shard_map.149 = (f32[27,64,64]{2,1,0:T(8,128)}, f32[512,128]{1,0:T(8,128)}, bf16[64,1024]{1,0:T(8,128)(2,1)}) custom-call(bf16[64,2432]{1,0:T(8,128)(2,1)S(1)} %collective-permute-done.9.given_ref, f32[14,64,64]{2,1,0:T(8,128)S(1)} %get-tuple-element.61.own_conv_ref, f32[4,64,128]{2,1,0:T(8,128)S(1)} %get-tuple-element.62.own_up_ref, ...), custom_call_target="tpu_custom_call" | custom-call | bytes 1773824 | tf_op jit(solution)/shard_map/pallas_call | solution.py:50
  (5 shorter events, 0.0 us)
Async XLA Ops:
  0.6 9.3 %copy-start.3 = (bf16[27,64,64]{2,1,0:T(8,128)(2,1)S(1)}, bf16[27,64,64]{2,1,0:T(8,128)(2,1)}, u32[]{:S(2)}) copy-start(bf16[27,64,64]{2,1,0:T(8,128)(2,1)} %weight_ref.3) | copy-start | bytes 663556
  2.5 14.7 %all-to-all-start = ((bf16[16,8,512]{2,1,0:T(8,128)(2,1)}), bf16[16,8,512]{2,1,0:T(8,128)(2,1)S(1)}, u32[]{:S(2)}, u32[]{:S(2)}) async-start(bf16[16,8,512]{2,1,0:T(8,128)(2,1)} %bitcast.41), calls=%async_computation | async-start | bytes 262144 | tf_op jit(solution)/shard_map/all_to_all | solution.py:543
  9.9 0.7 %copy-start.6 = (s32[8,128]{1,0:T(8,128)S(1)}, s32[8,128]{1,0:T(8,128)}, u32[]{:S(2)}) copy-start(s32[8,128]{1,0:T(8,128)} %get-tuple-element.37.lists_ref) | copy-start | bytes 12292
  10.6 0.9 %copy-start.4 = (bf16[1,1,32,4096]{3,2,1,0:T(8,128)(2,1)S(1)}, bf16[1,1,32,4096]{3,2,1,0:T(8,128)(2,1)}, u32[]{:S(2)}) copy-start(bf16[1,1,32,4096]{3,2,1,0:T(8,128)(2,1)} %param.19) | copy-start | bytes 786436
  11.5 0.7 %copy-start.5 = (s32[1,1,32,27]{2,1,3,0:T(1,128)S(1)}, s32[1,1,32,27]{2,1,3,0:T(1,128)}, u32[]{:S(2)}) copy-start(s32[1,1,32,27]{2,1,3,0:T(1,128)} %param.14) | copy-start | bytes 10372
  12.2 5.0 %copy-start = (bf16[8,128,64]{1,2,0:T(8,128)(2,1)S(1)}, bf16[8,128,64]{1,2,0:T(8,128)(2,1)}, u32[]{:S(2)}) copy-start(bf16[8,128,64]{1,2,0:T(8,128)(2,1)} %param.13) | copy-start | bytes 393220
  12.2 5.0 %copy-start.1 = (bf16[1,1,32,4096]{3,2,1,0:T(8,128)(2,1)S(1)}, bf16[1,1,32,4096]{3,2,1,0:T(8,128)(2,1)}, u32[]{:S(2)}) copy-start(bf16[1,1,32,4096]{3,2,1,0:T(8,128)(2,1)} %param.10) | copy-start | bytes 786436
  17.9 4.5 %collective-permute-start = (bf16[8,5120]{1,0:T(8,128)(2,1)S(1)}, bf16[8,5120]{1,0:T(8,128)(2,1)S(1)}, u32[]{:S(2)}, u32[]{:S(2)}) collective-permute-start(bf16[8,5120]{1,0:T(8,128)(2,1)S(1)} %get-tuple-element.40), channel_id=1, source_target_pairs={{0,1},{2,3},{1,0},{3,2},{4,5},{6,7},{5,4},{7,6},{8,9},{10,11},{9,8... | collective-permute-start | bytes 245768 | tf_op jit(solution)/shard_map/ppermute | solution.py:532
  18.6 3.8 %collective-permute-start.1 = (bf16[8,5120]{1,0:T(8,128)(2,1)S(1)}, bf16[8,5120]{1,0:T(8,128)(2,1)S(1)}, u32[]{:S(2)}, u32[]{:S(2)}) collective-permute-start(bf16[8,5120]{1,0:T(8,128)(2,1)S(1)} %get-tuple-element.41), channel_id=1, source_target_pairs={{1,2},{2,1},{5,6},{6,5},{9,10},{10,9},{13,14},{14,13},{17,18},{18,... | collective-permute-start | bytes 245768 | tf_op jit(solution)/shard_map/ppermute | solution.py:532
  19.2 6.6 %collective-permute-start.4 = (bf16[8,4096]{1,0:T(8,128)(2,1)S(1)}, bf16[8,4096]{1,0:T(8,128)(2,1)S(1)}, u32[]{:S(2)}, u32[]{:S(2)}) collective-permute-start(bf16[8,4096]{1,0:T(8,128)(2,1)S(1)} %get-tuple-element.48), channel_id=1, source_target_pairs={{0,4},{8,12},{4,0},{12,8},{1,5},{9,13},{5,1},{13,9},{2,6},{10,14},... | collective-permute-start | bytes 196616 | tf_op jit(solution)/shard_map/ppermute | solution.py:532
  19.3 6.5 %collective-permute-start.5 = (bf16[8,4096]{1,0:T(8,128)(2,1)S(1)}, bf16[8,4096]{1,0:T(8,128)(2,1)S(1)}, u32[]{:S(2)}, u32[]{:S(2)}) collective-permute-start(bf16[8,4096]{1,0:T(8,128)(2,1)S(1)} %get-tuple-element.49), channel_id=1, source_target_pairs={{4,8},{8,4},{5,9},{9,5},{6,10},{10,6},{7,11},{11,7},{20,24},{24,20... | collective-permute-start | bytes 196616 | tf_op jit(solution)/shard_map/ppermute | solution.py:532
  22.7 3.7 %collective-permute-start.2 = (bf16[8,4096]{1,0:T(8,128)(2,1)S(1)}, bf16[8,4096]{1,0:T(8,128)(2,1)S(1)}, u32[]{:S(2)}, u32[]{:S(2)}) collective-permute-start(bf16[8,4096]{1,0:T(8,128)(2,1)S(1)} %get-tuple-element.42), channel_id=1, source_target_pairs={{4,8},{8,4},{5,9},{9,5},{6,10},{10,6},{7,11},{11,7},{20,24},{24,20... | collective-permute-start | bytes 196616 | tf_op jit(solution)/shard_map/ppermute | solution.py:532
  23.4 3.3 %collective-permute-start.3 = (bf16[8,4096]{1,0:T(8,128)(2,1)S(1)}, bf16[8,4096]{1,0:T(8,128)(2,1)S(1)}, u32[]{:S(2)}, u32[]{:S(2)}) collective-permute-start(bf16[8,4096]{1,0:T(8,128)(2,1)S(1)} %get-tuple-element.43), channel_id=1, source_target_pairs={{0,4},{8,12},{4,0},{12,8},{1,5},{9,13},{5,1},{13,9},{2,6},{10,14},... | collective-permute-start | bytes 196616 | tf_op jit(solution)/shard_map/ppermute | solution.py:532
  28.1 2.3 %collective-permute-start.8 = (bf16[64,1408]{1,0:T(8,128)(2,1)S(1)}, bf16[64,1408]{1,0:T(8,128)(2,1)S(1)}, u32[]{:S(2)}, u32[]{:S(2)}) collective-permute-start(bf16[64,1408]{1,0:T(8,128)(2,1)S(1)} %get-tuple-element.59), channel_id=1, source_target_pairs={{0,4},{4,0},{1,5},{5,1},{2,6},{6,2},{3,7},{7,3},{8,12},{12,8},{9,1... | collective-permute-start | bytes 540680 | tf_op jit(solution)/shard_map/ppermute | solution.py:532
  31.1 15.6 %all-to-all-start.1 = ((bf16[8,8,1408]{2,1,0:T(8,128)(2,1)}), bf16[8,8,1408]{2,1,0:T(8,128)(2,1)S(1)}, u32[]{:S(2)}, u32[]{:S(2)}) async-start(bf16[8,8,1408]{2,1,0:T(8,128)(2,1)} %bitcast.17), calls=%async_computation.1 | async-start | bytes 360448 | tf_op jit(solution)/shard_map/all_to_all | solution.py:543
  37.7 5.5 %collective-permute-start.6 = (bf16[8,4096]{1,0:T(8,128)(2,1)S(1)}, bf16[8,4096]{1,0:T(8,128)(2,1)S(1)}, u32[]{:S(2)}, u32[]{:S(2)}) collective-permute-start(bf16[8,4096]{1,0:T(8,128)(2,1)S(1)} %get-tuple-element.56), channel_id=1, source_target_pairs={{0,1},{2,3},{1,0},{3,2},{4,5},{6,7},{5,4},{7,6},{8,9},{10,11},{9,8... | collective-permute-start | bytes 196616 | tf_op jit(solution)/shard_map/ppermute | solution.py:532
  39.7 3.5 %collective-permute-start.7 = (bf16[8,4096]{1,0:T(8,128)(2,1)S(1)}, bf16[8,4096]{1,0:T(8,128)(2,1)S(1)}, u32[]{:S(2)}, u32[]{:S(2)}) collective-permute-start(bf16[8,4096]{1,0:T(8,128)(2,1)S(1)} %get-tuple-element.57), channel_id=1, source_target_pairs={{1,2},{2,1},{5,6},{6,5},{9,10},{10,9},{13,14},{14,13},{17,18},{18,... | collective-permute-start | bytes 196616 | tf_op jit(solution)/shard_map/ppermute | solution.py:532
  46.9 14.2 %copy-start.2 = (s32[1,1,16,4]{2,3,1,0:T(4,128)S(1)}, s32[1,1,16,4]{2,3,1,0:T(4,128)}, u32[]{:S(2)}) copy-start(s32[1,1,16,4]{2,3,1,0:T(4,128)} %param.18) | copy-start | bytes 772
  61.1 1.6 %collective-permute-start.9 = (bf16[64,2432]{1,0:T(8,128)(2,1)S(1)}, bf16[64,2432]{1,0:T(8,128)(2,1)S(1)}, u32[]{:S(2)}, u32[]{:S(2)}) collective-permute-start(bf16[64,2432]{1,0:T(8,128)(2,1)S(1)} %bitcast.27), channel_id=1, source_target_pairs={{0,4},{4,0},{1,5},{5,1},{2,6},{6,2},{3,7},{7,3},{8,12},{12,8},{9,1... | collective-permute-start | bytes 933896 | tf_op jit(solution)/shard_map/ppermute | solution.py:532

commit v20 on v16

--- a/solution.py
+++ b/solution.py
@@ -292,7 +292,7 @@
 
 def side_grad_body(
     ext_ref, lists_ref, even_grad_ref, odd_grad_ref, even_side_ref, odd_side_ref, parents_ref,
-    part_ref, to_even_ref, to_odd_ref, up_sums_ref,
+    conv_given_ref, part_ref, to_even_ref, to_odd_ref, up_kept_ref, given_ref, up_sums_ref,
 ):
     bricks, width = part_ref.shape
     face = to_even_ref.shape[0]
@@ -312,11 +312,16 @@
     count = up_sums_ref.shape[0]
     for q in range(up_sum.shape[0] // count):
         up_sums_ref[:, q * coarse : (q + 1) * coarse] = up_sum[q * count : (q + 1) * count]
+    kept, given = by_pair(lists_ref, GX, up_sums_ref[: count // 2], up_sums_ref[count // 2 :])
+    up_kept_ref[...] = kept
+    up_lanes = kept.shape[1]
+    given_ref[:, :up_lanes] = given.astype(BF)
+    given_ref[:, up_lanes:] = conv_given_ref[...]
 
 
 def given_sums_body(
     odd_cross_ref, even_cross_ref, merged_ref, even_side_ref, odd_side_ref, turned_ref, mains_ref, ends_ref, lists_ref,
-    up_sums_ref, given_ref, pad_ref, table_ref,
+    given_ref, pad_ref, table_ref,
 ):
     bricks, width = merged_ref.shape
     face = even_side_ref.shape[0]
@@ -346,15 +351,11 @@
                 for i, (X, Y, _, _) in enumerate(moved):
                     pad_ref[X, Y, :, :RUN] = got[i * bricks : (i + 1) * bricks]
 
-    half_sums(1 - lists_ref[5, GX], pad_ref, turned_ref, up_sums_ref, given_ref)
-
-
-def half_sums(group, pad_ref, turned_ref, up_sums_ref, out_ref):
+    half_sums(1 - lists_ref[5, GX], pad_ref, turned_ref, given_ref, 0)
+
+
+def half_sums(group, pad_ref, turned_ref, out_ref, start):
     turned = turned_ref[...]
-    half_count = out_ref.shape[0]
-    up_lanes = up_sums_ref.shape[1]
-    up_half = jnp.where(group == 0, up_sums_ref[:half_count], up_sums_ref[half_count:])
-    out_ref[:, :up_lanes] = up_half.astype(out_ref.dtype)
     bricks = pad_ref.shape[2]
     lanes_low = iota((C, 2 * C), 1) < C
     sums = []
@@ -373,12 +374,14 @@
     sums.append(jnp.zeros((C, 2 * C), F32))
     pairs = [jnp.where(lanes_low, sums[2 * k], sums[2 * k + 1]) for k in range(8)]
     for p in range(7):
-        at = up_lanes + p * 2 * C
+        at = start + p * 2 * C
         out_ref[:, at : at + 2 * C] = jnp.where(group == 0, pairs[p], pairs[p + 1]).astype(out_ref.dtype)
 
 
-def kept_sums_body(pad_ref, turned_ref, up_sums_ref, lists_ref, kept_ref):
-    half_sums(lists_ref[5, GX], pad_ref, turned_ref, up_sums_ref, kept_ref)
+def kept_sums_body(pad_ref, turned_ref, up_kept_ref, lists_ref, kept_ref):
+    up_lanes = up_kept_ref.shape[1]
+    kept_ref[:, :up_lanes] = up_kept_ref[...]
+    half_sums(lists_ref[5, GX], pad_ref, turned_ref, kept_ref, up_lanes)
 
 
 def pair_sum_body(kept_ref, given_ref, out_ref):
@@ -592,18 +595,23 @@
     to_even, to_odd = call(cross_body, [face_rows, face_rows], merged, *sides, lists)
     crosses = swap_pairs(to_even, to_odd, GX_AXES)
     half_sums_dims = (count // 2, sums_width)
-    fine_part, to_even, to_odd, up_sums = call(
+    conv_given, pad = call(
+        given_sums_body, [shape((count // 2, 14 * C)), shape((6, 6, bricks, WIDE))],
+        *crosses[::-1], merged, *sides, turned, mains, ends, lists,
+        scratch=[pltpu.VMEM((table_rows, width), BF)], flops=conv_flops,
+    )
+    up_lanes = sums_width - 14 * C
+    fine_part, to_even, to_odd, up_kept, given = call(
         side_grad_body,
-        [shape((bricks, width), F32), face_rows, face_rows, shape((count, sums_width - 14 * C), F32)],
-        ext_grad, lists, *cross_grads, *sides, parents,
+        [
+            shape((bricks, width), F32), face_rows, face_rows, shape((count // 2, up_lanes), F32),
+            shape(half_sums_dims),
+        ],
+        ext_grad, lists, *cross_grads, *sides, parents, conv_given,
+        scratch=[pltpu.VMEM((count, up_lanes), F32)],
     )
     side_grads = swap_pairs(to_even, to_odd, "gy")
-    given, pad = call(
-        given_sums_body, [shape(half_sums_dims), shape((6, 6, bricks, WIDE))],
-        *crosses[::-1], merged, *sides, turned, mains, ends, lists, up_sums,
-        scratch=[pltpu.VMEM((table_rows, width), BF)], flops=conv_flops,
-    )
-    (kept,) = call(kept_sums_body, [shape(half_sums_dims, F32)], pad, turned, up_sums, lists, flops=conv_flops)
+    (kept,) = call(kept_sums_body, [shape(half_sums_dims, F32)], pad, turned, up_kept, lists, flops=conv_flops)
     given = swap(given, "core", 0)
     (sums,) = call(pair_sum_body, [shape(half_sums_dims)], kept, given)
     sums = trade_rows(sums, ("x", "gy"))

time: 64.6 us -> 66.6 us (1.031)
  starting transfers between devices: 23 us -> 24.3 us
  waiting for transfers between devices: 10.4 us -> 11.1 us
    ppermute x10, starting transfers between devices: 9.1 us -> 11.8 us  [swap(): lax.ppermute(value, axis, [(i, i + 1) for i in lower] + [(i + 1, i) for i...]
    ppermute x10, waiting for transfers between devices: 4.99 us -> 7.23 us  [swap(): lax.ppermute(value, axis, [(i, i + 1) for i in lower] + [(i + 1, i) for i...]
    all_to_all x2, waiting for transfers between devices: 5.4 us -> 3.85 us  [trade_rows(): lax.all_to_all(grid_view, axes, split_axis=0, concat_axis=0, tiled=True)]
    all_to_all x2, starting transfers between devices: 13.9 us -> 12.6 us  [trade_rows(): lax.all_to_all(grid_view, axes, split_axis=0, concat_axis=0, tiled=True)]
  transfers between devices with their start and end apart: 12 -> 12, of which waited for: 7 -> 7; matrix products, arithmetic and copies ran while one was open for 0% -> 0% of each run, Pallas kernels for 11% -> 12%
where the time goes in v20:
time: 66.6 us; the launch traced here: 66.1 us
  starting transfers between devices  24.3 us (36%)
  blocking collectives  14.2 us (21%)
  Pallas kernels  13.3 us (20%)
  waiting for transfers between devices  11.1 us (17%)
  local copies, waits for them, and re-layouts  2.34 us (4%)
  between operations  0.82 us (1%)
    all_to_all x1, blocking collectives, trade_rows(): lax.all_to_all(grid_view, axes, split_axis=0, concat_axis=0, tiled=True)  14.2 us
    pallas_call x12, Pallas kernels, call(): pl.pallas_call(body, out_shape=tuple(outs), in_specs=[pl.BlockSpec(memory...  13.3 us
    all_to_all x2, starting transfers between devices, trade_rows(): lax.all_to_all(grid_view, axes, split_axis=0, concat_axis=0, tiled=True)  12.6 us
    ppermute x10, starting transfers between devices, swap(): lax.ppermute(value, axis, [(i, i + 1) for i in lower] + [(i + 1, i) for i...  11.8 us
    ppermute x10, waiting for transfers between devices, swap(): lax.ppermute(value, axis, [(i, i + 1) for i in lower] + [(i + 1, i) for i...  7.23 us
    all_to_all x2, waiting for transfers between devices, trade_rows(): lax.all_to_all(grid_view, axes, split_axis=0, concat_axis=0, tiled=True)  3.85 us
    unnamed x14, local copies, waits for them, and re-layouts  2.34 us
  transfers between devices with their start and end apart: 12, of which 7 were waited for; matrix products, arithmetic and copies ran while one was open for 0% of the time, Pallas kernels for 12%

profile of v20, /device:TPU:0, one launch (start us, length us, event | category | flops | bytes accessed | tf_op | source)
XLA Modules:
  0.0 66.1 jit_solution(10178888873751851973)
XLA Ops:
  0.6 0.0 copy-start.3
  0.6 1.9 %shard_map.137 = (bf16[128,512]{1,0:T(8,128)(2,1)}, s32[8,128]{1,0:T(8,128)}) custom-call(s32[4,16]{1,0:T(4,128)} %bitcast.35, bf16[64,1024]{1,0:T(8,128)(2,1)} %bitcast.39, s32[2,8]{1,0:T(2,128)} %bitcast.41, s32[2,8]{1,0:T(2,128)} %bitcast.42, s32[1,32]{1,0:T(1,128)} %bitcast.43), custom_call_target="tpu_custom_call" | custom-call | bytes 266752 | tf_op jit(solution)/shard_map/pallas_call | solution.py:50
  2.5 7.4 %all-to-all-start = ((bf16[16,8,512]{2,1,0:T(8,128)(2,1)}), bf16[16,8,512]{2,1,0:T(8,128)(2,1)S(1)}, u32[]{:S(2)}, u32[]{:S(2)}) async-start(bf16[16,8,512]{2,1,0:T(8,128)(2,1)} %bitcast.40), calls=%async_computation | async-start | bytes 262144 | tf_op jit(solution)/shard_map/all_to_all | solution.py:535
  9.9 0.0 copy-start.6
  9.9 0.0 copy-done.3
  9.9 0.7 copy-done.6
  10.6 0.0 copy-start.4
  10.6 0.9 %copy-done.4 = bf16[1,1,32,4096]{3,2,1,0:T(8,128)(2,1)S(1)} copy-done((bf16[1,1,32,4096]{3,2,1,0:T(8,128)(2,1)S(1)}, bf16[1,1,32,4096]{3,2,1,0:T(8,128)(2,1)}, u32[]{:S(2)}) %copy-start.4) | copy-done | bytes 262168
  11.5 0.7 %copy-done.5 = s32[1,1,32,27]{2,1,3,0:T(1,128)S(1)} copy-done((s32[1,1,32,27]{2,1,3,0:T(1,128)S(1)}, s32[1,1,32,27]{2,1,3,0:T(1,128)}, u32[]{:S(2)}) %copy-start.5) | copy-done | bytes 3480
  12.2 2.0 %shard_map.138 = (f32[48,4096]{1,0:T(8,128)S(1)}, bf16[8,4096]{1,0:T(8,128)(2,1)S(1)}, bf16[8,4096]{1,0:T(8,128)(2,1)S(1)}, bf16[256,512]{1,0:T(8,128)(2,1)S(1)}...) custom-call(bf16[32,4096]{1,0:T(8,128)(2,1)S(1)} %bitcast.37, ...), custom_call_target="tpu_custom_call" | custom-call | flops 1811939328 | bytes 1785728 | tf_op jit(solution)/shard_map/pallas_call | solution.py:50
  14.2 3.0 %all-to-all-done = bf16[16,8,512]{2,1,0:T(8,128)(2,1)S(1)} async-done(((bf16[16,8,512]{2,1,0:T(8,128)(2,1)}), bf16[16,8,512]{2,1,0:T(8,128)(2,1)S(1)}, u32[]{:S(2)}, u32[]{:S(2)}) %all-to-all-start) | async-done | bytes 131104 | tf_op jit(solution)/shard_map/all_to_all | solution.py:535
  17.2 0.0 copy-done
  17.2 0.0 copy-done.1
  17.2 0.6 shard_map.139
  17.9 0.7 %collective-permute-start = (bf16[8,5120]{1,0:T(8,128)(2,1)S(1)}, bf16[8,5120]{1,0:T(8,128)(2,1)S(1)}, u32[]{:S(2)}, u32[]{:S(2)}) collective-permute-start(bf16[8,5120]{1,0:T(8,128)(2,1)S(1)} %get-tuple-element.38), channel_id=1, source_target_pairs={{0,1},{2,3},{1,0},{3,2},{4,5},{6,7},{5,4},{7,6},{8,9},{10,11},{9,8... | collective-permute-start | bytes 245768 | tf_op jit(solution)/shard_map/ppermute | solution.py:524
  18.6 0.7 collective-permute-start.1
  19.2 3.1 %collective-permute-done.even_ref.even_side_ref = bf16[8,5120]{1,0:T(8,128)(2,1)S(1)} collective-permute-done((bf16[8,5120]{1,0:T(8,128)(2,1)S(1)}, bf16[8,5120]{1,0:T(8,128)(2,1)S(1)}, u32[]{:S(2)}, u32[]{:S(2)}) %collective-permute-start) | collective-permute-done | bytes 81952 | tf_op jit(solution)/shard_map/ppermute | solution.py:524
  22.4 0.0 collective-permute-done.1.odd_ref.odd_side_ref
  22.4 0.3 shard_map.140
  22.7 0.7 %collective-permute-start.2 = (bf16[8,4096]{1,0:T(8,128)(2,1)S(1)}, bf16[8,4096]{1,0:T(8,128)(2,1)S(1)}, u32[]{:S(2)}, u32[]{:S(2)}) collective-permute-start(bf16[8,4096]{1,0:T(8,128)(2,1)S(1)} %get-tuple-element.40), channel_id=1, source_target_pairs={{4,8},{8,4},{5,9},{9,5},{6,10},{10,6},{7,11},{11,7},{20,24},{24,20... | collective-permute-start | bytes 196616 | tf_op jit(solution)/shard_map/ppermute | solution.py:524
  23.4 2.4 %collective-permute-start.3 = (bf16[8,4096]{1,0:T(8,128)(2,1)S(1)}, bf16[8,4096]{1,0:T(8,128)(2,1)S(1)}, u32[]{:S(2)}, u32[]{:S(2)}) collective-permute-start(bf16[8,4096]{1,0:T(8,128)(2,1)S(1)} %get-tuple-element.41), channel_id=1, source_target_pairs={{0,4},{8,12},{4,0},{12,8},{1,5},{9,13},{5,1},{13,9},{2,6},{10,14},... | collective-permute-start | bytes 196616 | tf_op jit(solution)/shard_map/ppermute | solution.py:524
  25.8 0.1 collective-permute-start.4
  25.9 0.7 collective-permute-start.5
  26.5 0.0 collective-permute-done.2.odd_cross_ref
  26.5 0.2 collective-permute-done.3.even_cross_ref
  26.7 1.4 %shard_map.141 = (bf16[64,896]{1,0:T(8,128)(2,1)S(1)}, bf16[6,6,32,384]{3,2,1,0:T(8,128)(2,1)S(1)}) custom-call(bf16[8,4096]{1,0:T(8,128)(2,1)S(1)} %collective-permute-done.2.odd_cross_ref, bf16[8,4096]{1,0:T(8,128)(2,1)S(1)} %collective-permute-done.3.even_cross_ref, bf16[32,4096]{1,0:T(8,128)(2,1)S(1)} %get-tuple-element.37.merged_ref, ...), custom_call_target="tpu_custom_call" | custom-call | flops 905969664 | bytes 1933312 | tf_op jit(solution)/shard_map/pallas_call | solution.py:50
  28.1 0.0 collective-permute-done.4.even_grad_ref
  28.1 0.0 collective-permute-done.5.odd_grad_ref
  28.1 0.6 shard_map.143
  28.7 3.8 %collective-permute-start.8 = (bf16[64,1408]{1,0:T(8,128)(2,1)S(1)}, bf16[64,1408]{1,0:T(8,128)(2,1)S(1)}, u32[]{:S(2)}, u32[]{:S(2)}) collective-permute-start(bf16[64,1408]{1,0:T(8,128)(2,1)S(1)} %get-tuple-element.58), channel_id=1, source_target_pairs={{0,4},{4,0},{1,5},{5,1},{2,6},{6,2},{3,7},{7,3},{8,12},{12,8},{9,1... | collective-permute-start | bytes 540680 | tf_op jit(solution)/shard_map/ppermute | solution.py:524
  32.5 1.0 %shard_map.145.kept_ref = f32[64,1408]{1,0:T(8,128)S(1)} custom-call(bf16[6,6,32,384]{3,2,1,0:T(8,128)(2,1)S(1)} %get-tuple-element.45.pad_ref, bf16[256,512]{1,0:T(8,128)(2,1)S(1)} %get-tuple-element.42.turned_ref, f32[64,512]{1,0:T(8,128)S(1)} %get-tuple-element.57.up_kept_ref, s32[8,128]{1,0:T(8,128)S(1)} %get-tuple-element.36.lists_ref), custom_call_target="tpu_custom_call" | custom-call | flops 905969664 | bytes 1642496 | tf_op jit(solution)/shard_map/pallas_call | solution.py:50
  33.5 0.1 collective-permute-done.8.given_ref
  33.6 0.7 %shard_map.146 = bf16[64,1408]{1,0:T(8,128)(2,1)} custom-call(f32[64,1408]{1,0:T(8,128)S(1)} %shard_map.145.kept_ref, bf16[64,1408]{1,0:T(8,128)(2,1)S(1)} %collective-permute-done.8.given_ref), custom_call_target="tpu_custom_call" | custom-call | bytes 720896 | tf_op jit(solution)/shard_map/pallas_call | solution.py:50
  34.3 5.2 %all-to-all-start.1 = ((bf16[8,8,1408]{2,1,0:T(8,128)(2,1)}), bf16[8,8,1408]{2,1,0:T(8,128)(2,1)S(1)}, u32[]{:S(2)}, u32[]{:S(2)}) async-start(bf16[8,8,1408]{2,1,0:T(8,128)(2,1)} %bitcast.17), calls=%async_computation.1 | async-start | bytes 360448 | tf_op jit(solution)/shard_map/all_to_all | solution.py:535
  39.5 2.1 %collective-permute-start.6 = (bf16[8,4096]{1,0:T(8,128)(2,1)S(1)}, bf16[8,4096]{1,0:T(8,128)(2,1)S(1)}, u32[]{:S(2)}, u32[]{:S(2)}) collective-permute-start(bf16[8,4096]{1,0:T(8,128)(2,1)S(1)} %get-tuple-element.54), channel_id=1, source_target_pairs={{0,1},{2,3},{1,0},{3,2},{4,5},{6,7},{5,4},{7,6},{8,9},{10,11},{9,8... | collective-permute-start | bytes 196616 | tf_op jit(solution)/shard_map/ppermute | solution.py:524
  41.6 0.7 collective-permute-start.7
  42.3 2.2 %shard_map.142 = (bf16[32,4096]{1,0:T(8,128)(2,1)}, s32[8,128]{1,0:T(8,128)S(1)}) custom-call(bf16[6,6,32,384]{3,2,1,0:T(8,128)(2,1)S(1)} %get-tuple-element.45.pad_ref, bf16[27,64,64]{2,1,0:T(8,128)(2,1)S(1)} %copy-done.3, s32[8,128]{1,0:T(8,128)S(1)} %get-tuple-element.36.lists_ref), custom_call_target="tpu_custom_call" | custom-call | flops 905969664 | bytes 1376256 | tf_op jit(solution)/shard_map/pallas_call | solution.py:50
  44.5 2.2 %collective-permute-done.6.even_ref = bf16[8,4096]{1,0:T(8,128)(2,1)S(1)} collective-permute-done((bf16[8,4096]{1,0:T(8,128)(2,1)S(1)}, bf16[8,4096]{1,0:T(8,128)(2,1)S(1)}, u32[]{:S(2)}, u32[]{:S(2)}) %collective-permute-start.6) | collective-permute-done | bytes 65568 | tf_op jit(solution)/shard_map/ppermute | solution.py:524
  46.7 0.0 collective-permute-done.7.odd_ref
  46.7 1.1 %shard_map.144 = (bf16[32,4096]{1,0:T(8,128)(2,1)}, bf16[64,1024]{1,0:T(8,128)(2,1)S(1)}) custom-call(f32[32,4096]{1,0:T(8,128)S(1)} %get-tuple-element.52.part_ref, s32[8,128]{1,0:T(8,128)S(1)} %get-tuple-element.53.lists_ref, bf16[8,4096]{1,0:T(8,128)(2,1)S(1)} %collective-permute-done.6.even_ref, bf16[8,4096]{1,0:T(8,128)(2,1)S(1)} %collective-permute-done.7.odd_ref, ...), custom_call_target="tpu_custom_call" | custom-call | bytes 1183744 | tf_op jit(solution)/shard_map/pallas_call | solution.py:50
  47.8 0.8 %all-to-all-done.1 = bf16[8,8,1408]{2,1,0:T(8,128)(2,1)S(1)} async-done(((bf16[8,8,1408]{2,1,0:T(8,128)(2,1)}), bf16[8,8,1408]{2,1,0:T(8,128)(2,1)S(1)}, u32[]{:S(2)}, u32[]{:S(2)}) %all-to-all-start.1) | async-done | bytes 180256 | tf_op jit(solution)/shard_map/all_to_all | solution.py:535
  48.7 0.2 shard_map.147
  48.9 0.0 copy-start.2
  48.9 14.2 %all_to_all.15 = bf16[8,8,2432]{2,1,0:T(8,128)(2,1)S(1)} all-to-all(bf16[8,8,2432]{2,1,0:T(8,128)(2,1)S(1)} %bitcast.29), channel_id=1, replica_groups=mesh['groups'=2,'x'=2,'core'=2,'gy'=4] {'x','gy'}, dimensions={0} | all-to-all | bytes 622592 | tf_op jit(solution)/shard_map/all_to_all | solution.py:535
  63.1 0.0 collective-permute-start.9
  63.1 1.6 %collective-permute-done.9.given_ref = bf16[64,2432]{1,0:T(8,128)(2,1)S(1)} collective-permute-done((bf16[64,2432]{1,0:T(8,128)(2,1)S(1)}, bf16[64,2432]{1,0:T(8,128)(2,1)S(1)}, u32[]{:S(2)}, u32[]{:S(2)}) %collective-permute-start.9) | collective-permute-done | bytes 311328 | tf_op jit(solution)/shard_map/ppermute | solution.py:524
  64.7 0.0 copy-done.2
  64.7 1.4 %shard_map.148 = (f32[27,64,64]{2,1,0:T(8,128)}, f32[512,128]{1,0:T(8,128)}, bf16[64,1024]{1,0:T(8,128)(2,1)}) custom-call(bf16[64,2432]{1,0:T(8,128)(2,1)S(1)} %bitcast.28, bf16[64,2432]{1,0:T(8,128)(2,1)S(1)} %collective-permute-done.9.given_ref, s32[4,16]{1,0:T(4,128)S(1)} %bitcast.36, s32[8,128]{1,0:T(8,128)S(1)} %get-tuple-element.53.lists_ref), custom_call_target="tpu_custom_call" | custom-call | bytes 1462528 | tf_op jit(solution)/shard_map/pallas_call | solution.py:50
  (4 shorter events, 0.0 us)
Async XLA Ops:
  0.6 9.3 %copy-start.3 = (bf16[27,64,64]{2,1,0:T(8,128)(2,1)S(1)}, bf16[27,64,64]{2,1,0:T(8,128)(2,1)}, u32[]{:S(2)}) copy-start(bf16[27,64,64]{2,1,0:T(8,128)(2,1)} %weight_ref.3) | copy-start | bytes 663556
  2.5 14.7 %all-to-all-start = ((bf16[16,8,512]{2,1,0:T(8,128)(2,1)}), bf16[16,8,512]{2,1,0:T(8,128)(2,1)S(1)}, u32[]{:S(2)}, u32[]{:S(2)}) async-start(bf16[16,8,512]{2,1,0:T(8,128)(2,1)} %bitcast.40), calls=%async_computation | async-start | bytes 262144 | tf_op jit(solution)/shard_map/all_to_all | solution.py:535
  9.9 0.7 %copy-start.6 = (s32[8,128]{1,0:T(8,128)S(1)}, s32[8,128]{1,0:T(8,128)}, u32[]{:S(2)}) copy-start(s32[8,128]{1,0:T(8,128)} %get-tuple-element.35.lists_ref) | copy-start | bytes 12292
  10.6 0.9 %copy-start.4 = (bf16[1,1,32,4096]{3,2,1,0:T(8,128)(2,1)S(1)}, bf16[1,1,32,4096]{3,2,1,0:T(8,128)(2,1)}, u32[]{:S(2)}) copy-start(bf16[1,1,32,4096]{3,2,1,0:T(8,128)(2,1)} %param.19) | copy-start | bytes 786436
  11.5 0.7 %copy-start.5 = (s32[1,1,32,27]{2,1,3,0:T(1,128)S(1)}, s32[1,1,32,27]{2,1,3,0:T(1,128)}, u32[]{:S(2)}) copy-start(s32[1,1,32,27]{2,1,3,0:T(1,128)} %param.14) | copy-start | bytes 10372
  12.2 5.0 %copy-start = (bf16[8,128,64]{1,2,0:T(8,128)(2,1)S(1)}, bf16[8,128,64]{1,2,0:T(8,128)(2,1)}, u32[]{:S(2)}) copy-start(bf16[8,128,64]{1,2,0:T(8,128)(2,1)} %param.13) | copy-start | bytes 393220
  12.2 5.0 %copy-start.1 = (bf16[1,1,32,4096]{3,2,1,0:T(8,128)(2,1)S(1)}, bf16[1,1,32,4096]{3,2,1,0:T(8,128)(2,1)}, u32[]{:S(2)}) copy-start(bf16[1,1,32,4096]{3,2,1,0:T(8,128)(2,1)} %param.10) | copy-start | bytes 786436
  17.9 4.5 %collective-permute-start = (bf16[8,5120]{1,0:T(8,128)(2,1)S(1)}, bf16[8,5120]{1,0:T(8,128)(2,1)S(1)}, u32[]{:S(2)}, u32[]{:S(2)}) collective-permute-start(bf16[8,5120]{1,0:T(8,128)(2,1)S(1)} %get-tuple-element.38), channel_id=1, source_target_pairs={{0,1},{2,3},{1,0},{3,2},{4,5},{6,7},{5,4},{7,6},{8,9},{10,11},{9,8... | collective-permute-start | bytes 245768 | tf_op jit(solution)/shard_map/ppermute | solution.py:524
  18.6 3.8 %collective-permute-start.1 = (bf16[8,5120]{1,0:T(8,128)(2,1)S(1)}, bf16[8,5120]{1,0:T(8,128)(2,1)S(1)}, u32[]{:S(2)}, u32[]{:S(2)}) collective-permute-start(bf16[8,5120]{1,0:T(8,128)(2,1)S(1)} %get-tuple-element.39), channel_id=1, source_target_pairs={{1,2},{2,1},{5,6},{6,5},{9,10},{10,9},{13,14},{14,13},{17,18},{18,... | collective-permute-start | bytes 245768 | tf_op jit(solution)/shard_map/ppermute | solution.py:524
  22.7 3.8 %collective-permute-start.2 = (bf16[8,4096]{1,0:T(8,128)(2,1)S(1)}, bf16[8,4096]{1,0:T(8,128)(2,1)S(1)}, u32[]{:S(2)}, u32[]{:S(2)}) collective-permute-start(bf16[8,4096]{1,0:T(8,128)(2,1)S(1)} %get-tuple-element.40), channel_id=1, source_target_pairs={{4,8},{8,4},{5,9},{9,5},{6,10},{10,6},{7,11},{11,7},{20,24},{24,20... | collective-permute-start | bytes 196616 | tf_op jit(solution)/shard_map/ppermute | solution.py:524
  23.4 3.3 %collective-permute-start.3 = (bf16[8,4096]{1,0:T(8,128)(2,1)S(1)}, bf16[8,4096]{1,0:T(8,128)(2,1)S(1)}, u32[]{:S(2)}, u32[]{:S(2)}) collective-permute-start(bf16[8,4096]{1,0:T(8,128)(2,1)S(1)} %get-tuple-element.41), channel_id=1, source_target_pairs={{0,4},{8,12},{4,0},{12,8},{1,5},{9,13},{5,1},{13,9},{2,6},{10,14},... | collective-permute-start | bytes 196616 | tf_op jit(solution)/shard_map/ppermute | solution.py:524
  25.8 2.3 %collective-permute-start.4 = (bf16[8,4096]{1,0:T(8,128)(2,1)S(1)}, bf16[8,4096]{1,0:T(8,128)(2,1)S(1)}, u32[]{:S(2)}, u32[]{:S(2)}) collective-permute-start(bf16[8,4096]{1,0:T(8,128)(2,1)S(1)} %get-tuple-element.48), channel_id=1, source_target_pairs={{0,4},{8,12},{4,0},{12,8},{1,5},{9,13},{5,1},{13,9},{2,6},{10,14},... | collective-permute-start | bytes 196616 | tf_op jit(solution)/shard_map/ppermute | solution.py:524
  25.9 2.2 %collective-permute-start.5 = (bf16[8,4096]{1,0:T(8,128)(2,1)S(1)}, bf16[8,4096]{1,0:T(8,128)(2,1)S(1)}, u32[]{:S(2)}, u32[]{:S(2)}) collective-permute-start(bf16[8,4096]{1,0:T(8,128)(2,1)S(1)} %get-tuple-element.49), channel_id=1, source_target_pairs={{4,8},{8,4},{5,9},{9,5},{6,10},{10,6},{7,11},{11,7},{20,24},{24,20... | collective-permute-start | bytes 196616 | tf_op jit(solution)/shard_map/ppermute | solution.py:524
  28.7 4.9 %collective-permute-start.8 = (bf16[64,1408]{1,0:T(8,128)(2,1)S(1)}, bf16[64,1408]{1,0:T(8,128)(2,1)S(1)}, u32[]{:S(2)}, u32[]{:S(2)}) collective-permute-start(bf16[64,1408]{1,0:T(8,128)(2,1)S(1)} %get-tuple-element.58), channel_id=1, source_target_pairs={{0,4},{4,0},{1,5},{5,1},{2,6},{6,2},{3,7},{7,3},{8,12},{12,8},{9,1... | collective-permute-start | bytes 540680 | tf_op jit(solution)/shard_map/ppermute | solution.py:524
  34.3 14.4 %all-to-all-start.1 = ((bf16[8,8,1408]{2,1,0:T(8,128)(2,1)}), bf16[8,8,1408]{2,1,0:T(8,128)(2,1)S(1)}, u32[]{:S(2)}, u32[]{:S(2)}) async-start(bf16[8,8,1408]{2,1,0:T(8,128)(2,1)} %bitcast.17), calls=%async_computation.1 | async-start | bytes 360448 | tf_op jit(solution)/shard_map/all_to_all | solution.py:535
  39.5 7.2 %collective-permute-start.6 = (bf16[8,4096]{1,0:T(8,128)(2,1)S(1)}, bf16[8,4096]{1,0:T(8,128)(2,1)S(1)}, u32[]{:S(2)}, u32[]{:S(2)}) collective-permute-start(bf16[8,4096]{1,0:T(8,128)(2,1)S(1)} %get-tuple-element.54), channel_id=1, source_target_pairs={{0,1},{2,3},{1,0},{3,2},{4,5},{6,7},{5,4},{7,6},{8,9},{10,11},{9,8... | collective-permute-start | bytes 196616 | tf_op jit(solution)/shard_map/ppermute | solution.py:524
  41.6 5.1 %collective-permute-start.7 = (bf16[8,4096]{1,0:T(8,128)(2,1)S(1)}, bf16[8,4096]{1,0:T(8,128)(2,1)S(1)}, u32[]{:S(2)}, u32[]{:S(2)}) collective-permute-start(bf16[8,4096]{1,0:T(8,128)(2,1)S(1)} %get-tuple-element.55), channel_id=1, source_target_pairs={{1,2},{2,1},{5,6},{6,5},{9,10},{10,9},{13,14},{14,13},{17,18},{18,... | collective-permute-start | bytes 196616 | tf_op jit(solution)/shard_map/ppermute | solution.py:524
  48.9 15.8 %copy-start.2 = (s32[1,1,16,4]{2,3,1,0:T(4,128)S(1)}, s32[1,1,16,4]{2,3,1,0:T(4,128)}, u32[]{:S(2)}) copy-start(s32[1,1,16,4]{2,3,1,0:T(4,128)} %param.18) | copy-start | bytes 772
  63.1 1.6 %collective-permute-start.9 = (bf16[64,2432]{1,0:T(8,128)(2,1)S(1)}, bf16[64,2432]{1,0:T(8,128)(2,1)S(1)}, u32[]{:S(2)}, u32[]{:S(2)}) collective-permute-start(bf16[64,2432]{1,0:T(8,128)(2,1)S(1)} %bitcast.27), channel_id=1, source_target_pairs={{0,4},{4,0},{1,5},{5,1},{2,6},{6,2},{3,7},{7,3},{8,12},{12,8},{9,1... | collective-permute-start | bytes 933896 | tf_op jit(solution)/shard_map/ppermute | solution.py:524

commit v21 on v16

--- a/solution.py
+++ b/solution.py
@@ -434,14 +434,16 @@
     pieces = both_lanes // 2 // half
     capacity, group = chip_slots(count, pieces, across)
     slots = slots_of(lists_ref, bricks)
-    row = iota((count, bricks), 0)
+    slots = jnp.concatenate([slots, slots], axis=1)
+    stacked = jnp.concatenate([items[:, :half], items[:, half:]], axis=0)
+    row = iota((count, 2 * bricks), 0)
+    half_of = iota((count, 2 * bricks), 1) // bricks
     for other in range(2):
         owner = device_of(row // group, lists_ref, other, across)
         for j in range(pieces):
             piece = row % group * pieces + j
             named = owner * capacity + piece // 2 == slots
-            rows = dot(ones_where(named & (piece % 2 == 0)), items[:, :half])
-            rows += dot(ones_where(named & (piece % 2 == 1)), items[:, half:])
+            rows = dot(ones_where(named & (piece % 2 == half_of)), stacked)
             at = (other * pieces + j) * half
             replies_ref[:, at : at + half] = rows.astype(BF)
 

time: 64.6 us -> 64.5 us (level)
  no operation moved by 1% of the time
where the time goes in v21:
time: 64.5 us; the launch traced here: 63.9 us
  starting transfers between devices  23 us (36%)
  blocking collectives  14.1 us (22%)
  Pallas kernels  13.2 us (20%)
  waiting for transfers between devices  10.5 us (16%)
  local copies, waits for them, and re-layouts  2.34 us (4%)
  between operations  0.81 us (1%)
    all_to_all x1, blocking collectives, trade_rows(): lax.all_to_all(grid_view, axes, split_axis=0, concat_axis=0, tiled=True)  14.1 us
    all_to_all x2, starting transfers between devices, trade_rows(): lax.all_to_all(grid_view, axes, split_axis=0, concat_axis=0, tiled=True)  13.9 us
    pallas_call x12, Pallas kernels, call(): pl.pallas_call(body, out_shape=tuple(outs), in_specs=[pl.BlockSpec(memory...  13.2 us
    ppermute x10, starting transfers between devices, swap(): lax.ppermute(value, axis, [(i, i + 1) for i in lower] + [(i + 1, i) for i...  9.1 us
    all_to_all x2, waiting for transfers between devices, trade_rows(): lax.all_to_all(grid_view, axes, split_axis=0, concat_axis=0, tiled=True)  5.48 us
    ppermute x10, waiting for transfers between devices, swap(): lax.ppermute(value, axis, [(i, i + 1) for i in lower] + [(i + 1, i) for i...  4.99 us
    unnamed x14, local copies, waits for them, and re-layouts  2.34 us
  transfers between devices with their start and end apart: 12, of which 7 were waited for; matrix products, arithmetic and copies ran while one was open for 0% of the time, Pallas kernels for 11%

profile of v21, /device:TPU:0, one launch (start us, length us, event | category | flops | bytes accessed | tf_op | source)
XLA Modules:
  0.0 63.9 jit_solution(3812178528017542091)
XLA Ops:
  0.6 0.0 copy-start.3
  0.6 1.9 %shard_map.137 = (bf16[128,512]{1,0:T(8,128)(2,1)}, s32[8,128]{1,0:T(8,128)}) custom-call(s32[4,16]{1,0:T(4,128)} %bitcast.35, bf16[64,1024]{1,0:T(8,128)(2,1)} %bitcast.39, s32[2,8]{1,0:T(2,128)} %bitcast.41, s32[2,8]{1,0:T(2,128)} %bitcast.42, s32[1,32]{1,0:T(1,128)} %bitcast.43), custom_call_target="tpu_custom_call" | custom-call | bytes 266752 | tf_op jit(solution)/shard_map/pallas_call | solution.py:50
  2.5 7.4 %all-to-all-start = ((bf16[16,8,512]{2,1,0:T(8,128)(2,1)}), bf16[16,8,512]{2,1,0:T(8,128)(2,1)S(1)}, u32[]{:S(2)}, u32[]{:S(2)}) async-start(bf16[16,8,512]{2,1,0:T(8,128)(2,1)} %bitcast.40), calls=%async_computation | async-start | bytes 262144 | tf_op jit(solution)/shard_map/all_to_all | solution.py:534
  9.9 0.0 copy-start.6
  9.9 0.0 copy-done.3
  9.9 0.7 %copy-done.6 = s32[8,128]{1,0:T(8,128)S(1)} copy-done((s32[8,128]{1,0:T(8,128)S(1)}, s32[8,128]{1,0:T(8,128)}, u32[]{:S(2)}) %copy-start.6) | copy-done | bytes 4120
  10.6 0.0 copy-start.4
  10.6 0.9 %copy-done.4 = bf16[1,1,32,4096]{3,2,1,0:T(8,128)(2,1)S(1)} copy-done((bf16[1,1,32,4096]{3,2,1,0:T(8,128)(2,1)S(1)}, bf16[1,1,32,4096]{3,2,1,0:T(8,128)(2,1)}, u32[]{:S(2)}) %copy-start.4) | copy-done | bytes 262168
  11.5 0.7 %copy-done.5 = s32[1,1,32,27]{2,1,3,0:T(1,128)S(1)} copy-done((s32[1,1,32,27]{2,1,3,0:T(1,128)S(1)}, s32[1,1,32,27]{2,1,3,0:T(1,128)}, u32[]{:S(2)}) %copy-start.5) | copy-done | bytes 3480
  12.2 2.0 %shard_map.138 = (f32[48,4096]{1,0:T(8,128)S(1)}, bf16[8,4096]{1,0:T(8,128)(2,1)S(1)}, bf16[8,4096]{1,0:T(8,128)(2,1)S(1)}, bf16[256,512]{1,0:T(8,128)(2,1)S(1)}...) custom-call(bf16[32,4096]{1,0:T(8,128)(2,1)S(1)} %bitcast.37, ...), custom_call_target="tpu_custom_call" | custom-call | flops 1811939328 | bytes 1785728 | tf_op jit(solution)/shard_map/pallas_call | solution.py:50
  14.2 3.0 %all-to-all-done = bf16[16,8,512]{2,1,0:T(8,128)(2,1)S(1)} async-done(((bf16[16,8,512]{2,1,0:T(8,128)(2,1)}), bf16[16,8,512]{2,1,0:T(8,128)(2,1)S(1)}, u32[]{:S(2)}, u32[]{:S(2)}) %all-to-all-start) | async-done | bytes 131104 | tf_op jit(solution)/shard_map/all_to_all | solution.py:534
  17.2 0.0 copy-done
  17.2 0.0 copy-done.1
  17.2 0.6 shard_map.139
  17.9 0.7 %collective-permute-start = (bf16[8,5120]{1,0:T(8,128)(2,1)S(1)}, bf16[8,5120]{1,0:T(8,128)(2,1)S(1)}, u32[]{:S(2)}, u32[]{:S(2)}) collective-permute-start(bf16[8,5120]{1,0:T(8,128)(2,1)S(1)} %get-tuple-element.37), channel_id=1, source_target_pairs={{0,1},{2,3},{1,0},{3,2},{4,5},{6,7},{5,4},{7,6},{8,9},{10,11},{9,8... | collective-permute-start | bytes 245768 | tf_op jit(solution)/shard_map/ppermute | solution.py:523
  18.6 0.7 %collective-permute-start.1 = (bf16[8,5120]{1,0:T(8,128)(2,1)S(1)}, bf16[8,5120]{1,0:T(8,128)(2,1)S(1)}, u32[]{:S(2)}, u32[]{:S(2)}) collective-permute-start(bf16[8,5120]{1,0:T(8,128)(2,1)S(1)} %get-tuple-element.38), channel_id=1, source_target_pairs={{1,2},{2,1},{5,6},{6,5},{9,10},{10,9},{13,14},{14,13},{17,18},{18,... | collective-permute-start | bytes 245768 | tf_op jit(solution)/shard_map/ppermute | solution.py:523
  19.2 0.1 collective-permute-start.4
  19.3 0.7 %collective-permute-start.5 = (bf16[8,4096]{1,0:T(8,128)(2,1)S(1)}, bf16[8,4096]{1,0:T(8,128)(2,1)S(1)}, u32[]{:S(2)}, u32[]{:S(2)}) collective-permute-start(bf16[8,4096]{1,0:T(8,128)(2,1)S(1)} %get-tuple-element.46), channel_id=1, source_target_pairs={{4,8},{8,4},{5,9},{9,5},{6,10},{10,6},{7,11},{11,7},{20,24},{24,20... | collective-permute-start | bytes 196616 | tf_op jit(solution)/shard_map/ppermute | solution.py:523
  20.0 2.4 %collective-permute-done.even_ref.even_side_ref = bf16[8,5120]{1,0:T(8,128)(2,1)S(1)} collective-permute-done((bf16[8,5120]{1,0:T(8,128)(2,1)S(1)}, bf16[8,5120]{1,0:T(8,128)(2,1)S(1)}, u32[]{:S(2)}, u32[]{:S(2)}) %collective-permute-start) | collective-permute-done | bytes 81952 | tf_op jit(solution)/shard_map/ppermute | solution.py:523
  22.4 0.0 collective-permute-done.1.odd_ref.odd_side_ref
  22.4 0.3 shard_map.140
  22.7 0.7 %collective-permute-start.2 = (bf16[8,4096]{1,0:T(8,128)(2,1)S(1)}, bf16[8,4096]{1,0:T(8,128)(2,1)S(1)}, u32[]{:S(2)}, u32[]{:S(2)}) collective-permute-start(bf16[8,4096]{1,0:T(8,128)(2,1)S(1)} %get-tuple-element.39), channel_id=1, source_target_pairs={{4,8},{8,4},{5,9},{9,5},{6,10},{10,6},{7,11},{11,7},{20,24},{24,20... | collective-permute-start | bytes 196616 | tf_op jit(solution)/shard_map/ppermute | solution.py:523
  23.4 2.4 %collective-permute-start.3 = (bf16[8,4096]{1,0:T(8,128)(2,1)S(1)}, bf16[8,4096]{1,0:T(8,128)(2,1)S(1)}, u32[]{:S(2)}, u32[]{:S(2)}) collective-permute-start(bf16[8,4096]{1,0:T(8,128)(2,1)S(1)} %get-tuple-element.40), channel_id=1, source_target_pairs={{0,4},{8,12},{4,0},{12,8},{1,5},{9,13},{5,1},{13,9},{2,6},{10,14},... | collective-permute-start | bytes 196616 | tf_op jit(solution)/shard_map/ppermute | solution.py:523
  25.8 0.0 collective-permute-done.4.even_grad_ref
  25.8 0.0 collective-permute-done.5.odd_grad_ref
  25.8 0.6 shard_map.141
  26.4 0.0 collective-permute-done.2.odd_cross_ref
  26.4 0.3 collective-permute-done.3.even_cross_ref
  26.7 1.4 %shard_map.142 = (bf16[64,1408]{1,0:T(8,128)(2,1)S(1)}, bf16[6,6,32,384]{3,2,1,0:T(8,128)(2,1)S(1)}) custom-call(bf16[8,4096]{1,0:T(8,128)(2,1)S(1)} %collective-permute-done.2.odd_cross_ref, bf16[8,4096]{1,0:T(8,128)(2,1)S(1)} %collective-permute-done.3.even_cross_ref, bf16[32,4096]{1,0:T(8,128)(2,1)S(1)} %get-tuple-element.36.merged_ref, ...), custom_call_target="tpu_custom_call" | custom-call | flops 905969664 | bytes 2260992 | tf_op jit(solution)/shard_map/pallas_call | solution.py:50
  28.1 1.2 %collective-permute-start.8 = (bf16[64,1408]{1,0:T(8,128)(2,1)S(1)}, bf16[64,1408]{1,0:T(8,128)(2,1)S(1)}, u32[]{:S(2)}, u32[]{:S(2)}) collective-permute-start(bf16[64,1408]{1,0:T(8,128)(2,1)S(1)} %get-tuple-element.56), channel_id=1, source_target_pairs={{0,4},{4,0},{1,5},{5,1},{2,6},{6,2},{3,7},{7,3},{8,12},{12,8},{9,1... | collective-permute-start | bytes 540680 | tf_op jit(solution)/shard_map/ppermute | solution.py:523
  29.4 0.9 %shard_map.145.kept_ref = f32[64,1408]{1,0:T(8,128)S(1)} custom-call(bf16[6,6,32,384]{3,2,1,0:T(8,128)(2,1)S(1)} %get-tuple-element.49.pad_ref, bf16[256,512]{1,0:T(8,128)(2,1)S(1)} %get-tuple-element.41.turned_ref, f32[128,512]{1,0:T(8,128)S(1)} %get-tuple-element.48.up_sums_ref, s32[8,128]{1,0:T(8,128)S(1)} %get-tuple-element.35.lists_ref), custom_call_target="tpu_custom_call" | custom-call | flops 905969664 | bytes 1773568 | tf_op jit(solution)/shard_map/pallas_call | solution.py:50
  30.3 0.1 collective-permute-done.8.given_ref
  30.4 0.7 %shard_map.146 = bf16[64,1408]{1,0:T(8,128)(2,1)} custom-call(f32[64,1408]{1,0:T(8,128)S(1)} %shard_map.145.kept_ref, bf16[64,1408]{1,0:T(8,128)(2,1)S(1)} %collective-permute-done.8.given_ref), custom_call_target="tpu_custom_call" | custom-call | bytes 720896 | tf_op jit(solution)/shard_map/pallas_call | solution.py:50
  31.1 6.6 %all-to-all-start.1 = ((bf16[8,8,1408]{2,1,0:T(8,128)(2,1)}), bf16[8,8,1408]{2,1,0:T(8,128)(2,1)S(1)}, u32[]{:S(2)}, u32[]{:S(2)}) async-start(bf16[8,8,1408]{2,1,0:T(8,128)(2,1)} %bitcast.17), calls=%async_computation.1 | async-start | bytes 360448 | tf_op jit(solution)/shard_map/all_to_all | solution.py:534
  37.7 2.0 %collective-permute-start.6 = (bf16[8,4096]{1,0:T(8,128)(2,1)S(1)}, bf16[8,4096]{1,0:T(8,128)(2,1)S(1)}, u32[]{:S(2)}, u32[]{:S(2)}) collective-permute-start(bf16[8,4096]{1,0:T(8,128)(2,1)S(1)} %get-tuple-element.53), channel_id=1, source_target_pairs={{0,1},{2,3},{1,0},{3,2},{4,5},{6,7},{5,4},{7,6},{8,9},{10,11},{9,8... | collective-permute-start | bytes 196616 | tf_op jit(solution)/shard_map/ppermute | solution.py:523
  39.7 0.7 %collective-permute-start.7 = (bf16[8,4096]{1,0:T(8,128)(2,1)S(1)}, bf16[8,4096]{1,0:T(8,128)(2,1)S(1)}, u32[]{:S(2)}, u32[]{:S(2)}) collective-permute-start(bf16[8,4096]{1,0:T(8,128)(2,1)S(1)} %get-tuple-element.54), channel_id=1, source_target_pairs={{1,2},{2,1},{5,6},{6,5},{9,10},{10,9},{13,14},{14,13},{17,18},{18,... | collective-permute-start | bytes 196616 | tf_op jit(solution)/shard_map/ppermute | solution.py:523
  40.4 2.2 %shard_map.143 = (bf16[32,4096]{1,0:T(8,128)(2,1)}, s32[8,128]{1,0:T(8,128)S(1)}) custom-call(bf16[6,6,32,384]{3,2,1,0:T(8,128)(2,1)S(1)} %get-tuple-element.49.pad_ref, bf16[27,64,64]{2,1,0:T(8,128)(2,1)S(1)} %copy-done.3, s32[8,128]{1,0:T(8,128)S(1)} %get-tuple-element.35.lists_ref), custom_call_target="tpu_custom_call" | custom-call | flops 905969664 | bytes 1376256 | tf_op jit(solution)/shard_map/pallas_call | solution.py:50
  42.6 0.6 collective-permute-done.6.even_ref
  43.2 0.0 collective-permute-done.7.odd_ref
  43.2 1.0 %shard_map.144 = (bf16[32,4096]{1,0:T(8,128)(2,1)}, bf16[64,1024]{1,0:T(8,128)(2,1)S(1)}) custom-call(f32[32,4096]{1,0:T(8,128)S(1)} %get-tuple-element.51.part_ref, s32[8,128]{1,0:T(8,128)S(1)} %get-tuple-element.52.lists_ref, bf16[8,4096]{1,0:T(8,128)(2,1)S(1)} %collective-permute-done.6.even_ref, bf16[8,4096]{1,0:T(8,128)(2,1)S(1)} %collective-permute-done.7.odd_ref, ...), custom_call_target="tpu_custom_call" | custom-call | bytes 1183744 | tf_op jit(solution)/shard_map/pallas_call | solution.py:50
  44.2 2.5 %all-to-all-done.1 = bf16[8,8,1408]{2,1,0:T(8,128)(2,1)S(1)} async-done(((bf16[8,8,1408]{2,1,0:T(8,128)(2,1)}), bf16[8,8,1408]{2,1,0:T(8,128)(2,1)S(1)}, u32[]{:S(2)}, u32[]{:S(2)}) %all-to-all-start.1) | async-done | bytes 180256 | tf_op jit(solution)/shard_map/all_to_all | solution.py:534
  46.7 0.2 shard_map.147
  46.9 0.0 copy-start.2
  46.9 14.1 %all_to_all.15 = bf16[8,8,2432]{2,1,0:T(8,128)(2,1)S(1)} all-to-all(bf16[8,8,2432]{2,1,0:T(8,128)(2,1)S(1)} %bitcast.29), channel_id=1, replica_groups=mesh['groups'=2,'x'=2,'core'=2,'gy'=4] {'x','gy'}, dimensions={0} | all-to-all | bytes 622592 | tf_op jit(solution)/shard_map/all_to_all | solution.py:534
  61.0 0.0 collective-permute-start.9
  61.0 1.6 %collective-permute-done.9.given_ref = bf16[64,2432]{1,0:T(8,128)(2,1)S(1)} collective-permute-done((bf16[64,2432]{1,0:T(8,128)(2,1)S(1)}, bf16[64,2432]{1,0:T(8,128)(2,1)S(1)}, u32[]{:S(2)}, u32[]{:S(2)}) %collective-permute-start.9) | collective-permute-done | bytes 311328 | tf_op jit(solution)/shard_map/ppermute | solution.py:523
  62.6 0.0 copy-done.2
  62.6 1.4 %shard_map.148 = (f32[27,64,64]{2,1,0:T(8,128)}, f32[512,128]{1,0:T(8,128)}, bf16[64,1024]{1,0:T(8,128)(2,1)}) custom-call(bf16[64,2432]{1,0:T(8,128)(2,1)S(1)} %bitcast.28, bf16[64,2432]{1,0:T(8,128)(2,1)S(1)} %collective-permute-done.9.given_ref, s32[4,16]{1,0:T(4,128)S(1)} %bitcast.36, s32[8,128]{1,0:T(8,128)S(1)} %get-tuple-element.52.lists_ref), custom_call_target="tpu_custom_call" | custom-call | bytes 1462528 | tf_op jit(solution)/shard_map/pallas_call | solution.py:50
  (4 shorter events, 0.0 us)
Async XLA Ops:
  0.6 9.3 %copy-start.3 = (bf16[27,64,64]{2,1,0:T(8,128)(2,1)S(1)}, bf16[27,64,64]{2,1,0:T(8,128)(2,1)}, u32[]{:S(2)}) copy-start(bf16[27,64,64]{2,1,0:T(8,128)(2,1)} %weight_ref.3) | copy-start | bytes 663556
  2.5 14.7 %all-to-all-start = ((bf16[16,8,512]{2,1,0:T(8,128)(2,1)}), bf16[16,8,512]{2,1,0:T(8,128)(2,1)S(1)}, u32[]{:S(2)}, u32[]{:S(2)}) async-start(bf16[16,8,512]{2,1,0:T(8,128)(2,1)} %bitcast.40), calls=%async_computation | async-start | bytes 262144 | tf_op jit(solution)/shard_map/all_to_all | solution.py:534
  9.9 0.7 %copy-start.6 = (s32[8,128]{1,0:T(8,128)S(1)}, s32[8,128]{1,0:T(8,128)}, u32[]{:S(2)}) copy-start(s32[8,128]{1,0:T(8,128)} %get-tuple-element.34.lists_ref) | copy-start | bytes 12292
  10.6 0.9 %copy-start.4 = (bf16[1,1,32,4096]{3,2,1,0:T(8,128)(2,1)S(1)}, bf16[1,1,32,4096]{3,2,1,0:T(8,128)(2,1)}, u32[]{:S(2)}) copy-start(bf16[1,1,32,4096]{3,2,1,0:T(8,128)(2,1)} %param.19) | copy-start | bytes 786436
  11.5 0.7 %copy-start.5 = (s32[1,1,32,27]{2,1,3,0:T(1,128)S(1)}, s32[1,1,32,27]{2,1,3,0:T(1,128)}, u32[]{:S(2)}) copy-start(s32[1,1,32,27]{2,1,3,0:T(1,128)} %param.14) | copy-start | bytes 10372
  12.2 5.0 %copy-start = (bf16[8,128,64]{1,2,0:T(8,128)(2,1)S(1)}, bf16[8,128,64]{1,2,0:T(8,128)(2,1)}, u32[]{:S(2)}) copy-start(bf16[8,128,64]{1,2,0:T(8,128)(2,1)} %param.13) | copy-start | bytes 393220
  12.2 5.0 %copy-start.1 = (bf16[1,1,32,4096]{3,2,1,0:T(8,128)(2,1)S(1)}, bf16[1,1,32,4096]{3,2,1,0:T(8,128)(2,1)}, u32[]{:S(2)}) copy-start(bf16[1,1,32,4096]{3,2,1,0:T(8,128)(2,1)} %param.10) | copy-start | bytes 786436
  17.9 4.5 %collective-permute-start = (bf16[8,5120]{1,0:T(8,128)(2,1)S(1)}, bf16[8,5120]{1,0:T(8,128)(2,1)S(1)}, u32[]{:S(2)}, u32[]{:S(2)}) collective-permute-start(bf16[8,5120]{1,0:T(8,128)(2,1)S(1)} %get-tuple-element.37), channel_id=1, source_target_pairs={{0,1},{2,3},{1,0},{3,2},{4,5},{6,7},{5,4},{7,6},{8,9},{10,11},{9,8... | collective-permute-start | bytes 245768 | tf_op jit(solution)/shard_map/ppermute | solution.py:523
  18.6 3.8 %collective-permute-start.1 = (bf16[8,5120]{1,0:T(8,128)(2,1)S(1)}, bf16[8,5120]{1,0:T(8,128)(2,1)S(1)}, u32[]{:S(2)}, u32[]{:S(2)}) collective-permute-start(bf16[8,5120]{1,0:T(8,128)(2,1)S(1)} %get-tuple-element.38), channel_id=1, source_target_pairs={{1,2},{2,1},{5,6},{6,5},{9,10},{10,9},{13,14},{14,13},{17,18},{18,... | collective-permute-start | bytes 245768 | tf_op jit(solution)/shard_map/ppermute | solution.py:523
  19.2 6.6 %collective-permute-start.4 = (bf16[8,4096]{1,0:T(8,128)(2,1)S(1)}, bf16[8,4096]{1,0:T(8,128)(2,1)S(1)}, u32[]{:S(2)}, u32[]{:S(2)}) collective-permute-start(bf16[8,4096]{1,0:T(8,128)(2,1)S(1)} %get-tuple-element.45), channel_id=1, source_target_pairs={{0,4},{8,12},{4,0},{12,8},{1,5},{9,13},{5,1},{13,9},{2,6},{10,14},... | collective-permute-start | bytes 196616 | tf_op jit(solution)/shard_map/ppermute | solution.py:523
  19.3 6.5 %collective-permute-start.5 = (bf16[8,4096]{1,0:T(8,128)(2,1)S(1)}, bf16[8,4096]{1,0:T(8,128)(2,1)S(1)}, u32[]{:S(2)}, u32[]{:S(2)}) collective-permute-start(bf16[8,4096]{1,0:T(8,128)(2,1)S(1)} %get-tuple-element.46), channel_id=1, source_target_pairs={{4,8},{8,4},{5,9},{9,5},{6,10},{10,6},{7,11},{11,7},{20,24},{24,20... | collective-permute-start | bytes 196616 | tf_op jit(solution)/shard_map/ppermute | solution.py:523
  22.7 3.7 %collective-permute-start.2 = (bf16[8,4096]{1,0:T(8,128)(2,1)S(1)}, bf16[8,4096]{1,0:T(8,128)(2,1)S(1)}, u32[]{:S(2)}, u32[]{:S(2)}) collective-permute-start(bf16[8,4096]{1,0:T(8,128)(2,1)S(1)} %get-tuple-element.39), channel_id=1, source_target_pairs={{4,8},{8,4},{5,9},{9,5},{6,10},{10,6},{7,11},{11,7},{20,24},{24,20... | collective-permute-start | bytes 196616 | tf_op jit(solution)/shard_map/ppermute | solution.py:523
  23.4 3.3 %collective-permute-start.3 = (bf16[8,4096]{1,0:T(8,128)(2,1)S(1)}, bf16[8,4096]{1,0:T(8,128)(2,1)S(1)}, u32[]{:S(2)}, u32[]{:S(2)}) collective-permute-start(bf16[8,4096]{1,0:T(8,128)(2,1)S(1)} %get-tuple-element.40), channel_id=1, source_target_pairs={{0,4},{8,12},{4,0},{12,8},{1,5},{9,13},{5,1},{13,9},{2,6},{10,14},... | collective-permute-start | bytes 196616 | tf_op jit(solution)/shard_map/ppermute | solution.py:523
  28.1 2.3 %collective-permute-start.8 = (bf16[64,1408]{1,0:T(8,128)(2,1)S(1)}, bf16[64,1408]{1,0:T(8,128)(2,1)S(1)}, u32[]{:S(2)}, u32[]{:S(2)}) collective-permute-start(bf16[64,1408]{1,0:T(8,128)(2,1)S(1)} %get-tuple-element.56), channel_id=1, source_target_pairs={{0,4},{4,0},{1,5},{5,1},{2,6},{6,2},{3,7},{7,3},{8,12},{12,8},{9,1... | collective-permute-start | bytes 540680 | tf_op jit(solution)/shard_map/ppermute | solution.py:523
  31.1 15.6 %all-to-all-start.1 = ((bf16[8,8,1408]{2,1,0:T(8,128)(2,1)}), bf16[8,8,1408]{2,1,0:T(8,128)(2,1)S(1)}, u32[]{:S(2)}, u32[]{:S(2)}) async-start(bf16[8,8,1408]{2,1,0:T(8,128)(2,1)} %bitcast.17), calls=%async_computation.1 | async-start | bytes 360448 | tf_op jit(solution)/shard_map/all_to_all | solution.py:534
  37.7 5.5 %collective-permute-start.6 = (bf16[8,4096]{1,0:T(8,128)(2,1)S(1)}, bf16[8,4096]{1,0:T(8,128)(2,1)S(1)}, u32[]{:S(2)}, u32[]{:S(2)}) collective-permute-start(bf16[8,4096]{1,0:T(8,128)(2,1)S(1)} %get-tuple-element.53), channel_id=1, source_target_pairs={{0,1},{2,3},{1,0},{3,2},{4,5},{6,7},{5,4},{7,6},{8,9},{10,11},{9,8... | collective-permute-start | bytes 196616 | tf_op jit(solution)/shard_map/ppermute | solution.py:523
  39.7 3.5 %collective-permute-start.7 = (bf16[8,4096]{1,0:T(8,128)(2,1)S(1)}, bf16[8,4096]{1,0:T(8,128)(2,1)S(1)}, u32[]{:S(2)}, u32[]{:S(2)}) collective-permute-start(bf16[8,4096]{1,0:T(8,128)(2,1)S(1)} %get-tuple-element.54), channel_id=1, source_target_pairs={{1,2},{2,1},{5,6},{6,5},{9,10},{10,9},{13,14},{14,13},{17,18},{18,... | collective-permute-start | bytes 196616 | tf_op jit(solution)/shard_map/ppermute | solution.py:523
  46.9 15.7 %copy-start.2 = (s32[1,1,16,4]{2,3,1,0:T(4,128)S(1)}, s32[1,1,16,4]{2,3,1,0:T(4,128)}, u32[]{:S(2)}) copy-start(s32[1,1,16,4]{2,3,1,0:T(4,128)} %param.18) | copy-start | bytes 772
  61.0 1.6 %collective-permute-start.9 = (bf16[64,2432]{1,0:T(8,128)(2,1)S(1)}, bf16[64,2432]{1,0:T(8,128)(2,1)S(1)}, u32[]{:S(2)}, u32[]{:S(2)}) collective-permute-start(bf16[64,2432]{1,0:T(8,128)(2,1)S(1)} %bitcast.27), channel_id=1, source_target_pairs={{0,4},{4,0},{1,5},{5,1},{2,6},{6,2},{3,7},{7,3},{8,12},{12,8},{9,1... | collective-permute-start | bytes 933896 | tf_op jit(solution)/shard_map/ppermute | solution.py:523
